TPU v7x, 32 devices: a whole 2x2x4 slice. The times are simulated.
32 devices in a mesh: gx: 8 (over z, x), gy: 4 (over y, core).
Axes of the slice: x: 2, y: 2, z: 4, core: 2. Of those that a mesh axis runs over, the one named last changes fastest.
Arguments:
- position: float32 [2, 64, 64, 128], P(None, 'gx', 'gy'), may hold values from 0 to 1
- velocity: float32 [2, 64, 64, 128], P(None, 'gx', 'gy'), may hold values from -12 to 12
- volume: float32 [64, 64, 128], P('gx', 'gy'), may hold values from 0.5 to 2
- pressure_prev: float32 [64, 64, 128], P('gx', 'gy'), may hold values from -6 to 6
- fill: int32 [64, 64], P('gx', 'gy'), may hold values from 1 to 128, as said below
- drift_from: int32 [64, 64], P('gx', 'gy'), may hold values from 0 to 8
Outputs:
- pressure: float32 [64, 64, 128], P('gx', 'gy')
- velocity_new: float32 [2, 64, 64, 128], P(None, 'gx', 'gy')
Inputs may be any that keep to these rules, and one draw needn't show every extreme that they name: fill lies in 1 to 128, and some bin holds 128 live particles. `drift_from`: code c names the bin at offset (c // 3 - 1, c % 3 - 1).
All inputs are finite; a program needn't handle non-finite values. Where the computation divides by a largest or mean magnitude, that divisor is 1e-20 or more.
Results may differ from a plain program's by a relative error of at most 0.0035.
Values may be sent and summed in bfloat16 or wider, within the bound.
No kernel may reach another device: no remote copies, remote signals or barrier semaphores. Data moves between devices by JAX's collectives and lax.ppermute only.
A program may use at most 256 MiB of HBM per device.

v0:
```python
import jax
import jax.numpy as jnp
import numpy as np
from jax import lax
from jax.sharding import PartitionSpec as P

SWEEPS = 4


cfl_number = 0.25
speed_eps = 1e-06
soft_sq = 0.01
shift_term = 1.0


def with_halo(shard, sides, width):
    for axis, dim in sides:
        devices, length = (lax.axis_size(axis), shard.shape[dim])
        up = [(i, (i + 1) % devices) for i in range(devices - 1)]
        down = [(j, i) for i, j in up]
        last = lax.slice_in_dim(shard, length - width, length, axis=dim)
        leading = lax.slice_in_dim(shard, 0, width, axis=dim)
        before = lax.ppermute(last, axis, up)
        after = lax.ppermute(leading, axis, down)
        shard = jnp.concatenate([before, shard, after], axis=dim)
    return shard


def drift_bins(extended, codes, step):
    rows = codes.shape[0]
    cols = codes.shape[1]
    result = jnp.zeros((extended.shape[0], rows, cols, extended.shape[3]), extended.dtype)
    for offset in range(9):
        shift_x = offset // 3
        shift_y = offset % 3
        source = extended[:, shift_x : shift_x + rows, shift_y : shift_y + cols, :]
        moved_x = source[0] + float(shift_x - 1) + step * source[2]
        moved_y = source[1] + float(shift_y - 1) + step * source[3]
        moved = jnp.concatenate([moved_x[None], moved_y[None], source[2:]], axis=0)
        chosen = (codes == offset + 1)[None, :, :, None]
        result = result + jnp.where(chosen, moved, 0.0)
    return result


def gather_row(extended, row, cols):
    axis_pos = extended.ndim - 3
    block = lax.dynamic_slice_in_dim(extended, row, 3, axis=axis_pos)
    center = block[..., 1, 1 : 1 + cols, :]
    pieces = [block[..., code // 3, code % 3 : code % 3 + cols, :] for code in range(9)]
    beside_all = jnp.stack(pieces, axis=-2)
    beside_all = beside_all.reshape(beside_all.shape[:-2] + (9 * beside_all.shape[-1],))
    return (center, beside_all)


def geometry(center, beside_all):
    width = center.shape[-1]
    off_x = jnp.asarray(np.repeat(np.arange(9) // 3 - 1, width).astype(np.float32))
    off_y = jnp.asarray(np.repeat(np.arange(9) % 3 - 1, width).astype(np.float32))
    delta_x = center[0][:, :, None] - (beside_all[0][:, None, :] + off_x)
    delta_y = center[1][:, :, None] - (beside_all[1][:, None, :] + off_y)
    dist_sq = delta_x * delta_x + delta_y * delta_y
    remain = jnp.maximum(1.0 - jnp.sqrt(dist_sq), 0.0)
    cubed = remain * remain * remain
    return (delta_x, delta_y, dist_sq, cubed)


def first_pass(center, beside_all, kappa):
    delta_x, delta_y, dist_sq, cubed = geometry(center, beside_all)
    lap = kappa * 40.0 * beside_all[4][:, None, :] * dist_sq * cubed / (dist_sq + soft_sq)
    coef = lap.astype(jnp.bfloat16)
    den = shift_term + jnp.sum(coef.astype(jnp.float32), axis=-1)
    grad_w = 20.0 * cubed * beside_all[4][:, None, :]
    flow = (beside_all[2][:, None, :] - center[2][:, :, None]) * delta_x + (
        beside_all[3][:, None, :] - center[3][:, :, None]
    ) * delta_y
    source = kappa * jnp.sum(grad_w * flow, axis=-1)
    return (coef, source, den)


def push_row(center, beside_all, center_p, around_p, kappa):
    delta_x, delta_y, dist_sq, cubed = geometry(center, beside_all)
    weight = 20.0 * cubed * beside_all[4][:, None, :]
    diff = around_p.astype(jnp.float32)[:, None, :] - center_p.astype(jnp.float32)[:, :, None]
    grad_x = -jnp.sum(weight * diff * delta_x, axis=-1)
    grad_y = -jnp.sum(weight * diff * delta_y, axis=-1)
    alive = (center[4] > 0.0).astype(jnp.float32)
    return jnp.stack([(center[2] - kappa * grad_x) * alive, (center[3] - kappa * grad_y) * alive])


def pressure_cycle(values):
    return with_halo(values, (("gx", 0), ("gy", 1)), 1)


def local(position, velocity, volume, pressure_prev, fill, drift_from):
    width = position.shape[3]
    rows = position.shape[1]
    cols = position.shape[2]
    slots = jnp.arange(width, dtype=jnp.int32)
    live = (slots[None, None, :] < fill[:, :, None]).astype(jnp.float32)
    held = volume * live
    local_top = jnp.max(jnp.abs(velocity) * live[None])
    top = lax.pmax(local_top, ("gx", "gy"))
    step = cfl_number / (top + speed_eps)
    old = jnp.concatenate([position, velocity, held[None], pressure_prev[None]], axis=0)
    codes = drift_from + 1
    around_old = with_halo(old, (("gx", 1), ("gy", 2)), 1)
    fresh = drift_bins(around_old, codes, step)
    ext = with_halo(fresh, (("gx", 1), ("gy", 2)), 1)
    fresh_center = ext[:, 1:-1, 1:-1, :]
    kappa = 1.0 / width
    row_ids = jnp.arange(rows, dtype=jnp.int32)

    def setup(row):
        center, beside_all = gather_row(ext, row, cols)
        return first_pass(center, beside_all, kappa)

    coef_all, source, den = lax.map(setup, row_ids)
    press = fresh_center[5]
    for sweep in range(SWEEPS):
        if sweep == 0:
            pext = ext[5].astype(jnp.bfloat16)
        else:
            pext = pressure_cycle(press.astype(jnp.bfloat16))

        def relax_kept(items):
            row, coef = items
            center_p, around_p = gather_row(pext, row, cols)
            return jnp.einsum("yij,yj->yi", coef, around_p, preferred_element_type=jnp.float32)

        totals = lax.map(relax_kept, (row_ids, coef_all))
        press = (source + totals) / den
    alive = (fresh_center[4] > 0.0).astype(jnp.float32)
    pressure = press * alive
    final_ext = pressure_cycle(press.astype(jnp.bfloat16))

    def update(row):
        center, beside_all = gather_row(ext, row, cols)
        center_p, around_p = gather_row(final_ext, row, cols)
        return push_row(center, beside_all, center_p, around_p, kappa)

    moved = lax.map(update, row_ids)
    velocity_new = jnp.transpose(moved, (1, 0, 2, 3))
    return (pressure, velocity_new)


def solution(mesh):
    return jax.shard_map(
        local,
        mesh=mesh,
        in_specs=(
            P(None, "gx", "gy", None),
            P(None, "gx", "gy", None),
            P("gx", "gy", None),
            P("gx", "gy", None),
            P("gx", "gy"),
            P("gx", "gy"),
        ),
        out_specs=(P("gx", "gy", None), P(None, "gx", "gy", None)),
        check_vma=False,
    )
```

profile of v0, /device:TPU:17, one launch (start us, length us, event | category | flops | bytes accessed | tf_op | source)
XLA Modules:
  0.0 631.7 jit_solution(12656542321908731131)
XLA Ops:
  3.1 39.9 %pmax.7 = f32[]{:T(128)} all-reduce(f32[]{:T(128)} %multiply_reduce_fusion), channel_id=1, replica_groups=mesh['gx'=8,'gy'=4] {'gx','gy'}, use_global_device_ids=true, to_apply=%region_1.0 | all-reduce | flops 1 | bytes 8 | tf_op jit(solution)/shard_map/pmax | solution.py:102
  89.6 177.6 %while.70 = (s32[]{:T(128)}, bf16[8,16,128,1152]{3,2,1,0:T(8,128)(2,1)}, f32[8,16,128]{2,1,0:T(8,128)S(1)}, f32[8,16,128]{2,1,0:T(8,128)S(1)}, s32[8]{0:T(128)S(...) while((s32[]{:T(128)}, ...), condition=%wide.region_5.6_spmd.clone, body=%wide.region_2.5_spmd.sunk.clone.sunk | while | flops 89726984 | bytes 9021247 | solution.py:117
  92.5 11.2 %convert_reduce_fusion.2 = (f32[16,128]{1,0:T(8,128)S(1)}, f32[16,128]{1,0:T(8,128)S(1)}) fusion(f32[16,1152]{1,0:T(8,128)S(1)} %bitcast.663, f32[16,1152]{1,0:T(8,128)S(1)} %bitcast_add_fusion.7, f32[16,128]{1,0:T(8,128)S(1)} %get-tuple-element.619, f32[16,1152]{1,0:T(8,128)S(1)} %bitcast_add_fusion.8, f32[16,128]{1,0:T(8,128)S(1)} %get-tuple-element.621, ...), kind=kLoop, calls=%fused_computation.111.clone.1 | loop fusion | flops 56619008 | bytes 491520 | tf_op jit(solution)/shard_map/while/body/eval_jaxpr/reduce_sum | solution.py:71
  114.7 11.2 %convert_reduce_fusion.2 = (f32[16,128]{1,0:T(8,128)S(1)}, f32[16,128]{1,0:T(8,128)S(1)}) fusion(f32[16,1152]{1,0:T(8,128)S(1)} %bitcast.663, f32[16,1152]{1,0:T(8,128)S(1)} %bitcast_add_fusion.7, f32[16,128]{1,0:T(8,128)S(1)} %get-tuple-element.619, f32[16,1152]{1,0:T(8,128)S(1)} %bitcast_add_fusion.8, f32[16,128]{1,0:T(8,128)S(1)} %get-tuple-element.621, ...), kind=kLoop, calls=%fused_computation.111.clone.1 | loop fusion | flops 56619008 | bytes 491520 | tf_op jit(solution)/shard_map/while/body/eval_jaxpr/reduce_sum | solution.py:71
  136.9 11.2 %convert_reduce_fusion.2 = (f32[16,128]{1,0:T(8,128)S(1)}, f32[16,128]{1,0:T(8,128)S(1)}) fusion(f32[16,1152]{1,0:T(8,128)S(1)} %bitcast.663, f32[16,1152]{1,0:T(8,128)S(1)} %bitcast_add_fusion.7, f32[16,128]{1,0:T(8,128)S(1)} %get-tuple-element.619, f32[16,1152]{1,0:T(8,128)S(1)} %bitcast_add_fusion.8, f32[16,128]{1,0:T(8,128)S(1)} %get-tuple-element.621, ...), kind=kLoop, calls=%fused_computation.111.clone.1 | loop fusion | flops 56619008 | bytes 491520 | tf_op jit(solution)/shard_map/while/body/eval_jaxpr/reduce_sum | solution.py:71
  159.1 11.2 %convert_reduce_fusion.2 = (f32[16,128]{1,0:T(8,128)S(1)}, f32[16,128]{1,0:T(8,128)S(1)}) fusion(f32[16,1152]{1,0:T(8,128)S(1)} %bitcast.663, f32[16,1152]{1,0:T(8,128)S(1)} %bitcast_add_fusion.7, f32[16,128]{1,0:T(8,128)S(1)} %get-tuple-element.619, f32[16,1152]{1,0:T(8,128)S(1)} %bitcast_add_fusion.8, f32[16,128]{1,0:T(8,128)S(1)} %get-tuple-element.621, ...), kind=kLoop, calls=%fused_computation.111.clone.1 | loop fusion | flops 56619008 | bytes 491520 | tf_op jit(solution)/shard_map/while/body/eval_jaxpr/reduce_sum | solution.py:71
  181.3 11.2 %convert_reduce_fusion.2 = (f32[16,128]{1,0:T(8,128)S(1)}, f32[16,128]{1,0:T(8,128)S(1)}) fusion(f32[16,1152]{1,0:T(8,128)S(1)} %bitcast.663, f32[16,1152]{1,0:T(8,128)S(1)} %bitcast_add_fusion.7, f32[16,128]{1,0:T(8,128)S(1)} %get-tuple-element.619, f32[16,1152]{1,0:T(8,128)S(1)} %bitcast_add_fusion.8, f32[16,128]{1,0:T(8,128)S(1)} %get-tuple-element.621, ...), kind=kLoop, calls=%fused_computation.111.clone.1 | loop fusion | flops 56619008 | bytes 491520 | tf_op jit(solution)/shard_map/while/body/eval_jaxpr/reduce_sum | solution.py:71
  192.5 8.1 %fusion.179 = bf16[8,16,128,1152]{3,2,1,0:T(8,128)(2,1)} fusion(bf16[8,16,128,1152]{3,2,1,0:T(8,128)(2,1)} %get-tuple-element.663, s32[]{:T(128)} %get-tuple-element.662, f32[16,1152]{1,0:T(8,128)S(1)} %bitcast_add_fusion.7, f32[16,128]{1,0:T(8,128)S(1)} %get-tuple-element.619, f32[16,1152]{1,0:T(8,128)S(1)} %bitcast_add_fusion.8, ...), kind=kLoop, calls=%fused_computation.114.clone.1 | loop fusion | flops 33030144 | bytes 4956672 | tf_op jit(solution)/shard_map/while/body/jit(dynamic_update_index_in_dim)/dynamic_update_slice | solution.py:117
  203.5 11.2 %convert_reduce_fusion.2 = (f32[16,128]{1,0:T(8,128)S(1)}, f32[16,128]{1,0:T(8,128)S(1)}) fusion(f32[16,1152]{1,0:T(8,128)S(1)} %bitcast.663, f32[16,1152]{1,0:T(8,128)S(1)} %bitcast_add_fusion.7, f32[16,128]{1,0:T(8,128)S(1)} %get-tuple-element.619, f32[16,1152]{1,0:T(8,128)S(1)} %bitcast_add_fusion.8, f32[16,128]{1,0:T(8,128)S(1)} %get-tuple-element.621, ...), kind=kLoop, calls=%fused_computation.111.clone.1 | loop fusion | flops 56619008 | bytes 491520 | tf_op jit(solution)/shard_map/while/body/eval_jaxpr/reduce_sum | solution.py:71
  225.7 11.2 %convert_reduce_fusion.2 = (f32[16,128]{1,0:T(8,128)S(1)}, f32[16,128]{1,0:T(8,128)S(1)}) fusion(f32[16,1152]{1,0:T(8,128)S(1)} %bitcast.663, f32[16,1152]{1,0:T(8,128)S(1)} %bitcast_add_fusion.7, f32[16,128]{1,0:T(8,128)S(1)} %get-tuple-element.619, f32[16,1152]{1,0:T(8,128)S(1)} %bitcast_add_fusion.8, f32[16,128]{1,0:T(8,128)S(1)} %get-tuple-element.621, ...), kind=kLoop, calls=%fused_computation.111.clone.1 | loop fusion | flops 56619008 | bytes 491520 | tf_op jit(solution)/shard_map/while/body/eval_jaxpr/reduce_sum | solution.py:71
  247.9 11.2 %convert_reduce_fusion.2 = (f32[16,128]{1,0:T(8,128)S(1)}, f32[16,128]{1,0:T(8,128)S(1)}) fusion(f32[16,1152]{1,0:T(8,128)S(1)} %bitcast.663, f32[16,1152]{1,0:T(8,128)S(1)} %bitcast_add_fusion.7, f32[16,128]{1,0:T(8,128)S(1)} %get-tuple-element.619, f32[16,1152]{1,0:T(8,128)S(1)} %bitcast_add_fusion.8, f32[16,128]{1,0:T(8,128)S(1)} %get-tuple-element.621, ...), kind=kLoop, calls=%fused_computation.111.clone.1 | loop fusion | flops 56619008 | bytes 491520 | tf_op jit(solution)/shard_map/while/body/eval_jaxpr/reduce_sum | solution.py:71
  267.2 53.1 %while.66 = (s32[]{:T(128)}, f32[8,16,128]{2,1,0:T(8,128)S(1)}, bf16[8,16,128,1152]{3,2,1,0:T(8,128)(2,1)}, s32[8]{0:T(128)S(1)}, bf16[10,18,128]{2,1,0:T(8,128)...) while((s32[]{:T(128)}, f32[8,16,128]{2,1,0:T(8,128)S(1)}, ...), condition=%wide.region_7.8_spmd, body=%wide.region_6.7_spmd.sunk | while | flops 4718601 | bytes 5001987 | solution.py:130
  335.6 53.1 %while.67 = (s32[]{:T(128)}, f32[8,16,128]{2,1,0:T(8,128)S(1)}, bf16[8,16,128,1152]{3,2,1,0:T(8,128)(2,1)}, s32[8]{0:T(128)S(1)}, bf16[10,18,128]{2,1,0:T(8,128)...) while((s32[]{:T(128)}, f32[8,16,128]{2,1,0:T(8,128)S(1)}, ...), condition=%wide.region_9.10_spmd, body=%wide.region_8.9_spmd.sunk | while | flops 4718601 | bytes 5001987 | solution.py:130
  404.0 53.1 %while.68 = (s32[]{:T(128)}, f32[8,16,128]{2,1,0:T(8,128)S(1)}, bf16[8,16,128,1152]{3,2,1,0:T(8,128)(2,1)}, s32[8]{0:T(128)S(1)}, bf16[10,18,128]{2,1,0:T(8,128)...) while((s32[]{:T(128)}, f32[8,16,128]{2,1,0:T(8,128)S(1)}, ...), condition=%wide.region_11.12_spmd, body=%wide.region_10.11_spmd.sunk | while | flops 4718601 | bytes 5001987 | solution.py:130
  472.4 53.1 %while.69 = (s32[]{:T(128)}, f32[8,16,128]{2,1,0:T(8,128)S(1)}, bf16[8,16,128,1152]{3,2,1,0:T(8,128)(2,1)}, s32[8]{0:T(128)S(1)}, bf16[10,18,128]{2,1,0:T(8,128)...) while((s32[]{:T(128)}, f32[8,16,128]{2,1,0:T(8,128)S(1)}, ...), condition=%wide.region_13.14_spmd, body=%wide.region_12.13_spmd.sunk | while | flops 4718601 | bytes 5001987 | solution.py:130
  541.5 89.6 %while.71 = (s32[]{:T(128)}, f32[8,2,16,128]{3,2,0,1:T(8,128)S(1)}, s32[8]{0:T(128)S(1)}, f32[6,10,18,128]{3,2,1,0:T(8,128)S(1)}, bf16[10,18,128]{2,1,0:T(8,128)...) while((s32[]{:T(128)}, f32[8,2,16,128]{3,2,0,1:T(8,128)S(1)}, ...), condition=%wide.region_17.18_spmd.clone, body=%wide.region_14.17_spmd.sunk.clone.sunk | while | flops 37842952 | bytes 2880931 | solution.py:141
  544.4 8.1 %fusion.190 = (f32[16,128]{1,0:T(8,128)S(1)}, f32[16,128]{1,0:T(8,128)S(1)}) fusion(f32[16,128]{1,0:T(8,128)S(1)} %bitcast_convert_fusion.2, f32[16,1152]{1,0:T(8,128)S(1)} %copy_bitcast_fusion.7, f32[16,1152]{1,0:T(8,128)S(1)} %bitcast.674, f32[16,1152]{1,0:T(8,128)S(1)} %get-tuple-element.640, f32[16,128]{1,0:T(8,128)S(1)} %get-tuple-element.641, ...), kind=kLoop, calls=%fused_computation.156.clone.1 | loop fusion | flops 37744640 | bytes 335872 | tf_op jit(solution)/shard_map/while/body/eval_jaxpr/reduce_sum | solution.py:84
  555.6 8.1 %fusion.190 = (f32[16,128]{1,0:T(8,128)S(1)}, f32[16,128]{1,0:T(8,128)S(1)}) fusion(f32[16,128]{1,0:T(8,128)S(1)} %bitcast_convert_fusion.2, f32[16,1152]{1,0:T(8,128)S(1)} %copy_bitcast_fusion.7, f32[16,1152]{1,0:T(8,128)S(1)} %bitcast.674, f32[16,1152]{1,0:T(8,128)S(1)} %get-tuple-element.640, f32[16,128]{1,0:T(8,128)S(1)} %get-tuple-element.641, ...), kind=kLoop, calls=%fused_computation.156.clone.1 | loop fusion | flops 37744640 | bytes 335872 | tf_op jit(solution)/shard_map/while/body/eval_jaxpr/reduce_sum | solution.py:84
  566.8 8.1 %fusion.190 = (f32[16,128]{1,0:T(8,128)S(1)}, f32[16,128]{1,0:T(8,128)S(1)}) fusion(f32[16,128]{1,0:T(8,128)S(1)} %bitcast_convert_fusion.2, f32[16,1152]{1,0:T(8,128)S(1)} %copy_bitcast_fusion.7, f32[16,1152]{1,0:T(8,128)S(1)} %bitcast.674, f32[16,1152]{1,0:T(8,128)S(1)} %get-tuple-element.640, f32[16,128]{1,0:T(8,128)S(1)} %get-tuple-element.641, ...), kind=kLoop, calls=%fused_computation.156.clone.1 | loop fusion | flops 37744640 | bytes 335872 | tf_op jit(solution)/shard_map/while/body/eval_jaxpr/reduce_sum | solution.py:84
  578.0 8.1 %fusion.190 = (f32[16,128]{1,0:T(8,128)S(1)}, f32[16,128]{1,0:T(8,128)S(1)}) fusion(f32[16,128]{1,0:T(8,128)S(1)} %bitcast_convert_fusion.2, f32[16,1152]{1,0:T(8,128)S(1)} %copy_bitcast_fusion.7, f32[16,1152]{1,0:T(8,128)S(1)} %bitcast.674, f32[16,1152]{1,0:T(8,128)S(1)} %get-tuple-element.640, f32[16,128]{1,0:T(8,128)S(1)} %get-tuple-element.641, ...), kind=kLoop, calls=%fused_computation.156.clone.1 | loop fusion | flops 37744640 | bytes 335872 | tf_op jit(solution)/shard_map/while/body/eval_jaxpr/reduce_sum | solution.py:84
  589.2 8.1 %fusion.190 = (f32[16,128]{1,0:T(8,128)S(1)}, f32[16,128]{1,0:T(8,128)S(1)}) fusion(f32[16,128]{1,0:T(8,128)S(1)} %bitcast_convert_fusion.2, f32[16,1152]{1,0:T(8,128)S(1)} %copy_bitcast_fusion.7, f32[16,1152]{1,0:T(8,128)S(1)} %bitcast.674, f32[16,1152]{1,0:T(8,128)S(1)} %get-tuple-element.640, f32[16,128]{1,0:T(8,128)S(1)} %get-tuple-element.641, ...), kind=kLoop, calls=%fused_computation.156.clone.1 | loop fusion | flops 37744640 | bytes 335872 | tf_op jit(solution)/shard_map/while/body/eval_jaxpr/reduce_sum | solution.py:84
  600.4 8.1 %fusion.190 = (f32[16,128]{1,0:T(8,128)S(1)}, f32[16,128]{1,0:T(8,128)S(1)}) fusion(f32[16,128]{1,0:T(8,128)S(1)} %bitcast_convert_fusion.2, f32[16,1152]{1,0:T(8,128)S(1)} %copy_bitcast_fusion.7, f32[16,1152]{1,0:T(8,128)S(1)} %bitcast.674, f32[16,1152]{1,0:T(8,128)S(1)} %get-tuple-element.640, f32[16,128]{1,0:T(8,128)S(1)} %get-tuple-element.641, ...), kind=kLoop, calls=%fused_computation.156.clone.1 | loop fusion | flops 37744640 | bytes 335872 | tf_op jit(solution)/shard_map/while/body/eval_jaxpr/reduce_sum | solution.py:84
  611.6 8.1 %fusion.190 = (f32[16,128]{1,0:T(8,128)S(1)}, f32[16,128]{1,0:T(8,128)S(1)}) fusion(f32[16,128]{1,0:T(8,128)S(1)} %bitcast_convert_fusion.2, f32[16,1152]{1,0:T(8,128)S(1)} %copy_bitcast_fusion.7, f32[16,1152]{1,0:T(8,128)S(1)} %bitcast.674, f32[16,1152]{1,0:T(8,128)S(1)} %get-tuple-element.640, f32[16,128]{1,0:T(8,128)S(1)} %get-tuple-element.641, ...), kind=kLoop, calls=%fused_computation.156.clone.1 | loop fusion | flops 37744640 | bytes 335872 | tf_op jit(solution)/shard_map/while/body/eval_jaxpr/reduce_sum | solution.py:84
  622.8 8.1 %fusion.190 = (f32[16,128]{1,0:T(8,128)S(1)}, f32[16,128]{1,0:T(8,128)S(1)}) fusion(f32[16,128]{1,0:T(8,128)S(1)} %bitcast_convert_fusion.2, f32[16,1152]{1,0:T(8,128)S(1)} %copy_bitcast_fusion.7, f32[16,1152]{1,0:T(8,128)S(1)} %bitcast.674, f32[16,1152]{1,0:T(8,128)S(1)} %get-tuple-element.640, f32[16,128]{1,0:T(8,128)S(1)} %get-tuple-element.641, ...), kind=kLoop, calls=%fused_computation.156.clone.1 | loop fusion | flops 37744640 | bytes 335872 | tf_op jit(solution)/shard_map/while/body/eval_jaxpr/reduce_sum | solution.py:84
  (1016 shorter events, 334.0 us)
Async XLA Ops:
  48.1 7.7 %collective-permute-start = (f32[6,1,16,128]{3,2,1,0:T(8,128)S(1)}, f32[6,1,16,128]{3,2,1,0:T(8,128)S(1)}, u32[]{:S(2)}, u32[]{:S(2)}) collective-permute-start(f32[6,1,16,128]{3,2,1,0:T(8,128)S(1)} %get-tuple-element.374), channel_id=1, source_target_pairs={{0,4},{4,8},{8,12},{12,16},{16,20},{20,24},{24,28},{1,5},{5,9},{9,... | collective-permute-start | bytes 147464 | tf_op jit(solution)/shard_map/ppermute | solution.py:23
  51.0 5.0 collective-permute-start.1
  57.1 11.2 %collective-permute-start.2 = (f32[6,10,1,128]{3,2,1,0:T(1,128)S(1)}, f32[6,10,1,128]{3,2,1,0:T(1,128)S(1)}, u32[]{:S(2)}, u32[]{:S(2)}) collective-permute-start(f32[6,10,1,128]{3,2,1,0:T(1,128)S(1)} %get-tuple-element.371), channel_id=1, source_target_pairs={{0,1},{1,2},{2,3},{4,5},{5,6},{6,7},{8,9},{9,10},{10,11},{12,13},{... | collective-permute-start | bytes 92168 | tf_op jit(solution)/shard_map/ppermute | solution.py:23
  62.9 5.4 collective-permute-start.3
  70.4 6.8 %collective-permute-start.4 = (f32[6,1,16,128]{3,2,1,0:T(8,128)S(1)}, f32[6,1,16,128]{3,2,1,0:T(8,128)S(1)}, u32[]{:S(2)}, u32[]{:S(2)}) collective-permute-start(f32[6,1,16,128]{3,2,1,0:T(8,128)S(1)} %get-tuple-element.372), channel_id=1, source_target_pairs={{0,4},{4,8},{8,12},{12,16},{16,20},{20,24},{24,28},{1,5},{5,9},{9,... | collective-permute-start | bytes 147464 | tf_op jit(solution)/shard_map/ppermute | solution.py:23
  74.2 4.8 collective-permute-start.5
  79.1 7.0 %collective-permute-start.6 = (f32[6,10,1,128]{3,2,1,0:T(1,128)S(1)}, f32[6,10,1,128]{3,2,1,0:T(1,128)S(1)}, u32[]{:S(2)}, u32[]{:S(2)}) collective-permute-start(f32[6,10,1,128]{3,2,1,0:T(1,128)S(1)} %get-tuple-element.366), channel_id=1, source_target_pairs={{0,1},{1,2},{2,3},{4,5},{5,6},{6,7},{8,9},{9,10},{10,11},{12,13},{... | collective-permute-start | bytes 92168 | tf_op jit(solution)/shard_map/ppermute | solution.py:23
  84.2 5.2 collective-permute-start.7
  320.3 6.2 collective-permute-start.8
  322.9 4.4 collective-permute-start.9
  327.3 5.3 collective-permute-start.10
  330.6 4.9 collective-permute-start.11
  388.7 6.5 %collective-permute-start.12 = (bf16[1,16,128]{2,1,0:T(8,128)(2,1)S(1)}, bf16[1,16,128]{2,1,0:T(8,128)(2,1)S(1)}, u32[]{:S(2)}, u32[]{:S(2)}) collective-permute-start(bf16[1,16,128]{2,1,0:T(8,128)(2,1)S(1)} %get-tuple-element.390), channel_id=1, source_target_pairs={{0,4},{4,8},{8,12},{12,16},{16,20},{20,24},{24,28},{1,5},{5,9},{9,... | collective-permute-start | bytes 12296 | tf_op jit(solution)/shard_map/ppermute | solution.py:23
  391.3 4.7 collective-permute-start.13
  395.9 5.0 collective-permute-start.14
  399.0 4.9 collective-permute-start.15
  457.1 6.5 %collective-permute-start.16 = (bf16[1,16,128]{2,1,0:T(8,128)(2,1)S(1)}, bf16[1,16,128]{2,1,0:T(8,128)(2,1)S(1)}, u32[]{:S(2)}, u32[]{:S(2)}) collective-permute-start(bf16[1,16,128]{2,1,0:T(8,128)(2,1)S(1)} %get-tuple-element.388), channel_id=1, source_target_pairs={{0,4},{4,8},{8,12},{12,16},{16,20},{20,24},{24,28},{1,5},{5,9},{9,... | collective-permute-start | bytes 12296 | tf_op jit(solution)/shard_map/ppermute | solution.py:23
  459.7 4.7 collective-permute-start.17
  464.4 5.0 collective-permute-start.18
  467.4 4.9 collective-permute-start.19
  526.2 6.5 %collective-permute-start.20 = (bf16[1,16,128]{2,1,0:T(8,128)(2,1)S(1)}, bf16[1,16,128]{2,1,0:T(8,128)(2,1)S(1)}, u32[]{:S(2)}, u32[]{:S(2)}) collective-permute-start(bf16[1,16,128]{2,1,0:T(8,128)(2,1)S(1)} %get-tuple-element.386), channel_id=1, source_target_pairs={{0,4},{4,8},{8,12},{12,16},{16,20},{20,24},{24,28},{1,5},{5,9},{9,... | collective-permute-start | bytes 12296 | tf_op jit(solution)/shard_map/ppermute | solution.py:23
  528.7 4.7 collective-permute-start.21
  533.4 5.2 collective-permute-start.22
  536.5 4.9 collective-permute-start.23
  (6 other events, 386.0 us)
where the time goes:
time: 641 us; the launch traced here: 632 us
  other arithmetic  235 us (37%)
  matrix products  121 us (19%)
  loops' own time  93.3 us (15%)
  starting transfers between devices  73.6 us (11%)
  local copies, waits for them, and re-layouts  46.5 us (7%)
  blocking collectives  39.9 us (6%)
  waiting for transfers between devices  20.1 us (3%)
    dot_general x32, matrix products, relax_kept(): jnp.einsum('yij,yj->yi', coef, around_p, preferred_element_type=jnp.float32)  121 us
    reduce_sum x8, other arithmetic, first_pass(): den = shift_term + jnp.sum(coef.astype(jnp.float32), axis=-1)  89.3 us
    reduce_sum x8, other arithmetic, push_row(): grad_x = -jnp.sum(weight * diff * delta_x, axis=-1)  65.1 us
    dynamic_update_slice x16, other arithmetic, local(): coef_all, source, den = lax.map(setup, row_ids)  64.7 us
    another operation x4, loops' own time, local(): totals = lax.map(relax_kept, (row_ids, coef_all))  63.7 us
    ppermute x12, starting transfers between devices, with_halo(): before = lax.ppermute(last, axis, up)  40.3 us
    pmax x1, blocking collectives, local(): top = lax.pmax(local_top, ('gx', 'gy'))  39.9 us
    ppermute x12, starting transfers between devices, with_halo(): after = lax.ppermute(leading, axis, down)  33.3 us
  transfers between devices with their start and end apart: 24, of which 11 were waited for; matrix products, arithmetic and copies ran while one was open for 1% of the time, Pallas kernels for 0%

commit v1 on v0

--- a/solution.py
+++ b/solution.py
@@ -13,17 +13,33 @@
 shift_term = 1.0
 
 
-def with_halo(shard, sides, width):
-    for axis, dim in sides:
-        devices, length = (lax.axis_size(axis), shard.shape[dim])
-        up = [(i, (i + 1) % devices) for i in range(devices - 1)]
-        down = [(j, i) for i, j in up]
-        last = lax.slice_in_dim(shard, length - width, length, axis=dim)
-        leading = lax.slice_in_dim(shard, 0, width, axis=dim)
-        before = lax.ppermute(last, axis, up)
-        after = lax.ppermute(leading, axis, down)
-        shard = jnp.concatenate([before, shard, after], axis=dim)
-    return shard
+def with_halo(shard, dims, width):
+    dim_x, dim_y = dims
+    size_x, size_y = lax.axis_size("gx"), lax.axis_size("gy")
+
+    def part(dim, toward, array):
+        if toward == 0:
+            return array
+        length = array.shape[dim]
+        low = length - width if toward > 0 else 0
+        return lax.slice_in_dim(array, low, low + width, axis=dim)
+
+    def received(move_x, move_y):
+        if move_x == 0 and move_y == 0:
+            return shard
+        pairs = [
+            (x * size_y + y, (x + move_x) * size_y + y + move_y)
+            for x in range(size_x)
+            for y in range(size_y)
+            if 0 <= x + move_x < size_x and 0 <= y + move_y < size_y
+        ]
+        return lax.ppermute(part(dim_y, move_y, part(dim_x, move_x, shard)), ("gx", "gy"), pairs)
+
+    rows = [
+        jnp.concatenate([received(move_x, move_y) for move_y in (1, 0, -1)], axis=dim_y)
+        for move_x in (1, 0, -1)
+    ]
+    return jnp.concatenate(rows, axis=dim_x)
 
 
 def drift_bins(extended, codes, step):
@@ -88,7 +104,7 @@
 
 
 def pressure_cycle(values):
-    return with_halo(values, (("gx", 0), ("gy", 1)), 1)
+    return with_halo(values, (0, 1), 1)
 
 
 def local(position, velocity, volume, pressure_prev, fill, drift_from):
@@ -99,13 +115,14 @@
     live = (slots[None, None, :] < fill[:, :, None]).astype(jnp.float32)
     held = volume * live
     local_top = jnp.max(jnp.abs(velocity) * live[None])
-    top = lax.pmax(local_top, ("gx", "gy"))
+    top = jnp.max(lax.all_gather(jnp.broadcast_to(local_top, (8, 128)), ("gx", "gy"), tiled=True))
     step = cfl_number / (top + speed_eps)
     old = jnp.concatenate([position, velocity, held[None], pressure_prev[None]], axis=0)
     codes = drift_from + 1
-    around_old = with_halo(old, (("gx", 1), ("gy", 2)), 1)
-    fresh = drift_bins(around_old, codes, step)
-    ext = with_halo(fresh, (("gx", 1), ("gy", 2)), 1)
+    code_channel = jnp.broadcast_to(codes.astype(jnp.float32)[None, :, :, None], (1, rows, cols, width))
+    around_old = with_halo(jnp.concatenate([old, code_channel], axis=0), (1, 2), 2)
+    around_codes = around_old[6, 1:-1, 1:-1, 0].astype(jnp.int32)
+    ext = drift_bins(around_old[:6], around_codes, step)
     fresh_center = ext[:, 1:-1, 1:-1, :]
     kappa = 1.0 / width
     row_ids = jnp.arange(rows, dtype=jnp.int32)

time: 641 us -> 881 us (1.37)
  local copies, waits for them, and re-layouts: 46.5 us -> 162 us
  other arithmetic: 235 us -> 279 us
  starting transfers between devices: 73.6 us -> 113 us
  waiting for transfers between devices: 20.1 us -> 54.8 us
    slice x1 -> x11, local copies, waits for them, and re-layouts: 0.11 us -> 62 us  [drift_bins(): moved = jnp.concatenate([moved_x[None], moved_y[None], source[2:]], axis=0)]
    pmax x1 -> x0, blocking collectives: 39.9 us -> none  [local(): top = lax.pmax(local_top, ('gx', 'gy'))]
    ppermute x24 -> x40, starting transfers between devices: 73.6 us -> 113 us  [received(): lax.ppermute(part(dim_y, move_y, part(dim_x, move_x, shard)), ('gx', 'gy'...]
    unnamed x0 -> x1, blocking collectives: none -> 37.9 us
    ppermute x24 -> x40, waiting for transfers between devices: 20.1 us -> 54.8 us  [received(): lax.ppermute(part(dim_y, move_y, part(dim_x, move_x, shard)), ('gx', 'gy'...]
    add x0 -> x18, local copies, waits for them, and re-layouts: none -> 33.8 us  [the longest x9 17.5 us: drift_bins(): moved_x = source[0] + float(shift_x - 1) + step * source[2]]
    concatenate x7 -> x6, other arithmetic: 2.56 us -> 29.7 us  [with_halo(): return jnp.concatenate(rows, axis=dim_x)]
    add x4 -> x3, other arithmetic: 1.81 us -> 19.9 us  [drift_bins(): moved_x = source[0] + float(shift_x - 1) + step * source[2]]
  transfers between devices with their start and end apart: 24 -> 40, of which waited for: 11 -> 16; matrix products, arithmetic and copies ran while one was open for 1% -> 2% of each run, Pallas kernels for 0% -> 0%
where the time goes in v1:
time: 881 us; the launch traced here: 867 us
  other arithmetic  279 us (32%)
  local copies, waits for them, and re-layouts  162 us (18%)
  matrix products  121 us (14%)
  starting transfers between devices  113 us (13%)
  loops' own time  96.9 us (11%)
  waiting for transfers between devices  54.8 us (6%)
  blocking collectives  37.9 us (4%)
    dot_general x32, matrix products, relax_kept(): jnp.einsum('yij,yj->yi', coef, around_p, preferred_element_type=jnp.float32)  121 us
    ppermute x40, starting transfers between devices, received(): lax.ppermute(part(dim_y, move_y, part(dim_x, move_x, shard)), ('gx', 'gy'...  113 us
    reduce_sum x8, other arithmetic, first_pass(): den = shift_term + jnp.sum(coef.astype(jnp.float32), axis=-1)  89.3 us
    reduce_sum x8, other arithmetic, push_row(): grad_x = -jnp.sum(weight * diff * delta_x, axis=-1)  65.1 us
    dynamic_update_slice x16, other arithmetic, local(): coef_all, source, den = lax.map(setup, row_ids)  64.8 us
    another operation x4, loops' own time, local(): totals = lax.map(relax_kept, (row_ids, coef_all))  63.7 us
    slice x11, local copies, waits for them, and re-layouts, drift_bins(): moved = jnp.concatenate([moved_x[None], moved_y[None], source[2:]], axis=0)  62 us
    ppermute x40, waiting for transfers between devices, received(): lax.ppermute(part(dim_y, move_y, part(dim_x, move_x, shard)), ('gx', 'gy'...  54.8 us
  transfers between devices with their start and end apart: 40, of which 16 were waited for; matrix products, arithmetic and copies ran while one was open for 2% of the time, Pallas kernels for 0%

profile of v1, /device:TPU:17, one launch (start us, length us, event | category | flops | bytes accessed | tf_op | source)
XLA Modules:
  0.0 867.5 jit_solution(16445148258117939753)
XLA Ops:
  24.9 37.9 %all-reduce = f32[32]{0:T(128)S(1)} all-reduce(f32[32]{0:T(128)S(1)} %dynamic-update-slice), channel_id=2, replica_groups=mesh['gx'=8,'gy'=4] {'gx','gy'}, use_global_device_ids=true, to_apply=%add | all-reduce | flops 32 | bytes 256
  88.3 19.2 %maximum_maximum_fusion.2 = (f32[7,10,20,128]{2,1,3,0:T(8,128)}, f32[7,10,20,128]{2,1,3,0:T(8,128)}) fusion(f32[7,2,2,128]{2,1,3,0:T(2,128)} %copy.268, f32[7,2,16,128]{2,1,3,0:T(2,128)} %copy.267, f32[7,2,2,128]{2,1,3,0:T(2,128)S(1)} %copy.266, f32[7,8,2,128]{2,1,3,0:T(8,128)} %copy.265, f32[7,8,16,128]{2,1,3,0:T(8,128)} %copy.264, ...), kind=kLoop, calls=%fused_computation.225 | loop fusion | flops 1792000 | bytes 2293760 | tf_op jit(solution)/shard_map/concatenate | solution.py:42
  107.5 19.1 %fusion.105 = (f32[4,10,18,128]{2,1,3,0:T(8,128)}, f32[4,10,18,128]{2,1,3,0:T(8,128)}, f32[4,10,18,128]{2,1,3,0:T(8,128)}, f32[4,10,18,128]{2,1,3,0:T(8,128)}, f...) fusion(f32[7,10,20,128]{2,1,3,0:T(8,128)} %get-tuple-element.387, f32[7,10,20,128]{2,1,3,0:T(8,128)} %get-tuple-element.388), kind=kLoop, calls=%fused_computation.326 | loop fusion | bytes 4423680 | tf_op jit(solution)/shard_map/slice | solution.py:55
  126.7 9.7 %fusion.85 = (f32[1,10,18,128]{2,1,3,0:T(8,128)}, f32[1,10,18,128]{2,1,3,0:T(8,128)}, f32[1,10,18,128]{2,1,3,0:T(8,128)}, f32[1,10,18,128]{2,1,3,0:T(8,128)}, f3...) fusion(f32[7,10,20,128]{2,1,3,0:T(8,128)} %get-tuple-element.388, f32[]{:T(128)S(6)} %div.27), kind=kLoop, calls=%fused_computation.261 | loop fusion | flops 391680 | bytes 1658884 | tf_op jit(solution)/shard_map/add | solution.py:53
  142.8 10.4 %maximum_maximum_fusion = f32[7,12,20,128]{2,1,3,0:T(8,128)S(1)} fusion(f32[7,2,2,128]{2,1,3,0:T(2,128)} %copy.268, f32[7,2,16,128]{2,1,3,0:T(2,128)} %copy.267, f32[7,2,2,128]{2,1,3,0:T(2,128)} %copy-done.7, f32[7,8,2,128]{2,1,3,0:T(8,128)S(1)} %copy-done.3, f32[7,8,16,128]{2,1,3,0:T(8,128)S(1)} %copy-done.4, f32[7,8,2,128]{2,1,3,0:T(8,128)S(1)} %copy-done.2, ...), kind=kLoop, calls=%fused_computation.223 | loop fusion | flops 1720320 | bytes 1720320 | tf_op jit(solution)/shard_map/concatenate | solution.py:42
  161.0 11.7 %fusion.106 = (f32[4,10,18,128]{2,1,3,0:T(8,128)}, f32[4,10,18,128]{2,1,3,0:T(8,128)}, f32[4,10,18,128]{2,1,3,0:T(8,128)}) fusion(f32[7,12,20,128]{2,1,3,0:T(8,128)} %copy-done), kind=kLoop, calls=%fused_computation.327 | loop fusion | bytes 2211840 | tf_op jit(solution)/shard_map/slice | solution.py:55
  240.5 180.5 %while.70 = (s32[]{:T(128)}, bf16[8,16,128,1152]{3,2,1,0:T(8,128)(2,1)}, f32[8,16,128]{2,1,0:T(8,128)S(1)}, f32[8,16,128]{2,1,0:T(8,128)S(1)}, s32[8]{0:T(128)S(...) while((s32[]{:T(128)}, ...), condition=%wide.region_5.6_spmd.clone, body=%wide.region_2.5_spmd.sunk.clone.sunk | while | flops 89726984 | bytes 9021247 | solution.py:134
  244.0 11.2 %convert_reduce_fusion.2 = (f32[16,128]{1,0:T(8,128)S(1)}, f32[16,128]{1,0:T(8,128)S(1)}) fusion(f32[16,1152]{1,0:T(8,128)S(1)} %bitcast.681, f32[16,1152]{1,0:T(8,128)S(1)} %bitcast_add_fusion.7, f32[16,128]{1,0:T(8,128)S(1)} %get-tuple-element.684, f32[16,1152]{1,0:T(8,128)S(1)} %bitcast_add_fusion.8, f32[16,128]{1,0:T(8,128)S(1)} %get-tuple-element.686, ...), kind=kLoop, calls=%fused_computation.111.clone.1 | loop fusion | flops 56619008 | bytes 491520 | tf_op jit(solution)/shard_map/while/body/eval_jaxpr/reduce_sum | solution.py:87
  266.6 11.2 %convert_reduce_fusion.2 = (f32[16,128]{1,0:T(8,128)S(1)}, f32[16,128]{1,0:T(8,128)S(1)}) fusion(f32[16,1152]{1,0:T(8,128)S(1)} %bitcast.681, f32[16,1152]{1,0:T(8,128)S(1)} %bitcast_add_fusion.7, f32[16,128]{1,0:T(8,128)S(1)} %get-tuple-element.684, f32[16,1152]{1,0:T(8,128)S(1)} %bitcast_add_fusion.8, f32[16,128]{1,0:T(8,128)S(1)} %get-tuple-element.686, ...), kind=kLoop, calls=%fused_computation.111.clone.1 | loop fusion | flops 56619008 | bytes 491520 | tf_op jit(solution)/shard_map/while/body/eval_jaxpr/reduce_sum | solution.py:87
  289.1 11.2 %convert_reduce_fusion.2 = (f32[16,128]{1,0:T(8,128)S(1)}, f32[16,128]{1,0:T(8,128)S(1)}) fusion(f32[16,1152]{1,0:T(8,128)S(1)} %bitcast.681, f32[16,1152]{1,0:T(8,128)S(1)} %bitcast_add_fusion.7, f32[16,128]{1,0:T(8,128)S(1)} %get-tuple-element.684, f32[16,1152]{1,0:T(8,128)S(1)} %bitcast_add_fusion.8, f32[16,128]{1,0:T(8,128)S(1)} %get-tuple-element.686, ...), kind=kLoop, calls=%fused_computation.111.clone.1 | loop fusion | flops 56619008 | bytes 491520 | tf_op jit(solution)/shard_map/while/body/eval_jaxpr/reduce_sum | solution.py:87
  311.6 11.2 %convert_reduce_fusion.2 = (f32[16,128]{1,0:T(8,128)S(1)}, f32[16,128]{1,0:T(8,128)S(1)}) fusion(f32[16,1152]{1,0:T(8,128)S(1)} %bitcast.681, f32[16,1152]{1,0:T(8,128)S(1)} %bitcast_add_fusion.7, f32[16,128]{1,0:T(8,128)S(1)} %get-tuple-element.684, f32[16,1152]{1,0:T(8,128)S(1)} %bitcast_add_fusion.8, f32[16,128]{1,0:T(8,128)S(1)} %get-tuple-element.686, ...), kind=kLoop, calls=%fused_computation.111.clone.1 | loop fusion | flops 56619008 | bytes 491520 | tf_op jit(solution)/shard_map/while/body/eval_jaxpr/reduce_sum | solution.py:87
  334.2 11.2 %convert_reduce_fusion.2 = (f32[16,128]{1,0:T(8,128)S(1)}, f32[16,128]{1,0:T(8,128)S(1)}) fusion(f32[16,1152]{1,0:T(8,128)S(1)} %bitcast.681, f32[16,1152]{1,0:T(8,128)S(1)} %bitcast_add_fusion.7, f32[16,128]{1,0:T(8,128)S(1)} %get-tuple-element.684, f32[16,1152]{1,0:T(8,128)S(1)} %bitcast_add_fusion.8, f32[16,128]{1,0:T(8,128)S(1)} %get-tuple-element.686, ...), kind=kLoop, calls=%fused_computation.111.clone.1 | loop fusion | flops 56619008 | bytes 491520 | tf_op jit(solution)/shard_map/while/body/eval_jaxpr/reduce_sum | solution.py:87
  356.7 11.2 %convert_reduce_fusion.2 = (f32[16,128]{1,0:T(8,128)S(1)}, f32[16,128]{1,0:T(8,128)S(1)}) fusion(f32[16,1152]{1,0:T(8,128)S(1)} %bitcast.681, f32[16,1152]{1,0:T(8,128)S(1)} %bitcast_add_fusion.7, f32[16,128]{1,0:T(8,128)S(1)} %get-tuple-element.684, f32[16,1152]{1,0:T(8,128)S(1)} %bitcast_add_fusion.8, f32[16,128]{1,0:T(8,128)S(1)} %get-tuple-element.686, ...), kind=kLoop, calls=%fused_computation.111.clone.1 | loop fusion | flops 56619008 | bytes 491520 | tf_op jit(solution)/shard_map/while/body/eval_jaxpr/reduce_sum | solution.py:87
  379.2 11.2 %convert_reduce_fusion.2 = (f32[16,128]{1,0:T(8,128)S(1)}, f32[16,128]{1,0:T(8,128)S(1)}) fusion(f32[16,1152]{1,0:T(8,128)S(1)} %bitcast.681, f32[16,1152]{1,0:T(8,128)S(1)} %bitcast_add_fusion.7, f32[16,128]{1,0:T(8,128)S(1)} %get-tuple-element.684, f32[16,1152]{1,0:T(8,128)S(1)} %bitcast_add_fusion.8, f32[16,128]{1,0:T(8,128)S(1)} %get-tuple-element.686, ...), kind=kLoop, calls=%fused_computation.111.clone.1 | loop fusion | flops 56619008 | bytes 491520 | tf_op jit(solution)/shard_map/while/body/eval_jaxpr/reduce_sum | solution.py:87
  401.8 11.2 %convert_reduce_fusion.2 = (f32[16,128]{1,0:T(8,128)S(1)}, f32[16,128]{1,0:T(8,128)S(1)}) fusion(f32[16,1152]{1,0:T(8,128)S(1)} %bitcast.681, f32[16,1152]{1,0:T(8,128)S(1)} %bitcast_add_fusion.7, f32[16,128]{1,0:T(8,128)S(1)} %get-tuple-element.684, f32[16,1152]{1,0:T(8,128)S(1)} %bitcast_add_fusion.8, f32[16,128]{1,0:T(8,128)S(1)} %get-tuple-element.686, ...), kind=kLoop, calls=%fused_computation.111.clone.1 | loop fusion | flops 56619008 | bytes 491520 | tf_op jit(solution)/shard_map/while/body/eval_jaxpr/reduce_sum | solution.py:87
  421.1 53.1 %while.66 = (s32[]{:T(128)}, f32[8,16,128]{2,1,0:T(8,128)S(1)}, bf16[8,16,128,1152]{3,2,1,0:T(8,128)(2,1)}, s32[8]{0:T(128)S(1)}, bf16[10,18,128]{2,1,0:T(8,128)...) while((s32[]{:T(128)}, f32[8,16,128]{2,1,0:T(8,128)S(1)}, ...), condition=%wide.region_7.8_spmd, body=%wide.region_6.7_spmd.sunk | while | flops 4718601 | bytes 5001987 | solution.py:147
  508.9 53.1 %while.67 = (s32[]{:T(128)}, f32[8,16,128]{2,1,0:T(8,128)S(1)}, bf16[8,16,128,1152]{3,2,1,0:T(8,128)(2,1)}, s32[8]{0:T(128)S(1)}, bf16[10,18,128]{2,1,0:T(8,128)...) while((s32[]{:T(128)}, f32[8,16,128]{2,1,0:T(8,128)S(1)}, ...), condition=%wide.region_9.10_spmd, body=%wide.region_8.9_spmd.sunk | while | flops 4718601 | bytes 5001987 | solution.py:147
  597.8 53.1 %while.68 = (s32[]{:T(128)}, f32[8,16,128]{2,1,0:T(8,128)S(1)}, bf16[8,16,128,1152]{3,2,1,0:T(8,128)(2,1)}, s32[8]{0:T(128)S(1)}, bf16[10,18,128]{2,1,0:T(8,128)...) while((s32[]{:T(128)}, f32[8,16,128]{2,1,0:T(8,128)S(1)}, ...), condition=%wide.region_11.12_spmd, body=%wide.region_10.11_spmd.sunk | while | flops 4718601 | bytes 5001987 | solution.py:147
  686.4 53.1 %while.69 = (s32[]{:T(128)}, f32[8,16,128]{2,1,0:T(8,128)S(1)}, bf16[8,16,128,1152]{3,2,1,0:T(8,128)(2,1)}, s32[8]{0:T(128)S(1)}, bf16[10,18,128]{2,1,0:T(8,128)...) while((s32[]{:T(128)}, f32[8,16,128]{2,1,0:T(8,128)S(1)}, ...), condition=%wide.region_13.14_spmd, body=%wide.region_12.13_spmd.sunk | while | flops 4718601 | bytes 5001987 | solution.py:147
  775.6 90.8 %while.71 = (s32[]{:T(128)}, f32[8,2,16,128]{3,2,0,1:T(8,128)S(1)}, s32[8]{0:T(128)S(1)}, f32[6,10,18,128]{3,2,1,0:T(8,128)S(1)}, bf16[10,18,128]{2,1,0:T(8,128)...) while((s32[]{:T(128)}, f32[8,2,16,128]{3,2,0,1:T(8,128)S(1)}, ...), condition=%wide.region_17.18_spmd.clone, body=%wide.region_14.17_spmd.sunk.clone.sunk | while | flops 37842952 | bytes 2880931 | solution.py:158
  778.9 8.1 fusion.195
  790.2 8.1 fusion.195
  801.6 8.1 fusion.195
  812.9 8.1 fusion.195
  (1125 shorter events, 537.9 us)
Async XLA Ops:
  6.4 56.3 %collective-permute-start = (f32[7,2,2,128]{3,2,1,0:T(2,128)S(1)}, f32[7,2,2,128]{3,2,1,0:T(2,128)S(1)}, u32[]{:S(2)}, u32[]{:S(2)}) collective-permute-start(f32[7,2,2,128]{3,2,1,0:T(2,128)S(1)} %get-tuple-element.419), channel_id=1, source_target_pairs={{0,5},{1,6},{2,7},{4,9},{5,10},{6,11},{8,13},{9,14},{10,15},{12,17... | collective-permute-start | bytes 43016 | tf_op jit(solution)/shard_map/ppermute | solution.py:36
  11.1 55.0 %collective-permute-start.2 = (f32[7,2,2,128]{3,2,1,0:T(2,128)S(1)}, f32[7,2,2,128]{3,2,1,0:T(2,128)S(1)}, u32[]{:S(2)}, u32[]{:S(2)}) collective-permute-start(f32[7,2,2,128]{3,2,1,0:T(2,128)S(1)} %get-tuple-element.418), channel_id=1, source_target_pairs={{1,4},{2,5},{3,6},{5,8},{6,9},{7,10},{9,12},{10,13},{11,14},{13,16... | collective-permute-start | bytes 43016 | tf_op jit(solution)/shard_map/ppermute | solution.py:36
  13.0 57.0 %collective-permute-start.5 = (f32[7,2,2,128]{3,2,1,0:T(2,128)S(1)}, f32[7,2,2,128]{3,2,1,0:T(2,128)S(1)}, u32[]{:S(2)}, u32[]{:S(2)}) collective-permute-start(f32[7,2,2,128]{3,2,1,0:T(2,128)S(1)} %get-tuple-element.416), channel_id=1, source_target_pairs={{4,1},{5,2},{6,3},{8,5},{9,6},{10,7},{12,9},{13,10},{14,11},{16,13... | collective-permute-start | bytes 43016 | tf_op jit(solution)/shard_map/ppermute | solution.py:36
  18.5 60.9 %collective-permute-start.7 = (f32[7,2,2,128]{3,2,1,0:T(2,128)S(1)}, f32[7,2,2,128]{3,2,1,0:T(2,128)S(1)}, u32[]{:S(2)}, u32[]{:S(2)}) collective-permute-start(f32[7,2,2,128]{3,2,1,0:T(2,128)S(1)} %get-tuple-element.417), channel_id=1, source_target_pairs={{5,0},{6,1},{7,2},{9,4},{10,5},{11,6},{13,8},{14,9},{15,10},{17,12... | collective-permute-start | bytes 43016 | tf_op jit(solution)/shard_map/ppermute | solution.py:36
  20.5 60.2 %collective-permute-start.3 = (f32[7,8,2,128]{3,1,2,0:T(8,128)S(1)}, f32[7,8,2,128]{3,1,2,0:T(8,128)S(1)}, u32[]{:S(2)}, u32[]{:S(2)}) collective-permute-start(f32[7,8,2,128]{3,1,2,0:T(8,128)S(1)} %copy.317), channel_id=1, source_target_pairs={{0,1},{1,2},{2,3},{4,5},{5,6},{6,7},{8,9},{9,10},{10,11},{12,13},{... | collective-permute-start | bytes 172040 | tf_op jit(solution)/shard_map/ppermute | solution.py:36
  62.7 20.5 %collective-permute-start.4 = (f32[7,8,2,128]{3,1,2,0:T(8,128)S(1)}, f32[7,8,2,128]{3,1,2,0:T(8,128)S(1)}, u32[]{:S(2)}, u32[]{:S(2)}) collective-permute-start(f32[7,8,2,128]{3,1,2,0:T(8,128)S(1)} %copy.318), channel_id=1, source_target_pairs={{1,0},{2,1},{3,2},{5,4},{6,5},{7,6},{9,8},{10,9},{11,10},{13,12},{... | collective-permute-start | bytes 172040 | tf_op jit(solution)/shard_map/ppermute | solution.py:36
  66.1 19.5 %collective-permute-start.1 = (f32[7,2,16,128]{3,2,1,0:T(8,128)S(1)}, f32[7,2,16,128]{3,2,1,0:T(8,128)S(1)}, u32[]{:S(2)}, u32[]{:S(2)}) collective-permute-start(f32[7,2,16,128]{3,2,1,0:T(8,128)S(1)} %get-tuple-element.421), channel_id=1, source_target_pairs={{0,4},{1,5},{2,6},{3,7},{4,8},{5,9},{6,10},{7,11},{8,12},{9,13},{1... | collective-permute-start | bytes 344072 | tf_op jit(solution)/shard_map/ppermute | solution.py:36
  70.1 16.9 %collective-permute-start.6 = (f32[7,2,16,128]{3,2,1,0:T(8,128)S(1)}, f32[7,2,16,128]{3,2,1,0:T(8,128)S(1)}, u32[]{:S(2)}, u32[]{:S(2)}) collective-permute-start(f32[7,2,16,128]{3,2,1,0:T(8,128)S(1)} %get-tuple-element.420), channel_id=1, source_target_pairs={{4,0},{5,1},{6,2},{7,3},{8,4},{9,5},{10,6},{11,7},{12,8},{13,9},{1... | collective-permute-start | bytes 344072 | tf_op jit(solution)/shard_map/ppermute | solution.py:36
  474.2 34.6 %collective-permute-start.11 = (bf16[8,1,128]{2,1,0:T(2,128)(2,1)S(1)}, bf16[8,1,128]{2,1,0:T(2,128)(2,1)S(1)}, u32[]{:S(2)}, u32[]{:S(2)}) collective-permute-start(bf16[8,1,128]{2,1,0:T(2,128)(2,1)S(1)} %get-tuple-element.458), channel_id=1, source_target_pairs={{0,1},{1,2},{2,3},{4,5},{5,6},{6,7},{8,9},{9,10},{10,11},{12,13},{... | collective-permute-start | bytes 6152 | tf_op jit(solution)/shard_map/ppermute | solution.py:36
  478.6 30.2 %collective-permute-start.12 = (bf16[8,1,128]{2,1,0:T(2,128)(2,1)S(1)}, bf16[8,1,128]{2,1,0:T(2,128)(2,1)S(1)}, u32[]{:S(2)}, u32[]{:S(2)}) collective-permute-start(bf16[8,1,128]{2,1,0:T(2,128)(2,1)S(1)} %get-tuple-element.459), channel_id=1, source_target_pairs={{1,0},{2,1},{3,2},{5,4},{6,5},{7,6},{9,8},{10,9},{11,10},{13,12},{... | collective-permute-start | bytes 6152 | tf_op jit(solution)/shard_map/ppermute | solution.py:36
  480.5 28.3 %collective-permute-start.14 = (bf16[1,16,128]{2,1,0:T(8,128)(2,1)S(1)}, bf16[1,16,128]{2,1,0:T(8,128)(2,1)S(1)}, u32[]{:S(2)}, u32[]{:S(2)}) collective-permute-start(bf16[1,16,128]{2,1,0:T(8,128)(2,1)S(1)} %get-tuple-element.457), channel_id=1, source_target_pairs={{4,0},{5,1},{6,2},{7,3},{8,4},{9,5},{10,6},{11,7},{12,8},{13,9},{1... | collective-permute-start | bytes 12296 | tf_op jit(solution)/shard_map/ppermute | solution.py:36
  482.4 26.4 %collective-permute-start.9 = (bf16[1,16,128]{2,1,0:T(8,128)(2,1)S(1)}, bf16[1,16,128]{2,1,0:T(8,128)(2,1)S(1)}, u32[]{:S(2)}, u32[]{:S(2)}) collective-permute-start(bf16[1,16,128]{2,1,0:T(8,128)(2,1)S(1)} %get-tuple-element.456), channel_id=1, source_target_pairs={{0,4},{1,5},{2,6},{3,7},{4,8},{5,9},{6,10},{7,11},{8,12},{9,13},{1... | collective-permute-start | bytes 12296 | tf_op jit(solution)/shard_map/ppermute | solution.py:36
  562.1 35.6 %collective-permute-start.17 = (bf16[1,16,128]{2,1,0:T(8,128)(2,1)S(1)}, bf16[1,16,128]{2,1,0:T(8,128)(2,1)S(1)}, u32[]{:S(2)}, u32[]{:S(2)}) collective-permute-start(bf16[1,16,128]{2,1,0:T(8,128)(2,1)S(1)} %get-tuple-element.448), channel_id=1, source_target_pairs={{0,4},{1,5},{2,6},{3,7},{4,8},{5,9},{6,10},{7,11},{8,12},{9,13},{1... | collective-permute-start | bytes 12296 | tf_op jit(solution)/shard_map/ppermute | solution.py:36
  564.8 32.9 %collective-permute-start.19 = (bf16[8,1,128]{2,1,0:T(2,128)(2,1)S(1)}, bf16[8,1,128]{2,1,0:T(2,128)(2,1)S(1)}, u32[]{:S(2)}, u32[]{:S(2)}) collective-permute-start(bf16[8,1,128]{2,1,0:T(2,128)(2,1)S(1)} %get-tuple-element.450), channel_id=1, source_target_pairs={{0,1},{1,2},{2,3},{4,5},{5,6},{6,7},{8,9},{9,10},{10,11},{12,13},{... | collective-permute-start | bytes 6152 | tf_op jit(solution)/shard_map/ppermute | solution.py:36
  568.7 29.0 %collective-permute-start.20 = (bf16[8,1,128]{2,1,0:T(2,128)(2,1)S(1)}, bf16[8,1,128]{2,1,0:T(2,128)(2,1)S(1)}, u32[]{:S(2)}, u32[]{:S(2)}) collective-permute-start(bf16[8,1,128]{2,1,0:T(2,128)(2,1)S(1)} %get-tuple-element.451), channel_id=1, source_target_pairs={{1,0},{2,1},{3,2},{5,4},{6,5},{7,6},{9,8},{10,9},{11,10},{13,12},{... | collective-permute-start | bytes 6152 | tf_op jit(solution)/shard_map/ppermute | solution.py:36
  570.6 27.1 %collective-permute-start.22 = (bf16[1,16,128]{2,1,0:T(8,128)(2,1)S(1)}, bf16[1,16,128]{2,1,0:T(8,128)(2,1)S(1)}, u32[]{:S(2)}, u32[]{:S(2)}) collective-permute-start(bf16[1,16,128]{2,1,0:T(8,128)(2,1)S(1)} %get-tuple-element.449), channel_id=1, source_target_pairs={{4,0},{5,1},{6,2},{7,3},{8,4},{9,5},{10,6},{11,7},{12,8},{13,9},{1... | collective-permute-start | bytes 12296 | tf_op jit(solution)/shard_map/ppermute | solution.py:36
  650.9 35.4 %collective-permute-start.25 = (bf16[1,16,128]{2,1,0:T(8,128)(2,1)S(1)}, bf16[1,16,128]{2,1,0:T(8,128)(2,1)S(1)}, u32[]{:S(2)}, u32[]{:S(2)}) collective-permute-start(bf16[1,16,128]{2,1,0:T(8,128)(2,1)S(1)} %get-tuple-element.440), channel_id=1, source_target_pairs={{0,4},{1,5},{2,6},{3,7},{4,8},{5,9},{6,10},{7,11},{8,12},{9,13},{1... | collective-permute-start | bytes 12296 | tf_op jit(solution)/shard_map/ppermute | solution.py:36
  655.2 31.1 %collective-permute-start.27 = (bf16[8,1,128]{2,1,0:T(2,128)(2,1)S(1)}, bf16[8,1,128]{2,1,0:T(2,128)(2,1)S(1)}, u32[]{:S(2)}, u32[]{:S(2)}) collective-permute-start(bf16[8,1,128]{2,1,0:T(2,128)(2,1)S(1)} %get-tuple-element.442), channel_id=1, source_target_pairs={{0,1},{1,2},{2,3},{4,5},{5,6},{6,7},{8,9},{9,10},{10,11},{12,13},{... | collective-permute-start | bytes 6152 | tf_op jit(solution)/shard_map/ppermute | solution.py:36
  657.1 29.2 %collective-permute-start.28 = (bf16[8,1,128]{2,1,0:T(2,128)(2,1)S(1)}, bf16[8,1,128]{2,1,0:T(2,128)(2,1)S(1)}, u32[]{:S(2)}, u32[]{:S(2)}) collective-permute-start(bf16[8,1,128]{2,1,0:T(2,128)(2,1)S(1)} %get-tuple-element.443), channel_id=1, source_target_pairs={{1,0},{2,1},{3,2},{5,4},{6,5},{7,6},{9,8},{10,9},{11,10},{13,12},{... | collective-permute-start | bytes 6152 | tf_op jit(solution)/shard_map/ppermute | solution.py:36
  659.5 26.8 %collective-permute-start.30 = (bf16[1,16,128]{2,1,0:T(8,128)(2,1)S(1)}, bf16[1,16,128]{2,1,0:T(8,128)(2,1)S(1)}, u32[]{:S(2)}, u32[]{:S(2)}) collective-permute-start(bf16[1,16,128]{2,1,0:T(8,128)(2,1)S(1)} %get-tuple-element.441), channel_id=1, source_target_pairs={{4,0},{5,1},{6,2},{7,3},{8,4},{9,5},{10,6},{11,7},{12,8},{13,9},{1... | collective-permute-start | bytes 12296 | tf_op jit(solution)/shard_map/ppermute | solution.py:36
  740.1 35.4 %collective-permute-start.33 = (bf16[1,16,128]{2,1,0:T(8,128)(2,1)S(1)}, bf16[1,16,128]{2,1,0:T(8,128)(2,1)S(1)}, u32[]{:S(2)}, u32[]{:S(2)}) collective-permute-start(bf16[1,16,128]{2,1,0:T(8,128)(2,1)S(1)} %get-tuple-element.432), channel_id=1, source_target_pairs={{0,4},{1,5},{2,6},{3,7},{4,8},{5,9},{6,10},{7,11},{8,12},{9,13},{1... | collective-permute-start | bytes 12296 | tf_op jit(solution)/shard_map/ppermute | solution.py:36
  744.4 31.1 %collective-permute-start.35 = (bf16[8,1,128]{2,1,0:T(2,128)(2,1)S(1)}, bf16[8,1,128]{2,1,0:T(2,128)(2,1)S(1)}, u32[]{:S(2)}, u32[]{:S(2)}) collective-permute-start(bf16[8,1,128]{2,1,0:T(2,128)(2,1)S(1)} %get-tuple-element.434), channel_id=1, source_target_pairs={{0,1},{1,2},{2,3},{4,5},{5,6},{6,7},{8,9},{9,10},{10,11},{12,13},{... | collective-permute-start | bytes 6152 | tf_op jit(solution)/shard_map/ppermute | solution.py:36
  746.3 29.2 %collective-permute-start.36 = (bf16[8,1,128]{2,1,0:T(2,128)(2,1)S(1)}, bf16[8,1,128]{2,1,0:T(2,128)(2,1)S(1)}, u32[]{:S(2)}, u32[]{:S(2)}) collective-permute-start(bf16[8,1,128]{2,1,0:T(2,128)(2,1)S(1)} %get-tuple-element.435), channel_id=1, source_target_pairs={{1,0},{2,1},{3,2},{5,4},{6,5},{7,6},{9,8},{10,9},{11,10},{13,12},{... | collective-permute-start | bytes 6152 | tf_op jit(solution)/shard_map/ppermute | solution.py:36
  748.7 26.8 %collective-permute-start.38 = (bf16[1,16,128]{2,1,0:T(8,128)(2,1)S(1)}, bf16[1,16,128]{2,1,0:T(8,128)(2,1)S(1)}, u32[]{:S(2)}, u32[]{:S(2)}) collective-permute-start(bf16[1,16,128]{2,1,0:T(8,128)(2,1)S(1)} %get-tuple-element.433), channel_id=1, source_target_pairs={{4,0},{5,1},{6,2},{7,3},{8,4},{9,5},{10,6},{11,7},{12,8},{13,9},{1... | collective-permute-start | bytes 12296 | tf_op jit(solution)/shard_map/ppermute | solution.py:36
  (39 other events, 420.6 us)

commit v2 on v0

v2 whole, which is shorter than its diff:
```python
import functools

import jax
import jax.numpy as jnp
from jax import lax
from jax.experimental import pallas as pl
from jax.experimental.pallas import tpu as pltpu
from jax.sharding import PartitionSpec as P

SWEEPS = 4
CFL = 0.25
SPEED_EPS = 1e-06
SOFT = 0.01
CHUNK = 32
VMEM_LIMIT = 56 * 1024 * 1024

X, Y, U, V, VOL, PRES, CODE = range(7)
S_0, S_X, S_Y, S_SOURCE, S_RDEN, S_VOL = range(6)


def call(kernel, **kwargs):
    return pl.pallas_call(
        kernel, compiler_params=pltpu.CompilerParams(vmem_limit_bytes=VMEM_LIMIT), **kwargs
    )


def row_index(width):
    return lax.broadcasted_iota(jnp.int32, (8, width), 0)


def split(value):
    high = value.astype(jnp.bfloat16).astype(jnp.float32)
    return jnp.concatenate([high, value - high], axis=0).astype(jnp.bfloat16)


def dot(left, right):
    return jnp.dot(left, right, preferred_element_type=jnp.float32)


def prepare_kernel(position, velocity, volume, pressure, fill, code, old, top):
    rows, cols, width = volume.shape
    slots = lax.broadcasted_iota(jnp.int32, (cols, width), 1)
    most = jnp.zeros((cols, width), jnp.float32)
    for row in range(rows):
        live = (slots < fill[row]).astype(jnp.float32)
        most = jnp.maximum(most, jnp.abs(velocity[0, row]) * live)
        most = jnp.maximum(most, jnp.abs(velocity[1, row]) * live)
        channels = [
            position[0, row],
            position[1, row],
            velocity[0, row],
            velocity[1, row],
            volume[row] * live,
            pressure[row],
            jnp.broadcast_to((code[row] + 1).astype(jnp.float32), (cols, width)),
            jnp.zeros((cols, width), jnp.float32),
        ]
        for channel, value in enumerate(channels):
            old[row, :, channel, :] = value
    top[...] = jnp.broadcast_to(jnp.max(most), top.shape)


def prepare(position, velocity, volume, pressure, fill, code):
    rows, cols, width = volume.shape
    return call(
        prepare_kernel,
        out_shape=(
            jax.ShapeDtypeStruct((rows, cols, 8, width), jnp.float32),
            jax.ShapeDtypeStruct((8, width), jnp.float32),
        ),
        name="prepare",
    )(position, velocity, volume, pressure, fill[:, :, None], code[:, :, None])


def neighbours(axis, low_side, high_side):
    devices = lax.axis_size(axis)
    up = [(i, i + 1) for i in range(devices - 1)]
    down = [(i + 1, i) for i in range(devices - 1)]
    return lax.ppermute(high_side, axis, up), lax.ppermute(low_side, axis, down)


def exchange(shard, depth):
    above, below = neighbours("gx", shard[:depth], shard[-depth:])
    low = jnp.concatenate([above[:, :depth], shard[:, :depth], below[:, :depth]], axis=0)
    high = jnp.concatenate([above[:, -depth:], shard[:, -depth:], below[:, -depth:]], axis=0)
    left, right = neighbours("gy", low, high)
    return above, below, left, right


def assemble(out, center, above, below, left, right, depth):
    rows, cols = center.shape[:2]
    out[:depth, depth : depth + cols] = above[...]
    out[depth : depth + rows, depth : depth + cols] = center[...]
    out[depth + rows :, depth : depth + cols] = below[...]
    out[:, :depth] = left[...]
    out[:, depth + cols :] = right[...]


def drift_kernel(top, center, above, below, left, right, fresh, old):
    rows, cols, _, width = fresh.shape
    assemble(old, center, above, below, left, right, 2)
    step = CFL / (jnp.max(top[...]) + SPEED_EPS)
    index = row_index(width)

    def one_row(row, carry):
        for col in range(cols):
            code = old[row + 1, col + 1, CODE : CODE + 1, :]
            tile = jnp.zeros((8, width), jnp.float32)
            for k in range(9):
                off_x, off_y = k // 3, k % 3
                offset = jnp.where(index == X, off_x - 1.0, jnp.where(index == Y, off_y - 1.0, 0.0))
                source = old[row + off_x, col + off_y] + offset
                tile = jnp.where(code == k + 1.0, source, tile)
            moved = tile + step * pltpu.roll(tile, 6, 0)
            fresh[row, col] = jnp.where(index <= Y, moved, tile)
        return carry

    lax.fori_loop(0, rows, one_row, 0)


def drift(top, center, above, below, left, right):
    rows, cols, _, width = center.shape
    return call(
        drift_kernel,
        out_shape=jax.ShapeDtypeStruct((rows + 2, cols + 2, 8, width), jnp.float32),
        scratch_shapes=[pltpu.VMEM((rows + 4, cols + 4, 8, width), jnp.float32)],
        name="drift",
    )(top, center, above, below, left, right)


def setup_kernel(kappa, fresh, coef, weight, sums, pv, xs, ys, feat):
    cols = coef.shape[0]
    width = coef.shape[2]
    wide = fresh.shape[1]
    row = pl.program_id(0)

    def columns(source_row):
        slot = lax.rem(source_row, 3)

        def one(col, carry):
            tile = fresh[source_row, col]
            xs[slot, col] = jnp.broadcast_to(tile[X : X + 1], (width, width)).T
            ys[slot, col] = jnp.broadcast_to(tile[Y : Y + 1], (width, width)).T
            x, y, u, v = (tile[i : i + 1] for i in range(4))
            vol = tile[VOL : VOL + 1]
            zero = jnp.zeros_like(vol)
            flow = vol * (u * x + v * y)
            base = [vol, vol * x, vol * y, vol * u, vol * v, flow, vol * tile[PRES : PRES + 1], zero]
            feat[slot, col, 0] = jnp.concatenate(base, axis=0)
            feat[slot, col, 1] = jnp.concatenate([zero, vol, zero, zero, zero, vol * u, zero, zero], axis=0)
            feat[slot, col, 2] = jnp.concatenate([zero, zero, vol, zero, zero, vol * v, zero, zero], axis=0)
            return carry

        lax.fori_loop(0, wide, one, 0)

    @pl.when(row == 0)
    def _():
        columns(0)
        columns(1)

    columns(row + 2)

    def one_bin(col, carry):
        tile = fresh[row + 1, col + 1]
        x, y, u, v = (tile[i : i + 1] for i in range(4))
        vol = tile[VOL : VOL + 1]
        total_w = jnp.zeros((16, width), jnp.float32)
        total_c = jnp.zeros((16, width), jnp.float32)
        for k in range(9):
            off_x, off_y = k // 3 - 1, k % 3 - 1
            slot = lax.rem(row + k // 3, 3)
            xi, yi = x - off_x, y - off_y
            for part in range(width // CHUNK):
                span = pl.ds(part * CHUNK, CHUNK)
                dx = xi - xs[slot, col + k % 3, span]
                dy = yi - ys[slot, col + k % 3, span]
                square = jnp.maximum(dx * dx + dy * dy, 1e-14)
                remain = jnp.maximum(1.0 - square * lax.rsqrt(square), 0.0)
                cubed = remain * remain * remain
                ratio = square * pl.reciprocal(square + SOFT, approx=True)
                place = pl.ds(k * width + part * CHUNK, CHUNK)
                weight[col, place] = cubed.astype(jnp.bfloat16)
                coef[col, place] = (cubed * ratio).astype(jnp.bfloat16)
            features = feat[slot, col + k % 3, 0]
            if off_x:
                features = features + float(off_x) * feat[slot, col + k % 3, 1]
            if off_y:
                features = features + float(off_y) * feat[slot, col + k % 3, 2]
            features = split(features)
            place = pl.ds(k * width, width)
            total_w += dot(features, weight[col, place])
            total_c += dot(features, coef[col, place])
        total_w = total_w[:8] + total_w[8:]
        total_c = total_c[:8] + total_c[8:]
        w_0, w_x, w_y, w_u, w_v, w_flow = (total_w[i : i + 1] for i in range(6))
        source = x * w_u + y * w_v - w_flow - (u * x + v * y) * w_0 + u * w_x + v * w_y
        source = kappa * 20.0 * source
        rden = 1.0 / (1.0 + kappa * 40.0 * total_c[0:1])
        first = (source + kappa * 40.0 * total_c[6:7]) * rden
        sums[col] = jnp.concatenate([w_0, w_x, w_y, source, rden, vol, first, vol], axis=0)
        pv[pl.ds(col, 1), :] = first * vol
        return carry

    lax.fori_loop(0, cols, one_bin, 0)


def setup(fresh, kappa):
    rows, cols, _, width = fresh.shape
    rows, cols = rows - 2, cols - 2
    matrix = jax.ShapeDtypeStruct((rows, cols, 9 * width, width), jnp.bfloat16)
    matrix_spec = pl.BlockSpec((None, cols, 9 * width, width), lambda row: (row, 0, 0, 0))
    return call(
        functools.partial(setup_kernel, kappa),
        grid=(rows,),
        in_specs=[pl.BlockSpec(memory_space=pltpu.VMEM)],
        out_specs=(
            matrix_spec,
            matrix_spec,
            pl.BlockSpec((None, cols, 8, width), lambda row: (row, 0, 0, 0)),
            pl.BlockSpec((None, cols, width), lambda row: (row, 0, 0)),
        ),
        out_shape=(
            matrix,
            matrix,
            jax.ShapeDtypeStruct((rows, cols, 8, width), jnp.float32),
            jax.ShapeDtypeStruct((rows, cols, width), jnp.float32),
        ),
        scratch_shapes=[
            pltpu.VMEM((3, cols + 2, width, width), jnp.float32),
            pltpu.VMEM((3, cols + 2, width, width), jnp.float32),
            pltpu.VMEM((3, cols + 2, 3, 8, width), jnp.float32),
        ],
        name="setup",
    )(fresh)


def sweep_kernel(kappa, last, center, above, below, left, right, coef, sums, pv, *rest):
    pressure = rest[0] if last else None
    ext, tiles = rest[-2:]
    row = pl.program_id(0)
    cols, _, width = coef.shape

    @pl.when(row == 0)
    def _():
        assemble(ext, center, above, below, left, right, 1)

        def one_row(r, carry):
            for col in range(cols + 2):
                value = ext[r, col : col + 1, :]
                high = value.astype(jnp.bfloat16).astype(jnp.float32)
                both = jnp.concatenate([high, value - high, jnp.zeros((14, width), jnp.float32)], axis=0)
                tiles[r, col] = both.astype(jnp.bfloat16)
            return carry

        lax.fori_loop(0, ext.shape[0], one_row, 0)

    def one_bin(col, carry):
        around = [tiles[row + k // 3, col + k % 3] for k in range(9)]
        total = dot(jnp.concatenate(around, axis=1), coef[col])
        total = total[0:1] + total[1:2]
        tile = sums[col]
        value = (tile[S_SOURCE : S_SOURCE + 1] + kappa * 40.0 * total) * tile[S_RDEN : S_RDEN + 1]
        vol = tile[S_VOL : S_VOL + 1]
        pv[pl.ds(col, 1), :] = value * vol
        if last:
            pressure[pl.ds(col, 1), :] = jnp.where(vol > 0.0, value, 0.0)
        return carry

    lax.fori_loop(0, cols, one_bin, 0)


def sweep(kappa, last, pv, halo, coef, sums):
    rows, cols, deep, width = coef.shape
    whole = pl.BlockSpec(memory_space=pltpu.VMEM)
    out = jax.ShapeDtypeStruct((rows, cols, width), jnp.float32)
    out_spec = pl.BlockSpec((None, cols, width), lambda row: (row, 0, 0))
    count = 2 if last else 1
    return call(
        functools.partial(sweep_kernel, kappa, last),
        grid=(rows,),
        in_specs=[whole] * 5
        + [
            pl.BlockSpec((None, cols, deep, width), lambda row: (row, 0, 0, 0)),
            pl.BlockSpec((None, cols, 8, width), lambda row: (row, 0, 0, 0)),
        ],
        out_specs=[out_spec] * count,
        out_shape=[out] * count,
        scratch_shapes=[
            pltpu.VMEM((rows + 2, cols + 2, width), jnp.float32),
            pltpu.VMEM((rows + 2, cols + 2, 16, width), jnp.bfloat16),
        ],
        name="sweep",
    )(pv, *halo, coef, sums)


def push_kernel(kappa, center, above, below, left, right, fresh, weight, sums, pressure, out, ext, feat):
    row = pl.program_id(0)
    cols, _, width = weight.shape

    @pl.when(row == 0)
    def _():
        assemble(ext, center, above, below, left, right, 1)

        def one_row(r, carry):
            for col in range(cols + 2):
                value = ext[r, col : col + 1, :]
                tile = fresh[r, col]
                parts = [value, value * tile[X : X + 1], value * tile[Y : Y + 1], jnp.zeros((5, width), jnp.float32)]
                feat[r, col] = jnp.concatenate(parts, axis=0)
            return carry

        lax.fori_loop(0, ext.shape[0], one_row, 0)

    index = row_index(width)

    def one_bin(col, carry):
        around = []
        for k in range(9):
            tile = feat[row + k // 3, col + k % 3]
            off_x, off_y = k // 3 - 1.0, k % 3 - 1.0
            scale = jnp.where(index == 1, off_x, jnp.where(index == 2, off_y, 0.0))
            around.append(split(tile + scale * tile[0:1]))
        total = dot(jnp.concatenate(around, axis=1), weight[col])
        total = total[:8] + total[8:]
        tile = fresh[row + 1, col + 1]
        summed = sums[col]
        x, y, u, v = (tile[i : i + 1] for i in range(4))
        alive = tile[VOL : VOL + 1] > 0.0
        own = pressure[pl.ds(col, 1), :]
        grad_x = x * total[0:1] - total[1:2] - own * (x * summed[S_0 : S_0 + 1] - summed[S_X : S_X + 1])
        grad_y = y * total[0:1] - total[2:3] - own * (y * summed[S_0 : S_0 + 1] - summed[S_Y : S_Y + 1])
        out[0, pl.ds(col, 1), :] = jnp.where(alive, u + kappa * 20.0 * grad_x, 0.0)
        out[1, pl.ds(col, 1), :] = jnp.where(alive, v + kappa * 20.0 * grad_y, 0.0)
        return carry

    lax.fori_loop(0, cols, one_bin, 0)


def push(kappa, pv, halo, fresh, weight, sums, pressure):
    rows, cols, deep, width = weight.shape
    whole = pl.BlockSpec(memory_space=pltpu.VMEM)
    return call(
        functools.partial(push_kernel, kappa),
        grid=(rows,),
        in_specs=[whole] * 6
        + [
            pl.BlockSpec((None, cols, deep, width), lambda row: (row, 0, 0, 0)),
            pl.BlockSpec((None, cols, 8, width), lambda row: (row, 0, 0, 0)),
            pl.BlockSpec((None, cols, width), lambda row: (row, 0, 0)),
        ],
        out_specs=pl.BlockSpec((2, None, cols, width), lambda row: (0, row, 0, 0)),
        out_shape=jax.ShapeDtypeStruct((2, rows, cols, width), jnp.float32),
        scratch_shapes=[
            pltpu.VMEM((rows + 2, cols + 2, width), jnp.float32),
            pltpu.VMEM((rows + 2, cols + 2, 8, width), jnp.float32),
        ],
        name="push",
    )(pv, *halo, fresh, weight, sums, pressure)


def local(position, velocity, volume, pressure_prev, fill, drift_from):
    kappa = 1.0 / volume.shape[2]
    old, top = prepare(position, velocity, volume, pressure_prev, fill, drift_from)
    top = lax.pmax(top[0, 0], ("gx", "gy")).reshape(1, 1)
    fresh = drift(top, old, *exchange(old, 2))
    coef, weight, sums, pv = setup(fresh, kappa)
    for step in range(1, SWEEPS):
        last = step == SWEEPS - 1
        pv, *pressure = sweep(kappa, last, pv, exchange(pv, 1), coef, sums)
    velocity_new = push(kappa, pv, exchange(pv, 1), fresh, weight, sums, pressure[0])
    return (pressure[0], velocity_new)


def solution(mesh):
    return jax.shard_map(
        local,
        mesh=mesh,
        in_specs=(
            P(None, "gx", "gy", None),
            P(None, "gx", "gy", None),
            P("gx", "gy", None),
            P("gx", "gy", None),
            P("gx", "gy"),
            P("gx", "gy"),
        ),
        out_specs=(P("gx", "gy", None), P(None, "gx", "gy", None)),
        check_vma=False,
    )
```

time: 641 us -> 350 us (0.55); the launches traced: 632 us -> 348 us
  other arithmetic: 235 us -> 0.09 us
  Pallas kernels: 0 us -> 210 us
  matrix products: 121 us -> 0 us
  loops' own time: 93.3 us -> 0 us
  local copies, waits for them, and re-layouts: 46.5 us -> 15.6 us
  starting transfers between devices: 73.6 us -> 57.4 us
    pallas_call x0 -> x7, Pallas kernels: none -> 210 us  [the longest x1 98.4 us: setup(): call(functools.partial(setup_kernel, kappa), grid=(rows,), in_specs=[pl.B...]
    reduce_sum x16 -> x0, other arithmetic: 154 us -> none  [the longest x8 89.3 us: first_pass(): den = shift_term + jnp.sum(coef.astype(jnp.float32), axis=-1)]
    dot_general x32 -> x0, matrix products: 121 us -> none  [relax_kept(): jnp.einsum('yij,yj->yi', coef, around_p, preferred_element_type=jnp.float32)]
    another operation x6 -> x0, loops' own time: 93.3 us -> none  [the longest x4 63.7 us: local(): totals = lax.map(relax_kept, (row_ids, coef_all))]
    dynamic_update_slice x24 -> x0, other arithmetic: 64.8 us -> none  [the longest x16 64.7 us: local(): coef_all, source, den = lax.map(setup, row_ids)]
    dynamic_slice x48 -> x0, local copies, waits for them, and re-layouts: 28.1 us -> none  [local(): coef_all, source, den = lax.map(setup, row_ids)]
    ppermute x24 -> x20, starting transfers between devices: 73.6 us -> 57.4 us  [the longest x10 33.9 us: neighbours(): lax.ppermute(high_side, axis, up)]
    while x488 -> x0, local copies, waits for them, and re-layouts: 10.2 us -> none
  transfers between devices with their start and end apart: 24 -> 20, of which waited for: 11 -> 10; matrix products, arithmetic and copies ran while one was open for 1% -> 2% of each run, Pallas kernels for 0% -> 0%
where the time goes in v2:
time: 350 us; the launch traced here: 348 us
  Pallas kernels  210 us (60%)
  starting transfers between devices  57.4 us (16%)
  blocking collectives  38.4 us (11%)
  waiting for transfers between devices  25.6 us (7%)
  local copies, waits for them, and re-layouts  15.6 us (4%)
    pallas_call x1, Pallas kernels, setup(): call(functools.partial(setup_kernel, kappa), grid=(rows,), in_specs=[pl.B...  98.4 us
    pallas_call x3, Pallas kernels, sweep(): call(functools.partial(sweep_kernel, kappa, last), grid=(rows,), in_specs...  77.9 us
    pmax x1, blocking collectives, local(): top = lax.pmax(top[0, 0], ('gx', 'gy')).reshape(1, 1)  38.4 us
    ppermute x10, starting transfers between devices, neighbours(): lax.ppermute(high_side, axis, up)  33.9 us
    pallas_call x1, Pallas kernels, push(): call(functools.partial(push_kernel, kappa), grid=(rows,), in_specs=[whole...  27.3 us
    ppermute x10, starting transfers between devices, neighbours(): lax.ppermute(low_side, axis, down)  23.5 us
    ppermute x10, waiting for transfers between devices, neighbours(): lax.ppermute(high_side, axis, up)  13.6 us
    ppermute x10, waiting for transfers between devices, neighbours(): lax.ppermute(low_side, axis, down)  12 us
  transfers between devices with their start and end apart: 20, of which 10 were waited for; matrix products, arithmetic and copies ran while one was open for 2% of the time, Pallas kernels for 0%

profile of v2, /device:TPU:17, one launch (start us, length us, event | category | flops | bytes accessed | tf_op | source)
XLA Modules:
  0.0 348.4 jit_solution(1551643758509092814)
XLA Ops:
  6.7 3.0 collective-permute-start.1
  12.9 3.8 %collective-permute-done.above = f32[2,16,8,128]{3,2,1,0:T(8,128)S(1)} collective-permute-done((f32[2,16,8,128]{3,2,1,0:T(8,128)S(1)}, f32[2,16,8,128]{3,2,1,0:T(8,128)S(1)}, u32[]{:S(2)}, u32[]{:S(2)}) %collective-permute-start) | collective-permute-done | bytes 131104 | tf_op jit(solution)/shard_map/ppermute | solution.py:79
  16.7 4.7 %collective-permute-start.2 = (f32[12,2,8,128]{3,2,1,0:T(8,128)S(1)}, f32[12,2,8,128]{3,2,1,0:T(8,128)S(1)}, u32[]{:S(2)}, u32[]{:S(2)}) collective-permute-start(f32[12,2,8,128]{3,2,1,0:T(8,128)S(1)} %pad_maximum_fusion), channel_id=1, source_target_pairs={{0,1},{1,2},{2,3},{4,5},{5,6},{6,7},{8,9},{9,10},{10,11},{12,13},{... | collective-permute-start | bytes 294920 | tf_op jit(solution)/shard_map/ppermute | solution.py:79
  24.6 38.4 %pmax.7.top = f32[1,1]{1,0:T(1,128)} all-reduce(f32[1,1]{1,0:T(1,128)} %slice.123), channel_id=1, replica_groups=mesh['gx'=8,'gy'=4] {'gx','gy'}, use_global_device_ids=true, to_apply=%region_0.0 | all-reduce | flops 1 | bytes 8 | tf_op jit(solution)/shard_map/pmax | solution.py:364
  64.3 4.3 %drift.1.fresh = f32[10,18,8,128]{3,2,1,0:T(8,128)} custom-call(f32[1,1]{1,0:T(1,128)} %pmax.7.top, f32[8,16,8,128]{3,2,1,0:T(8,128)} %get-tuple-element.11.center, f32[2,16,8,128]{3,2,1,0:T(8,128)} %copy-done.1, f32[2,16,8,128]{3,2,1,0:T(8,128)} %copy-done, f32[12,2,8,128]{3,2,1,0:T(8,128)} %copy-done.2, f32[12,2,8,128]{3,2,1,0:T(8,128)} %copy-done.3), custom_call_target="tpu_custom_call" | custom-call | tf_op jit(solution)/shard_map/drift/pallas_call | solution.py:123
  68.6 98.4 %setup.1 = (bf16[8,16,1152,128]{3,2,1,0:T(8,128)(2,1)}, bf16[8,16,1152,128]{3,2,1,0:T(8,128)(2,1)}, f32[8,16,8,128]{3,2,1,0:T(8,128)}, f32[8,16,128]{2,1,0:T(8,128)}) custom-call(f32[10,18,8,128]{3,2,1,0:T(8,128)} %drift.1.fresh), custom_call_target="tpu_custom_call" | custom-call | tf_op jit(solution)/shard_map/setup/pallas_call | solution.py:212
  167.8 4.4 %collective-permute-start.5 = (f32[1,16,128]{2,1,0:T(8,128)S(1)}, f32[1,16,128]{2,1,0:T(8,128)S(1)}, u32[]{:S(2)}, u32[]{:S(2)}) collective-permute-start(f32[1,16,128]{2,1,0:T(8,128)S(1)} %get-tuple-element.40), channel_id=1, source_target_pairs={{4,0},{8,4},{12,8},{16,12},{20,16},{24,20},{28,24},{5,1},{9,5},{13... | collective-permute-start | bytes 24584 | tf_op jit(solution)/shard_map/ppermute | solution.py:79
  174.9 3.3 collective-permute-done.4.above
  178.3 5.9 %collective-permute-start.6 = (f32[10,1,128]{2,1,0:T(1,128)S(1)}, f32[10,1,128]{2,1,0:T(1,128)S(1)}, u32[]{:S(2)}, u32[]{:S(2)}) collective-permute-start(f32[10,1,128]{2,1,0:T(1,128)S(1)} %pad_maximum_fusion.2), channel_id=1, source_target_pairs={{0,1},{1,2},{2,3},{4,5},{5,6},{6,7},{8,9},{9,10},{10,11},{12,13},{... | collective-permute-start | bytes 15368 | tf_op jit(solution)/shard_map/ppermute | solution.py:79
  186.1 3.0 collective-permute-done.7.right
  189.7 25.9 %sweep.3.center = f32[8,16,128]{2,1,0:T(8,128)} custom-call(f32[8,16,128]{2,1,0:T(8,128)} %get-tuple-element.12.center, f32[1,16,128]{2,1,0:T(8,128)} %copy-done.10, f32[1,16,128]{2,1,0:T(8,128)} %copy-done.6, f32[10,1,128]{2,1,0:T(1,128)} %copy-done.13, f32[10,1,128]{2,1,0:T(1,128)} %copy-done.16, bf16[8,16,1152,128]{3,2,1,0:T(8,128)(2,1)} %get-tuple-element.13.coef, ...), custom_call_target="tpu_custom_call" | custom-call | tf_op jit(solution)/shard_map/sweep/pallas_call | solution.py:278
  219.1 3.4 collective-permute-start.8
  224.4 3.1 collective-permute-start.10
  229.4 3.0 collective-permute-done.11.right
  233.0 25.9 %sweep.4.center = f32[8,16,128]{2,1,0:T(8,128)} custom-call(f32[8,16,128]{2,1,0:T(8,128)} %sweep.3.center, f32[1,16,128]{2,1,0:T(8,128)} %copy-done.11, f32[1,16,128]{2,1,0:T(8,128)} %copy-done.7, f32[10,1,128]{2,1,0:T(1,128)} %copy-done.14, f32[10,1,128]{2,1,0:T(1,128)} %copy-done.17, bf16[8,16,1152,128]{3,2,1,0:T(8,128)(2,1)} %get-tuple-element.13.coef, ...), custom_call_target="tpu_custom_call" | custom-call | tf_op jit(solution)/shard_map/sweep/pallas_call | solution.py:278
  259.6 2.7 collective-permute-start.13
  265.7 2.7 collective-permute-done.12.above
  268.4 3.4 collective-permute-start.14
  273.8 3.0 collective-permute-done.15.right
  277.4 26.1 %sweep.5 = (f32[8,16,128]{2,1,0:T(8,128)}, f32[8,16,128]{2,1,0:T(8,128)}) custom-call(f32[8,16,128]{2,1,0:T(8,128)} %sweep.4.center, f32[1,16,128]{2,1,0:T(8,128)} %copy-done.9, f32[1,16,128]{2,1,0:T(8,128)} %copy-done.5, f32[10,1,128]{2,1,0:T(1,128)} %copy-done.12, f32[10,1,128]{2,1,0:T(1,128)} %copy-done.15, ...), custom_call_target="tpu_custom_call" | custom-call | tf_op jit(solution)/shard_map/sweep/pallas_call | solution.py:278
  306.8 3.4 collective-permute-start.16
  312.1 3.4 collective-permute-start.18
  317.5 3.0 collective-permute-done.19.right
  321.1 27.3 %push.1 = f32[2,8,16,128]{3,2,1,0:T(8,128)} custom-call(f32[8,16,128]{2,1,0:T(8,128)} %get-tuple-element.16.center, f32[1,16,128]{2,1,0:T(8,128)} %copy-done.8, f32[1,16,128]{2,1,0:T(8,128)} %copy-done.4, f32[10,1,128]{2,1,0:T(1,128)} %copy-done.18, f32[10,1,128]{2,1,0:T(1,128)} %copy-done.19, f32[10,18,8,128]{3,2,1,0:T(8,128)} %drift.1.fresh, ...), custom_call_target="tpu_custom_call" | custom-call | tf_op jit(solution)/shard_map/push/pallas_call | solution.py:342
  (97 shorter events, 41.9 us)
Async XLA Ops:
  6.7 6.3 %collective-permute-start.1 = (f32[2,16,8,128]{3,2,1,0:T(8,128)S(1)}, f32[2,16,8,128]{3,2,1,0:T(8,128)S(1)}, u32[]{:S(2)}, u32[]{:S(2)}) collective-permute-start(f32[2,16,8,128]{3,2,1,0:T(8,128)S(1)} %get-tuple-element.20), channel_id=1, source_target_pairs={{4,0},{8,4},{12,8},{16,12},{20,16},{24,20},{28,24},{5,1},{9,5},{13... | collective-permute-start | bytes 393224 | tf_op jit(solution)/shard_map/ppermute | solution.py:79
  9.7 7.0 %collective-permute-start = (f32[2,16,8,128]{3,2,1,0:T(8,128)S(1)}, f32[2,16,8,128]{3,2,1,0:T(8,128)S(1)}, u32[]{:S(2)}, u32[]{:S(2)}) collective-permute-start(f32[2,16,8,128]{3,2,1,0:T(8,128)S(1)} %get-tuple-element.21), channel_id=1, source_target_pairs={{0,4},{4,8},{8,12},{12,16},{16,20},{20,24},{24,28},{1,5},{5,9},{9,... | collective-permute-start | bytes 393224 | tf_op jit(solution)/shard_map/ppermute | solution.py:79
  12.9 50.1 %copy-start = (f32[2,16,8,128]{3,2,1,0:T(8,128)}, f32[2,16,8,128]{3,2,1,0:T(8,128)S(1)}, u32[]{:S(2)}) copy-start(f32[2,16,8,128]{3,2,1,0:T(8,128)S(1)} %collective-permute-done.1.below) | copy-start | bytes 393220
  16.7 46.4 %copy-start.1 = (f32[2,16,8,128]{3,2,1,0:T(8,128)}, f32[2,16,8,128]{3,2,1,0:T(8,128)S(1)}, u32[]{:S(2)}) copy-start(f32[2,16,8,128]{3,2,1,0:T(8,128)S(1)} %collective-permute-done.above) | copy-start | bytes 393220
  16.7 46.3 %collective-permute-start.2 = (f32[12,2,8,128]{3,2,1,0:T(8,128)S(1)}, f32[12,2,8,128]{3,2,1,0:T(8,128)S(1)}, u32[]{:S(2)}, u32[]{:S(2)}) collective-permute-start(f32[12,2,8,128]{3,2,1,0:T(8,128)S(1)} %pad_maximum_fusion), channel_id=1, source_target_pairs={{0,1},{1,2},{2,3},{4,5},{5,6},{6,7},{8,9},{9,10},{10,11},{12,13},{... | collective-permute-start | bytes 294920 | tf_op jit(solution)/shard_map/ppermute | solution.py:79
  21.5 41.6 %collective-permute-start.3 = (f32[12,2,8,128]{3,2,1,0:T(8,128)S(1)}, f32[12,2,8,128]{3,2,1,0:T(8,128)S(1)}, u32[]{:S(2)}, u32[]{:S(2)}) collective-permute-start(f32[12,2,8,128]{3,2,1,0:T(8,128)S(1)} %pad_maximum_fusion.1), channel_id=1, source_target_pairs={{1,0},{2,1},{3,2},{5,4},{6,5},{7,6},{9,8},{10,9},{11,10},{13,12},{... | collective-permute-start | bytes 294920 | tf_op jit(solution)/shard_map/ppermute | solution.py:79
  167.8 7.1 %collective-permute-start.5 = (f32[1,16,128]{2,1,0:T(8,128)S(1)}, f32[1,16,128]{2,1,0:T(8,128)S(1)}, u32[]{:S(2)}, u32[]{:S(2)}) collective-permute-start(f32[1,16,128]{2,1,0:T(8,128)S(1)} %get-tuple-element.40), channel_id=1, source_target_pairs={{4,0},{8,4},{12,8},{16,12},{20,16},{24,20},{28,24},{5,1},{9,5},{13... | collective-permute-start | bytes 24584 | tf_op jit(solution)/shard_map/ppermute | solution.py:79
  173.0 5.3 %collective-permute-start.4 = (f32[1,16,128]{2,1,0:T(8,128)S(1)}, f32[1,16,128]{2,1,0:T(8,128)S(1)}, u32[]{:S(2)}, u32[]{:S(2)}) collective-permute-start(f32[1,16,128]{2,1,0:T(8,128)S(1)} %get-tuple-element.41), channel_id=1, source_target_pairs={{0,4},{4,8},{8,12},{12,16},{16,20},{20,24},{24,28},{1,5},{5,9},{9,... | collective-permute-start | bytes 24584 | tf_op jit(solution)/shard_map/ppermute | solution.py:79
  174.9 14.2 %copy-start.6 = (f32[1,16,128]{2,1,0:T(8,128)}, f32[1,16,128]{2,1,0:T(8,128)S(1)}, u32[]{:S(2)}) copy-start(f32[1,16,128]{2,1,0:T(8,128)S(1)} %collective-permute-done.5.below) | copy-start | bytes 24580
  178.3 7.9 %collective-permute-start.6 = (f32[10,1,128]{2,1,0:T(1,128)S(1)}, f32[10,1,128]{2,1,0:T(1,128)S(1)}, u32[]{:S(2)}, u32[]{:S(2)}) collective-permute-start(f32[10,1,128]{2,1,0:T(1,128)S(1)} %pad_maximum_fusion.2), channel_id=1, source_target_pairs={{0,1},{1,2},{2,3},{4,5},{5,6},{6,7},{8,9},{9,10},{10,11},{12,13},{... | collective-permute-start | bytes 15368 | tf_op jit(solution)/shard_map/ppermute | solution.py:79
  184.2 4.9 %collective-permute-start.7 = (f32[10,1,128]{2,1,0:T(1,128)S(1)}, f32[10,1,128]{2,1,0:T(1,128)S(1)}, u32[]{:S(2)}, u32[]{:S(2)}) collective-permute-start(f32[10,1,128]{2,1,0:T(1,128)S(1)} %pad_maximum_fusion.3), channel_id=1, source_target_pairs={{1,0},{2,1},{3,2},{5,4},{6,5},{7,6},{9,8},{10,9},{11,10},{13,12},{... | collective-permute-start | bytes 15368 | tf_op jit(solution)/shard_map/ppermute | solution.py:79
  216.4 6.1 %collective-permute-start.9 = (f32[1,16,128]{2,1,0:T(8,128)S(1)}, f32[1,16,128]{2,1,0:T(8,128)S(1)}, u32[]{:S(2)}, u32[]{:S(2)}) collective-permute-start(f32[1,16,128]{2,1,0:T(8,128)S(1)} %get-tuple-element.36), channel_id=1, source_target_pairs={{4,0},{8,4},{12,8},{16,12},{20,16},{24,20},{28,24},{5,1},{9,5},{13... | collective-permute-start | bytes 24584 | tf_op jit(solution)/shard_map/ppermute | solution.py:79
  219.1 5.3 %collective-permute-start.8 = (f32[1,16,128]{2,1,0:T(8,128)S(1)}, f32[1,16,128]{2,1,0:T(8,128)S(1)}, u32[]{:S(2)}, u32[]{:S(2)}) collective-permute-start(f32[1,16,128]{2,1,0:T(8,128)S(1)} %get-tuple-element.37), channel_id=1, source_target_pairs={{0,4},{4,8},{8,12},{12,16},{16,20},{20,24},{24,28},{1,5},{5,9},{9,... | collective-permute-start | bytes 24584 | tf_op jit(solution)/shard_map/ppermute | solution.py:79
  224.4 5.1 %collective-permute-start.10 = (f32[10,1,128]{2,1,0:T(1,128)S(1)}, f32[10,1,128]{2,1,0:T(1,128)S(1)}, u32[]{:S(2)}, u32[]{:S(2)}) collective-permute-start(f32[10,1,128]{2,1,0:T(1,128)S(1)} %pad_maximum_fusion.4), channel_id=1, source_target_pairs={{0,1},{1,2},{2,3},{4,5},{5,6},{6,7},{8,9},{9,10},{10,11},{12,13},{... | collective-permute-start | bytes 15368 | tf_op jit(solution)/shard_map/ppermute | solution.py:79
  227.5 4.9 %collective-permute-start.11 = (f32[10,1,128]{2,1,0:T(1,128)S(1)}, f32[10,1,128]{2,1,0:T(1,128)S(1)}, u32[]{:S(2)}, u32[]{:S(2)}) collective-permute-start(f32[10,1,128]{2,1,0:T(1,128)S(1)} %pad_maximum_fusion.5), channel_id=1, source_target_pairs={{1,0},{2,1},{3,2},{5,4},{6,5},{7,6},{9,8},{10,9},{11,10},{13,12},{... | collective-permute-start | bytes 15368 | tf_op jit(solution)/shard_map/ppermute | solution.py:79
  259.6 6.1 %collective-permute-start.13 = (f32[1,16,128]{2,1,0:T(8,128)S(1)}, f32[1,16,128]{2,1,0:T(8,128)S(1)}, u32[]{:S(2)}, u32[]{:S(2)}) collective-permute-start(f32[1,16,128]{2,1,0:T(8,128)S(1)} %get-tuple-element.32), channel_id=1, source_target_pairs={{4,0},{8,4},{12,8},{16,12},{20,16},{24,20},{28,24},{5,1},{9,5},{13... | collective-permute-start | bytes 24584 | tf_op jit(solution)/shard_map/ppermute | solution.py:79
  263.1 5.3 %collective-permute-start.12 = (f32[1,16,128]{2,1,0:T(8,128)S(1)}, f32[1,16,128]{2,1,0:T(8,128)S(1)}, u32[]{:S(2)}, u32[]{:S(2)}) collective-permute-start(f32[1,16,128]{2,1,0:T(8,128)S(1)} %get-tuple-element.33), channel_id=1, source_target_pairs={{0,4},{4,8},{8,12},{12,16},{16,20},{20,24},{24,28},{1,5},{5,9},{9,... | collective-permute-start | bytes 24584 | tf_op jit(solution)/shard_map/ppermute | solution.py:79
  265.7 11.1 %copy-start.5 = (f32[1,16,128]{2,1,0:T(8,128)}, f32[1,16,128]{2,1,0:T(8,128)S(1)}, u32[]{:S(2)}) copy-start(f32[1,16,128]{2,1,0:T(8,128)S(1)} %collective-permute-done.13.below) | copy-start | bytes 24580
  268.4 5.3 %collective-permute-start.14 = (f32[10,1,128]{2,1,0:T(1,128)S(1)}, f32[10,1,128]{2,1,0:T(1,128)S(1)}, u32[]{:S(2)}, u32[]{:S(2)}) collective-permute-start(f32[10,1,128]{2,1,0:T(1,128)S(1)} %pad_maximum_fusion.6), channel_id=1, source_target_pairs={{0,1},{1,2},{2,3},{4,5},{5,6},{6,7},{8,9},{9,10},{10,11},{12,13},{... | collective-permute-start | bytes 15368 | tf_op jit(solution)/shard_map/ppermute | solution.py:79
  271.8 4.9 %collective-permute-start.15 = (f32[10,1,128]{2,1,0:T(1,128)S(1)}, f32[10,1,128]{2,1,0:T(1,128)S(1)}, u32[]{:S(2)}, u32[]{:S(2)}) collective-permute-start(f32[10,1,128]{2,1,0:T(1,128)S(1)} %pad_maximum_fusion.7), channel_id=1, source_target_pairs={{1,0},{2,1},{3,2},{5,4},{6,5},{7,6},{9,8},{10,9},{11,10},{13,12},{... | collective-permute-start | bytes 15368 | tf_op jit(solution)/shard_map/ppermute | solution.py:79
  304.1 6.1 %collective-permute-start.17 = (f32[1,16,128]{2,1,0:T(8,128)S(1)}, f32[1,16,128]{2,1,0:T(8,128)S(1)}, u32[]{:S(2)}, u32[]{:S(2)}) collective-permute-start(f32[1,16,128]{2,1,0:T(8,128)S(1)} %get-tuple-element.28), channel_id=1, source_target_pairs={{4,0},{8,4},{12,8},{16,12},{20,16},{24,20},{28,24},{5,1},{9,5},{13... | collective-permute-start | bytes 24584 | tf_op jit(solution)/shard_map/ppermute | solution.py:79
  306.8 5.3 %collective-permute-start.16 = (f32[1,16,128]{2,1,0:T(8,128)S(1)}, f32[1,16,128]{2,1,0:T(8,128)S(1)}, u32[]{:S(2)}, u32[]{:S(2)}) collective-permute-start(f32[1,16,128]{2,1,0:T(8,128)S(1)} %get-tuple-element.29), channel_id=1, source_target_pairs={{0,4},{4,8},{8,12},{12,16},{16,20},{20,24},{24,28},{1,5},{5,9},{9,... | collective-permute-start | bytes 24584 | tf_op jit(solution)/shard_map/ppermute | solution.py:79
  312.1 5.3 %collective-permute-start.18 = (f32[10,1,128]{2,1,0:T(1,128)S(1)}, f32[10,1,128]{2,1,0:T(1,128)S(1)}, u32[]{:S(2)}, u32[]{:S(2)}) collective-permute-start(f32[10,1,128]{2,1,0:T(1,128)S(1)} %pad_maximum_fusion.8), channel_id=1, source_target_pairs={{0,1},{1,2},{2,3},{4,5},{5,6},{6,7},{8,9},{9,10},{10,11},{12,13},{... | collective-permute-start | bytes 15368 | tf_op jit(solution)/shard_map/ppermute | solution.py:79
  315.5 4.9 %collective-permute-start.19 = (f32[10,1,128]{2,1,0:T(1,128)S(1)}, f32[10,1,128]{2,1,0:T(1,128)S(1)}, u32[]{:S(2)}, u32[]{:S(2)}) collective-permute-start(f32[10,1,128]{2,1,0:T(1,128)S(1)} %pad_maximum_fusion.9), channel_id=1, source_target_pairs={{1,0},{2,1},{3,2},{5,4},{6,5},{7,6},{9,8},{10,9},{11,10},{13,12},{... | collective-permute-start | bytes 15368 | tf_op jit(solution)/shard_map/ppermute | solution.py:79
  (16 other events, 71.6 us)

commit v3 on v2

v3 whole, which is shorter than its diff:
```python
import functools

import jax
import jax.numpy as jnp
from jax import lax
from jax.experimental import pallas as pl
from jax.experimental.pallas import tpu as pltpu
from jax.sharding import PartitionSpec as P

SWEEPS = 4
CFL = 0.25
SPEED_EPS = 1e-06
SOFT = 0.01
CHUNK = 32
GROUP = 4
VMEM_LIMIT = 20 * 1024 * 1024

X, Y, U, V, VOL, PRES, CODE = range(7)
S_0, S_X, S_Y, S_SOURCE, S_RDEN, S_VOL = range(6)


def call(kernel, **kwargs):
    return pl.pallas_call(
        kernel, compiler_params=pltpu.CompilerParams(vmem_limit_bytes=VMEM_LIMIT), **kwargs
    )


def row_index(width):
    return lax.broadcasted_iota(jnp.int32, (8, width), 0)


def split(value):
    high = value.astype(jnp.bfloat16).astype(jnp.float32)
    return jnp.concatenate([high, value - high], axis=0).astype(jnp.bfloat16)


def dot(left, right):
    return jnp.dot(left, right, preferred_element_type=jnp.float32)


def prepare_kernel(position, velocity, volume, pressure, fill, code, old, top):
    rows, cols, width = volume.shape
    slots = lax.broadcasted_iota(jnp.int32, (cols, width), 1)
    most = jnp.zeros((cols, width), jnp.float32)
    for row in range(rows):
        live = (slots < fill[row]).astype(jnp.float32)
        most = jnp.maximum(most, jnp.abs(velocity[0, row]) * live)
        most = jnp.maximum(most, jnp.abs(velocity[1, row]) * live)
        channels = [
            position[0, row],
            position[1, row],
            velocity[0, row],
            velocity[1, row],
            volume[row] * live,
            pressure[row],
            jnp.broadcast_to((code[row] + 1).astype(jnp.float32), (cols, width)),
            jnp.zeros((cols, width), jnp.float32),
        ]
        for channel, value in enumerate(channels):
            old[row, :, channel, :] = value
    top[...] = jnp.broadcast_to(jnp.max(most), top.shape)


def prepare(position, velocity, volume, pressure, fill, code):
    rows, cols, width = volume.shape
    return call(
        prepare_kernel,
        out_shape=(
            jax.ShapeDtypeStruct((rows, cols, 8, width), jnp.float32),
            jax.ShapeDtypeStruct((8, width), jnp.float32),
        ),
        name="prepare",
    )(position, velocity, volume, pressure, fill[:, :, None], code[:, :, None])


def neighbours(axis, low_side, high_side):
    devices = lax.axis_size(axis)
    up = [(i, i + 1) for i in range(devices - 1)]
    down = [(i + 1, i) for i in range(devices - 1)]
    return lax.ppermute(high_side, axis, up), lax.ppermute(low_side, axis, down)


def exchange(shard, depth):
    above, below = neighbours("gx", shard[:depth], shard[-depth:])
    low = jnp.concatenate([above[:, :depth], shard[:, :depth], below[:, :depth]], axis=0)
    high = jnp.concatenate([above[:, -depth:], shard[:, -depth:], below[:, -depth:]], axis=0)
    left, right = neighbours("gy", low, high)
    return above, below, left, right


def assemble(out, center, above, below, left, right, depth):
    rows, cols = center.shape[:2]
    out[:depth, depth : depth + cols] = above[...]
    out[depth : depth + rows, depth : depth + cols] = center[...]
    out[depth + rows :, depth : depth + cols] = below[...]
    out[:, :depth] = left[...]
    out[:, depth + cols :] = right[...]


def drift_kernel(top, center, above, below, left, right, fresh, old):
    rows, cols, _, width = fresh.shape
    assemble(old, center, above, below, left, right, 2)
    step = CFL / (jnp.max(top[...]) + SPEED_EPS)
    index = row_index(width)

    def one_row(row, carry):
        for col in range(cols):
            code = old[row + 1, col + 1, CODE : CODE + 1, :]
            tile = jnp.zeros((8, width), jnp.float32)
            for k in range(9):
                off_x, off_y = k // 3, k % 3
                offset = jnp.where(index == X, off_x - 1.0, jnp.where(index == Y, off_y - 1.0, 0.0))
                source = old[row + off_x, col + off_y] + offset
                tile = jnp.where(code == k + 1.0, source, tile)
            moved = tile + step * pltpu.roll(tile, 6, 0)
            fresh[row, col] = jnp.where(index <= Y, moved, tile)
        return carry

    lax.fori_loop(0, rows, one_row, 0)


def drift(top, center, above, below, left, right):
    rows, cols, _, width = center.shape
    return call(
        drift_kernel,
        out_shape=jax.ShapeDtypeStruct((rows + 2, cols + 2, 8, width), jnp.float32),
        scratch_shapes=[pltpu.VMEM((rows + 4, cols + 4, 8, width), jnp.float32)],
        name="drift",
    )(top, center, above, below, left, right)


def dot_nt(left, right):
    return lax.dot_general(left, right, (((1,), (1,)), ((), ())), preferred_element_type=jnp.float32)


def setup_kernel(kappa, fresh, coef, weight, sums, pv, xcol, ycol, feat, both_a, both_b, sem):
    rows, cols, width, deep = coef.shape
    wide = cols + 2

    def features_of(place, carry):
        row, col = place // wide, lax.rem(place, wide)
        tile = fresh[row, col]
        x, y, u, v = (tile[i : i + 1] for i in range(4))
        vol = tile[VOL : VOL + 1]
        zero = jnp.zeros_like(vol)
        vol_u, vol_v = vol * u, vol * v
        base = [vol, vol * x, vol * y, vol_u, vol_v, vol_u * x + vol_v * y, vol * tile[PRES : PRES + 1], zero]
        feat[row, col, 0] = jnp.concatenate(base, axis=0)
        feat[row, col, 1] = jnp.concatenate([zero, vol, zero, zero, zero, vol_u, zero, zero], axis=0)
        feat[row, col, 2] = jnp.concatenate([zero, zero, vol, zero, zero, vol_v, zero, zero], axis=0)
        return carry

    lax.fori_loop(0, (rows + 2) * wide, features_of, 0)

    def columns(bin_id, slot):
        tile = fresh[bin_id // cols + 1, lax.rem(bin_id, cols) + 1]
        xcol[slot] = jnp.broadcast_to(tile[X : X + 1], (width, width)).T
        ycol[slot] = jnp.broadcast_to(tile[Y : Y + 1], (width, width)).T

    def blocks(bin_id, slot, both):
        row, col = bin_id // cols, lax.rem(bin_id, cols)
        for k in range(9):
            tile = fresh[row + k // 3, col + k % 3]
            xj = tile[X : X + 1] + (k // 3 - 1.0)
            yj = tile[Y : Y + 1] + (k % 3 - 1.0)
            lanes = pl.ds(k * width, width)
            for part in range(width // CHUNK):
                span = pl.ds(part * CHUNK, CHUNK)
                dx = xcol[slot, span] - xj
                dy = ycol[slot, span] - yj
                square = jnp.maximum(dx * dx + dy * dy, 1e-14)
                remain = jnp.maximum(1.0 - square * lax.rsqrt(square), 0.0)
                cubed = remain * remain * remain
                ratio = square * pl.reciprocal(square + SOFT, approx=True)
                value = (cubed * ratio).astype(jnp.bfloat16)
                both[span, lanes] = cubed.astype(jnp.bfloat16)
                both[pl.ds(width + part * CHUNK, CHUNK), lanes] = value
                coef[row, col, span, lanes] = value

    def finish(bin_id, both):
        row, col = bin_id // cols, lax.rem(bin_id, cols)
        around = []
        for k in range(9):
            off_x, off_y = k // 3 - 1, k % 3 - 1
            features = feat[row + k // 3, col + k % 3, 0]
            if off_x:
                features = features + float(off_x) * feat[row + k // 3, col + k % 3, 1]
            if off_y:
                features = features + float(off_y) * feat[row + k // 3, col + k % 3, 2]
            around.append(split(features))
        total = dot_nt(both[...], jnp.concatenate(around, axis=1))
        total = total[:, :8] + total[:, 8:]
        total_w, total_c = total[:width].T, total[width:].T
        tile = fresh[row + 1, col + 1]
        x, y, u, v = (tile[i : i + 1] for i in range(4))
        vol = tile[VOL : VOL + 1]
        w_0, w_x, w_y, w_u, w_v, w_flow = (total_w[i : i + 1] for i in range(6))
        source = x * w_u + y * w_v - w_flow - (u * x + v * y) * w_0 + u * w_x + v * w_y
        source = kappa * 20.0 * source
        rden = 1.0 / (1.0 + kappa * 40.0 * total_c[0:1])
        first = (source + kappa * 40.0 * total_c[6:7]) * rden
        sums[row, col] = jnp.concatenate([w_0, w_x, w_y, source, rden, vol, first, vol], axis=0)
        pv[row, pl.ds(col, 1), :] = first * vol

    def copy_out(bin_id, both, slot):
        target = weight.at[bin_id // cols, lax.rem(bin_id, cols)]
        return pltpu.make_async_copy(both.at[pl.ds(0, width)], target, sem.at[slot])

    count = rows * cols
    columns(0, 0)
    columns(1, 1)

    def two_bins(step, carry):
        even = 2 * step

        @pl.when(step > 0)
        def _():
            copy_out(even - 2, both_a, 0).wait()

        blocks(even, 0, both_a)
        columns(jnp.minimum(even + 2, count - 1), 0)

        @pl.when(step > 0)
        def _():
            copy_out(even - 1, both_b, 1).wait()

        copy_out(even, both_a, 0).start()
        finish(even, both_a)
        blocks(even + 1, 1, both_b)
        columns(jnp.minimum(even + 3, count - 1), 1)
        copy_out(even + 1, both_b, 1).start()
        finish(even + 1, both_b)
        return carry

    lax.fori_loop(0, count // 2, two_bins, 0)
    copy_out(count - 2, both_a, 0).wait()
    copy_out(count - 1, both_b, 1).wait()


def setup(fresh, kappa):
    rows, cols, _, width = fresh.shape
    rows, cols = rows - 2, cols - 2
    vmem = pl.BlockSpec(memory_space=pltpu.VMEM)
    return call(
        functools.partial(setup_kernel, kappa),
        in_specs=[vmem],
        out_specs=(vmem, pl.BlockSpec(memory_space=pltpu.HBM), vmem, vmem),
        out_shape=(
            pltpu.VMEM((rows, cols, width, 9 * width), jnp.bfloat16),
            jax.ShapeDtypeStruct((rows, cols, width, 9 * width), jnp.bfloat16),
            jax.ShapeDtypeStruct((rows, cols, 8, width), jnp.float32),
            jax.ShapeDtypeStruct((rows, cols, width), jnp.float32),
        ),
        scratch_shapes=[
            pltpu.VMEM((2, width, width), jnp.float32),
            pltpu.VMEM((2, width, width), jnp.float32),
            pltpu.VMEM((rows + 2, cols + 2, 3, 8, width), jnp.float32),
            pltpu.VMEM((2 * width, 9 * width), jnp.bfloat16),
            pltpu.VMEM((2 * width, 9 * width), jnp.bfloat16),
            pltpu.SemaphoreType.DMA((2,)),
        ],
        name="setup",
    )(fresh)


def sweep_kernel(kappa, last, center, above, below, left, right, coef, sums, pv, *rest):
    pressure = rest[0] if last else None
    ext, tiles = rest[-2:]
    rows, cols, width, _ = coef.shape
    assemble(ext, center, above, below, left, right, 1)

    def spread(row, carry):
        for col in range(cols + 2):
            tiles[row, col] = jnp.broadcast_to(ext[row, col : col + 1, :], (16, width)).astype(jnp.bfloat16)
        return carry

    lax.fori_loop(0, rows + 2, spread, 0)
    ones = jnp.ones((16, width), jnp.bfloat16)

    def some_bins(step, carry):
        row, first = step // (cols // GROUP), lax.rem(step, cols // GROUP) * GROUP
        for col in range(GROUP):
            col = first + col
            parts = []
            for part in range(width // 16):
                total = None
                for k in range(9):
                    term = coef[row, col, pl.ds(part * 16, 16), pl.ds(k * width, width)] * tiles[row + k // 3, col + k % 3]
                    total = term if total is None else total + term
                parts.append(total)
            total = dot_nt(ones, jnp.concatenate(parts, axis=0))[0:1]
            tile = sums[row, col]
            value = (tile[S_SOURCE : S_SOURCE + 1] + kappa * 40.0 * total) * tile[S_RDEN : S_RDEN + 1]
            vol = tile[S_VOL : S_VOL + 1]
            pv[row, pl.ds(col, 1), :] = value * vol
            if last:
                pressure[row, pl.ds(col, 1), :] = jnp.where(vol > 0.0, value, 0.0)
        return carry

    lax.fori_loop(0, rows * cols // GROUP, some_bins, 0)


def sweep(kappa, last, pv, halo, coef, sums):
    rows, cols, width, _ = coef.shape
    vmem = pl.BlockSpec(memory_space=pltpu.VMEM)
    out = jax.ShapeDtypeStruct((rows, cols, width), jnp.float32)
    count = 2 if last else 1
    return call(
        functools.partial(sweep_kernel, kappa, last),
        in_specs=[vmem] * 7,
        out_specs=[vmem] * count,
        out_shape=[out] * count,
        scratch_shapes=[
            pltpu.VMEM((rows + 2, cols + 2, width), jnp.float32),
            pltpu.VMEM((rows + 2, cols + 2, 16, width), jnp.bfloat16),
        ],
        name="sweep",
    )(pv, *halo, pltpu.with_memory_space_constraint(coef, pltpu.VMEM), sums)


def push_kernel(kappa, center, above, below, left, right, fresh, weight, sums, pressure, out, ext, feat):
    row, half = pl.program_id(0), pl.program_id(1)
    cols, width, _ = weight.shape

    @pl.when((row == 0) & (half == 0))
    def _():
        assemble(ext, center, above, below, left, right, 1)

        def one_row(r, carry):
            for col in range(ext.shape[1]):
                value = ext[r, col : col + 1, :]
                tile = fresh[r, col]
                parts = [value, value * tile[X : X + 1], value * tile[Y : Y + 1], jnp.zeros((5, width), jnp.float32)]
                feat[r, col] = jnp.concatenate(parts, axis=0)
            return carry

        lax.fori_loop(0, ext.shape[0], one_row, 0)

    index = row_index(width)

    def some_bins(step, carry):
        for col in range(4):
            col = step * 4 + col
            place = half * cols + col
            around = []
            for k in range(9):
                tile = feat[row + k // 3, place + k % 3]
                off_x, off_y = k // 3 - 1.0, k % 3 - 1.0
                scale = jnp.where(index == 1, off_x, jnp.where(index == 2, off_y, 0.0))
                around.append(split(tile + scale * tile[0:1]))
            total = dot_nt(weight[col], jnp.concatenate(around, axis=1))
            total = (total[:, :8] + total[:, 8:]).T
            tile = fresh[row + 1, place + 1]
            summed = sums[col]
            x, y, u, v = (tile[i : i + 1] for i in range(4))
            alive = tile[VOL : VOL + 1] > 0.0
            own = pressure[pl.ds(col, 1), :]
            grad_x = x * total[0:1] - total[1:2] - own * (x * summed[S_0 : S_0 + 1] - summed[S_X : S_X + 1])
            grad_y = y * total[0:1] - total[2:3] - own * (y * summed[S_0 : S_0 + 1] - summed[S_Y : S_Y + 1])
            out[0, pl.ds(col, 1), :] = jnp.where(alive, u + kappa * 20.0 * grad_x, 0.0)
            out[1, pl.ds(col, 1), :] = jnp.where(alive, v + kappa * 20.0 * grad_y, 0.0)
        return carry

    lax.fori_loop(0, cols // 4, some_bins, 0)


def push(kappa, pv, halo, fresh, weight, sums, pressure):
    rows, cols, width, deep = weight.shape
    half = cols // 2
    whole = pl.BlockSpec(memory_space=pltpu.VMEM)
    return call(
        functools.partial(push_kernel, kappa),
        grid=(rows, 2),
        in_specs=[whole] * 6
        + [
            pl.BlockSpec((None, half, width, deep), lambda row, part: (row, part, 0, 0)),
            pl.BlockSpec((None, half, 8, width), lambda row, part: (row, part, 0, 0)),
            pl.BlockSpec((None, half, width), lambda row, part: (row, part, 0)),
        ],
        out_specs=pl.BlockSpec((2, None, half, width), lambda row, part: (0, row, part, 0)),
        out_shape=jax.ShapeDtypeStruct((2, rows, cols, width), jnp.float32),
        scratch_shapes=[
            pltpu.VMEM((rows + 2, cols + 2, width), jnp.float32),
            pltpu.VMEM((rows + 2, cols + 2, 8, width), jnp.float32),
        ],
        name="push",
    )(pv, *halo, fresh, weight, sums, pressure)


def local(position, velocity, volume, pressure_prev, fill, drift_from):
    kappa = 1.0 / volume.shape[2]
    old, top = prepare(position, velocity, volume, pressure_prev, fill, drift_from)
    top = lax.pmax(top[0, 0], ("gx", "gy")).reshape(1, 1)
    fresh = drift(top, old, *exchange(old, 2))
    coef, weight, sums, pv = setup(fresh, kappa)
    for step in range(1, SWEEPS):
        last = step == SWEEPS - 1
        pv, *pressure = sweep(kappa, last, pv, exchange(pv, 1), coef, sums)
    velocity_new = push(kappa, pv, exchange(pv, 1), fresh, weight, sums, pressure[0])
    return (pressure[0], velocity_new)


def solution(mesh):
    return jax.shard_map(
        local,
        mesh=mesh,
        in_specs=(
            P(None, "gx", "gy", None),
            P(None, "gx", "gy", None),
            P("gx", "gy", None),
            P("gx", "gy", None),
            P("gx", "gy"),
            P("gx", "gy"),
        ),
        out_specs=(P("gx", "gy", None), P(None, "gx", "gy", None)),
        check_vma=False,
    )
```

time: 350 us -> 309 us (0.88)
  Pallas kernels: 210 us -> 167 us
    pallas_call x5, Pallas kernels: 204 us -> 165 us  [the longest x1 106 us: setup(): call(functools.partial(setup_kernel, kappa), in_specs=[vmem], out_specs=(...]
    unnamed x40 -> x42, local copies, waits for them, and re-layouts: 3.63 us -> 7.81 us
  transfers between devices with their start and end apart: 20 -> 20, of which waited for: 10 -> 10; matrix products, arithmetic and copies ran while one was open for 2% -> 1% of each run, Pallas kernels for 0% -> 0%
where the time goes in v3:
time: 309 us; the launch traced here: 307 us
  Pallas kernels  167 us (54%)
  starting transfers between devices  57.6 us (19%)
  blocking collectives  38.4 us (12%)
  waiting for transfers between devices  26.5 us (9%)
  local copies, waits for them, and re-layouts  16 us (5%)
    pallas_call x1, Pallas kernels, setup(): call(functools.partial(setup_kernel, kappa), in_specs=[vmem], out_specs=(...  106 us
    pmax x1, blocking collectives, local(): top = lax.pmax(top[0, 0], ('gx', 'gy')).reshape(1, 1)  38.4 us
    ppermute x10, starting transfers between devices, neighbours(): lax.ppermute(high_side, axis, up)  33.9 us
    pallas_call x3, Pallas kernels, sweep(): call(functools.partial(sweep_kernel, kappa, last), in_specs=[vmem] * 7, o...  33.1 us
    pallas_call x1, Pallas kernels, push(): call(functools.partial(push_kernel, kappa), grid=(rows, 2), in_specs=[who...  25.4 us
    ppermute x10, starting transfers between devices, neighbours(): lax.ppermute(low_side, axis, down)  23.7 us
    ppermute x10, waiting for transfers between devices, neighbours(): lax.ppermute(high_side, axis, up)  13.6 us
    ppermute x10, waiting for transfers between devices, neighbours(): lax.ppermute(low_side, axis, down)  12.9 us
  transfers between devices with their start and end apart: 20, of which 10 were waited for; matrix products, arithmetic and copies ran while one was open for 1% of the time, Pallas kernels for 0%

profile of v3, /device:TPU:17, one launch (start us, length us, event | category | flops | bytes accessed | tf_op | source)
XLA Modules:
  0.0 306.8 jit_solution(2212752432992278015)
XLA Ops:
  6.1 3.0 collective-permute-start.1
  12.4 3.8 %collective-permute-done.above = f32[2,16,8,128]{3,2,1,0:T(8,128)S(1)} collective-permute-done((f32[2,16,8,128]{3,2,1,0:T(8,128)S(1)}, f32[2,16,8,128]{3,2,1,0:T(8,128)S(1)}, u32[]{:S(2)}, u32[]{:S(2)}) %collective-permute-start) | collective-permute-done | bytes 131104 | tf_op jit(solution)/shard_map/ppermute | solution.py:80
  16.2 4.7 %collective-permute-start.2 = (f32[12,2,8,128]{3,2,1,0:T(8,128)S(1)}, f32[12,2,8,128]{3,2,1,0:T(8,128)S(1)}, u32[]{:S(2)}, u32[]{:S(2)}) collective-permute-start(f32[12,2,8,128]{3,2,1,0:T(8,128)S(1)} %pad_maximum_fusion), channel_id=1, source_target_pairs={{0,1},{1,2},{2,3},{4,5},{5,6},{6,7},{8,9},{9,10},{10,11},{12,13},{... | collective-permute-start | bytes 294920 | tf_op jit(solution)/shard_map/ppermute | solution.py:80
  23.4 38.4 %pmax.7.top = f32[1,1]{1,0:T(1,128)} all-reduce(f32[1,1]{1,0:T(1,128)} %slice.123), channel_id=1, replica_groups=mesh['gx'=8,'gy'=4] {'gx','gy'}, use_global_device_ids=true, to_apply=%region_0.0 | all-reduce | flops 1 | bytes 8 | tf_op jit(solution)/shard_map/pmax | solution.py:393
  64.9 106.1 %setup.1 = (bf16[8,16,128,1152]{3,2,1,0:T(8,128)(2,1)S(1)}, bf16[8,16,128,1152]{3,2,1,0:T(8,128)(2,1)}, f32[8,16,8,128]{3,2,1,0:T(8,128)}, f32[8,16,128]{2,1,0:T(8,128)}) custom-call(f32[10,18,8,128]{3,2,1,0:T(8,128)} %copy-done.1), custom_call_target="tpu_custom_call" | custom-call | tf_op jit(solution)/shard_map/setup/pallas_call | solution.py:244
  171.7 4.4 %collective-permute-start.5 = (f32[1,16,128]{2,1,0:T(8,128)S(1)}, f32[1,16,128]{2,1,0:T(8,128)S(1)}, u32[]{:S(2)}, u32[]{:S(2)}) collective-permute-start(f32[1,16,128]{2,1,0:T(8,128)S(1)} %get-tuple-element.40), channel_id=1, source_target_pairs={{4,0},{8,4},{12,8},{16,12},{20,16},{24,20},{28,24},{5,1},{9,5},{13... | collective-permute-start | bytes 24584 | tf_op jit(solution)/shard_map/ppermute | solution.py:80
  178.8 3.3 %collective-permute-done.4.above = f32[1,16,128]{2,1,0:T(8,128)S(1)} collective-permute-done((f32[1,16,128]{2,1,0:T(8,128)S(1)}, f32[1,16,128]{2,1,0:T(8,128)S(1)}, u32[]{:S(2)}, u32[]{:S(2)}) %collective-permute-start.4) | collective-permute-done | bytes 8224 | tf_op jit(solution)/shard_map/ppermute | solution.py:80
  182.2 5.9 %collective-permute-start.6 = (f32[10,1,128]{2,1,0:T(1,128)S(1)}, f32[10,1,128]{2,1,0:T(1,128)S(1)}, u32[]{:S(2)}, u32[]{:S(2)}) collective-permute-start(f32[10,1,128]{2,1,0:T(1,128)S(1)} %pad_maximum_fusion.2), channel_id=1, source_target_pairs={{0,1},{1,2},{2,3},{4,5},{5,6},{6,7},{8,9},{9,10},{10,11},{12,13},{... | collective-permute-start | bytes 15368 | tf_op jit(solution)/shard_map/ppermute | solution.py:80
  190.0 3.0 collective-permute-done.7.right
  193.6 11.0 %sweep.3.center = f32[8,16,128]{2,1,0:T(8,128)} custom-call(f32[8,16,128]{2,1,0:T(8,128)} %get-tuple-element.12.center, f32[1,16,128]{2,1,0:T(8,128)} %copy-done.13, f32[1,16,128]{2,1,0:T(8,128)} %copy-done.10, f32[10,1,128]{2,1,0:T(1,128)} %copy-done.16, f32[10,1,128]{2,1,0:T(1,128)} %copy-done.19, bf16[8,16,128,1152]{3,2,1,0:T(8,128)(2,1)S(1)} %get-tuple-element.13.coef, ...), custom_call_target="tpu_custom_call" | custom-call | tf_op jit(solution)/shard_map/sweep/pallas_call | solution.py:308
  208.1 3.4 %collective-permute-start.8 = (f32[1,16,128]{2,1,0:T(8,128)S(1)}, f32[1,16,128]{2,1,0:T(8,128)S(1)}, u32[]{:S(2)}, u32[]{:S(2)}) collective-permute-start(f32[1,16,128]{2,1,0:T(8,128)S(1)} %get-tuple-element.37), channel_id=1, source_target_pairs={{0,4},{4,8},{8,12},{12,16},{16,20},{20,24},{24,28},{1,5},{5,9},{9,... | collective-permute-start | bytes 24584 | tf_op jit(solution)/shard_map/ppermute | solution.py:80
  213.4 3.1 %collective-permute-start.10 = (f32[10,1,128]{2,1,0:T(1,128)S(1)}, f32[10,1,128]{2,1,0:T(1,128)S(1)}, u32[]{:S(2)}, u32[]{:S(2)}) collective-permute-start(f32[10,1,128]{2,1,0:T(1,128)S(1)} %pad_maximum_fusion.4), channel_id=1, source_target_pairs={{0,1},{1,2},{2,3},{4,5},{5,6},{6,7},{8,9},{9,10},{10,11},{12,13},{... | collective-permute-start | bytes 15368 | tf_op jit(solution)/shard_map/ppermute | solution.py:80
  218.6 3.0 collective-permute-done.11.right
  222.2 11.0 %sweep.4.center = f32[8,16,128]{2,1,0:T(8,128)} custom-call(f32[8,16,128]{2,1,0:T(8,128)} %sweep.3.center, f32[1,16,128]{2,1,0:T(8,128)} %copy-done.14, f32[1,16,128]{2,1,0:T(8,128)} %copy-done.11, f32[10,1,128]{2,1,0:T(1,128)} %copy-done.17, f32[10,1,128]{2,1,0:T(1,128)} %copy-done.20, bf16[8,16,128,1152]{3,2,1,0:T(8,128)(2,1)S(1)} %get-tuple-element.13.coef, ...), custom_call_target="tpu_custom_call" | custom-call | tf_op jit(solution)/shard_map/sweep/pallas_call | solution.py:308
  233.9 2.7 collective-permute-start.13
  237.4 2.6 collective-permute-start.12
  240.0 2.7 collective-permute-done.12.above
  242.7 3.4 %collective-permute-start.14 = (f32[10,1,128]{2,1,0:T(1,128)S(1)}, f32[10,1,128]{2,1,0:T(1,128)S(1)}, u32[]{:S(2)}, u32[]{:S(2)}) collective-permute-start(f32[10,1,128]{2,1,0:T(1,128)S(1)} %pad_maximum_fusion.6), channel_id=1, source_target_pairs={{0,1},{1,2},{2,3},{4,5},{5,6},{6,7},{8,9},{9,10},{10,11},{12,13},{... | collective-permute-start | bytes 15368 | tf_op jit(solution)/shard_map/ppermute | solution.py:80
  248.0 3.0 collective-permute-done.15.right
  251.6 11.1 %sweep.5 = (f32[8,16,128]{2,1,0:T(8,128)}, f32[8,16,128]{2,1,0:T(8,128)}) custom-call(f32[8,16,128]{2,1,0:T(8,128)} %sweep.4.center, f32[1,16,128]{2,1,0:T(8,128)} %copy-done.12, f32[1,16,128]{2,1,0:T(8,128)} %copy-done.9, f32[10,1,128]{2,1,0:T(1,128)} %copy-done.15, f32[10,1,128]{2,1,0:T(1,128)} %copy-done.18, ...), custom_call_target="tpu_custom_call" | custom-call | tf_op jit(solution)/shard_map/sweep/pallas_call | solution.py:308
  266.1 3.4 %collective-permute-start.16 = (f32[1,16,128]{2,1,0:T(8,128)S(1)}, f32[1,16,128]{2,1,0:T(8,128)S(1)}, u32[]{:S(2)}, u32[]{:S(2)}) collective-permute-start(f32[1,16,128]{2,1,0:T(8,128)S(1)} %get-tuple-element.29), channel_id=1, source_target_pairs={{0,4},{4,8},{8,12},{12,16},{16,20},{20,24},{24,28},{1,5},{5,9},{9,... | collective-permute-start | bytes 24584 | tf_op jit(solution)/shard_map/ppermute | solution.py:80
  271.4 3.4 %collective-permute-start.18 = (f32[10,1,128]{2,1,0:T(1,128)S(1)}, f32[10,1,128]{2,1,0:T(1,128)S(1)}, u32[]{:S(2)}, u32[]{:S(2)}) collective-permute-start(f32[10,1,128]{2,1,0:T(1,128)S(1)} %pad_maximum_fusion.8), channel_id=1, source_target_pairs={{0,1},{1,2},{2,3},{4,5},{5,6},{6,7},{8,9},{9,10},{10,11},{12,13},{... | collective-permute-start | bytes 15368 | tf_op jit(solution)/shard_map/ppermute | solution.py:80
  276.7 3.0 collective-permute-done.19.right
  281.4 25.4 %push.1 = f32[2,8,16,128]{3,2,1,0:T(8,128)} custom-call(f32[8,16,128]{2,1,0:T(8,128)S(1)} %copy-done.5, f32[1,16,128]{2,1,0:T(8,128)S(1)} %collective-permute-done.16.above, f32[1,16,128]{2,1,0:T(8,128)S(1)} %collective-permute-done.17.below, f32[10,1,128]{2,1,0:T(1,128)S(1)} %collective-permute-done.18.left, ...), custom_call_target="tpu_custom_call" | custom-call | tf_op jit(solution)/shard_map/push/pallas_call | solution.py:371
  (99 shorter events, 41.1 us)
Async XLA Ops:
  6.1 6.3 %collective-permute-start.1 = (f32[2,16,8,128]{3,2,1,0:T(8,128)S(1)}, f32[2,16,8,128]{3,2,1,0:T(8,128)S(1)}, u32[]{:S(2)}, u32[]{:S(2)}) collective-permute-start(f32[2,16,8,128]{3,2,1,0:T(8,128)S(1)} %get-tuple-element.20), channel_id=1, source_target_pairs={{4,0},{8,4},{12,8},{16,12},{20,16},{24,20},{28,24},{5,1},{9,5},{13... | collective-permute-start | bytes 393224 | tf_op jit(solution)/shard_map/ppermute | solution.py:80
  9.1 7.0 %collective-permute-start = (f32[2,16,8,128]{3,2,1,0:T(8,128)S(1)}, f32[2,16,8,128]{3,2,1,0:T(8,128)S(1)}, u32[]{:S(2)}, u32[]{:S(2)}) collective-permute-start(f32[2,16,8,128]{3,2,1,0:T(8,128)S(1)} %get-tuple-element.21), channel_id=1, source_target_pairs={{0,4},{4,8},{8,12},{12,16},{16,20},{20,24},{24,28},{1,5},{5,9},{9,... | collective-permute-start | bytes 393224 | tf_op jit(solution)/shard_map/ppermute | solution.py:80
  16.2 45.6 %collective-permute-start.2 = (f32[12,2,8,128]{3,2,1,0:T(8,128)S(1)}, f32[12,2,8,128]{3,2,1,0:T(8,128)S(1)}, u32[]{:S(2)}, u32[]{:S(2)}) collective-permute-start(f32[12,2,8,128]{3,2,1,0:T(8,128)S(1)} %pad_maximum_fusion), channel_id=1, source_target_pairs={{0,1},{1,2},{2,3},{4,5},{5,6},{6,7},{8,9},{9,10},{10,11},{12,13},{... | collective-permute-start | bytes 294920 | tf_op jit(solution)/shard_map/ppermute | solution.py:80
  20.9 40.9 %collective-permute-start.3 = (f32[12,2,8,128]{3,2,1,0:T(8,128)S(1)}, f32[12,2,8,128]{3,2,1,0:T(8,128)S(1)}, u32[]{:S(2)}, u32[]{:S(2)}) collective-permute-start(f32[12,2,8,128]{3,2,1,0:T(8,128)S(1)} %pad_maximum_fusion.1), channel_id=1, source_target_pairs={{1,0},{2,1},{3,2},{5,4},{6,5},{7,6},{9,8},{10,9},{11,10},{13,12},{... | collective-permute-start | bytes 294920 | tf_op jit(solution)/shard_map/ppermute | solution.py:80
  171.7 7.1 %collective-permute-start.5 = (f32[1,16,128]{2,1,0:T(8,128)S(1)}, f32[1,16,128]{2,1,0:T(8,128)S(1)}, u32[]{:S(2)}, u32[]{:S(2)}) collective-permute-start(f32[1,16,128]{2,1,0:T(8,128)S(1)} %get-tuple-element.40), channel_id=1, source_target_pairs={{4,0},{8,4},{12,8},{16,12},{20,16},{24,20},{28,24},{5,1},{9,5},{13... | collective-permute-start | bytes 24584 | tf_op jit(solution)/shard_map/ppermute | solution.py:80
  176.9 5.3 %collective-permute-start.4 = (f32[1,16,128]{2,1,0:T(8,128)S(1)}, f32[1,16,128]{2,1,0:T(8,128)S(1)}, u32[]{:S(2)}, u32[]{:S(2)}) collective-permute-start(f32[1,16,128]{2,1,0:T(8,128)S(1)} %get-tuple-element.41), channel_id=1, source_target_pairs={{0,4},{4,8},{8,12},{12,16},{16,20},{20,24},{24,28},{1,5},{5,9},{9,... | collective-permute-start | bytes 24584 | tf_op jit(solution)/shard_map/ppermute | solution.py:80
  178.8 14.2 %copy-start.10 = (f32[1,16,128]{2,1,0:T(8,128)}, f32[1,16,128]{2,1,0:T(8,128)S(1)}, u32[]{:S(2)}) copy-start(f32[1,16,128]{2,1,0:T(8,128)S(1)} %collective-permute-done.5.below) | copy-start | bytes 24580
  182.2 7.9 %collective-permute-start.6 = (f32[10,1,128]{2,1,0:T(1,128)S(1)}, f32[10,1,128]{2,1,0:T(1,128)S(1)}, u32[]{:S(2)}, u32[]{:S(2)}) collective-permute-start(f32[10,1,128]{2,1,0:T(1,128)S(1)} %pad_maximum_fusion.2), channel_id=1, source_target_pairs={{0,1},{1,2},{2,3},{4,5},{5,6},{6,7},{8,9},{9,10},{10,11},{12,13},{... | collective-permute-start | bytes 15368 | tf_op jit(solution)/shard_map/ppermute | solution.py:80
  188.1 4.9 %collective-permute-start.7 = (f32[10,1,128]{2,1,0:T(1,128)S(1)}, f32[10,1,128]{2,1,0:T(1,128)S(1)}, u32[]{:S(2)}, u32[]{:S(2)}) collective-permute-start(f32[10,1,128]{2,1,0:T(1,128)S(1)} %pad_maximum_fusion.3), channel_id=1, source_target_pairs={{1,0},{2,1},{3,2},{5,4},{6,5},{7,6},{9,8},{10,9},{11,10},{13,12},{... | collective-permute-start | bytes 15368 | tf_op jit(solution)/shard_map/ppermute | solution.py:80
  205.4 6.1 %collective-permute-start.9 = (f32[1,16,128]{2,1,0:T(8,128)S(1)}, f32[1,16,128]{2,1,0:T(8,128)S(1)}, u32[]{:S(2)}, u32[]{:S(2)}) collective-permute-start(f32[1,16,128]{2,1,0:T(8,128)S(1)} %get-tuple-element.36), channel_id=1, source_target_pairs={{4,0},{8,4},{12,8},{16,12},{20,16},{24,20},{28,24},{5,1},{9,5},{13... | collective-permute-start | bytes 24584 | tf_op jit(solution)/shard_map/ppermute | solution.py:80
  208.1 5.3 %collective-permute-start.8 = (f32[1,16,128]{2,1,0:T(8,128)S(1)}, f32[1,16,128]{2,1,0:T(8,128)S(1)}, u32[]{:S(2)}, u32[]{:S(2)}) collective-permute-start(f32[1,16,128]{2,1,0:T(8,128)S(1)} %get-tuple-element.37), channel_id=1, source_target_pairs={{0,4},{4,8},{8,12},{12,16},{16,20},{20,24},{24,28},{1,5},{5,9},{9,... | collective-permute-start | bytes 24584 | tf_op jit(solution)/shard_map/ppermute | solution.py:80
  213.4 5.2 %collective-permute-start.10 = (f32[10,1,128]{2,1,0:T(1,128)S(1)}, f32[10,1,128]{2,1,0:T(1,128)S(1)}, u32[]{:S(2)}, u32[]{:S(2)}) collective-permute-start(f32[10,1,128]{2,1,0:T(1,128)S(1)} %pad_maximum_fusion.4), channel_id=1, source_target_pairs={{0,1},{1,2},{2,3},{4,5},{5,6},{6,7},{8,9},{9,10},{10,11},{12,13},{... | collective-permute-start | bytes 15368 | tf_op jit(solution)/shard_map/ppermute | solution.py:80
  216.5 63.2 %copy-start = (f32[8,16,8,128]{3,2,1,0:T(8,128)S(1)}, f32[8,16,8,128]{3,2,1,0:T(8,128)}, u32[]{:S(2)}) copy-start(f32[8,16,8,128]{3,2,1,0:T(8,128)} %get-tuple-element.14.sums) | copy-start | bytes 1572868
  216.5 63.2 %copy-start.2 = (f32[10,18,8,128]{3,2,1,0:T(8,128)S(1)}, f32[10,18,8,128]{3,2,1,0:T(8,128)}, u32[]{:S(2)}) copy-start(f32[10,18,8,128]{3,2,1,0:T(8,128)} %copy-done.1) | copy-start | bytes 2211844
  216.5 5.1 %collective-permute-start.11 = (f32[10,1,128]{2,1,0:T(1,128)S(1)}, f32[10,1,128]{2,1,0:T(1,128)S(1)}, u32[]{:S(2)}, u32[]{:S(2)}) collective-permute-start(f32[10,1,128]{2,1,0:T(1,128)S(1)} %pad_maximum_fusion.5), channel_id=1, source_target_pairs={{1,0},{2,1},{3,2},{5,4},{6,5},{7,6},{9,8},{10,9},{11,10},{13,12},{... | collective-permute-start | bytes 15368 | tf_op jit(solution)/shard_map/ppermute | solution.py:80
  233.9 6.1 %collective-permute-start.13 = (f32[1,16,128]{2,1,0:T(8,128)S(1)}, f32[1,16,128]{2,1,0:T(8,128)S(1)}, u32[]{:S(2)}, u32[]{:S(2)}) collective-permute-start(f32[1,16,128]{2,1,0:T(8,128)S(1)} %get-tuple-element.32), channel_id=1, source_target_pairs={{4,0},{8,4},{12,8},{16,12},{20,16},{24,20},{28,24},{5,1},{9,5},{13... | collective-permute-start | bytes 24584 | tf_op jit(solution)/shard_map/ppermute | solution.py:80
  237.4 5.3 %collective-permute-start.12 = (f32[1,16,128]{2,1,0:T(8,128)S(1)}, f32[1,16,128]{2,1,0:T(8,128)S(1)}, u32[]{:S(2)}, u32[]{:S(2)}) collective-permute-start(f32[1,16,128]{2,1,0:T(8,128)S(1)} %get-tuple-element.33), channel_id=1, source_target_pairs={{0,4},{4,8},{8,12},{12,16},{16,20},{20,24},{24,28},{1,5},{5,9},{9,... | collective-permute-start | bytes 24584 | tf_op jit(solution)/shard_map/ppermute | solution.py:80
  240.0 11.0 %copy-start.9 = (f32[1,16,128]{2,1,0:T(8,128)}, f32[1,16,128]{2,1,0:T(8,128)S(1)}, u32[]{:S(2)}) copy-start(f32[1,16,128]{2,1,0:T(8,128)S(1)} %collective-permute-done.13.below) | copy-start | bytes 24580
  242.7 5.3 %collective-permute-start.14 = (f32[10,1,128]{2,1,0:T(1,128)S(1)}, f32[10,1,128]{2,1,0:T(1,128)S(1)}, u32[]{:S(2)}, u32[]{:S(2)}) collective-permute-start(f32[10,1,128]{2,1,0:T(1,128)S(1)} %pad_maximum_fusion.6), channel_id=1, source_target_pairs={{0,1},{1,2},{2,3},{4,5},{5,6},{6,7},{8,9},{9,10},{10,11},{12,13},{... | collective-permute-start | bytes 15368 | tf_op jit(solution)/shard_map/ppermute | solution.py:80
  246.1 4.9 %collective-permute-start.15 = (f32[10,1,128]{2,1,0:T(1,128)S(1)}, f32[10,1,128]{2,1,0:T(1,128)S(1)}, u32[]{:S(2)}, u32[]{:S(2)}) collective-permute-start(f32[10,1,128]{2,1,0:T(1,128)S(1)} %pad_maximum_fusion.7), channel_id=1, source_target_pairs={{1,0},{2,1},{3,2},{5,4},{6,5},{7,6},{9,8},{10,9},{11,10},{13,12},{... | collective-permute-start | bytes 15368 | tf_op jit(solution)/shard_map/ppermute | solution.py:80
  263.4 6.1 %collective-permute-start.17 = (f32[1,16,128]{2,1,0:T(8,128)S(1)}, f32[1,16,128]{2,1,0:T(8,128)S(1)}, u32[]{:S(2)}, u32[]{:S(2)}) collective-permute-start(f32[1,16,128]{2,1,0:T(8,128)S(1)} %get-tuple-element.28), channel_id=1, source_target_pairs={{4,0},{8,4},{12,8},{16,12},{20,16},{24,20},{28,24},{5,1},{9,5},{13... | collective-permute-start | bytes 24584 | tf_op jit(solution)/shard_map/ppermute | solution.py:80
  266.1 5.3 %collective-permute-start.16 = (f32[1,16,128]{2,1,0:T(8,128)S(1)}, f32[1,16,128]{2,1,0:T(8,128)S(1)}, u32[]{:S(2)}, u32[]{:S(2)}) collective-permute-start(f32[1,16,128]{2,1,0:T(8,128)S(1)} %get-tuple-element.29), channel_id=1, source_target_pairs={{0,4},{4,8},{8,12},{12,16},{16,20},{20,24},{24,28},{1,5},{5,9},{9,... | collective-permute-start | bytes 24584 | tf_op jit(solution)/shard_map/ppermute | solution.py:80
  271.4 5.3 %collective-permute-start.18 = (f32[10,1,128]{2,1,0:T(1,128)S(1)}, f32[10,1,128]{2,1,0:T(1,128)S(1)}, u32[]{:S(2)}, u32[]{:S(2)}) collective-permute-start(f32[10,1,128]{2,1,0:T(1,128)S(1)} %pad_maximum_fusion.8), channel_id=1, source_target_pairs={{0,1},{1,2},{2,3},{4,5},{5,6},{6,7},{8,9},{9,10},{10,11},{12,13},{... | collective-permute-start | bytes 15368 | tf_op jit(solution)/shard_map/ppermute | solution.py:80
  274.8 4.9 %collective-permute-start.19 = (f32[10,1,128]{2,1,0:T(1,128)S(1)}, f32[10,1,128]{2,1,0:T(1,128)S(1)}, u32[]{:S(2)}, u32[]{:S(2)}) collective-permute-start(f32[10,1,128]{2,1,0:T(1,128)S(1)} %pad_maximum_fusion.9), channel_id=1, source_target_pairs={{1,0},{2,1},{3,2},{5,4},{6,5},{7,6},{9,8},{10,9},{11,10},{13,12},{... | collective-permute-start | bytes 15368 | tf_op jit(solution)/shard_map/ppermute | solution.py:80
  (17 other events, 54.4 us)

commit v4 on v3

--- a/solution.py
+++ b/solution.py
@@ -281,11 +281,12 @@
         row, first = step // (cols // GROUP), lax.rem(step, cols // GROUP) * GROUP
         for col in range(GROUP):
             col = first + col
+            around = [tiles[row + k // 3, col + k % 3] for k in range(9)]
             parts = []
             for part in range(width // 16):
                 total = None
                 for k in range(9):
-                    term = coef[row, col, pl.ds(part * 16, 16), pl.ds(k * width, width)] * tiles[row + k // 3, col + k % 3]
+                    term = coef[row, col, pl.ds(part * 16, 16), pl.ds(k * width, width)] * around[k]
                     total = term if total is None else total + term
                 parts.append(total)
             total = dot_nt(ones, jnp.concatenate(parts, axis=0))[0:1]
@@ -390,7 +391,7 @@
 def local(position, velocity, volume, pressure_prev, fill, drift_from):
     kappa = 1.0 / volume.shape[2]
     old, top = prepare(position, velocity, volume, pressure_prev, fill, drift_from)
-    top = lax.pmax(top[0, 0], ("gx", "gy")).reshape(1, 1)
+    top = lax.all_gather(top, ("gx", "gy"), tiled=True)
     fresh = drift(top, old, *exchange(old, 2))
     coef, weight, sums, pv = setup(fresh, kappa)
     for step in range(1, SWEEPS):

time: 309 us -> 304 us (0.984)
  blocking collectives: 38.4 us -> 32 us
  waiting for transfers between devices: 26.5 us -> 30.9 us
    pmax x1 -> x0, blocking collectives: 38.4 us -> none  [local(): top = lax.pmax(top[0, 0], ('gx', 'gy')).reshape(1, 1)]
    all_gather x0 -> x1, blocking collectives: none -> 32 us  [local(): top = lax.all_gather(top, ('gx', 'gy'), tiled=True)]
    ppermute x10, starting transfers between devices: 33.9 us -> 27.9 us  [neighbours(): lax.ppermute(high_side, axis, up)]
    ppermute x10, waiting for transfers between devices: 13.6 us -> 18.6 us  [neighbours(): lax.ppermute(high_side, axis, up)]
    ppermute x10, starting transfers between devices: 23.7 us -> 28.1 us  [neighbours(): lax.ppermute(low_side, axis, down)]
where the time goes in v4:
time: 304 us; the launch traced here: 302 us
  Pallas kernels  167 us (55%)
  starting transfers between devices  55.9 us (18%)
  blocking collectives  32 us (11%)
  waiting for transfers between devices  30.9 us (10%)
  local copies, waits for them, and re-layouts  15.5 us (5%)
    pallas_call x1, Pallas kernels, setup(): call(functools.partial(setup_kernel, kappa), in_specs=[vmem], out_specs=(...  106 us
    pallas_call x3, Pallas kernels, sweep(): call(functools.partial(sweep_kernel, kappa, last), in_specs=[vmem] * 7, o...  33.1 us
    all_gather x1, blocking collectives, local(): top = lax.all_gather(top, ('gx', 'gy'), tiled=True)  32 us
    ppermute x10, starting transfers between devices, neighbours(): lax.ppermute(low_side, axis, down)  28.1 us
    ppermute x10, starting transfers between devices, neighbours(): lax.ppermute(high_side, axis, up)  27.9 us
    pallas_call x1, Pallas kernels, push(): call(functools.partial(push_kernel, kappa), grid=(rows, 2), in_specs=[who...  25.4 us
    ppermute x10, waiting for transfers between devices, neighbours(): lax.ppermute(high_side, axis, up)  18.6 us
    ppermute x10, waiting for transfers between devices, neighbours(): lax.ppermute(low_side, axis, down)  12.2 us
  transfers between devices with their start and end apart: 20, of which 10 were waited for; matrix products, arithmetic and copies ran while one was open for 1% of the time, Pallas kernels for 0%

profile of v4, /device:TPU:17, one launch (start us, length us, event | category | flops | bytes accessed | tf_op | source)
XLA Modules:
  0.0 302.0 jit_solution(6620172923274699464)
XLA Ops:
  6.1 3.0 collective-permute-start.1
  12.4 3.8 %collective-permute-done.above = f32[2,16,8,128]{3,2,1,0:T(8,128)S(1)} collective-permute-done((f32[2,16,8,128]{3,2,1,0:T(8,128)S(1)}, f32[2,16,8,128]{3,2,1,0:T(8,128)S(1)}, u32[]{:S(2)}, u32[]{:S(2)}) %collective-permute-start) | collective-permute-done | bytes 131104 | tf_op jit(solution)/shard_map/ppermute | solution.py:80
  16.2 4.7 %collective-permute-start.2 = (f32[12,2,8,128]{3,2,1,0:T(8,128)S(1)}, f32[12,2,8,128]{3,2,1,0:T(8,128)S(1)}, u32[]{:S(2)}, u32[]{:S(2)}) collective-permute-start(f32[12,2,8,128]{3,2,1,0:T(8,128)S(1)} %pad_maximum_fusion), channel_id=1, source_target_pairs={{0,1},{1,2},{2,3},{4,5},{5,6},{6,7},{8,9},{9,10},{10,11},{12,13},{... | collective-permute-start | bytes 294920 | tf_op jit(solution)/shard_map/ppermute | solution.py:80
  22.8 32.0 %all_gather.3.top = f32[256,128]{1,0:T(8,128)S(1)} all-gather(f32[8,128]{1,0:T(8,128)S(1)} %get-tuple-element.10), channel_id=1, replica_groups=mesh['gx'=8,'gy'=4] {'gx','gy'}, dimensions={0}, use_global_device_ids=true | all-gather | bytes 135168 | tf_op jit(solution)/shard_map/all_gather | solution.py:394
  57.4 106.0 %setup.1 = (bf16[8,16,128,1152]{3,2,1,0:T(8,128)(2,1)S(1)}, bf16[8,16,128,1152]{3,2,1,0:T(8,128)(2,1)}, f32[8,16,8,128]{3,2,1,0:T(8,128)}, f32[8,16,128]{2,1,0:T(8,128)}) custom-call(f32[10,18,8,128]{3,2,1,0:T(8,128)} %copy-done.1), custom_call_target="tpu_custom_call" | custom-call | tf_op jit(solution)/shard_map/setup/pallas_call | solution.py:244
  166.9 3.4 %collective-permute-start.4 = (f32[1,16,128]{2,1,0:T(8,128)S(1)}, f32[1,16,128]{2,1,0:T(8,128)S(1)}, u32[]{:S(2)}, u32[]{:S(2)}) collective-permute-start(f32[1,16,128]{2,1,0:T(8,128)S(1)} %get-tuple-element.41), channel_id=1, source_target_pairs={{0,4},{4,8},{8,12},{12,16},{16,20},{20,24},{24,28},{1,5},{5,9},{9,... | collective-permute-start | bytes 24584 | tf_op jit(solution)/shard_map/ppermute | solution.py:80
  170.2 3.3 %collective-permute-done.4.above = f32[1,16,128]{2,1,0:T(8,128)S(1)} collective-permute-done((f32[1,16,128]{2,1,0:T(8,128)S(1)}, f32[1,16,128]{2,1,0:T(8,128)S(1)}, u32[]{:S(2)}, u32[]{:S(2)}) %collective-permute-start.4) | collective-permute-done | bytes 8224 | tf_op jit(solution)/shard_map/ppermute | solution.py:80
  175.5 2.6 collective-permute-start.7
  181.0 11.0 %sweep.3.center = f32[8,16,128]{2,1,0:T(8,128)} custom-call(f32[8,16,128]{2,1,0:T(8,128)} %get-tuple-element.12.center, f32[1,16,128]{2,1,0:T(8,128)} %copy-done.13, f32[1,16,128]{2,1,0:T(8,128)} %copy-done.10, f32[10,1,128]{2,1,0:T(1,128)} %copy-done.16, f32[10,1,128]{2,1,0:T(1,128)} %copy-done.19, bf16[8,16,128,1152]{3,2,1,0:T(8,128)(2,1)S(1)} %get-tuple-element.13.coef, ...), custom_call_target="tpu_custom_call" | custom-call | tf_op jit(solution)/shard_map/sweep/pallas_call | solution.py:309
  192.8 5.8 %collective-permute-start.9 = (f32[1,16,128]{2,1,0:T(8,128)S(1)}, f32[1,16,128]{2,1,0:T(8,128)S(1)}, u32[]{:S(2)}, u32[]{:S(2)}) collective-permute-start(f32[1,16,128]{2,1,0:T(8,128)S(1)} %get-tuple-element.36), channel_id=1, source_target_pairs={{4,0},{8,4},{12,8},{16,12},{20,16},{24,20},{28,24},{5,1},{9,5},{13... | collective-permute-start | bytes 24584 | tf_op jit(solution)/shard_map/ppermute | solution.py:80
  201.3 4.9 %collective-permute-done.8.above = f32[1,16,128]{2,1,0:T(8,128)S(1)} collective-permute-done((f32[1,16,128]{2,1,0:T(8,128)S(1)}, f32[1,16,128]{2,1,0:T(8,128)S(1)}, u32[]{:S(2)}, u32[]{:S(2)}) %collective-permute-start.8) | collective-permute-done | bytes 8224 | tf_op jit(solution)/shard_map/ppermute | solution.py:80
  206.2 3.1 %collective-permute-start.10 = (f32[10,1,128]{2,1,0:T(1,128)S(1)}, f32[10,1,128]{2,1,0:T(1,128)S(1)}, u32[]{:S(2)}, u32[]{:S(2)}) collective-permute-start(f32[10,1,128]{2,1,0:T(1,128)S(1)} %pad_maximum_fusion.4), channel_id=1, source_target_pairs={{0,1},{1,2},{2,3},{4,5},{5,6},{6,7},{8,9},{9,10},{10,11},{12,13},{... | collective-permute-start | bytes 15368 | tf_op jit(solution)/shard_map/ppermute | solution.py:80
  211.4 3.0 collective-permute-done.11.right
  215.0 11.0 %sweep.4.center = f32[8,16,128]{2,1,0:T(8,128)} custom-call(f32[8,16,128]{2,1,0:T(8,128)} %sweep.3.center, f32[1,16,128]{2,1,0:T(8,128)} %copy-done.14, f32[1,16,128]{2,1,0:T(8,128)} %copy-done.11, f32[10,1,128]{2,1,0:T(1,128)} %copy-done.17, f32[10,1,128]{2,1,0:T(1,128)} %copy-done.20, bf16[8,16,128,1152]{3,2,1,0:T(8,128)(2,1)S(1)} %get-tuple-element.13.coef, ...), custom_call_target="tpu_custom_call" | custom-call | tf_op jit(solution)/shard_map/sweep/pallas_call | solution.py:309
  226.7 3.6 %collective-permute-start.13 = (f32[1,16,128]{2,1,0:T(8,128)S(1)}, f32[1,16,128]{2,1,0:T(8,128)S(1)}, u32[]{:S(2)}, u32[]{:S(2)}) collective-permute-start(f32[1,16,128]{2,1,0:T(8,128)S(1)} %get-tuple-element.32), channel_id=1, source_target_pairs={{4,0},{8,4},{12,8},{16,12},{20,16},{24,20},{28,24},{5,1},{9,5},{13... | collective-permute-start | bytes 24584 | tf_op jit(solution)/shard_map/ppermute | solution.py:80
  233.1 3.3 %collective-permute-done.12.above = f32[1,16,128]{2,1,0:T(8,128)S(1)} collective-permute-done((f32[1,16,128]{2,1,0:T(8,128)S(1)}, f32[1,16,128]{2,1,0:T(8,128)S(1)}, u32[]{:S(2)}, u32[]{:S(2)}) %collective-permute-start.12) | collective-permute-done | bytes 8224 | tf_op jit(solution)/shard_map/ppermute | solution.py:80
  236.5 3.4 %collective-permute-start.14 = (f32[10,1,128]{2,1,0:T(1,128)S(1)}, f32[10,1,128]{2,1,0:T(1,128)S(1)}, u32[]{:S(2)}, u32[]{:S(2)}) collective-permute-start(f32[10,1,128]{2,1,0:T(1,128)S(1)} %pad_maximum_fusion.6), channel_id=1, source_target_pairs={{0,1},{1,2},{2,3},{4,5},{5,6},{6,7},{8,9},{9,10},{10,11},{12,13},{... | collective-permute-start | bytes 15368 | tf_op jit(solution)/shard_map/ppermute | solution.py:80
  241.8 3.0 collective-permute-done.15.right
  245.4 11.1 %sweep.5 = (f32[8,16,128]{2,1,0:T(8,128)}, f32[8,16,128]{2,1,0:T(8,128)}) custom-call(f32[8,16,128]{2,1,0:T(8,128)} %sweep.4.center, f32[1,16,128]{2,1,0:T(8,128)} %copy-done.12, f32[1,16,128]{2,1,0:T(8,128)} %copy-done.9, f32[10,1,128]{2,1,0:T(1,128)} %copy-done.15, f32[10,1,128]{2,1,0:T(1,128)} %copy-done.18, ...), custom_call_target="tpu_custom_call" | custom-call | tf_op jit(solution)/shard_map/sweep/pallas_call | solution.py:309
  257.2 3.4 %collective-permute-start.17 = (f32[1,16,128]{2,1,0:T(8,128)S(1)}, f32[1,16,128]{2,1,0:T(8,128)S(1)}, u32[]{:S(2)}, u32[]{:S(2)}) collective-permute-start(f32[1,16,128]{2,1,0:T(8,128)S(1)} %get-tuple-element.28), channel_id=1, source_target_pairs={{4,0},{8,4},{12,8},{16,12},{20,16},{24,20},{28,24},{5,1},{9,5},{13... | collective-permute-start | bytes 24584 | tf_op jit(solution)/shard_map/ppermute | solution.py:80
  263.2 3.3 %collective-permute-done.16.above = f32[1,16,128]{2,1,0:T(8,128)S(1)} collective-permute-done((f32[1,16,128]{2,1,0:T(8,128)S(1)}, f32[1,16,128]{2,1,0:T(8,128)S(1)}, u32[]{:S(2)}, u32[]{:S(2)}) %collective-permute-start.16) | collective-permute-done | bytes 8224 | tf_op jit(solution)/shard_map/ppermute | solution.py:80
  266.6 3.4 %collective-permute-start.18 = (f32[10,1,128]{2,1,0:T(1,128)S(1)}, f32[10,1,128]{2,1,0:T(1,128)S(1)}, u32[]{:S(2)}, u32[]{:S(2)}) collective-permute-start(f32[10,1,128]{2,1,0:T(1,128)S(1)} %pad_maximum_fusion.8), channel_id=1, source_target_pairs={{0,1},{1,2},{2,3},{4,5},{5,6},{6,7},{8,9},{9,10},{10,11},{12,13},{... | collective-permute-start | bytes 15368 | tf_op jit(solution)/shard_map/ppermute | solution.py:80
  271.9 3.0 collective-permute-done.19.right
  276.6 25.4 %push.1 = f32[2,8,16,128]{3,2,1,0:T(8,128)} custom-call(f32[8,16,128]{2,1,0:T(8,128)S(1)} %copy-done.5, f32[1,16,128]{2,1,0:T(8,128)S(1)} %collective-permute-done.16.above, f32[1,16,128]{2,1,0:T(8,128)S(1)} %collective-permute-done.17.below, f32[10,1,128]{2,1,0:T(1,128)S(1)} %collective-permute-done.18.left, ...), custom_call_target="tpu_custom_call" | custom-call | tf_op jit(solution)/shard_map/push/pallas_call | solution.py:372
  (98 shorter events, 40.5 us)
Async XLA Ops:
  6.1 6.3 %collective-permute-start.1 = (f32[2,16,8,128]{3,2,1,0:T(8,128)S(1)}, f32[2,16,8,128]{3,2,1,0:T(8,128)S(1)}, u32[]{:S(2)}, u32[]{:S(2)}) collective-permute-start(f32[2,16,8,128]{3,2,1,0:T(8,128)S(1)} %get-tuple-element.20), channel_id=1, source_target_pairs={{4,0},{8,4},{12,8},{16,12},{20,16},{24,20},{28,24},{5,1},{9,5},{13... | collective-permute-start | bytes 393224 | tf_op jit(solution)/shard_map/ppermute | solution.py:80
  9.1 7.0 %collective-permute-start = (f32[2,16,8,128]{3,2,1,0:T(8,128)S(1)}, f32[2,16,8,128]{3,2,1,0:T(8,128)S(1)}, u32[]{:S(2)}, u32[]{:S(2)}) collective-permute-start(f32[2,16,8,128]{3,2,1,0:T(8,128)S(1)} %get-tuple-element.21), channel_id=1, source_target_pairs={{0,4},{4,8},{8,12},{12,16},{16,20},{20,24},{24,28},{1,5},{5,9},{9,... | collective-permute-start | bytes 393224 | tf_op jit(solution)/shard_map/ppermute | solution.py:80
  16.2 38.7 %collective-permute-start.2 = (f32[12,2,8,128]{3,2,1,0:T(8,128)S(1)}, f32[12,2,8,128]{3,2,1,0:T(8,128)S(1)}, u32[]{:S(2)}, u32[]{:S(2)}) collective-permute-start(f32[12,2,8,128]{3,2,1,0:T(8,128)S(1)} %pad_maximum_fusion), channel_id=1, source_target_pairs={{0,1},{1,2},{2,3},{4,5},{5,6},{6,7},{8,9},{9,10},{10,11},{12,13},{... | collective-permute-start | bytes 294920 | tf_op jit(solution)/shard_map/ppermute | solution.py:80
  20.9 33.9 %collective-permute-start.3 = (f32[12,2,8,128]{3,2,1,0:T(8,128)S(1)}, f32[12,2,8,128]{3,2,1,0:T(8,128)S(1)}, u32[]{:S(2)}, u32[]{:S(2)}) collective-permute-start(f32[12,2,8,128]{3,2,1,0:T(8,128)S(1)} %pad_maximum_fusion.1), channel_id=1, source_target_pairs={{1,0},{2,1},{3,2},{5,4},{6,5},{7,6},{9,8},{10,9},{11,10},{13,12},{... | collective-permute-start | bytes 294920 | tf_op jit(solution)/shard_map/ppermute | solution.py:80
  164.2 6.1 %collective-permute-start.5 = (f32[1,16,128]{2,1,0:T(8,128)S(1)}, f32[1,16,128]{2,1,0:T(8,128)S(1)}, u32[]{:S(2)}, u32[]{:S(2)}) collective-permute-start(f32[1,16,128]{2,1,0:T(8,128)S(1)} %get-tuple-element.40), channel_id=1, source_target_pairs={{4,0},{8,4},{12,8},{16,12},{20,16},{24,20},{28,24},{5,1},{9,5},{13... | collective-permute-start | bytes 24584 | tf_op jit(solution)/shard_map/ppermute | solution.py:80
  166.9 6.7 %collective-permute-start.4 = (f32[1,16,128]{2,1,0:T(8,128)S(1)}, f32[1,16,128]{2,1,0:T(8,128)S(1)}, u32[]{:S(2)}, u32[]{:S(2)}) collective-permute-start(f32[1,16,128]{2,1,0:T(8,128)S(1)} %get-tuple-element.41), channel_id=1, source_target_pairs={{0,4},{4,8},{8,12},{12,16},{16,20},{20,24},{24,28},{1,5},{5,9},{9,... | collective-permute-start | bytes 24584 | tf_op jit(solution)/shard_map/ppermute | solution.py:80
  173.6 4.5 %collective-permute-start.6 = (f32[10,1,128]{2,1,0:T(1,128)S(1)}, f32[10,1,128]{2,1,0:T(1,128)S(1)}, u32[]{:S(2)}, u32[]{:S(2)}) collective-permute-start(f32[10,1,128]{2,1,0:T(1,128)S(1)} %pad_maximum_fusion.2), channel_id=1, source_target_pairs={{0,1},{1,2},{2,3},{4,5},{5,6},{6,7},{8,9},{9,10},{10,11},{12,13},{... | collective-permute-start | bytes 15368 | tf_op jit(solution)/shard_map/ppermute | solution.py:80
  175.5 4.9 %collective-permute-start.7 = (f32[10,1,128]{2,1,0:T(1,128)S(1)}, f32[10,1,128]{2,1,0:T(1,128)S(1)}, u32[]{:S(2)}, u32[]{:S(2)}) collective-permute-start(f32[10,1,128]{2,1,0:T(1,128)S(1)} %pad_maximum_fusion.3), channel_id=1, source_target_pairs={{1,0},{2,1},{3,2},{5,4},{6,5},{7,6},{9,8},{10,9},{11,10},{13,12},{... | collective-permute-start | bytes 15368 | tf_op jit(solution)/shard_map/ppermute | solution.py:80
  192.8 8.5 %collective-permute-start.9 = (f32[1,16,128]{2,1,0:T(8,128)S(1)}, f32[1,16,128]{2,1,0:T(8,128)S(1)}, u32[]{:S(2)}, u32[]{:S(2)}) collective-permute-start(f32[1,16,128]{2,1,0:T(8,128)S(1)} %get-tuple-element.36), channel_id=1, source_target_pairs={{4,0},{8,4},{12,8},{16,12},{20,16},{24,20},{28,24},{5,1},{9,5},{13... | collective-permute-start | bytes 24584 | tf_op jit(solution)/shard_map/ppermute | solution.py:80
  199.3 6.8 %collective-permute-start.8 = (f32[1,16,128]{2,1,0:T(8,128)S(1)}, f32[1,16,128]{2,1,0:T(8,128)S(1)}, u32[]{:S(2)}, u32[]{:S(2)}) collective-permute-start(f32[1,16,128]{2,1,0:T(8,128)S(1)} %get-tuple-element.37), channel_id=1, source_target_pairs={{0,4},{4,8},{8,12},{12,16},{16,20},{20,24},{24,28},{1,5},{5,9},{9,... | collective-permute-start | bytes 24584 | tf_op jit(solution)/shard_map/ppermute | solution.py:80
  201.3 13.1 %copy-start.11 = (f32[1,16,128]{2,1,0:T(8,128)}, f32[1,16,128]{2,1,0:T(8,128)S(1)}, u32[]{:S(2)}) copy-start(f32[1,16,128]{2,1,0:T(8,128)S(1)} %collective-permute-done.9.below) | copy-start | bytes 24580
  206.2 5.2 %collective-permute-start.10 = (f32[10,1,128]{2,1,0:T(1,128)S(1)}, f32[10,1,128]{2,1,0:T(1,128)S(1)}, u32[]{:S(2)}, u32[]{:S(2)}) collective-permute-start(f32[10,1,128]{2,1,0:T(1,128)S(1)} %pad_maximum_fusion.4), channel_id=1, source_target_pairs={{0,1},{1,2},{2,3},{4,5},{5,6},{6,7},{8,9},{9,10},{10,11},{12,13},{... | collective-permute-start | bytes 15368 | tf_op jit(solution)/shard_map/ppermute | solution.py:80
  209.3 65.6 %copy-start = (f32[8,16,8,128]{3,2,1,0:T(8,128)S(1)}, f32[8,16,8,128]{3,2,1,0:T(8,128)}, u32[]{:S(2)}) copy-start(f32[8,16,8,128]{3,2,1,0:T(8,128)} %get-tuple-element.14.sums) | copy-start | bytes 1572868
  209.3 65.6 %copy-start.2 = (f32[10,18,8,128]{3,2,1,0:T(8,128)S(1)}, f32[10,18,8,128]{3,2,1,0:T(8,128)}, u32[]{:S(2)}) copy-start(f32[10,18,8,128]{3,2,1,0:T(8,128)} %copy-done.1) | copy-start | bytes 2211844
  209.3 5.1 %collective-permute-start.11 = (f32[10,1,128]{2,1,0:T(1,128)S(1)}, f32[10,1,128]{2,1,0:T(1,128)S(1)}, u32[]{:S(2)}, u32[]{:S(2)}) collective-permute-start(f32[10,1,128]{2,1,0:T(1,128)S(1)} %pad_maximum_fusion.5), channel_id=1, source_target_pairs={{1,0},{2,1},{3,2},{5,4},{6,5},{7,6},{9,8},{10,9},{11,10},{13,12},{... | collective-permute-start | bytes 15368 | tf_op jit(solution)/shard_map/ppermute | solution.py:80
  226.7 6.3 %collective-permute-start.13 = (f32[1,16,128]{2,1,0:T(8,128)S(1)}, f32[1,16,128]{2,1,0:T(8,128)S(1)}, u32[]{:S(2)}, u32[]{:S(2)}) collective-permute-start(f32[1,16,128]{2,1,0:T(8,128)S(1)} %get-tuple-element.32), channel_id=1, source_target_pairs={{4,0},{8,4},{12,8},{16,12},{20,16},{24,20},{28,24},{5,1},{9,5},{13... | collective-permute-start | bytes 24584 | tf_op jit(solution)/shard_map/ppermute | solution.py:80
  231.2 5.3 %collective-permute-start.12 = (f32[1,16,128]{2,1,0:T(8,128)S(1)}, f32[1,16,128]{2,1,0:T(8,128)S(1)}, u32[]{:S(2)}, u32[]{:S(2)}) collective-permute-start(f32[1,16,128]{2,1,0:T(8,128)S(1)} %get-tuple-element.33), channel_id=1, source_target_pairs={{0,4},{4,8},{8,12},{12,16},{16,20},{20,24},{24,28},{1,5},{5,9},{9,... | collective-permute-start | bytes 24584 | tf_op jit(solution)/shard_map/ppermute | solution.py:80
  233.1 11.7 %copy-start.9 = (f32[1,16,128]{2,1,0:T(8,128)}, f32[1,16,128]{2,1,0:T(8,128)S(1)}, u32[]{:S(2)}) copy-start(f32[1,16,128]{2,1,0:T(8,128)S(1)} %collective-permute-done.13.below) | copy-start | bytes 24580
  236.5 5.3 %collective-permute-start.14 = (f32[10,1,128]{2,1,0:T(1,128)S(1)}, f32[10,1,128]{2,1,0:T(1,128)S(1)}, u32[]{:S(2)}, u32[]{:S(2)}) collective-permute-start(f32[10,1,128]{2,1,0:T(1,128)S(1)} %pad_maximum_fusion.6), channel_id=1, source_target_pairs={{0,1},{1,2},{2,3},{4,5},{5,6},{6,7},{8,9},{9,10},{10,11},{12,13},{... | collective-permute-start | bytes 15368 | tf_op jit(solution)/shard_map/ppermute | solution.py:80
  239.9 4.9 %collective-permute-start.15 = (f32[10,1,128]{2,1,0:T(1,128)S(1)}, f32[10,1,128]{2,1,0:T(1,128)S(1)}, u32[]{:S(2)}, u32[]{:S(2)}) collective-permute-start(f32[10,1,128]{2,1,0:T(1,128)S(1)} %pad_maximum_fusion.7), channel_id=1, source_target_pairs={{1,0},{2,1},{3,2},{5,4},{6,5},{7,6},{9,8},{10,9},{11,10},{13,12},{... | collective-permute-start | bytes 15368 | tf_op jit(solution)/shard_map/ppermute | solution.py:80
  257.2 6.1 %collective-permute-start.17 = (f32[1,16,128]{2,1,0:T(8,128)S(1)}, f32[1,16,128]{2,1,0:T(8,128)S(1)}, u32[]{:S(2)}, u32[]{:S(2)}) collective-permute-start(f32[1,16,128]{2,1,0:T(8,128)S(1)} %get-tuple-element.28), channel_id=1, source_target_pairs={{4,0},{8,4},{12,8},{16,12},{20,16},{24,20},{28,24},{5,1},{9,5},{13... | collective-permute-start | bytes 24584 | tf_op jit(solution)/shard_map/ppermute | solution.py:80
  261.3 5.3 %collective-permute-start.16 = (f32[1,16,128]{2,1,0:T(8,128)S(1)}, f32[1,16,128]{2,1,0:T(8,128)S(1)}, u32[]{:S(2)}, u32[]{:S(2)}) collective-permute-start(f32[1,16,128]{2,1,0:T(8,128)S(1)} %get-tuple-element.29), channel_id=1, source_target_pairs={{0,4},{4,8},{8,12},{12,16},{16,20},{20,24},{24,28},{1,5},{5,9},{9,... | collective-permute-start | bytes 24584 | tf_op jit(solution)/shard_map/ppermute | solution.py:80
  266.6 5.3 %collective-permute-start.18 = (f32[10,1,128]{2,1,0:T(1,128)S(1)}, f32[10,1,128]{2,1,0:T(1,128)S(1)}, u32[]{:S(2)}, u32[]{:S(2)}) collective-permute-start(f32[10,1,128]{2,1,0:T(1,128)S(1)} %pad_maximum_fusion.8), channel_id=1, source_target_pairs={{0,1},{1,2},{2,3},{4,5},{5,6},{6,7},{8,9},{9,10},{10,11},{12,13},{... | collective-permute-start | bytes 15368 | tf_op jit(solution)/shard_map/ppermute | solution.py:80
  270.0 4.9 %collective-permute-start.19 = (f32[10,1,128]{2,1,0:T(1,128)S(1)}, f32[10,1,128]{2,1,0:T(1,128)S(1)}, u32[]{:S(2)}, u32[]{:S(2)}) collective-permute-start(f32[10,1,128]{2,1,0:T(1,128)S(1)} %pad_maximum_fusion.9), channel_id=1, source_target_pairs={{1,0},{2,1},{3,2},{5,4},{6,5},{7,6},{9,8},{10,9},{11,10},{13,12},{... | collective-permute-start | bytes 15368 | tf_op jit(solution)/shard_map/ppermute | solution.py:80
  (17 other events, 49.9 us)

commit v5 on v4

--- a/solution.py
+++ b/solution.py
@@ -12,11 +12,9 @@
 SPEED_EPS = 1e-06
 SOFT = 0.01
 CHUNK = 32
-GROUP = 4
 VMEM_LIMIT = 20 * 1024 * 1024
 
 X, Y, U, V, VOL, PRES, CODE = range(7)
-S_0, S_X, S_Y, S_SOURCE, S_RDEN, S_VOL = range(6)
 
 
 def call(kernel, **kwargs):
@@ -88,6 +86,18 @@
     return above, below, left, right
 
 
+def largest(value):
+    for axis in ("gy", "gx"):
+        devices = lax.axis_size(axis)
+        if devices & (devices - 1):
+            value = lax.pmax(value, axis)
+            continue
+        for bit in range(devices.bit_length() - 1):
+            pairs = [(i, i ^ (1 << bit)) for i in range(devices)]
+            value = jnp.maximum(value, lax.ppermute(value, axis, pairs))
+    return value
+
+
 def assemble(out, center, above, below, left, right, depth):
     rows, cols = center.shape[:2]
     out[:depth, depth : depth + cols] = above[...]
@@ -159,23 +169,29 @@
 
     def blocks(bin_id, slot, both):
         row, col = bin_id // cols, lax.rem(bin_id, cols)
-        for k in range(9):
-            tile = fresh[row + k // 3, col + k % 3]
-            xj = tile[X : X + 1] + (k // 3 - 1.0)
-            yj = tile[Y : Y + 1] + (k % 3 - 1.0)
-            lanes = pl.ds(k * width, width)
-            for part in range(width // CHUNK):
-                span = pl.ds(part * CHUNK, CHUNK)
-                dx = xcol[slot, span] - xj
-                dy = ycol[slot, span] - yj
-                square = jnp.maximum(dx * dx + dy * dy, 1e-14)
-                remain = jnp.maximum(1.0 - square * lax.rsqrt(square), 0.0)
-                cubed = remain * remain * remain
-                ratio = square * pl.reciprocal(square + SOFT, approx=True)
-                value = (cubed * ratio).astype(jnp.bfloat16)
-                both[span, lanes] = cubed.astype(jnp.bfloat16)
-                both[pl.ds(width + part * CHUNK, CHUNK), lanes] = value
-                coef[row, col, span, lanes] = value
+        around = [fresh[row + k // 3, col + k % 3] for k in range(9)]
+        xj = [jnp.broadcast_to(around[k][X : X + 1] + (k // 3 - 1.0), (8, width)) for k in range(9)]
+        yj = [jnp.broadcast_to(around[k][Y : Y + 1] + (k % 3 - 1.0), (8, width)) for k in range(9)]
+        for part in range(width // CHUNK):
+            spans = [pl.ds(part * CHUNK + 8 * i, 8) for i in range(CHUNK // 8)]
+            xi = [xcol[slot, span] for span in spans]
+            yi = [ycol[slot, span] for span in spans]
+            for k in range(9):
+                lanes = pl.ds(k * width, width)
+                weights, values = [], []
+                for x, y in zip(xi, yi):
+                    dx = x - xj[k]
+                    dy = y - yj[k]
+                    square = jnp.maximum(dx * dx + dy * dy, 1e-14)
+                    remain = jnp.maximum(1.0 - square * lax.rsqrt(square), 0.0)
+                    cubed = remain * remain * remain
+                    weights.append(cubed)
+                    values.append(cubed * (square * pltpu.reciprocal(square + SOFT, approx=True)))
+                weights = jnp.concatenate(weights, axis=0).astype(jnp.bfloat16)
+                values = jnp.concatenate(values, axis=0).astype(jnp.bfloat16)
+                both[pl.ds(part * CHUNK, CHUNK), lanes] = weights
+                both[pl.ds(width + part * CHUNK, CHUNK), lanes] = values
+                coef[row, col, pl.ds(part * CHUNK, CHUNK), lanes] = values
 
     def finish(bin_id, both):
         row, col = bin_id // cols, lax.rem(bin_id, cols)
@@ -199,7 +215,8 @@
         source = kappa * 20.0 * source
         rden = 1.0 / (1.0 + kappa * 40.0 * total_c[0:1])
         first = (source + kappa * 40.0 * total_c[6:7]) * rden
-        sums[row, col] = jnp.concatenate([w_0, w_x, w_y, source, rden, vol, first, vol], axis=0)
+        for place, value in enumerate((source, rden, vol)):
+            sums[place, row, pl.ds(col, 1), :] = value
         pv[row, pl.ds(col, 1), :] = first * vol
 
     def copy_out(bin_id, both, slot):
@@ -248,7 +265,7 @@
         out_shape=(
             pltpu.VMEM((rows, cols, width, 9 * width), jnp.bfloat16),
             jax.ShapeDtypeStruct((rows, cols, width, 9 * width), jnp.bfloat16),
-            jax.ShapeDtypeStruct((rows, cols, 8, width), jnp.float32),
+            jax.ShapeDtypeStruct((3, rows, cols, width), jnp.float32),
             jax.ShapeDtypeStruct((rows, cols, width), jnp.float32),
         ),
         scratch_shapes=[
@@ -277,10 +294,9 @@
     lax.fori_loop(0, rows + 2, spread, 0)
     ones = jnp.ones((16, width), jnp.bfloat16)
 
-    def some_bins(step, carry):
-        row, first = step // (cols // GROUP), lax.rem(step, cols // GROUP) * GROUP
-        for col in range(GROUP):
-            col = first + col
+    def one_row(row, carry):
+        totals = []
+        for col in range(cols):
             around = [tiles[row + k // 3, col + k % 3] for k in range(9)]
             parts = []
             for part in range(width // 16):
@@ -289,16 +305,16 @@
                     term = coef[row, col, pl.ds(part * 16, 16), pl.ds(k * width, width)] * around[k]
                     total = term if total is None else total + term
                 parts.append(total)
-            total = dot_nt(ones, jnp.concatenate(parts, axis=0))[0:1]
-            tile = sums[row, col]
-            value = (tile[S_SOURCE : S_SOURCE + 1] + kappa * 40.0 * total) * tile[S_RDEN : S_RDEN + 1]
-            vol = tile[S_VOL : S_VOL + 1]
-            pv[row, pl.ds(col, 1), :] = value * vol
-            if last:
-                pressure[row, pl.ds(col, 1), :] = jnp.where(vol > 0.0, value, 0.0)
+            totals.append(dot_nt(ones, jnp.concatenate(parts, axis=0))[0:1])
+        total = jnp.concatenate(totals, axis=0)
+        value = (sums[0, row] + kappa * 40.0 * total) * sums[1, row]
+        vol = sums[2, row]
+        pv[row] = value * vol
+        if last:
+            pressure[row] = jnp.where(vol > 0.0, value, 0.0)
         return carry
 
-    lax.fori_loop(0, rows * cols // GROUP, some_bins, 0)
+    lax.fori_loop(0, rows, one_row, 0)
 
 
 def sweep(kappa, last, pv, halo, coef, sums):
@@ -319,85 +335,85 @@
     )(pv, *halo, pltpu.with_memory_space_constraint(coef, pltpu.VMEM), sums)
 
 
-def push_kernel(kappa, center, above, below, left, right, fresh, weight, sums, pressure, out, ext, feat):
-    row, half = pl.program_id(0), pl.program_id(1)
+def push_kernel(kappa, center, above, below, left, right, fresh, weight, pressure, out, ext, feat):
+    row = pl.program_id(0)
     cols, width, _ = weight.shape
 
-    @pl.when((row == 0) & (half == 0))
+    @pl.when(row == 0)
     def _():
         assemble(ext, center, above, below, left, right, 1)
 
         def one_row(r, carry):
+            tiles = []
             for col in range(ext.shape[1]):
                 value = ext[r, col : col + 1, :]
                 tile = fresh[r, col]
-                parts = [value, value * tile[X : X + 1], value * tile[Y : Y + 1], jnp.zeros((5, width), jnp.float32)]
-                feat[r, col] = jnp.concatenate(parts, axis=0)
+                x, y, vol = tile[X : X + 1], tile[Y : Y + 1], tile[VOL : VOL + 1]
+                zero = jnp.zeros_like(x)
+                tiles.append(jnp.concatenate([value, value * x, value * y, zero, vol, vol * x, vol * y, zero], axis=0))
+            for col in range(ext.shape[1]):
+                feat[r, col] = tiles[col]
             return carry
 
         lax.fori_loop(0, ext.shape[0], one_row, 0)
 
     index = row_index(width)
-
-    def some_bins(step, carry):
-        for col in range(4):
-            col = step * 4 + col
-            place = half * cols + col
-            around = []
-            for k in range(9):
-                tile = feat[row + k // 3, place + k % 3]
-                off_x, off_y = k // 3 - 1.0, k % 3 - 1.0
-                scale = jnp.where(index == 1, off_x, jnp.where(index == 2, off_y, 0.0))
-                around.append(split(tile + scale * tile[0:1]))
-            total = dot_nt(weight[col], jnp.concatenate(around, axis=1))
-            total = (total[:, :8] + total[:, 8:]).T
-            tile = fresh[row + 1, place + 1]
-            summed = sums[col]
-            x, y, u, v = (tile[i : i + 1] for i in range(4))
-            alive = tile[VOL : VOL + 1] > 0.0
-            own = pressure[pl.ds(col, 1), :]
-            grad_x = x * total[0:1] - total[1:2] - own * (x * summed[S_0 : S_0 + 1] - summed[S_X : S_X + 1])
-            grad_y = y * total[0:1] - total[2:3] - own * (y * summed[S_0 : S_0 + 1] - summed[S_Y : S_Y + 1])
-            out[0, pl.ds(col, 1), :] = jnp.where(alive, u + kappa * 20.0 * grad_x, 0.0)
-            out[1, pl.ds(col, 1), :] = jnp.where(alive, v + kappa * 20.0 * grad_y, 0.0)
-        return carry
-
-    lax.fori_loop(0, cols // 4, some_bins, 0)
-
-
-def push(kappa, pv, halo, fresh, weight, sums, pressure):
+    news = ([], [])
+    for col in range(cols):
+        around = []
+        for k in range(9):
+            tile = feat[row + k // 3, col + k % 3]
+            off_x, off_y = k // 3 - 1.0, k % 3 - 1.0
+            pv, vol = tile[0:1], tile[4:5]
+            if off_x:
+                tile = tile + jnp.where(index == 1, off_x * pv, jnp.where(index == 5, off_x * vol, 0.0))
+            if off_y:
+                tile = tile + jnp.where(index == 2, off_y * pv, jnp.where(index == 6, off_y * vol, 0.0))
+            around.append(split(tile))
+        total = dot_nt(weight[col], jnp.concatenate(around, axis=1))
+        total = (total[:, :8] + total[:, 8:]).T
+        tile = fresh[row + 1, col + 1]
+        own = pressure[col : col + 1, :]
+        alive = tile[VOL : VOL + 1] > 0.0
+        for axis in (0, 1):
+            at = tile[axis : axis + 1]
+            grad = at * total[0:1] - total[1 + axis : 2 + axis] - own * (at * total[4:5] - total[5 + axis : 6 + axis])
+            news[axis].append(jnp.where(alive, tile[2 + axis : 3 + axis] + kappa * 20.0 * grad, 0.0))
+    out[0] = jnp.concatenate(news[0], axis=0)
+    out[1] = jnp.concatenate(news[1], axis=0)
+
+
+def push(kappa, pv, halo, fresh, weight, pressure):
     rows, cols, width, deep = weight.shape
-    half = cols // 2
     whole = pl.BlockSpec(memory_space=pltpu.VMEM)
     return call(
         functools.partial(push_kernel, kappa),
-        grid=(rows, 2),
+        grid=(rows,),
         in_specs=[whole] * 6
         + [
-            pl.BlockSpec((None, half, width, deep), lambda row, part: (row, part, 0, 0)),
-            pl.BlockSpec((None, half, 8, width), lambda row, part: (row, part, 0, 0)),
-            pl.BlockSpec((None, half, width), lambda row, part: (row, part, 0)),
+            pl.BlockSpec((None, cols, width, deep), lambda row: (row, 0, 0, 0)),
+            pl.BlockSpec((None, cols, width), lambda row: (row, 0, 0)),
         ],
-        out_specs=pl.BlockSpec((2, None, half, width), lambda row, part: (0, row, part, 0)),
+        out_specs=pl.BlockSpec((2, None, cols, width), lambda row: (0, row, 0, 0)),
         out_shape=jax.ShapeDtypeStruct((2, rows, cols, width), jnp.float32),
         scratch_shapes=[
             pltpu.VMEM((rows + 2, cols + 2, width), jnp.float32),
             pltpu.VMEM((rows + 2, cols + 2, 8, width), jnp.float32),
         ],
         name="push",
-    )(pv, *halo, fresh, weight, sums, pressure)
+    )(pv, *halo, fresh, weight, pressure)
 
 
 def local(position, velocity, volume, pressure_prev, fill, drift_from):
     kappa = 1.0 / volume.shape[2]
     old, top = prepare(position, velocity, volume, pressure_prev, fill, drift_from)
-    top = lax.all_gather(top, ("gx", "gy"), tiled=True)
+    top = largest(top)
     fresh = drift(top, old, *exchange(old, 2))
     coef, weight, sums, pv = setup(fresh, kappa)
     for step in range(1, SWEEPS):
         last = step == SWEEPS - 1
         pv, *pressure = sweep(kappa, last, pv, exchange(pv, 1), coef, sums)
-    velocity_new = push(kappa, pv, exchange(pv, 1), fresh, weight, sums, pressure[0])
+    velocity_new = push(kappa, pv, exchange(pv, 1), fresh, weight, pressure[0])
     return (pressure[0], velocity_new)
 
 

time: 304 us -> 254 us (0.84)
  blocking collectives: 32 us -> 0 us
  Pallas kernels: 167 us -> 138 us
  starting transfers between devices: 55.9 us -> 63.8 us
  waiting for transfers between devices: 30.9 us -> 34 us
    all_gather x1 -> x0, blocking collectives: 32 us -> none  [local(): top = lax.all_gather(top, ('gx', 'gy'), tiled=True)]
    pallas_call x1, Pallas kernels: 106 us -> 93.9 us  [setup(): call(functools.partial(setup_kernel, kappa), in_specs=[vmem], out_specs=(...]
    ppermute x10, starting transfers between devices: 27.9 us -> 38 us  [neighbours(): lax.ppermute(high_side, axis, up)]
    pallas_call x3, Pallas kernels: 33.1 us -> 23.2 us  [sweep(): call(functools.partial(sweep_kernel, kappa, last), in_specs=[vmem] * 7, o...]
    ppermute x0 -> x5, waiting for transfers between devices: none -> 8.13 us  [largest(): value = jnp.maximum(value, lax.ppermute(value, axis, pairs))]
    pallas_call x1, Pallas kernels: 25.4 us -> 18.6 us  [push(): call(functools.partial(push_kernel, kappa), grid=(rows,), in_specs=[whole...]
    ppermute x10, starting transfers between devices: 28.1 us -> 22 us  [neighbours(): lax.ppermute(low_side, axis, down)]
    ppermute x10, waiting for transfers between devices: 18.6 us -> 12.9 us  [neighbours(): lax.ppermute(high_side, axis, up)]
  transfers between devices with their start and end apart: 20 -> 25, of which waited for: 10 -> 15; matrix products, arithmetic and copies ran while one was open for 1% -> 1% of each run, Pallas kernels for 0% -> 0%
where the time goes in v5:
time: 254 us; the launch traced here: 252 us
  Pallas kernels  138 us (54%)
  starting transfers between devices  63.8 us (25%)
  waiting for transfers between devices  34 us (13%)
  local copies, waits for them, and re-layouts  15.5 us (6%)
    pallas_call x1, Pallas kernels, setup(): call(functools.partial(setup_kernel, kappa), in_specs=[vmem], out_specs=(...  93.9 us
    ppermute x10, starting transfers between devices, neighbours(): lax.ppermute(high_side, axis, up)  38 us
    pallas_call x3, Pallas kernels, sweep(): call(functools.partial(sweep_kernel, kappa, last), in_specs=[vmem] * 7, o...  23.2 us
    ppermute x10, starting transfers between devices, neighbours(): lax.ppermute(low_side, axis, down)  22 us
    pallas_call x1, Pallas kernels, push(): call(functools.partial(push_kernel, kappa), grid=(rows,), in_specs=[whole...  18.6 us
    ppermute x10, waiting for transfers between devices, neighbours(): lax.ppermute(high_side, axis, up)  12.9 us
    ppermute x10, waiting for transfers between devices, neighbours(): lax.ppermute(low_side, axis, down)  12.9 us
    ppermute x5, waiting for transfers between devices, largest(): value = jnp.maximum(value, lax.ppermute(value, axis, pairs))  8.13 us
  transfers between devices with their start and end apart: 25, of which 15 were waited for; matrix products, arithmetic and copies ran while one was open for 1% of the time, Pallas kernels for 0%

profile of v5, /device:TPU:17, one launch (start us, length us, event | category | flops | bytes accessed | tf_op | source)
XLA Modules:
  0.0 252.2 jit_solution(7986297549077189872)
XLA Ops:
  6.1 3.0 %collective-permute-start.6 = (f32[2,16,8,128]{3,2,1,0:T(8,128)S(1)}, f32[2,16,8,128]{3,2,1,0:T(8,128)S(1)}, u32[]{:S(2)}, u32[]{:S(2)}) collective-permute-start(f32[2,16,8,128]{3,2,1,0:T(8,128)S(1)} %get-tuple-element.20), channel_id=1, source_target_pairs={{4,0},{8,4},{12,8},{16,12},{20,16},{24,20},{28,24},{5,1},{9,5},{13... | collective-permute-start | bytes 393224 | tf_op jit(solution)/shard_map/ppermute | solution.py:78
  12.4 3.8 %collective-permute-done.5.above = f32[2,16,8,128]{3,2,1,0:T(8,128)S(1)} collective-permute-done((f32[2,16,8,128]{3,2,1,0:T(8,128)S(1)}, f32[2,16,8,128]{3,2,1,0:T(8,128)S(1)}, u32[]{:S(2)}, u32[]{:S(2)}) %collective-permute-start.5) | collective-permute-done | bytes 131104 | tf_op jit(solution)/shard_map/ppermute | solution.py:78
  16.2 4.7 %collective-permute-start.7 = (f32[12,2,8,128]{3,2,1,0:T(8,128)S(1)}, f32[12,2,8,128]{3,2,1,0:T(8,128)S(1)}, u32[]{:S(2)}, u32[]{:S(2)}) collective-permute-start(f32[12,2,8,128]{3,2,1,0:T(8,128)S(1)} %pad_maximum_fusion), channel_id=1, source_target_pairs={{0,1},{1,2},{2,3},{4,5},{5,6},{6,7},{8,9},{9,10},{10,11},{12,13},{... | collective-permute-start | bytes 294920 | tf_op jit(solution)/shard_map/ppermute | solution.py:78
  31.5 3.4 %collective-permute-done.4 = f32[8,128]{1,0:T(8,128)S(1)} collective-permute-done((f32[8,128]{1,0:T(8,128)S(1)}, f32[8,128]{1,0:T(8,128)S(1)}, u32[]{:S(2)}, u32[]{:S(2)}) %collective-permute-start.4) | collective-permute-done | bytes 4128 | tf_op jit(solution)/shard_map/ppermute | solution.py:97
  37.4 93.9 %setup.1 = (bf16[8,16,128,1152]{3,2,1,0:T(8,128)(2,1)S(1)}, bf16[8,16,128,1152]{3,2,1,0:T(8,128)(2,1)}, f32[3,8,16,128]{3,2,1,0:T(8,128)}, f32[8,16,128]{2,1,0:T(8,128)}) custom-call(f32[10,18,8,128]{3,2,1,0:T(8,128)} %copy-done), custom_call_target="tpu_custom_call" | custom-call | tf_op jit(solution)/shard_map/setup/pallas_call | solution.py:261
  132.0 2.8 %collective-permute-start.10 = (f32[1,16,128]{2,1,0:T(8,128)S(1)}, f32[1,16,128]{2,1,0:T(8,128)S(1)}, u32[]{:S(2)}, u32[]{:S(2)}) collective-permute-start(f32[1,16,128]{2,1,0:T(8,128)S(1)} %get-tuple-element.40), channel_id=1, source_target_pairs={{4,0},{8,4},{12,8},{16,12},{20,16},{24,20},{28,24},{5,1},{9,5},{13... | collective-permute-start | bytes 24584 | tf_op jit(solution)/shard_map/ppermute | solution.py:78
  138.1 2.8 %collective-permute-done.9.above = f32[1,16,128]{2,1,0:T(8,128)S(1)} collective-permute-done((f32[1,16,128]{2,1,0:T(8,128)S(1)}, f32[1,16,128]{2,1,0:T(8,128)S(1)}, u32[]{:S(2)}, u32[]{:S(2)}) %collective-permute-start.9) | collective-permute-done | bytes 8224 | tf_op jit(solution)/shard_map/ppermute | solution.py:78
  140.8 9.6 %collective-permute-start.11 = (f32[10,1,128]{2,1,0:T(1,128)S(1)}, f32[10,1,128]{2,1,0:T(1,128)S(1)}, u32[]{:S(2)}, u32[]{:S(2)}) collective-permute-start(f32[10,1,128]{2,1,0:T(1,128)S(1)} %pad_maximum_fusion.2), channel_id=1, source_target_pairs={{0,1},{1,2},{2,3},{4,5},{5,6},{6,7},{8,9},{9,10},{10,11},{12,13},{... | collective-permute-start | bytes 15368 | tf_op jit(solution)/shard_map/ppermute | solution.py:78
  152.4 3.0 %collective-permute-done.12.right = f32[10,1,128]{2,1,0:T(1,128)S(1)} collective-permute-done((f32[10,1,128]{2,1,0:T(1,128)S(1)}, f32[10,1,128]{2,1,0:T(1,128)S(1)}, u32[]{:S(2)}, u32[]{:S(2)}) %collective-permute-start.12) | collective-permute-done | bytes 5152 | tf_op jit(solution)/shard_map/ppermute | solution.py:78
  156.0 7.7 %sweep.3.center = f32[8,16,128]{2,1,0:T(8,128)} custom-call(f32[8,16,128]{2,1,0:T(8,128)} %get-tuple-element.12.center, f32[1,16,128]{2,1,0:T(8,128)} %copy-done.12, f32[1,16,128]{2,1,0:T(8,128)} %copy-done.9, f32[10,1,128]{2,1,0:T(1,128)} %copy-done.15, f32[10,1,128]{2,1,0:T(1,128)} %copy-done.18, bf16[8,16,128,1152]{3,2,1,0:T(8,128)(2,1)S(1)} %get-tuple-element.13.coef, ...), custom_call_target="tpu_custom_call" | custom-call | tf_op jit(solution)/shard_map/sweep/pallas_call | solution.py:325
  167.2 3.4 %collective-permute-start.13 = (f32[1,16,128]{2,1,0:T(8,128)S(1)}, f32[1,16,128]{2,1,0:T(8,128)S(1)}, u32[]{:S(2)}, u32[]{:S(2)}) collective-permute-start(f32[1,16,128]{2,1,0:T(8,128)S(1)} %get-tuple-element.37), channel_id=1, source_target_pairs={{0,4},{4,8},{8,12},{12,16},{16,20},{20,24},{24,28},{1,5},{5,9},{9,... | collective-permute-start | bytes 24584 | tf_op jit(solution)/shard_map/ppermute | solution.py:78
  172.5 3.1 %collective-permute-start.15 = (f32[10,1,128]{2,1,0:T(1,128)S(1)}, f32[10,1,128]{2,1,0:T(1,128)S(1)}, u32[]{:S(2)}, u32[]{:S(2)}) collective-permute-start(f32[10,1,128]{2,1,0:T(1,128)S(1)} %pad_maximum_fusion.4), channel_id=1, source_target_pairs={{0,1},{1,2},{2,3},{4,5},{5,6},{6,7},{8,9},{9,10},{10,11},{12,13},{... | collective-permute-start | bytes 15368 | tf_op jit(solution)/shard_map/ppermute | solution.py:78
  177.7 3.0 %collective-permute-done.16.right = f32[10,1,128]{2,1,0:T(1,128)S(1)} collective-permute-done((f32[10,1,128]{2,1,0:T(1,128)S(1)}, f32[10,1,128]{2,1,0:T(1,128)S(1)}, u32[]{:S(2)}, u32[]{:S(2)}) %collective-permute-start.16) | collective-permute-done | bytes 5152 | tf_op jit(solution)/shard_map/ppermute | solution.py:78
  181.3 7.7 %sweep.4.center = f32[8,16,128]{2,1,0:T(8,128)} custom-call(f32[8,16,128]{2,1,0:T(8,128)} %sweep.3.center, f32[1,16,128]{2,1,0:T(8,128)} %copy-done.13, f32[1,16,128]{2,1,0:T(8,128)} %copy-done.10, f32[10,1,128]{2,1,0:T(1,128)} %copy-done.16, f32[10,1,128]{2,1,0:T(1,128)} %copy-done.19, bf16[8,16,128,1152]{3,2,1,0:T(8,128)(2,1)S(1)} %get-tuple-element.13.coef, ...), custom_call_target="tpu_custom_call" | custom-call | tf_op jit(solution)/shard_map/sweep/pallas_call | solution.py:325
  189.7 2.6 %collective-permute-start.18 = (f32[1,16,128]{2,1,0:T(8,128)S(1)}, f32[1,16,128]{2,1,0:T(8,128)S(1)}, u32[]{:S(2)}, u32[]{:S(2)}) collective-permute-start(f32[1,16,128]{2,1,0:T(8,128)S(1)} %get-tuple-element.32), channel_id=1, source_target_pairs={{4,0},{8,4},{12,8},{16,12},{20,16},{24,20},{28,24},{5,1},{9,5},{13... | collective-permute-start | bytes 24584 | tf_op jit(solution)/shard_map/ppermute | solution.py:78
  193.2 2.6 %collective-permute-start.17 = (f32[1,16,128]{2,1,0:T(8,128)S(1)}, f32[1,16,128]{2,1,0:T(8,128)S(1)}, u32[]{:S(2)}, u32[]{:S(2)}) collective-permute-start(f32[1,16,128]{2,1,0:T(8,128)S(1)} %get-tuple-element.33), channel_id=1, source_target_pairs={{0,4},{4,8},{8,12},{12,16},{16,20},{20,24},{24,28},{1,5},{5,9},{9,... | collective-permute-start | bytes 24584 | tf_op jit(solution)/shard_map/ppermute | solution.py:78
  195.8 2.6 %collective-permute-done.17.above = f32[1,16,128]{2,1,0:T(8,128)S(1)} collective-permute-done((f32[1,16,128]{2,1,0:T(8,128)S(1)}, f32[1,16,128]{2,1,0:T(8,128)S(1)}, u32[]{:S(2)}, u32[]{:S(2)}) %collective-permute-start.17) | collective-permute-done | bytes 8224 | tf_op jit(solution)/shard_map/ppermute | solution.py:78
  198.5 3.4 %collective-permute-start.19 = (f32[10,1,128]{2,1,0:T(1,128)S(1)}, f32[10,1,128]{2,1,0:T(1,128)S(1)}, u32[]{:S(2)}, u32[]{:S(2)}) collective-permute-start(f32[10,1,128]{2,1,0:T(1,128)S(1)} %pad_maximum_fusion.6), channel_id=1, source_target_pairs={{0,1},{1,2},{2,3},{4,5},{5,6},{6,7},{8,9},{9,10},{10,11},{12,13},{... | collective-permute-start | bytes 15368 | tf_op jit(solution)/shard_map/ppermute | solution.py:78
  203.8 3.0 %collective-permute-done.20.right = f32[10,1,128]{2,1,0:T(1,128)S(1)} collective-permute-done((f32[10,1,128]{2,1,0:T(1,128)S(1)}, f32[10,1,128]{2,1,0:T(1,128)S(1)}, u32[]{:S(2)}, u32[]{:S(2)}) %collective-permute-start.20) | collective-permute-done | bytes 5152 | tf_op jit(solution)/shard_map/ppermute | solution.py:78
  207.4 7.8 %sweep.5 = (f32[8,16,128]{2,1,0:T(8,128)}, f32[8,16,128]{2,1,0:T(8,128)}) custom-call(f32[8,16,128]{2,1,0:T(8,128)} %sweep.4.center, f32[1,16,128]{2,1,0:T(8,128)} %copy-done.11, f32[1,16,128]{2,1,0:T(8,128)} %copy-done.8, f32[10,1,128]{2,1,0:T(1,128)} %copy-done.14, f32[10,1,128]{2,1,0:T(1,128)} %copy-done.17, ...), custom_call_target="tpu_custom_call" | custom-call | tf_op jit(solution)/shard_map/sweep/pallas_call | solution.py:325
  218.6 3.4 %collective-permute-start.21 = (f32[1,16,128]{2,1,0:T(8,128)S(1)}, f32[1,16,128]{2,1,0:T(8,128)S(1)}, u32[]{:S(2)}, u32[]{:S(2)}) collective-permute-start(f32[1,16,128]{2,1,0:T(8,128)S(1)} %get-tuple-element.29), channel_id=1, source_target_pairs={{0,4},{4,8},{8,12},{12,16},{16,20},{20,24},{24,28},{1,5},{5,9},{9,... | collective-permute-start | bytes 24584 | tf_op jit(solution)/shard_map/ppermute | solution.py:78
  223.9 3.1 %collective-permute-start.23 = (f32[10,1,128]{2,1,0:T(1,128)S(1)}, f32[10,1,128]{2,1,0:T(1,128)S(1)}, u32[]{:S(2)}, u32[]{:S(2)}) collective-permute-start(f32[10,1,128]{2,1,0:T(1,128)S(1)} %pad_maximum_fusion.8), channel_id=1, source_target_pairs={{0,1},{1,2},{2,3},{4,5},{5,6},{6,7},{8,9},{9,10},{10,11},{12,13},{... | collective-permute-start | bytes 15368 | tf_op jit(solution)/shard_map/ppermute | solution.py:78
  228.9 3.0 %collective-permute-done.24.right = f32[10,1,128]{2,1,0:T(1,128)S(1)} collective-permute-done((f32[10,1,128]{2,1,0:T(1,128)S(1)}, f32[10,1,128]{2,1,0:T(1,128)S(1)}, u32[]{:S(2)}, u32[]{:S(2)}) %collective-permute-start.24) | collective-permute-done | bytes 5152 | tf_op jit(solution)/shard_map/ppermute | solution.py:78
  233.6 18.6 %push.1 = f32[2,8,16,128]{3,2,1,0:T(8,128)} custom-call(f32[8,16,128]{2,1,0:T(8,128)S(1)} %copy-done.4, f32[1,16,128]{2,1,0:T(8,128)S(1)} %collective-permute-done.21.above, f32[1,16,128]{2,1,0:T(8,128)S(1)} %collective-permute-done.22.below, f32[10,1,128]{2,1,0:T(1,128)S(1)} %collective-permute-done.23.left, ...), custom_call_target="tpu_custom_call" | custom-call | tf_op jit(solution)/shard_map/push/pallas_call | solution.py:389
  (110 shorter events, 49.3 us)
Async XLA Ops:
  6.1 6.3 %collective-permute-start.6 = (f32[2,16,8,128]{3,2,1,0:T(8,128)S(1)}, f32[2,16,8,128]{3,2,1,0:T(8,128)S(1)}, u32[]{:S(2)}, u32[]{:S(2)}) collective-permute-start(f32[2,16,8,128]{3,2,1,0:T(8,128)S(1)} %get-tuple-element.20), channel_id=1, source_target_pairs={{4,0},{8,4},{12,8},{16,12},{20,16},{24,20},{28,24},{5,1},{9,5},{13... | collective-permute-start | bytes 393224 | tf_op jit(solution)/shard_map/ppermute | solution.py:78
  9.1 7.0 %collective-permute-start.5 = (f32[2,16,8,128]{3,2,1,0:T(8,128)S(1)}, f32[2,16,8,128]{3,2,1,0:T(8,128)S(1)}, u32[]{:S(2)}, u32[]{:S(2)}) collective-permute-start(f32[2,16,8,128]{3,2,1,0:T(8,128)S(1)} %get-tuple-element.21), channel_id=1, source_target_pairs={{0,4},{4,8},{8,12},{12,16},{16,20},{20,24},{24,28},{1,5},{5,9},{9,... | collective-permute-start | bytes 393224 | tf_op jit(solution)/shard_map/ppermute | solution.py:78
  16.2 18.7 %collective-permute-start.7 = (f32[12,2,8,128]{3,2,1,0:T(8,128)S(1)}, f32[12,2,8,128]{3,2,1,0:T(8,128)S(1)}, u32[]{:S(2)}, u32[]{:S(2)}) collective-permute-start(f32[12,2,8,128]{3,2,1,0:T(8,128)S(1)} %pad_maximum_fusion), channel_id=1, source_target_pairs={{0,1},{1,2},{2,3},{4,5},{5,6},{6,7},{8,9},{9,10},{10,11},{12,13},{... | collective-permute-start | bytes 294920 | tf_op jit(solution)/shard_map/ppermute | solution.py:78
  20.9 14.0 %collective-permute-start.8 = (f32[12,2,8,128]{3,2,1,0:T(8,128)S(1)}, f32[12,2,8,128]{3,2,1,0:T(8,128)S(1)}, u32[]{:S(2)}, u32[]{:S(2)}) collective-permute-start(f32[12,2,8,128]{3,2,1,0:T(8,128)S(1)} %pad_maximum_fusion.1), channel_id=1, source_target_pairs={{1,0},{2,1},{3,2},{5,4},{6,5},{7,6},{9,8},{10,9},{11,10},{13,12},{... | collective-permute-start | bytes 294920 | tf_op jit(solution)/shard_map/ppermute | solution.py:78
  24.1 2.5 collective-permute-start.1
  26.6 2.5 collective-permute-start.2
  29.0 2.5 collective-permute-start.3
  31.5 3.4 %collective-permute-start.4 = (f32[8,128]{1,0:T(8,128)S(1)}, f32[8,128]{1,0:T(8,128)S(1)}, u32[]{:S(2)}, u32[]{:S(2)}) collective-permute-start(f32[8,128]{1,0:T(8,128)S(1)} %max.18), channel_id=1, source_target_pairs={{0,16},{4,20},{8,24},{12,28},{16,0},{20,4},{24,8},{28,12},{1,17},{... | collective-permute-start | bytes 12296 | tf_op jit(solution)/shard_map/ppermute | solution.py:97
  132.0 6.1 %collective-permute-start.10 = (f32[1,16,128]{2,1,0:T(8,128)S(1)}, f32[1,16,128]{2,1,0:T(8,128)S(1)}, u32[]{:S(2)}, u32[]{:S(2)}) collective-permute-start(f32[1,16,128]{2,1,0:T(8,128)S(1)} %get-tuple-element.40), channel_id=1, source_target_pairs={{4,0},{8,4},{12,8},{16,12},{20,16},{24,20},{28,24},{5,1},{9,5},{13... | collective-permute-start | bytes 24584 | tf_op jit(solution)/shard_map/ppermute | solution.py:78
  135.5 5.3 %collective-permute-start.9 = (f32[1,16,128]{2,1,0:T(8,128)S(1)}, f32[1,16,128]{2,1,0:T(8,128)S(1)}, u32[]{:S(2)}, u32[]{:S(2)}) collective-permute-start(f32[1,16,128]{2,1,0:T(8,128)S(1)} %get-tuple-element.41), channel_id=1, source_target_pairs={{0,4},{4,8},{8,12},{12,16},{16,20},{20,24},{24,28},{1,5},{5,9},{9,... | collective-permute-start | bytes 24584 | tf_op jit(solution)/shard_map/ppermute | solution.py:78
  140.8 11.6 %collective-permute-start.11 = (f32[10,1,128]{2,1,0:T(1,128)S(1)}, f32[10,1,128]{2,1,0:T(1,128)S(1)}, u32[]{:S(2)}, u32[]{:S(2)}) collective-permute-start(f32[10,1,128]{2,1,0:T(1,128)S(1)} %pad_maximum_fusion.2), channel_id=1, source_target_pairs={{0,1},{1,2},{2,3},{4,5},{5,6},{6,7},{8,9},{9,10},{10,11},{12,13},{... | collective-permute-start | bytes 15368 | tf_op jit(solution)/shard_map/ppermute | solution.py:78
  150.5 4.9 %collective-permute-start.12 = (f32[10,1,128]{2,1,0:T(1,128)S(1)}, f32[10,1,128]{2,1,0:T(1,128)S(1)}, u32[]{:S(2)}, u32[]{:S(2)}) collective-permute-start(f32[10,1,128]{2,1,0:T(1,128)S(1)} %pad_maximum_fusion.3), channel_id=1, source_target_pairs={{1,0},{2,1},{3,2},{5,4},{6,5},{7,6},{9,8},{10,9},{11,10},{13,12},{... | collective-permute-start | bytes 15368 | tf_op jit(solution)/shard_map/ppermute | solution.py:78
  164.5 6.1 %collective-permute-start.14 = (f32[1,16,128]{2,1,0:T(8,128)S(1)}, f32[1,16,128]{2,1,0:T(8,128)S(1)}, u32[]{:S(2)}, u32[]{:S(2)}) collective-permute-start(f32[1,16,128]{2,1,0:T(8,128)S(1)} %get-tuple-element.36), channel_id=1, source_target_pairs={{4,0},{8,4},{12,8},{16,12},{20,16},{24,20},{28,24},{5,1},{9,5},{13... | collective-permute-start | bytes 24584 | tf_op jit(solution)/shard_map/ppermute | solution.py:78
  167.2 5.3 %collective-permute-start.13 = (f32[1,16,128]{2,1,0:T(8,128)S(1)}, f32[1,16,128]{2,1,0:T(8,128)S(1)}, u32[]{:S(2)}, u32[]{:S(2)}) collective-permute-start(f32[1,16,128]{2,1,0:T(8,128)S(1)} %get-tuple-element.37), channel_id=1, source_target_pairs={{0,4},{4,8},{8,12},{12,16},{16,20},{20,24},{24,28},{1,5},{5,9},{9,... | collective-permute-start | bytes 24584 | tf_op jit(solution)/shard_map/ppermute | solution.py:78
  172.5 5.2 %collective-permute-start.15 = (f32[10,1,128]{2,1,0:T(1,128)S(1)}, f32[10,1,128]{2,1,0:T(1,128)S(1)}, u32[]{:S(2)}, u32[]{:S(2)}) collective-permute-start(f32[10,1,128]{2,1,0:T(1,128)S(1)} %pad_maximum_fusion.4), channel_id=1, source_target_pairs={{0,1},{1,2},{2,3},{4,5},{5,6},{6,7},{8,9},{9,10},{10,11},{12,13},{... | collective-permute-start | bytes 15368 | tf_op jit(solution)/shard_map/ppermute | solution.py:78
  175.6 5.1 %collective-permute-start.16 = (f32[10,1,128]{2,1,0:T(1,128)S(1)}, f32[10,1,128]{2,1,0:T(1,128)S(1)}, u32[]{:S(2)}, u32[]{:S(2)}) collective-permute-start(f32[10,1,128]{2,1,0:T(1,128)S(1)} %pad_maximum_fusion.5), channel_id=1, source_target_pairs={{1,0},{2,1},{3,2},{5,4},{6,5},{7,6},{9,8},{10,9},{11,10},{13,12},{... | collective-permute-start | bytes 15368 | tf_op jit(solution)/shard_map/ppermute | solution.py:78
  189.7 6.1 %collective-permute-start.18 = (f32[1,16,128]{2,1,0:T(8,128)S(1)}, f32[1,16,128]{2,1,0:T(8,128)S(1)}, u32[]{:S(2)}, u32[]{:S(2)}) collective-permute-start(f32[1,16,128]{2,1,0:T(8,128)S(1)} %get-tuple-element.32), channel_id=1, source_target_pairs={{4,0},{8,4},{12,8},{16,12},{20,16},{24,20},{28,24},{5,1},{9,5},{13... | collective-permute-start | bytes 24584 | tf_op jit(solution)/shard_map/ppermute | solution.py:78
  193.2 5.3 %collective-permute-start.17 = (f32[1,16,128]{2,1,0:T(8,128)S(1)}, f32[1,16,128]{2,1,0:T(8,128)S(1)}, u32[]{:S(2)}, u32[]{:S(2)}) collective-permute-start(f32[1,16,128]{2,1,0:T(8,128)S(1)} %get-tuple-element.33), channel_id=1, source_target_pairs={{0,4},{4,8},{8,12},{12,16},{16,20},{20,24},{24,28},{1,5},{5,9},{9,... | collective-permute-start | bytes 24584 | tf_op jit(solution)/shard_map/ppermute | solution.py:78
  198.5 5.3 %collective-permute-start.19 = (f32[10,1,128]{2,1,0:T(1,128)S(1)}, f32[10,1,128]{2,1,0:T(1,128)S(1)}, u32[]{:S(2)}, u32[]{:S(2)}) collective-permute-start(f32[10,1,128]{2,1,0:T(1,128)S(1)} %pad_maximum_fusion.6), channel_id=1, source_target_pairs={{0,1},{1,2},{2,3},{4,5},{5,6},{6,7},{8,9},{9,10},{10,11},{12,13},{... | collective-permute-start | bytes 15368 | tf_op jit(solution)/shard_map/ppermute | solution.py:78
  201.9 4.9 %collective-permute-start.20 = (f32[10,1,128]{2,1,0:T(1,128)S(1)}, f32[10,1,128]{2,1,0:T(1,128)S(1)}, u32[]{:S(2)}, u32[]{:S(2)}) collective-permute-start(f32[10,1,128]{2,1,0:T(1,128)S(1)} %pad_maximum_fusion.7), channel_id=1, source_target_pairs={{1,0},{2,1},{3,2},{5,4},{6,5},{7,6},{9,8},{10,9},{11,10},{13,12},{... | collective-permute-start | bytes 15368 | tf_op jit(solution)/shard_map/ppermute | solution.py:78
  215.9 6.1 %collective-permute-start.22 = (f32[1,16,128]{2,1,0:T(8,128)S(1)}, f32[1,16,128]{2,1,0:T(8,128)S(1)}, u32[]{:S(2)}, u32[]{:S(2)}) collective-permute-start(f32[1,16,128]{2,1,0:T(8,128)S(1)} %get-tuple-element.28), channel_id=1, source_target_pairs={{4,0},{8,4},{12,8},{16,12},{20,16},{24,20},{28,24},{5,1},{9,5},{13... | collective-permute-start | bytes 24584 | tf_op jit(solution)/shard_map/ppermute | solution.py:78
  218.6 5.3 %collective-permute-start.21 = (f32[1,16,128]{2,1,0:T(8,128)S(1)}, f32[1,16,128]{2,1,0:T(8,128)S(1)}, u32[]{:S(2)}, u32[]{:S(2)}) collective-permute-start(f32[1,16,128]{2,1,0:T(8,128)S(1)} %get-tuple-element.29), channel_id=1, source_target_pairs={{0,4},{4,8},{8,12},{12,16},{16,20},{20,24},{24,28},{1,5},{5,9},{9,... | collective-permute-start | bytes 24584 | tf_op jit(solution)/shard_map/ppermute | solution.py:78
  223.9 5.0 %collective-permute-start.23 = (f32[10,1,128]{2,1,0:T(1,128)S(1)}, f32[10,1,128]{2,1,0:T(1,128)S(1)}, u32[]{:S(2)}, u32[]{:S(2)}) collective-permute-start(f32[10,1,128]{2,1,0:T(1,128)S(1)} %pad_maximum_fusion.8), channel_id=1, source_target_pairs={{0,1},{1,2},{2,3},{4,5},{5,6},{6,7},{8,9},{9,10},{10,11},{12,13},{... | collective-permute-start | bytes 15368 | tf_op jit(solution)/shard_map/ppermute | solution.py:78
  227.0 4.9 %collective-permute-start.24 = (f32[10,1,128]{2,1,0:T(1,128)S(1)}, f32[10,1,128]{2,1,0:T(1,128)S(1)}, u32[]{:S(2)}, u32[]{:S(2)}) collective-permute-start(f32[10,1,128]{2,1,0:T(1,128)S(1)} %pad_maximum_fusion.9), channel_id=1, source_target_pairs={{1,0},{2,1},{3,2},{5,4},{6,5},{7,6},{9,8},{10,9},{11,10},{13,12},{... | collective-permute-start | bytes 15368 | tf_op jit(solution)/shard_map/ppermute | solution.py:78
  (21 other events, 144.1 us)

commit v6 on v5

--- a/solution.py
+++ b/solution.py
@@ -64,18 +64,24 @@
     return call(
         prepare_kernel,
         out_shape=(
-            jax.ShapeDtypeStruct((rows, cols, 8, width), jnp.float32),
-            jax.ShapeDtypeStruct((8, width), jnp.float32),
+            pltpu.VMEM((rows, cols, 8, width), jnp.float32),
+            pltpu.VMEM((8, width), jnp.float32),
         ),
         name="prepare",
     )(position, velocity, volume, pressure, fill[:, :, None], code[:, :, None])
 
 
-def neighbours(axis, low_side, high_side):
+def neighbours(axis, low, high):
     devices = lax.axis_size(axis)
-    up = [(i, i + 1) for i in range(devices - 1)]
-    down = [(i + 1, i) for i in range(devices - 1)]
-    return lax.ppermute(high_side, axis, up), lax.ppermute(low_side, axis, down)
+    even = lax.axis_index(axis) % 2 == 0
+
+    def swap(value, first):
+        pairs = [(i, i + 1) for i in range(first, devices - 1, 2)]
+        return lax.ppermute(value, axis, pairs + [(j, i) for i, j in pairs])
+
+    one = swap(jnp.where(even, high, low), 0)
+    two = swap(jnp.where(even, low, high), 1)
+    return jnp.where(even, two, one), jnp.where(even, one, two)
 
 
 def exchange(shard, depth):
@@ -133,7 +139,7 @@
     rows, cols, _, width = center.shape
     return call(
         drift_kernel,
-        out_shape=jax.ShapeDtypeStruct((rows + 2, cols + 2, 8, width), jnp.float32),
+        out_shape=pltpu.VMEM((rows + 2, cols + 2, 8, width), jnp.float32),
         scratch_shapes=[pltpu.VMEM((rows + 4, cols + 4, 8, width), jnp.float32)],
         name="drift",
     )(top, center, above, below, left, right)
@@ -143,58 +149,123 @@
     return lax.dot_general(left, right, (((1,), (1,)), ((), ())), preferred_element_type=jnp.float32)
 
 
-def setup_kernel(kappa, fresh, coef, weight, sums, pv, xcol, ycol, feat, both_a, both_b, sem):
-    rows, cols, width, deep = coef.shape
-    wide = cols + 2
-
-    def features_of(place, carry):
-        row, col = place // wide, lax.rem(place, wide)
-        tile = fresh[row, col]
-        x, y, u, v = (tile[i : i + 1] for i in range(4))
-        vol = tile[VOL : VOL + 1]
-        zero = jnp.zeros_like(vol)
-        vol_u, vol_v = vol * u, vol * v
-        base = [vol, vol * x, vol * y, vol_u, vol_v, vol_u * x + vol_v * y, vol * tile[PRES : PRES + 1], zero]
-        feat[row, col, 0] = jnp.concatenate(base, axis=0)
-        feat[row, col, 1] = jnp.concatenate([zero, vol, zero, zero, zero, vol_u, zero, zero], axis=0)
-        feat[row, col, 2] = jnp.concatenate([zero, zero, vol, zero, zero, vol_v, zero, zero], axis=0)
-        return carry
-
-    lax.fori_loop(0, (rows + 2) * wide, features_of, 0)
+def setup_kernel(fresh, coef, weight, xcol, ycol, out_a, out_b, sem):
+    rows, cols, width, _ = coef.shape
 
     def columns(bin_id, slot):
         tile = fresh[bin_id // cols + 1, lax.rem(bin_id, cols) + 1]
         xcol[slot] = jnp.broadcast_to(tile[X : X + 1], (width, width)).T
         ycol[slot] = jnp.broadcast_to(tile[Y : Y + 1], (width, width)).T
 
-    def blocks(bin_id, slot, both):
+    def blocks(bin_id, slot, out):
         row, col = bin_id // cols, lax.rem(bin_id, cols)
         around = [fresh[row + k // 3, col + k % 3] for k in range(9)]
         xj = [jnp.broadcast_to(around[k][X : X + 1] + (k // 3 - 1.0), (8, width)) for k in range(9)]
         yj = [jnp.broadcast_to(around[k][Y : Y + 1] + (k % 3 - 1.0), (8, width)) for k in range(9)]
         for part in range(width // CHUNK):
+            span = pl.ds(part * CHUNK, CHUNK)
             spans = [pl.ds(part * CHUNK + 8 * i, 8) for i in range(CHUNK // 8)]
-            xi = [xcol[slot, span] for span in spans]
-            yi = [ycol[slot, span] for span in spans]
+            xi = [xcol[slot, piece] for piece in spans]
+            yi = [ycol[slot, piece] for piece in spans]
             for k in range(9):
                 lanes = pl.ds(k * width, width)
-                weights, values = [], []
+                squares, weights = [], []
                 for x, y in zip(xi, yi):
                     dx = x - xj[k]
                     dy = y - yj[k]
                     square = jnp.maximum(dx * dx + dy * dy, 1e-14)
                     remain = jnp.maximum(1.0 - square * lax.rsqrt(square), 0.0)
-                    cubed = remain * remain * remain
-                    weights.append(cubed)
-                    values.append(cubed * (square * pltpu.reciprocal(square + SOFT, approx=True)))
+                    squares.append(square)
+                    weights.append(remain * remain * remain)
+                squares = jnp.concatenate(squares, axis=0).astype(jnp.bfloat16)
                 weights = jnp.concatenate(weights, axis=0).astype(jnp.bfloat16)
-                values = jnp.concatenate(values, axis=0).astype(jnp.bfloat16)
-                both[pl.ds(part * CHUNK, CHUNK), lanes] = weights
-                both[pl.ds(width + part * CHUNK, CHUNK), lanes] = values
-                coef[row, col, pl.ds(part * CHUNK, CHUNK), lanes] = values
-
-    def finish(bin_id, both):
-        row, col = bin_id // cols, lax.rem(bin_id, cols)
+                ratio = squares * pltpu.reciprocal(squares + jnp.bfloat16(SOFT), approx=True)
+                out[span, lanes] = weights
+                coef[row, col, span, lanes] = weights * ratio
+
+    def copy_out(bin_id, out, slot):
+        target = weight.at[bin_id // cols, lax.rem(bin_id, cols)]
+        return pltpu.make_async_copy(out, target, sem.at[slot])
+
+    count = rows * cols
+    columns(0, 0)
+    columns(1, 1)
+
+    def two_bins(step, carry):
+        even = 2 * step
+
+        @pl.when(step > 0)
+        def _():
+            copy_out(even - 2, out_a, 0).wait()
+
+        blocks(even, 0, out_a)
+        columns(jnp.minimum(even + 2, count - 1), 0)
+        copy_out(even, out_a, 0).start()
+
+        @pl.when(step > 0)
+        def _():
+            copy_out(even - 1, out_b, 1).wait()
+
+        blocks(even + 1, 1, out_b)
+        columns(jnp.minimum(even + 3, count - 1), 1)
+        copy_out(even + 1, out_b, 1).start()
+        return carry
+
+    lax.fori_loop(0, count // 2, two_bins, 0)
+    copy_out(count - 2, out_a, 0).wait()
+    copy_out(count - 1, out_b, 1).wait()
+
+
+def setup(fresh):
+    rows, cols, _, width = fresh.shape
+    rows, cols = rows - 2, cols - 2
+    vmem = pl.BlockSpec(memory_space=pltpu.VMEM)
+    return call(
+        setup_kernel,
+        in_specs=[vmem],
+        out_specs=(vmem, pl.BlockSpec(memory_space=pltpu.HBM)),
+        out_shape=(
+            pltpu.VMEM((rows, cols, width, 9 * width), jnp.bfloat16),
+            jax.ShapeDtypeStruct((rows, cols, width, 9 * width), jnp.bfloat16),
+        ),
+        scratch_shapes=[
+            pltpu.VMEM((2, width, width), jnp.float32),
+            pltpu.VMEM((2, width, width), jnp.float32),
+            pltpu.VMEM((width, 9 * width), jnp.bfloat16),
+            pltpu.VMEM((width, 9 * width), jnp.bfloat16),
+            pltpu.SemaphoreType.DMA((2,)),
+        ],
+        name="setup",
+    )(fresh)
+
+
+def first_kernel(kappa, fresh, coef, weight, sums, pv, feat):
+    row = pl.program_id(0)
+    cols, width, _ = weight.shape
+
+    @pl.when(row == 0)
+    def _():
+        def one_row(r, carry):
+            tiles = []
+            for col in range(fresh.shape[1]):
+                tile = fresh[r, col]
+                x, y, u, v = (tile[i : i + 1] for i in range(4))
+                vol = tile[VOL : VOL + 1]
+                zero = jnp.zeros_like(vol)
+                vol_u, vol_v = vol * u, vol * v
+                base = [vol, vol * x, vol * y, vol_u, vol_v, vol_u * x + vol_v * y, vol * tile[PRES : PRES + 1], zero]
+                along_x = [zero, vol, zero, zero, zero, vol_u, zero, zero]
+                along_y = [zero, zero, vol, zero, zero, vol_v, zero, zero]
+                tiles.append([jnp.concatenate(rows, axis=0) for rows in (base, along_x, along_y)])
+            for col in range(fresh.shape[1]):
+                for i in range(3):
+                    feat[r, col, i] = tiles[col][i]
+            return carry
+
+        lax.fori_loop(0, fresh.shape[0], one_row, 0)
+
+    outs = ([], [], [], [])
+    for col in range(cols):
         around = []
         for k in range(9):
             off_x, off_y = k // 3 - 1, k % 3 - 1
@@ -204,9 +275,11 @@
             if off_y:
                 features = features + float(off_y) * feat[row + k // 3, col + k % 3, 2]
             around.append(split(features))
-        total = dot_nt(both[...], jnp.concatenate(around, axis=1))
-        total = total[:, :8] + total[:, 8:]
-        total_w, total_c = total[:width].T, total[width:].T
+        around = jnp.concatenate(around, axis=1)
+        total_w = dot_nt(weight[col], around)
+        total_c = dot_nt(coef[row, col], around)
+        total_w = (total_w[:, :8] + total_w[:, 8:]).T
+        total_c = (total_c[:, :8] + total_c[:, 8:]).T
         tile = fresh[row + 1, col + 1]
         x, y, u, v = (tile[i : i + 1] for i in range(4))
         vol = tile[VOL : VOL + 1]
@@ -215,69 +288,28 @@
         source = kappa * 20.0 * source
         rden = 1.0 / (1.0 + kappa * 40.0 * total_c[0:1])
         first = (source + kappa * 40.0 * total_c[6:7]) * rden
-        for place, value in enumerate((source, rden, vol)):
-            sums[place, row, pl.ds(col, 1), :] = value
-        pv[row, pl.ds(col, 1), :] = first * vol
-
-    def copy_out(bin_id, both, slot):
-        target = weight.at[bin_id // cols, lax.rem(bin_id, cols)]
-        return pltpu.make_async_copy(both.at[pl.ds(0, width)], target, sem.at[slot])
-
-    count = rows * cols
-    columns(0, 0)
-    columns(1, 1)
-
-    def two_bins(step, carry):
-        even = 2 * step
-
-        @pl.when(step > 0)
-        def _():
-            copy_out(even - 2, both_a, 0).wait()
-
-        blocks(even, 0, both_a)
-        columns(jnp.minimum(even + 2, count - 1), 0)
-
-        @pl.when(step > 0)
-        def _():
-            copy_out(even - 1, both_b, 1).wait()
-
-        copy_out(even, both_a, 0).start()
-        finish(even, both_a)
-        blocks(even + 1, 1, both_b)
-        columns(jnp.minimum(even + 3, count - 1), 1)
-        copy_out(even + 1, both_b, 1).start()
-        finish(even + 1, both_b)
-        return carry
-
-    lax.fori_loop(0, count // 2, two_bins, 0)
-    copy_out(count - 2, both_a, 0).wait()
-    copy_out(count - 1, both_b, 1).wait()
-
-
-def setup(fresh, kappa):
-    rows, cols, _, width = fresh.shape
-    rows, cols = rows - 2, cols - 2
+        for out, value in zip(outs, (source, rden, vol, first * vol)):
+            out.append(value)
+    for place in range(3):
+        sums[place, row] = jnp.concatenate(outs[place], axis=0)
+    pv[row] = jnp.concatenate(outs[3], axis=0)
+
+
+def first_sweep(kappa, fresh, coef, weight):
+    rows, cols, width, deep = weight.shape
     vmem = pl.BlockSpec(memory_space=pltpu.VMEM)
     return call(
-        functools.partial(setup_kernel, kappa),
-        in_specs=[vmem],
-        out_specs=(vmem, pl.BlockSpec(memory_space=pltpu.HBM), vmem, vmem),
+        functools.partial(first_kernel, kappa),
+        grid=(rows,),
+        in_specs=[vmem, vmem, pl.BlockSpec((None, cols, width, deep), lambda row: (row, 0, 0, 0))],
+        out_specs=(vmem, vmem),
         out_shape=(
-            pltpu.VMEM((rows, cols, width, 9 * width), jnp.bfloat16),
-            jax.ShapeDtypeStruct((rows, cols, width, 9 * width), jnp.bfloat16),
-            jax.ShapeDtypeStruct((3, rows, cols, width), jnp.float32),
-            jax.ShapeDtypeStruct((rows, cols, width), jnp.float32),
+            pltpu.VMEM((3, rows, cols, width), jnp.float32),
+            pltpu.VMEM((rows, cols, width), jnp.float32),
         ),
-        scratch_shapes=[
-            pltpu.VMEM((2, width, width), jnp.float32),
-            pltpu.VMEM((2, width, width), jnp.float32),
-            pltpu.VMEM((rows + 2, cols + 2, 3, 8, width), jnp.float32),
-            pltpu.VMEM((2 * width, 9 * width), jnp.bfloat16),
-            pltpu.VMEM((2 * width, 9 * width), jnp.bfloat16),
-            pltpu.SemaphoreType.DMA((2,)),
-        ],
-        name="setup",
-    )(fresh)
+        scratch_shapes=[pltpu.VMEM((rows + 2, cols + 2, 3, 8, width), jnp.float32)],
+        name="first_sweep",
+    )(fresh, pltpu.with_memory_space_constraint(coef, pltpu.VMEM), weight)
 
 
 def sweep_kernel(kappa, last, center, above, below, left, right, coef, sums, pv, *rest):
@@ -320,7 +352,7 @@
 def sweep(kappa, last, pv, halo, coef, sums):
     rows, cols, width, _ = coef.shape
     vmem = pl.BlockSpec(memory_space=pltpu.VMEM)
-    out = jax.ShapeDtypeStruct((rows, cols, width), jnp.float32)
+    out = pltpu.VMEM((rows, cols, width), jnp.float32)
     count = 2 if last else 1
     return call(
         functools.partial(sweep_kernel, kappa, last),
@@ -409,7 +441,8 @@
     old, top = prepare(position, velocity, volume, pressure_prev, fill, drift_from)
     top = largest(top)
     fresh = drift(top, old, *exchange(old, 2))
-    coef, weight, sums, pv = setup(fresh, kappa)
+    coef, weight = setup(fresh)
+    sums, pv = first_sweep(kappa, fresh, coef, weight)
     for step in range(1, SWEEPS):
         last = step == SWEEPS - 1
         pv, *pressure = sweep(kappa, last, pv, exchange(pv, 1), coef, sums)

time: 254 us -> 227 us (0.89)
  starting transfers between devices: 63.8 us -> 46.5 us
  local copies, waits for them, and re-layouts: 15.5 us -> 7.36 us
  waiting for transfers between devices: 34 us -> 31.2 us
    ppermute x20, starting transfers between devices: 60 us -> 44.5 us  [swap(): return lax.ppermute(value, axis, pairs + [(j, i) for i, j in pairs])]
    ppermute x20, waiting for transfers between devices: 25.9 us -> 21.2 us  [swap(): return lax.ppermute(value, axis, pairs + [(j, i) for i, j in pairs])]
    slice x5, local copies, waits for them, and re-layouts: 3.15 us -> 0.04 us  [exchange(): shard[:, :depth]]
    slice x5 -> x0, local copies, waits for them, and re-layouts: 2.88 us -> none  [exchange(): above, below = neighbours('gx', shard[:depth], shard[-depth:])]
    pallas_call x3 -> x4, Pallas kernels: 95.9 us -> 98.1 us  [the longest x1 70.7 us: setup(): call(setup_kernel, in_specs=[vmem], out_specs=(vmem, pl.BlockSpec(memory_...]
    unnamed x40 -> x33, local copies, waits for them, and re-layouts: 7.81 us -> 5.66 us
  transfers between devices with their start and end apart: 25 -> 25, of which waited for: 15 -> 15; matrix products, arithmetic and copies ran while one was open for 1% -> 0% of each run, Pallas kernels for 0% -> 0%
where the time goes in v6:
time: 227 us; the launch traced here: 226 us
  Pallas kernels  138 us (61%)
  starting transfers between devices  46.5 us (20%)
  waiting for transfers between devices  31.2 us (14%)
  local copies, waits for them, and re-layouts  7.36 us (3%)
    pallas_call x1, Pallas kernels, setup(): call(setup_kernel, in_specs=[vmem], out_specs=(vmem, pl.BlockSpec(memory_...  70.7 us
    ppermute x20, starting transfers between devices, swap(): return lax.ppermute(value, axis, pairs + [(j, i) for i, j in pairs])  44.5 us
    pallas_call x1, Pallas kernels, first_sweep(): call(functools.partial(first_kernel, kappa), grid=(rows,), in_specs=[vmem...  25.5 us
    pallas_call x3, Pallas kernels, sweep(): call(functools.partial(sweep_kernel, kappa, last), in_specs=[vmem] * 7, o...  21.4 us
    ppermute x20, waiting for transfers between devices, swap(): return lax.ppermute(value, axis, pairs + [(j, i) for i, j in pairs])  21.2 us
    pallas_call x1, Pallas kernels, push(): call(functools.partial(push_kernel, kappa), grid=(rows,), in_specs=[whole...  18.6 us
    ppermute x5, waiting for transfers between devices, largest(): value = jnp.maximum(value, lax.ppermute(value, axis, pairs))  9.96 us
    unnamed x33, local copies, waits for them, and re-layouts  5.66 us
  transfers between devices with their start and end apart: 25, of which 15 were waited for; matrix products, arithmetic and copies ran while one was open for 0% of the time, Pallas kernels for 0%

profile of v6, /device:TPU:17, one launch (start us, length us, event | category | flops | bytes accessed | tf_op | source)
XLA Modules:
  0.0 226.3 jit_solution(13487931832084064051)
XLA Ops:
  10.6 3.4 %collective-permute-done.5 = f32[2,16,8,128]{3,2,1,0:T(8,128)S(1)} collective-permute-done((f32[2,16,8,128]{3,2,1,0:T(8,128)S(1)}, f32[2,16,8,128]{3,2,1,0:T(8,128)S(1)}, u32[]{:S(2)}, u32[]{:S(2)}) %collective-permute-start.5) | collective-permute-done | bytes 131104 | tf_op jit(solution)/shard_map/ppermute | solution.py:80
  14.1 2.2 collective-permute-start.8
  16.2 3.0 %collective-permute-start.7 = (f32[12,2,8,128]{3,2,1,0:T(8,128)S(1)}, f32[12,2,8,128]{3,2,1,0:T(8,128)S(1)}, u32[]{:S(2)}, u32[]{:S(2)}) collective-permute-start(f32[12,2,8,128]{3,2,1,0:T(8,128)S(1)} %get-tuple-element.27), channel_id=1, source_target_pairs={{1,2},{2,1},{5,6},{6,5},{9,10},{10,9},{13,14},{14,13},{17,18},{18,... | collective-permute-start | bytes 294920 | tf_op jit(solution)/shard_map/ppermute | solution.py:80
  20.9 2.1 collective-permute-done.1
  23.2 2.2 collective-permute-done.2
  27.9 3.4 %collective-permute-done.4 = f32[8,128]{1,0:T(8,128)S(1)} collective-permute-done((f32[8,128]{1,0:T(8,128)S(1)}, f32[8,128]{1,0:T(8,128)S(1)}, u32[]{:S(2)}, u32[]{:S(2)}) %collective-permute-start.4) | collective-permute-done | bytes 4128 | tf_op jit(solution)/shard_map/ppermute | solution.py:103
  33.8 70.7 %setup.1 = (bf16[8,16,128,1152]{3,2,1,0:T(8,128)(2,1)S(1)}, bf16[8,16,128,1152]{3,2,1,0:T(8,128)(2,1)}) custom-call(f32[10,18,8,128]{3,2,1,0:T(8,128)} %copy-done), custom_call_target="tpu_custom_call" | custom-call | tf_op jit(solution)/shard_map/setup/pallas_call | solution.py:223
  104.5 25.5 %first_sweep.1 = (f32[3,8,16,128]{3,2,1,0:T(8,128)S(1)}, f32[8,16,128]{2,1,0:T(8,128)S(1)}) custom-call(f32[10,18,8,128]{3,2,1,0:T(8,128)} %copy-done, bf16[8,16,128,1152]{3,2,1,0:T(8,128)(2,1)S(1)} %get-tuple-element.12.coef, bf16[8,16,128,1152]{3,2,1,0:T(8,128)(2,1)} %get-tuple-element.13.weight), custom_call_target="tpu_custom_call" | custom-call | tf_op jit(solution)/shard_map/first_sweep/pallas_call | solution.py:301
  130.9 3.0 %collective-permute-start.9 = (f32[1,16,128]{2,1,0:T(8,128)S(1)}, f32[1,16,128]{2,1,0:T(8,128)S(1)}, u32[]{:S(2)}, u32[]{:S(2)}) collective-permute-start(f32[1,16,128]{2,1,0:T(8,128)S(1)} %get-tuple-element.47), channel_id=1, source_target_pairs={{4,8},{12,16},{20,24},{8,4},{16,12},{24,20},{5,9},{13,17},{21,25},... | collective-permute-start | bytes 24584 | tf_op jit(solution)/shard_map/ppermute | solution.py:80
  133.9 2.3 collective-permute-done.9
  136.2 6.3 %collective-permute-start.12 = (f32[10,1,128]{2,1,0:T(1,128)S(1)}, f32[10,1,128]{2,1,0:T(1,128)S(1)}, u32[]{:S(2)}, u32[]{:S(2)}) collective-permute-start(f32[10,1,128]{2,1,0:T(1,128)S(1)} %get-tuple-element.70), channel_id=1, source_target_pairs={{0,1},{2,3},{1,0},{3,2},{4,5},{6,7},{5,4},{7,6},{8,9},{10,11},{9,8... | collective-permute-start | bytes 15368 | tf_op jit(solution)/shard_map/ppermute | solution.py:80
  142.5 2.4 %collective-permute-start.11 = (f32[10,1,128]{2,1,0:T(1,128)S(1)}, f32[10,1,128]{2,1,0:T(1,128)S(1)}, u32[]{:S(2)}, u32[]{:S(2)}) collective-permute-start(f32[10,1,128]{2,1,0:T(1,128)S(1)} %get-tuple-element.71), channel_id=1, source_target_pairs={{1,2},{2,1},{5,6},{6,5},{9,10},{10,9},{13,14},{14,13},{17,18},{18,... | collective-permute-start | bytes 15368 | tf_op jit(solution)/shard_map/ppermute | solution.py:80
  144.8 2.6 %collective-permute-done.11 = f32[10,1,128]{2,1,0:T(1,128)S(1)} collective-permute-done((f32[10,1,128]{2,1,0:T(1,128)S(1)}, f32[10,1,128]{2,1,0:T(1,128)S(1)}, u32[]{:S(2)}, u32[]{:S(2)}) %collective-permute-start.11) | collective-permute-done | bytes 5152 | tf_op jit(solution)/shard_map/ppermute | solution.py:80
  148.0 7.1 %sweep.3.center = f32[8,16,128]{2,1,0:T(8,128)S(1)} custom-call(f32[8,16,128]{2,1,0:T(8,128)} %copy-done.7, f32[1,16,128]{2,1,0:T(8,128)} %copy-done.13, f32[1,16,128]{2,1,0:T(8,128)} %copy-done.12, f32[10,1,128]{2,1,0:T(1,128)} %get-tuple-element.69.left, f32[10,1,128]{2,1,0:T(1,128)} %get-tuple-element.68.right, ...), custom_call_target="tpu_custom_call" | custom-call | tf_op jit(solution)/shard_map/sweep/pallas_call | solution.py:357
  158.5 3.2 %collective-permute-done.13 = f32[1,16,128]{2,1,0:T(8,128)S(1)} collective-permute-done((f32[1,16,128]{2,1,0:T(8,128)S(1)}, f32[1,16,128]{2,1,0:T(8,128)S(1)}, u32[]{:S(2)}, u32[]{:S(2)}) %collective-permute-start.13) | collective-permute-done | bytes 8224 | tf_op jit(solution)/shard_map/ppermute | solution.py:80
  161.8 3.8 %collective-permute-start.15 = (f32[10,1,128]{2,1,0:T(1,128)S(1)}, f32[10,1,128]{2,1,0:T(1,128)S(1)}, u32[]{:S(2)}, u32[]{:S(2)}) collective-permute-start(f32[10,1,128]{2,1,0:T(1,128)S(1)} %get-tuple-element.67), channel_id=1, source_target_pairs={{1,2},{2,1},{5,6},{6,5},{9,10},{10,9},{13,14},{14,13},{17,18},{18,... | collective-permute-start | bytes 15368 | tf_op jit(solution)/shard_map/ppermute | solution.py:80
  167.6 7.2 %sweep.4.center = f32[8,16,128]{2,1,0:T(8,128)S(1)} custom-call(f32[8,16,128]{2,1,0:T(8,128)} %copy-done.4, f32[1,16,128]{2,1,0:T(8,128)} %copy-done.15, f32[1,16,128]{2,1,0:T(8,128)} %copy-done.14, f32[10,1,128]{2,1,0:T(1,128)} %get-tuple-element.65.left, f32[10,1,128]{2,1,0:T(1,128)} %get-tuple-element.64.right, ...), custom_call_target="tpu_custom_call" | custom-call | tf_op jit(solution)/shard_map/sweep/pallas_call | solution.py:357
  175.1 3.0 %collective-permute-start.17 = (f32[1,16,128]{2,1,0:T(8,128)S(1)}, f32[1,16,128]{2,1,0:T(8,128)S(1)}, u32[]{:S(2)}, u32[]{:S(2)}) collective-permute-start(f32[1,16,128]{2,1,0:T(8,128)S(1)} %get-tuple-element.39), channel_id=1, source_target_pairs={{4,8},{12,16},{20,24},{8,4},{16,12},{24,20},{5,9},{13,17},{21,25},... | collective-permute-start | bytes 24584 | tf_op jit(solution)/shard_map/ppermute | solution.py:80
  178.1 2.3 collective-permute-done.17
  180.5 5.1 %collective-permute-start.19 = (f32[10,1,128]{2,1,0:T(1,128)S(1)}, f32[10,1,128]{2,1,0:T(1,128)S(1)}, u32[]{:S(2)}, u32[]{:S(2)}) collective-permute-start(f32[10,1,128]{2,1,0:T(1,128)S(1)} %get-tuple-element.63), channel_id=1, source_target_pairs={{1,2},{2,1},{5,6},{6,5},{9,10},{10,9},{13,14},{14,13},{17,18},{18,... | collective-permute-start | bytes 15368 | tf_op jit(solution)/shard_map/ppermute | solution.py:80
  187.5 7.1 %sweep.5 = (f32[8,16,128]{2,1,0:T(8,128)S(1)}, f32[8,16,128]{2,1,0:T(8,128)S(1)}) custom-call(f32[8,16,128]{2,1,0:T(8,128)} %copy-done.3, f32[1,16,128]{2,1,0:T(8,128)} %copy-done.11, f32[1,16,128]{2,1,0:T(8,128)} %copy-done.10, f32[10,1,128]{2,1,0:T(1,128)} %get-tuple-element.61.left, f32[10,1,128]{2,1,0:T(1,128)} %get-tuple-element.60.right, ...), custom_call_target="tpu_custom_call" | custom-call | tf_op jit(solution)/shard_map/sweep/pallas_call | solution.py:357
  197.9 3.2 %collective-permute-done.21 = f32[1,16,128]{2,1,0:T(8,128)S(1)} collective-permute-done((f32[1,16,128]{2,1,0:T(8,128)S(1)}, f32[1,16,128]{2,1,0:T(8,128)S(1)}, u32[]{:S(2)}, u32[]{:S(2)}) %collective-permute-start.21) | collective-permute-done | bytes 8224 | tf_op jit(solution)/shard_map/ppermute | solution.py:80
  201.3 5.1 %collective-permute-start.23 = (f32[10,1,128]{2,1,0:T(1,128)S(1)}, f32[10,1,128]{2,1,0:T(1,128)S(1)}, u32[]{:S(2)}, u32[]{:S(2)}) collective-permute-start(f32[10,1,128]{2,1,0:T(1,128)S(1)} %get-tuple-element.59), channel_id=1, source_target_pairs={{1,2},{2,1},{5,6},{6,5},{9,10},{10,9},{13,14},{14,13},{17,18},{18,... | collective-permute-start | bytes 15368 | tf_op jit(solution)/shard_map/ppermute | solution.py:80
  207.7 18.6 %push.1 = f32[2,8,16,128]{3,2,1,0:T(8,128)} custom-call(f32[8,16,128]{2,1,0:T(8,128)S(1)} %get-tuple-element.17.center, f32[1,16,128]{2,1,0:T(8,128)S(1)} %get-tuple-element.49.above, f32[1,16,128]{2,1,0:T(8,128)S(1)} %get-tuple-element.48.below, f32[10,1,128]{2,1,0:T(1,128)S(1)} %get-tuple-element.57.left, f32[10,1,128]{2,1,0:T(1,128)S(1)} %get-tuple-element.56.right, ...), custom_call_target="tpu_custom_call" | custom-call | tf_op jit(solution)/shard_map/push/pallas_call | solution.py:421
  (108 shorter events, 30.7 us)
Async XLA Ops:
  6.1 4.4 %collective-permute-start.6 = (f32[2,16,8,128]{3,2,1,0:T(8,128)S(1)}, f32[2,16,8,128]{3,2,1,0:T(8,128)S(1)}, u32[]{:S(2)}, u32[]{:S(2)}) collective-permute-start(f32[2,16,8,128]{3,2,1,0:T(8,128)S(1)} %get-tuple-element.20), channel_id=1, source_target_pairs={{0,4},{8,12},{16,20},{24,28},{4,0},{12,8},{20,16},{28,24},{1,5},{9... | collective-permute-start | bytes 393224 | tf_op jit(solution)/shard_map/ppermute | solution.py:80
  7.4 6.6 %collective-permute-start.5 = (f32[2,16,8,128]{3,2,1,0:T(8,128)S(1)}, f32[2,16,8,128]{3,2,1,0:T(8,128)S(1)}, u32[]{:S(2)}, u32[]{:S(2)}) collective-permute-start(f32[2,16,8,128]{3,2,1,0:T(8,128)S(1)} %get-tuple-element.21), channel_id=1, source_target_pairs={{4,8},{12,16},{20,24},{8,4},{16,12},{24,20},{5,9},{13,17},{21,25},... | collective-permute-start | bytes 393224 | tf_op jit(solution)/shard_map/ppermute | solution.py:80
  14.1 17.2 %collective-permute-start.8 = (f32[12,2,8,128]{3,2,1,0:T(8,128)S(1)}, f32[12,2,8,128]{3,2,1,0:T(8,128)S(1)}, u32[]{:S(2)}, u32[]{:S(2)}) collective-permute-start(f32[12,2,8,128]{3,2,1,0:T(8,128)S(1)} %get-tuple-element.26), channel_id=1, source_target_pairs={{0,1},{2,3},{1,0},{3,2},{4,5},{6,7},{5,4},{7,6},{8,9},{10,11},{9,8... | collective-permute-start | bytes 294920 | tf_op jit(solution)/shard_map/ppermute | solution.py:80
  16.2 15.0 %collective-permute-start.7 = (f32[12,2,8,128]{3,2,1,0:T(8,128)S(1)}, f32[12,2,8,128]{3,2,1,0:T(8,128)S(1)}, u32[]{:S(2)}, u32[]{:S(2)}) collective-permute-start(f32[12,2,8,128]{3,2,1,0:T(8,128)S(1)} %get-tuple-element.27), channel_id=1, source_target_pairs={{1,2},{2,1},{5,6},{6,5},{9,10},{10,9},{13,14},{14,13},{17,18},{18,... | collective-permute-start | bytes 294920 | tf_op jit(solution)/shard_map/ppermute | solution.py:80
  20.5 2.5 %collective-permute-start.1 = (f32[8,128]{1,0:T(8,128)S(1)}, f32[8,128]{1,0:T(8,128)S(1)}, u32[]{:S(2)}, u32[]{:S(2)}) collective-permute-start(f32[8,128]{1,0:T(8,128)S(1)} %max.15), channel_id=1, source_target_pairs={{0,2},{1,3},{2,0},{3,1},{4,6},{5,7},{6,4},{7,5},{8,10},{9,11},{10,... | collective-permute-start | bytes 12296 | tf_op jit(solution)/shard_map/ppermute | solution.py:103
  23.0 2.5 %collective-permute-start.2 = (f32[8,128]{1,0:T(8,128)S(1)}, f32[8,128]{1,0:T(8,128)S(1)}, u32[]{:S(2)}, u32[]{:S(2)}) collective-permute-start(f32[8,128]{1,0:T(8,128)S(1)} %max.16), channel_id=1, source_target_pairs={{0,4},{4,0},{8,12},{12,8},{16,20},{20,16},{24,28},{28,24},{1,5},{5... | collective-permute-start | bytes 12296 | tf_op jit(solution)/shard_map/ppermute | solution.py:103
  25.4 2.5 %collective-permute-start.3 = (f32[8,128]{1,0:T(8,128)S(1)}, f32[8,128]{1,0:T(8,128)S(1)}, u32[]{:S(2)}, u32[]{:S(2)}) collective-permute-start(f32[8,128]{1,0:T(8,128)S(1)} %max.17), channel_id=1, source_target_pairs={{0,8},{4,12},{8,0},{12,4},{16,24},{20,28},{24,16},{28,20},{1,9},{5... | collective-permute-start | bytes 12296 | tf_op jit(solution)/shard_map/ppermute | solution.py:103
  27.9 3.4 %collective-permute-start.4 = (f32[8,128]{1,0:T(8,128)S(1)}, f32[8,128]{1,0:T(8,128)S(1)}, u32[]{:S(2)}, u32[]{:S(2)}) collective-permute-start(f32[8,128]{1,0:T(8,128)S(1)} %max.18), channel_id=1, source_target_pairs={{0,16},{4,20},{8,24},{12,28},{16,0},{20,4},{24,8},{28,12},{1,17},{... | collective-permute-start | bytes 12296 | tf_op jit(solution)/shard_map/ppermute | solution.py:103
  130.6 3.3 %collective-permute-start.10 = (f32[1,16,128]{2,1,0:T(8,128)S(1)}, f32[1,16,128]{2,1,0:T(8,128)S(1)}, u32[]{:S(2)}, u32[]{:S(2)}) collective-permute-start(f32[1,16,128]{2,1,0:T(8,128)S(1)} %get-tuple-element.46), channel_id=1, source_target_pairs={{0,4},{8,12},{16,20},{24,28},{4,0},{12,8},{20,16},{28,24},{1,5},{9... | collective-permute-start | bytes 24584 | tf_op jit(solution)/shard_map/ppermute | solution.py:80
  130.9 5.3 %collective-permute-start.9 = (f32[1,16,128]{2,1,0:T(8,128)S(1)}, f32[1,16,128]{2,1,0:T(8,128)S(1)}, u32[]{:S(2)}, u32[]{:S(2)}) collective-permute-start(f32[1,16,128]{2,1,0:T(8,128)S(1)} %get-tuple-element.47), channel_id=1, source_target_pairs={{4,8},{12,16},{20,24},{8,4},{16,12},{24,20},{5,9},{13,17},{21,25},... | collective-permute-start | bytes 24584 | tf_op jit(solution)/shard_map/ppermute | solution.py:80
  136.2 8.6 %collective-permute-start.12 = (f32[10,1,128]{2,1,0:T(1,128)S(1)}, f32[10,1,128]{2,1,0:T(1,128)S(1)}, u32[]{:S(2)}, u32[]{:S(2)}) collective-permute-start(f32[10,1,128]{2,1,0:T(1,128)S(1)} %get-tuple-element.70), channel_id=1, source_target_pairs={{0,1},{2,3},{1,0},{3,2},{4,5},{6,7},{5,4},{7,6},{8,9},{10,11},{9,8... | collective-permute-start | bytes 15368 | tf_op jit(solution)/shard_map/ppermute | solution.py:80
  142.5 4.9 %collective-permute-start.11 = (f32[10,1,128]{2,1,0:T(1,128)S(1)}, f32[10,1,128]{2,1,0:T(1,128)S(1)}, u32[]{:S(2)}, u32[]{:S(2)}) collective-permute-start(f32[10,1,128]{2,1,0:T(1,128)S(1)} %get-tuple-element.71), channel_id=1, source_target_pairs={{1,2},{2,1},{5,6},{6,5},{9,10},{10,9},{13,14},{14,13},{17,18},{18,... | collective-permute-start | bytes 15368 | tf_op jit(solution)/shard_map/ppermute | solution.py:80
  155.1 3.3 %collective-permute-start.14 = (f32[1,16,128]{2,1,0:T(8,128)S(1)}, f32[1,16,128]{2,1,0:T(8,128)S(1)}, u32[]{:S(2)}, u32[]{:S(2)}) collective-permute-start(f32[1,16,128]{2,1,0:T(8,128)S(1)} %get-tuple-element.42), channel_id=1, source_target_pairs={{0,4},{8,12},{16,20},{24,28},{4,0},{12,8},{20,16},{28,24},{1,5},{9... | collective-permute-start | bytes 24584 | tf_op jit(solution)/shard_map/ppermute | solution.py:80
  156.4 5.3 %collective-permute-start.13 = (f32[1,16,128]{2,1,0:T(8,128)S(1)}, f32[1,16,128]{2,1,0:T(8,128)S(1)}, u32[]{:S(2)}, u32[]{:S(2)}) collective-permute-start(f32[1,16,128]{2,1,0:T(8,128)S(1)} %get-tuple-element.43), channel_id=1, source_target_pairs={{4,8},{12,16},{20,24},{8,4},{16,12},{24,20},{5,9},{13,17},{21,25},... | collective-permute-start | bytes 24584 | tf_op jit(solution)/shard_map/ppermute | solution.py:80
  161.8 3.9 %collective-permute-start.16 = (f32[10,1,128]{2,1,0:T(1,128)S(1)}, f32[10,1,128]{2,1,0:T(1,128)S(1)}, u32[]{:S(2)}, u32[]{:S(2)}) collective-permute-start(f32[10,1,128]{2,1,0:T(1,128)S(1)} %get-tuple-element.66), channel_id=1, source_target_pairs={{0,1},{2,3},{1,0},{3,2},{4,5},{6,7},{5,4},{7,6},{8,9},{10,11},{9,8... | collective-permute-start | bytes 15368 | tf_op jit(solution)/shard_map/ppermute | solution.py:80
  161.8 5.1 %collective-permute-start.15 = (f32[10,1,128]{2,1,0:T(1,128)S(1)}, f32[10,1,128]{2,1,0:T(1,128)S(1)}, u32[]{:S(2)}, u32[]{:S(2)}) collective-permute-start(f32[10,1,128]{2,1,0:T(1,128)S(1)} %get-tuple-element.67), channel_id=1, source_target_pairs={{1,2},{2,1},{5,6},{6,5},{9,10},{10,9},{13,14},{14,13},{17,18},{18,... | collective-permute-start | bytes 15368 | tf_op jit(solution)/shard_map/ppermute | solution.py:80
  174.8 3.3 %collective-permute-start.18 = (f32[1,16,128]{2,1,0:T(8,128)S(1)}, f32[1,16,128]{2,1,0:T(8,128)S(1)}, u32[]{:S(2)}, u32[]{:S(2)}) collective-permute-start(f32[1,16,128]{2,1,0:T(8,128)S(1)} %get-tuple-element.38), channel_id=1, source_target_pairs={{0,4},{8,12},{16,20},{24,28},{4,0},{12,8},{20,16},{28,24},{1,5},{9... | collective-permute-start | bytes 24584 | tf_op jit(solution)/shard_map/ppermute | solution.py:80
  175.1 5.3 %collective-permute-start.17 = (f32[1,16,128]{2,1,0:T(8,128)S(1)}, f32[1,16,128]{2,1,0:T(8,128)S(1)}, u32[]{:S(2)}, u32[]{:S(2)}) collective-permute-start(f32[1,16,128]{2,1,0:T(8,128)S(1)} %get-tuple-element.39), channel_id=1, source_target_pairs={{4,8},{12,16},{20,24},{8,4},{16,12},{24,20},{5,9},{13,17},{21,25},... | collective-permute-start | bytes 24584 | tf_op jit(solution)/shard_map/ppermute | solution.py:80
  180.4 5.2 %collective-permute-start.20 = (f32[10,1,128]{2,1,0:T(1,128)S(1)}, f32[10,1,128]{2,1,0:T(1,128)S(1)}, u32[]{:S(2)}, u32[]{:S(2)}) collective-permute-start(f32[10,1,128]{2,1,0:T(1,128)S(1)} %get-tuple-element.62), channel_id=1, source_target_pairs={{0,1},{2,3},{1,0},{3,2},{4,5},{6,7},{5,4},{7,6},{8,9},{10,11},{9,8... | collective-permute-start | bytes 15368 | tf_op jit(solution)/shard_map/ppermute | solution.py:80
  180.5 6.4 %collective-permute-start.19 = (f32[10,1,128]{2,1,0:T(1,128)S(1)}, f32[10,1,128]{2,1,0:T(1,128)S(1)}, u32[]{:S(2)}, u32[]{:S(2)}) collective-permute-start(f32[10,1,128]{2,1,0:T(1,128)S(1)} %get-tuple-element.63), channel_id=1, source_target_pairs={{1,2},{2,1},{5,6},{6,5},{9,10},{10,9},{13,14},{14,13},{17,18},{18,... | collective-permute-start | bytes 15368 | tf_op jit(solution)/shard_map/ppermute | solution.py:80
  194.6 3.3 %collective-permute-start.22 = (f32[1,16,128]{2,1,0:T(8,128)S(1)}, f32[1,16,128]{2,1,0:T(8,128)S(1)}, u32[]{:S(2)}, u32[]{:S(2)}) collective-permute-start(f32[1,16,128]{2,1,0:T(8,128)S(1)} %get-tuple-element.34), channel_id=1, source_target_pairs={{0,4},{8,12},{16,20},{24,28},{4,0},{12,8},{20,16},{28,24},{1,5},{9... | collective-permute-start | bytes 24584 | tf_op jit(solution)/shard_map/ppermute | solution.py:80
  195.9 5.3 %collective-permute-start.21 = (f32[1,16,128]{2,1,0:T(8,128)S(1)}, f32[1,16,128]{2,1,0:T(8,128)S(1)}, u32[]{:S(2)}, u32[]{:S(2)}) collective-permute-start(f32[1,16,128]{2,1,0:T(8,128)S(1)} %get-tuple-element.35), channel_id=1, source_target_pairs={{4,8},{12,16},{20,24},{8,4},{16,12},{24,20},{5,9},{13,17},{21,25},... | collective-permute-start | bytes 24584 | tf_op jit(solution)/shard_map/ppermute | solution.py:80
  201.2 5.8 %collective-permute-start.24 = (f32[10,1,128]{2,1,0:T(1,128)S(1)}, f32[10,1,128]{2,1,0:T(1,128)S(1)}, u32[]{:S(2)}, u32[]{:S(2)}) collective-permute-start(f32[10,1,128]{2,1,0:T(1,128)S(1)} %get-tuple-element.58), channel_id=1, source_target_pairs={{0,1},{2,3},{1,0},{3,2},{4,5},{6,7},{5,4},{7,6},{8,9},{10,11},{9,8... | collective-permute-start | bytes 15368 | tf_op jit(solution)/shard_map/ppermute | solution.py:80
  201.3 6.4 %collective-permute-start.23 = (f32[10,1,128]{2,1,0:T(1,128)S(1)}, f32[10,1,128]{2,1,0:T(1,128)S(1)}, u32[]{:S(2)}, u32[]{:S(2)}) collective-permute-start(f32[10,1,128]{2,1,0:T(1,128)S(1)} %get-tuple-element.59), channel_id=1, source_target_pairs={{1,2},{2,1},{5,6},{6,5},{9,10},{10,9},{13,14},{14,13},{17,18},{18,... | collective-permute-start | bytes 15368 | tf_op jit(solution)/shard_map/ppermute | solution.py:80
  (17 other events, 138.5 us)

commit v7 on v6

--- a/solution.py
+++ b/solution.py
@@ -11,7 +11,7 @@
 CFL = 0.25
 SPEED_EPS = 1e-06
 SOFT = 0.01
-CHUNK = 32
+CHUNK = 64
 VMEM_LIMIT = 20 * 1024 * 1024
 
 X, Y, U, V, VOL, PRES, CODE = range(7)
@@ -84,12 +84,54 @@
     return jnp.where(even, two, one), jnp.where(even, one, two)
 
 
-def exchange(shard, depth):
+def exchange_old(shard, depth):
     above, below = neighbours("gx", shard[:depth], shard[-depth:])
     low = jnp.concatenate([above[:, :depth], shard[:, :depth], below[:, :depth]], axis=0)
     high = jnp.concatenate([above[:, -depth:], shard[:, -depth:], below[:, -depth:]], axis=0)
     left, right = neighbours("gy", low, high)
     return above, below, left, right
+
+
+def exchange_edges(edge, rows):
+    above, below = neighbours("gx", edge[0], edge[1])
+    half = edge.shape[1] // 2
+    low = jnp.concatenate([above[:1], edge[0, :1], edge[2, : rows - 2], edge[1, :1], below[:1]], axis=0)
+    high = jnp.concatenate([above[-1:], edge[0, -1:], edge[2, half : half + rows - 2], edge[1, -1:], below[-1:]], axis=0)
+    left, right = neighbours("gy", low, high)
+    return above, below, left, right
+
+
+def groups_of(edge, rows, cols):
+    return (3, cols) if edge else (rows - 2, cols - 2)
+
+
+def place_of(edge, group, index, rows, cols):
+    if not edge:
+        return group + 1, index + 1
+    half = cols // 2
+    left = index < half
+    side_row = jnp.minimum(jnp.where(left, index, index - half) + 1, rows - 2)
+    side_col = jnp.where(left, 0, cols - 1)
+    row = jnp.where(group == 0, 0, jnp.where(group == 1, rows - 1, side_row))
+    return row, jnp.where(group == 2, side_col, index)
+
+
+def join(out, at, edge, inner, rows, cols):
+    half = cols // 2
+    out[at, at : at + cols] = edge[0]
+    out[at + rows - 1, at : at + cols] = edge[1]
+    for row in range(1, rows - 1):
+        out[at + row, at : at + 1] = edge[2, row - 1 : row]
+        out[at + row, at + cols - 1 : at + cols] = edge[2, half + row - 1 : half + row]
+        out[at + row, at + 1 : at + cols - 1] = inner[row - 1]
+
+
+def frame(out, above, below, left, right, rows, cols):
+    out[0, 1 : cols + 1] = above[...]
+    out[rows + 1, 1 : cols + 1] = below[...]
+    for row in range(rows + 2):
+        out[row, 0:1] = left[row : row + 1]
+        out[row, cols + 1 : cols + 2] = right[row : row + 1]
 
 
 def largest(value):
@@ -149,16 +191,22 @@
     return lax.dot_general(left, right, (((1,), (1,)), ((), ())), preferred_element_type=jnp.float32)
 
 
-def setup_kernel(fresh, coef, weight, xcol, ycol, out_a, out_b, sem):
-    rows, cols, width, _ = coef.shape
+def setup_kernel(edge, fresh, coef, weight, xcol, ycol, out_a, out_b, sem):
+    groups, size, width, _ = coef.shape
+    rows, cols = fresh.shape[0] - 2, fresh.shape[1] - 2
+
+    def place(bin_id):
+        return place_of(edge, bin_id // size, lax.rem(bin_id, size), rows, cols)
 
     def columns(bin_id, slot):
-        tile = fresh[bin_id // cols + 1, lax.rem(bin_id, cols) + 1]
+        row, col = place(bin_id)
+        tile = fresh[row + 1, col + 1]
         xcol[slot] = jnp.broadcast_to(tile[X : X + 1], (width, width)).T
         ycol[slot] = jnp.broadcast_to(tile[Y : Y + 1], (width, width)).T
 
     def blocks(bin_id, slot, out):
-        row, col = bin_id // cols, lax.rem(bin_id, cols)
+        row, col = place(bin_id)
+        values = coef.at[bin_id // size, lax.rem(bin_id, size)]
         around = [fresh[row + k // 3, col + k % 3] for k in range(9)]
         xj = [jnp.broadcast_to(around[k][X : X + 1] + (k // 3 - 1.0), (8, width)) for k in range(9)]
         yj = [jnp.broadcast_to(around[k][Y : Y + 1] + (k % 3 - 1.0), (8, width)) for k in range(9)]
@@ -181,13 +229,13 @@
                 weights = jnp.concatenate(weights, axis=0).astype(jnp.bfloat16)
                 ratio = squares * pltpu.reciprocal(squares + jnp.bfloat16(SOFT), approx=True)
                 out[span, lanes] = weights
-                coef[row, col, span, lanes] = weights * ratio
+                values[span, lanes] = weights * ratio
 
     def copy_out(bin_id, out, slot):
-        target = weight.at[bin_id // cols, lax.rem(bin_id, cols)]
+        target = weight.at[bin_id // size, lax.rem(bin_id, size)]
         return pltpu.make_async_copy(out, target, sem.at[slot])
 
-    count = rows * cols
+    count = groups * size
     columns(0, 0)
     columns(1, 1)
 
@@ -216,17 +264,17 @@
     copy_out(count - 1, out_b, 1).wait()
 
 
-def setup(fresh):
+def setup(edge, fresh):
     rows, cols, _, width = fresh.shape
-    rows, cols = rows - 2, cols - 2
+    groups, size = groups_of(edge, rows - 2, cols - 2)
     vmem = pl.BlockSpec(memory_space=pltpu.VMEM)
     return call(
-        setup_kernel,
+        functools.partial(setup_kernel, edge),
         in_specs=[vmem],
         out_specs=(vmem, pl.BlockSpec(memory_space=pltpu.HBM)),
         out_shape=(
-            pltpu.VMEM((rows, cols, width, 9 * width), jnp.bfloat16),
-            jax.ShapeDtypeStruct((rows, cols, width, 9 * width), jnp.bfloat16),
+            pltpu.VMEM((groups, size, width, 9 * width), jnp.bfloat16),
+            jax.ShapeDtypeStruct((groups, size, width, 9 * width), jnp.bfloat16),
         ),
         scratch_shapes=[
             pltpu.VMEM((2, width, width), jnp.float32),
@@ -239,11 +287,11 @@
     )(fresh)
 
 
-def first_kernel(kappa, fresh, coef, weight, sums, pv, feat):
-    row = pl.program_id(0)
-    cols, width, _ = weight.shape
-
-    @pl.when(row == 0)
+def first_kernel(kappa, edge, fresh, coef, weight, sums, pv, feat):
+    group = pl.program_id(0)
+    size, width, _ = weight.shape
+
+    @pl.when(group == 0)
     def _():
         def one_row(r, carry):
             tiles = []
@@ -265,7 +313,8 @@
         lax.fori_loop(0, fresh.shape[0], one_row, 0)
 
     outs = ([], [], [], [])
-    for col in range(cols):
+    for index in range(size):
+        row, col = place_of(edge, group, index, fresh.shape[0] - 2, fresh.shape[1] - 2)
         around = []
         for k in range(9):
             off_x, off_y = k // 3 - 1, k % 3 - 1
@@ -276,8 +325,8 @@
                 features = features + float(off_y) * feat[row + k // 3, col + k % 3, 2]
             around.append(split(features))
         around = jnp.concatenate(around, axis=1)
-        total_w = dot_nt(weight[col], around)
-        total_c = dot_nt(coef[row, col], around)
+        total_w = dot_nt(weight[index], around)
+        total_c = dot_nt(coef[group, index], around)
         total_w = (total_w[:, :8] + total_w[:, 8:]).T
         total_c = (total_c[:, :8] + total_c[:, 8:]).T
         tile = fresh[row + 1, col + 1]
@@ -291,89 +340,106 @@
         for out, value in zip(outs, (source, rden, vol, first * vol)):
             out.append(value)
     for place in range(3):
-        sums[place, row] = jnp.concatenate(outs[place], axis=0)
-    pv[row] = jnp.concatenate(outs[3], axis=0)
-
-
-def first_sweep(kappa, fresh, coef, weight):
-    rows, cols, width, deep = weight.shape
+        sums[place, group] = jnp.concatenate(outs[place], axis=0)
+    pv[group] = jnp.concatenate(outs[3], axis=0)
+
+
+def first_sweep(kappa, edge, fresh, coef, weight):
+    groups, size, width, deep = weight.shape
+    rows, cols = fresh.shape[:2]
     vmem = pl.BlockSpec(memory_space=pltpu.VMEM)
     return call(
-        functools.partial(first_kernel, kappa),
-        grid=(rows,),
-        in_specs=[vmem, vmem, pl.BlockSpec((None, cols, width, deep), lambda row: (row, 0, 0, 0))],
+        functools.partial(first_kernel, kappa, edge),
+        grid=(groups,),
+        in_specs=[vmem, vmem, pl.BlockSpec((None, size, width, deep), lambda group: (group, 0, 0, 0))],
         out_specs=(vmem, vmem),
         out_shape=(
-            pltpu.VMEM((3, rows, cols, width), jnp.float32),
-            pltpu.VMEM((rows, cols, width), jnp.float32),
+            pltpu.VMEM((3, groups, size, width), jnp.float32),
+            pltpu.VMEM((groups, size, width), jnp.float32),
         ),
-        scratch_shapes=[pltpu.VMEM((rows + 2, cols + 2, 3, 8, width), jnp.float32)],
+        scratch_shapes=[pltpu.VMEM((rows, cols, 3, 8, width), jnp.float32)],
         name="first_sweep",
     )(fresh, pltpu.with_memory_space_constraint(coef, pltpu.VMEM), weight)
 
 
-def sweep_kernel(kappa, last, center, above, below, left, right, coef, sums, pv, *rest):
-    pressure = rest[0] if last else None
-    ext, tiles = rest[-2:]
-    rows, cols, width, _ = coef.shape
-    assemble(ext, center, above, below, left, right, 1)
+def sweep_kernel(kappa, last, edge, rows, cols, count, *refs):
+    before_edge, before_inner, *halo = refs[: count - 2]
+    coef, sums = refs[count - 2 : count]
+    pv, *pressure = refs[count:-2]
+    ext, tiles = refs[-2:]
+    groups, size, width, _ = coef.shape
+    join(ext, 1, before_edge, before_inner, rows, cols)
+    if edge:
+        frame(ext, *halo, rows, cols)
 
     def spread(row, carry):
         for col in range(cols + 2):
             tiles[row, col] = jnp.broadcast_to(ext[row, col : col + 1, :], (16, width)).astype(jnp.bfloat16)
         return carry
 
-    lax.fori_loop(0, rows + 2, spread, 0)
+    if edge:
+        lax.fori_loop(0, rows + 2, spread, 0)
+    else:
+        lax.fori_loop(1, rows + 1, spread, 0)
     ones = jnp.ones((16, width), jnp.bfloat16)
 
-    def one_row(row, carry):
+    def one_group(group, carry):
         totals = []
-        for col in range(cols):
+        for index in range(size):
+            row, col = place_of(edge, group, index, rows, cols)
             around = [tiles[row + k // 3, col + k % 3] for k in range(9)]
             parts = []
             for part in range(width // 16):
                 total = None
                 for k in range(9):
-                    term = coef[row, col, pl.ds(part * 16, 16), pl.ds(k * width, width)] * around[k]
+                    term = coef[group, index, pl.ds(part * 16, 16), pl.ds(k * width, width)] * around[k]
                     total = term if total is None else total + term
                 parts.append(total)
             totals.append(dot_nt(ones, jnp.concatenate(parts, axis=0))[0:1])
         total = jnp.concatenate(totals, axis=0)
-        value = (sums[0, row] + kappa * 40.0 * total) * sums[1, row]
-        vol = sums[2, row]
-        pv[row] = value * vol
+        value = (sums[0, group] + kappa * 40.0 * total) * sums[1, group]
+        vol = sums[2, group]
+        pv[group] = value * vol
         if last:
-            pressure[row] = jnp.where(vol > 0.0, value, 0.0)
+            pressure[0][group] = jnp.where(vol > 0.0, value, 0.0)
         return carry
 
-    lax.fori_loop(0, rows, one_row, 0)
-
-
-def sweep(kappa, last, pv, halo, coef, sums):
-    rows, cols, width, _ = coef.shape
+    lax.fori_loop(0, groups, one_group, 0)
+
+
+def sweep(kappa, last, edge, shape, pv, halo, coef, sums):
+    rows, cols, width = shape
+    groups, size = coef.shape[:2]
     vmem = pl.BlockSpec(memory_space=pltpu.VMEM)
-    out = pltpu.VMEM((rows, cols, width), jnp.float32)
-    count = 2 if last else 1
+    out = pltpu.VMEM((groups, size, width), jnp.float32)
+    outs = 2 if last else 1
+    args = (*pv, *(halo if edge else ()), pltpu.with_memory_space_constraint(coef, pltpu.VMEM), sums)
     return call(
-        functools.partial(sweep_kernel, kappa, last),
-        in_specs=[vmem] * 7,
-        out_specs=[vmem] * count,
-        out_shape=[out] * count,
+        functools.partial(sweep_kernel, kappa, last, edge, rows, cols, len(args)),
+        in_specs=[vmem] * len(args),
+        out_specs=[vmem] * outs,
+        out_shape=[out] * outs,
         scratch_shapes=[
             pltpu.VMEM((rows + 2, cols + 2, width), jnp.float32),
             pltpu.VMEM((rows + 2, cols + 2, 16, width), jnp.bfloat16),
         ],
         name="sweep",
-    )(pv, *halo, pltpu.with_memory_space_constraint(coef, pltpu.VMEM), sums)
-
-
-def push_kernel(kappa, center, above, below, left, right, fresh, weight, pressure, out, ext, feat):
-    row = pl.program_id(0)
-    cols, width, _ = weight.shape
-
-    @pl.when(row == 0)
+    )(*args)
+
+
+def push_kernel(kappa, edge, count, *refs):
+    before_edge, before_inner, *halo = refs[: count - (5 if edge else 3)]
+    fresh, weight, pressure = refs[count - (5 if edge else 3) : count][:3]
+    ext, feat = refs[-2:]
+    group = pl.program_id(0)
+    size, width, _ = weight.shape
+    rows, cols = fresh.shape[0] - 2, fresh.shape[1] - 2
+
+    @pl.when(group == 0)
     def _():
-        assemble(ext, center, above, below, left, right, 1)
+        join(ext, 1, before_edge, before_inner, rows, cols)
+        if edge:
+            frame(ext, *halo, rows, cols)
 
         def one_row(r, carry):
             tiles = []
@@ -387,67 +453,101 @@
                 feat[r, col] = tiles[col]
             return carry
 
-        lax.fori_loop(0, ext.shape[0], one_row, 0)
-
-    index = row_index(width)
+        lax.fori_loop(0, rows + 2, one_row, 0)
+
+    feature = row_index(width)
     news = ([], [])
-    for col in range(cols):
+    for index in range(size):
+        row, col = place_of(edge, group, index, rows, cols)
         around = []
         for k in range(9):
             tile = feat[row + k // 3, col + k % 3]
             off_x, off_y = k // 3 - 1.0, k % 3 - 1.0
             pv, vol = tile[0:1], tile[4:5]
             if off_x:
-                tile = tile + jnp.where(index == 1, off_x * pv, jnp.where(index == 5, off_x * vol, 0.0))
+                tile = tile + jnp.where(feature == 1, off_x * pv, jnp.where(feature == 5, off_x * vol, 0.0))
             if off_y:
-                tile = tile + jnp.where(index == 2, off_y * pv, jnp.where(index == 6, off_y * vol, 0.0))
+                tile = tile + jnp.where(feature == 2, off_y * pv, jnp.where(feature == 6, off_y * vol, 0.0))
             around.append(split(tile))
-        total = dot_nt(weight[col], jnp.concatenate(around, axis=1))
+        total = dot_nt(weight[index], jnp.concatenate(around, axis=1))
         total = (total[:, :8] + total[:, 8:]).T
         tile = fresh[row + 1, col + 1]
-        own = pressure[col : col + 1, :]
+        own = pressure[group, index : index + 1, :]
         alive = tile[VOL : VOL + 1] > 0.0
         for axis in (0, 1):
             at = tile[axis : axis + 1]
             grad = at * total[0:1] - total[1 + axis : 2 + axis] - own * (at * total[4:5] - total[5 + axis : 6 + axis])
             news[axis].append(jnp.where(alive, tile[2 + axis : 3 + axis] + kappa * 20.0 * grad, 0.0))
-    out[0] = jnp.concatenate(news[0], axis=0)
-    out[1] = jnp.concatenate(news[1], axis=0)
-
-
-def push(kappa, pv, halo, fresh, weight, pressure):
-    rows, cols, width, deep = weight.shape
-    whole = pl.BlockSpec(memory_space=pltpu.VMEM)
+    if not edge:
+        out = refs[count]
+        for axis in (0, 1):
+            out[axis, group] = jnp.concatenate(news[axis], axis=0)
+        return
+    inner_pressure, inner_new = refs[count - 2 : count]
+    out_pressure, out_new, new = refs[count:-2]
+    for axis in (0, 1):
+        new[axis, group] = jnp.concatenate(news[axis], axis=0)
+
+    @pl.when(group == 2)
+    def _():
+        join(out_pressure, 0, pressure, inner_pressure, rows, cols)
+        for axis in (0, 1):
+            join(out_new.at[axis], 0, new.at[axis], inner_new.at[axis], rows, cols)
+
+
+def push(kappa, edge, pv, halo, fresh, weight, pressure, inner):
+    groups, size, width, deep = weight.shape
+    rows, cols = fresh.shape[:2]
+    vmem = pl.BlockSpec(memory_space=pltpu.VMEM)
+    args = (*pv, *(halo if edge else ()), fresh, weight, pressure, *(inner if edge else ()))
+    specs = [vmem] * len(args)
+    specs[len(pv) + (len(halo) if edge else 0) + 1] = pl.BlockSpec(
+        (None, size, width, deep), lambda group: (group, 0, 0, 0)
+    )
+    if edge:
+        outs = [
+            jax.ShapeDtypeStruct((rows - 2, cols - 2, width), jnp.float32),
+            jax.ShapeDtypeStruct((2, rows - 2, cols - 2, width), jnp.float32),
+        ]
+    else:
+        outs = [pltpu.VMEM((2, groups, size, width), jnp.float32)]
     return call(
-        functools.partial(push_kernel, kappa),
-        grid=(rows,),
-        in_specs=[whole] * 6
+        functools.partial(push_kernel, kappa, edge, len(args)),
+        grid=(groups,),
+        in_specs=specs,
+        out_specs=[vmem] * len(outs),
+        out_shape=outs,
+        scratch_shapes=([pltpu.VMEM((2, groups, size, width), jnp.float32)] if edge else [])
         + [
-            pl.BlockSpec((None, cols, width, deep), lambda row: (row, 0, 0, 0)),
-            pl.BlockSpec((None, cols, width), lambda row: (row, 0, 0)),
-        ],
-        out_specs=pl.BlockSpec((2, None, cols, width), lambda row: (0, row, 0, 0)),
-        out_shape=jax.ShapeDtypeStruct((2, rows, cols, width), jnp.float32),
-        scratch_shapes=[
-            pltpu.VMEM((rows + 2, cols + 2, width), jnp.float32),
-            pltpu.VMEM((rows + 2, cols + 2, 8, width), jnp.float32),
+            pltpu.VMEM((rows, cols, width), jnp.float32),
+            pltpu.VMEM((rows, cols, 8, width), jnp.float32),
         ],
         name="push",
-    )(pv, *halo, fresh, weight, pressure)
+    )(*args)
 
 
 def local(position, velocity, volume, pressure_prev, fill, drift_from):
-    kappa = 1.0 / volume.shape[2]
+    shape = volume.shape
+    kappa = 1.0 / shape[2]
     old, top = prepare(position, velocity, volume, pressure_prev, fill, drift_from)
     top = largest(top)
-    fresh = drift(top, old, *exchange(old, 2))
-    coef, weight = setup(fresh)
-    sums, pv = first_sweep(kappa, fresh, coef, weight)
+    fresh = drift(top, old, *exchange_old(old, 2))
+    edge_coef, edge_weight = setup(True, fresh)
+    edge_sums, edge_pv = first_sweep(kappa, True, fresh, edge_coef, edge_weight)
+    inner_coef, inner_weight = setup(False, fresh)
+    inner_sums, inner_pv = first_sweep(kappa, False, fresh, inner_coef, inner_weight)
     for step in range(1, SWEEPS):
         last = step == SWEEPS - 1
-        pv, *pressure = sweep(kappa, last, pv, exchange(pv, 1), coef, sums)
-    velocity_new = push(kappa, pv, exchange(pv, 1), fresh, weight, pressure[0])
-    return (pressure[0], velocity_new)
+        before = (edge_pv, inner_pv)
+        halo = exchange_edges(edge_pv, shape[0])
+        inner_pv, *inner_pressure = sweep(kappa, last, False, shape, before, halo, inner_coef, inner_sums)
+        edge_pv, *edge_pressure = sweep(kappa, last, True, shape, before, halo, edge_coef, edge_sums)
+    pv = (edge_pv, inner_pv)
+    halo = exchange_edges(edge_pv, shape[0])
+    (inner_new,) = push(kappa, False, pv, halo, fresh, inner_weight, inner_pressure[0], ())
+    inner = (inner_pressure[0], inner_new)
+    pressure, velocity_new = push(kappa, True, pv, halo, fresh, edge_weight, edge_pressure[0], inner)
+    return (pressure, velocity_new)
 
 
 def solution(mesh):

time: 227 us -> 258 us (1.14)
  local copies, waits for them, and re-layouts: 7.36 us -> 48.6 us
  waiting for transfers between devices: 31.2 us -> 25.5 us
    unnamed x33 -> x42, local copies, waits for them, and re-layouts: 5.66 us -> 46.6 us
    ppermute x20, waiting for transfers between devices: 21.2 us -> 15.5 us  [swap(): return lax.ppermute(value, axis, pairs + [(j, i) for i, j in pairs])]
    pallas_call x6 -> x12, Pallas kernels: 136 us -> 135 us  [the longest x2 66.9 us: setup(): call(functools.partial(setup_kernel, edge), in_specs=[vmem], out_specs=(v...]
  transfers between devices with their start and end apart: 25 -> 25, of which waited for: 15 -> 11; matrix products, arithmetic and copies ran while one was open for 0% -> 0% of each run, Pallas kernels for 0% -> 35%
where the time goes in v7:
time: 258 us; the launch traced here: 257 us
  Pallas kernels  137 us (53%)
  local copies, waits for them, and re-layouts  48.6 us (19%)
  starting transfers between devices  44.3 us (17%)
  waiting for transfers between devices  25.5 us (10%)
    pallas_call x2, Pallas kernels, setup(): call(functools.partial(setup_kernel, edge), in_specs=[vmem], out_specs=(v...  66.9 us
    unnamed x42, local copies, waits for them, and re-layouts  46.6 us
    ppermute x20, starting transfers between devices, swap(): return lax.ppermute(value, axis, pairs + [(j, i) for i, j in pairs])  42.3 us
    pallas_call x2, Pallas kernels, first_sweep(): call(functools.partial(first_kernel, kappa, edge), grid=(groups,), in_spe...  33.7 us
    pallas_call x6, Pallas kernels, sweep(): call(functools.partial(sweep_kernel, kappa, last, edge, rows, cols, len(a...  20 us
    ppermute x20, waiting for transfers between devices, swap(): return lax.ppermute(value, axis, pairs + [(j, i) for i, j in pairs])  15.5 us
    pallas_call x2, Pallas kernels, push(): call(functools.partial(push_kernel, kappa, edge, len(args)), grid=(groups...  14.5 us
    ppermute x5, waiting for transfers between devices, largest(): value = jnp.maximum(value, lax.ppermute(value, axis, pairs))  9.96 us
  transfers between devices with their start and end apart: 25, of which 11 were waited for; matrix products, arithmetic and copies ran while one was open for 0% of the time, Pallas kernels for 35%

profile of v7, /device:TPU:17, one launch (start us, length us, event | category | flops | bytes accessed | tf_op | source)
XLA Modules:
  0.0 257.0 jit_solution(16285785242443175314)
XLA Ops:
  10.6 3.4 %collective-permute-done.5 = f32[2,16,8,128]{3,2,1,0:T(8,128)S(1)} collective-permute-done((f32[2,16,8,128]{3,2,1,0:T(8,128)S(1)}, f32[2,16,8,128]{3,2,1,0:T(8,128)S(1)}, u32[]{:S(2)}, u32[]{:S(2)}) %collective-permute-start.5) | collective-permute-done | bytes 131104 | tf_op jit(solution)/shard_map/ppermute | solution.py:80
  16.2 3.0 %collective-permute-start.7 = (f32[12,2,8,128]{3,2,1,0:T(8,128)S(1)}, f32[12,2,8,128]{3,2,1,0:T(8,128)S(1)}, u32[]{:S(2)}, u32[]{:S(2)}) collective-permute-start(f32[12,2,8,128]{3,2,1,0:T(8,128)S(1)} %get-tuple-element.39), channel_id=1, source_target_pairs={{1,2},{2,1},{5,6},{6,5},{9,10},{10,9},{13,14},{14,13},{17,18},{18,... | collective-permute-start | bytes 294920 | tf_op jit(solution)/shard_map/ppermute | solution.py:80
  27.9 3.4 %collective-permute-done.4 = f32[8,128]{1,0:T(8,128)S(1)} collective-permute-done((f32[8,128]{1,0:T(8,128)S(1)}, f32[8,128]{1,0:T(8,128)S(1)}, u32[]{:S(2)}, u32[]{:S(2)}) %collective-permute-start.4) | collective-permute-done | bytes 4128 | tf_op jit(solution)/shard_map/ppermute | solution.py:145
  33.0 21.2 %setup.2 = (bf16[3,16,128,1152]{3,2,1,0:T(8,128)(2,1)S(1)}, bf16[3,16,128,1152]{3,2,1,0:T(8,128)(2,1)S(1)}) custom-call(f32[10,18,8,128]{3,2,1,0:T(8,128)S(1)} %drift.1.fresh.refs_2_.refs_6_), custom_call_target="tpu_custom_call" | custom-call | tf_op jit(solution)/shard_map/setup/pallas_call | solution.py:271
  54.1 9.3 %first_sweep.2 = (f32[3,3,16,128]{3,2,1,0:T(8,128)S(1)}, f32[3,16,128]{2,1,0:T(8,128)S(1)}) custom-call(f32[10,18,8,128]{3,2,1,0:T(8,128)S(1)} %drift.1.fresh.refs_2_.refs_6_, bf16[3,16,128,1152]{3,2,1,0:T(8,128)(2,1)S(1)} %get-tuple-element.18.coef.refs_6_, bf16[3,16,128,1152]{3,2,1,0:T(8,128)(2,1)S(1)} %get-tuple-element.19.weight.refs_7_), custom_call_target="tpu_custom_call" | custom-call | tf_op jit(solution)/shard_map/first_sweep/pallas_call | solution.py:351
  63.4 4.9 %copy-done.4 = bf16[3,16,128,1152]{3,2,1,0:T(8,128)(2,1)} copy-done((bf16[3,16,128,1152]{3,2,1,0:T(8,128)(2,1)}, bf16[3,16,128,1152]{3,2,1,0:T(8,128)(2,1)S(1)}, u32[]{:S(2)}) %copy-start.4) | copy-done | bytes 14155800
  74.0 6.2 %collective-permute-start.12 = (f32[10,128]{1,0:T(8,128)S(1)}, f32[10,128]{1,0:T(8,128)S(1)}, u32[]{:S(2)}, u32[]{:S(2)}) collective-permute-start(f32[10,128]{1,0:T(8,128)S(1)} %get-tuple-element.96), channel_id=1, source_target_pairs={{0,1},{2,3},{1,0},{3,2},{4,5},{6,7},{5,4},{7,6},{8,9},{10,11},{9,8... | collective-permute-start | bytes 15368 | tf_op jit(solution)/shard_map/ppermute | solution.py:80
  82.7 45.8 %setup.3 = (bf16[6,14,128,1152]{3,2,1,0:T(8,128)(2,1)S(1)}, bf16[6,14,128,1152]{3,2,1,0:T(8,128)(2,1)}) custom-call(f32[10,18,8,128]{3,2,1,0:T(8,128)S(1)} %drift.1.fresh.refs_2_.refs_6_), custom_call_target="tpu_custom_call" | custom-call | tf_op jit(solution)/shard_map/setup/pallas_call | solution.py:271
  128.5 24.4 %first_sweep.3 = (f32[3,6,14,128]{3,2,1,0:T(8,128)S(1)}, f32[6,14,128]{2,1,0:T(8,128)S(1)}) custom-call(f32[10,18,8,128]{3,2,1,0:T(8,128)S(1)} %drift.1.fresh.refs_2_.refs_6_, bf16[6,14,128,1152]{3,2,1,0:T(8,128)(2,1)S(1)} %get-tuple-element.21.coef.refs_2_, bf16[6,14,128,1152]{3,2,1,0:T(8,128)(2,1)} %get-tuple-element.22.weight.refs_3_), custom_call_target="tpu_custom_call" | custom-call | tf_op jit(solution)/shard_map/first_sweep/pallas_call | solution.py:351
  158.9 3.2 %collective-permute-done.13 = f32[16,128]{1,0:T(8,128)S(1)} collective-permute-done((f32[16,128]{1,0:T(8,128)S(1)}, f32[16,128]{1,0:T(8,128)S(1)}, u32[]{:S(2)}, u32[]{:S(2)}) %collective-permute-start.13) | collective-permute-done | bytes 8224 | tf_op jit(solution)/shard_map/ppermute | solution.py:80
  162.3 4.6 %collective-permute-start.15 = (f32[10,128]{1,0:T(8,128)S(1)}, f32[10,128]{1,0:T(8,128)S(1)}, u32[]{:S(2)}, u32[]{:S(2)}) collective-permute-start(f32[10,128]{1,0:T(8,128)S(1)} %get-tuple-element.91), channel_id=1, source_target_pairs={{1,2},{2,1},{5,6},{6,5},{9,10},{10,9},{13,14},{14,13},{17,18},{18,... | collective-permute-start | bytes 15368 | tf_op jit(solution)/shard_map/ppermute | solution.py:80
  166.9 8.0 %copy-done.1 = bf16[6,14,128,1152]{3,2,1,0:T(8,128)(2,1)S(1)} copy-done((bf16[6,14,128,1152]{3,2,1,0:T(8,128)(2,1)S(1)}, bf16[6,14,128,1152]{3,2,1,0:T(8,128)(2,1)}, u32[]{:S(2)}) %copy-start.1) | copy-done | bytes 24772632
  174.9 4.1 %sweep.7.refs_1_ = f32[6,14,128]{2,1,0:T(8,128)S(1)} custom-call(f32[3,16,128]{2,1,0:T(8,128)S(1)} %get-tuple-element.20.refs_0_, f32[6,14,128]{2,1,0:T(8,128)S(1)} %get-tuple-element.23.refs_1_, bf16[6,14,128,1152]{3,2,1,0:T(8,128)(2,1)S(1)} %copy-done.1, f32[3,6,14,128]{3,2,1,0:T(8,128)S(1)} %get-tuple-element.25.refs_3_), custom_call_target="tpu_custom_call" | custom-call | tf_op jit(solution)/shard_map/sweep/pallas_call | solution.py:417
  179.1 5.0 %copy-done.5 = bf16[3,16,128,1152]{3,2,1,0:T(8,128)(2,1)S(1)} copy-done((bf16[3,16,128,1152]{3,2,1,0:T(8,128)(2,1)S(1)}, bf16[3,16,128,1152]{3,2,1,0:T(8,128)(2,1)}, u32[]{:S(2)}) %copy-start.5) | copy-done | bytes 14155800
  192.4 3.5 %collective-permute-start.19 = (f32[10,128]{1,0:T(8,128)S(1)}, f32[10,128]{1,0:T(8,128)S(1)}, u32[]{:S(2)}, u32[]{:S(2)}) collective-permute-start(f32[10,128]{1,0:T(8,128)S(1)} %get-tuple-element.85), channel_id=1, source_target_pairs={{1,2},{2,1},{5,6},{6,5},{9,10},{10,9},{13,14},{14,13},{17,18},{18,... | collective-permute-start | bytes 15368 | tf_op jit(solution)/shard_map/ppermute | solution.py:80
  196.0 8.0 %copy-done.2 = bf16[6,14,128,1152]{3,2,1,0:T(8,128)(2,1)S(1)} copy-done((bf16[6,14,128,1152]{3,2,1,0:T(8,128)(2,1)S(1)}, bf16[6,14,128,1152]{3,2,1,0:T(8,128)(2,1)}, u32[]{:S(2)}) %copy-start.2) | copy-done | bytes 24772632
  204.0 4.1 %sweep.9.refs_1_ = f32[6,14,128]{2,1,0:T(8,128)S(1)} custom-call(f32[3,16,128]{2,1,0:T(8,128)S(1)} %sweep.6.refs_0_, f32[6,14,128]{2,1,0:T(8,128)S(1)} %sweep.7.refs_1_, bf16[6,14,128,1152]{3,2,1,0:T(8,128)(2,1)S(1)} %copy-done.2, f32[3,6,14,128]{3,2,1,0:T(8,128)S(1)} %get-tuple-element.25.refs_3_), custom_call_target="tpu_custom_call" | custom-call | tf_op jit(solution)/shard_map/sweep/pallas_call | solution.py:417
  215.1 3.2 %collective-permute-done.21 = f32[16,128]{1,0:T(8,128)S(1)} collective-permute-done((f32[16,128]{1,0:T(8,128)S(1)}, f32[16,128]{1,0:T(8,128)S(1)}, u32[]{:S(2)}, u32[]{:S(2)}) %collective-permute-start.21) | collective-permute-done | bytes 8224 | tf_op jit(solution)/shard_map/ppermute | solution.py:80
  218.5 3.6 %collective-permute-start.23 = (f32[10,128]{1,0:T(8,128)S(1)}, f32[10,128]{1,0:T(8,128)S(1)}, u32[]{:S(2)}, u32[]{:S(2)}) collective-permute-start(f32[10,128]{1,0:T(8,128)S(1)} %get-tuple-element.79), channel_id=1, source_target_pairs={{1,2},{2,1},{5,6},{6,5},{9,10},{10,9},{13,14},{14,13},{17,18},{18,... | collective-permute-start | bytes 15368 | tf_op jit(solution)/shard_map/ppermute | solution.py:80
  222.1 8.0 %copy-done.3 = bf16[6,14,128,1152]{3,2,1,0:T(8,128)(2,1)S(1)} copy-done((bf16[6,14,128,1152]{3,2,1,0:T(8,128)(2,1)S(1)}, bf16[6,14,128,1152]{3,2,1,0:T(8,128)(2,1)}, u32[]{:S(2)}) %copy-start.3) | copy-done | bytes 24772632
  230.2 4.1 %sweep.11 = (f32[6,14,128]{2,1,0:T(8,128)S(1)}, f32[6,14,128]{2,1,0:T(8,128)S(1)}) custom-call(f32[3,16,128]{2,1,0:T(8,128)S(1)} %sweep.8.refs_0_, f32[6,14,128]{2,1,0:T(8,128)S(1)} %sweep.9.refs_1_, bf16[6,14,128,1152]{3,2,1,0:T(8,128)(2,1)S(1)} %copy-done.3, f32[3,6,14,128]{3,2,1,0:T(8,128)S(1)} %get-tuple-element.25.refs_3_), custom_call_target="tpu_custom_call" | custom-call | tf_op jit(solution)/shard_map/sweep/pallas_call | solution.py:417
  234.3 8.1 %copy-done.7 = bf16[6,14,128,1152]{3,2,1,0:T(8,128)(2,1)S(1)} copy-done((bf16[6,14,128,1152]{3,2,1,0:T(8,128)(2,1)S(1)}, bf16[6,14,128,1152]{3,2,1,0:T(8,128)(2,1)}, u32[]{:S(2)}) %copy-start.7) | copy-done | bytes 24772632
  242.4 8.7 %push.2.refs_10_ = f32[2,6,14,128]{3,2,1,0:T(8,128)S(1)} custom-call(f32[3,16,128]{2,1,0:T(8,128)S(1)} %get-tuple-element.26.refs_0_, f32[6,14,128]{2,1,0:T(8,128)S(1)} %get-tuple-element.27.refs_1_, f32[10,18,8,128]{3,2,1,0:T(8,128)S(1)} %drift.1.fresh.refs_2_.refs_6_, bf16[6,14,128,1152]{3,2,1,0:T(8,128)(2,1)S(1)} %copy-done.7, ...), custom_call_target="tpu_custom_call" | custom-call | tf_op jit(solution)/shard_map/push/pallas_call | solution.py:514
  251.1 5.8 %push.3 = (f32[8,16,128]{2,1,0:T(8,128)}, f32[2,8,16,128]{3,2,1,0:T(8,128)}) custom-call(f32[3,16,128]{2,1,0:T(8,128)S(1)} %get-tuple-element.26.refs_0_, f32[6,14,128]{2,1,0:T(8,128)S(1)} %get-tuple-element.27.refs_1_, f32[16,128]{1,0:T(8,128)S(1)} %get-tuple-element.81.refs_2_, f32[16,128]{1,0:T(8,128)S(1)} %get-tuple-element.80.refs_3_, ...), custom_call_target="tpu_custom_call" | custom-call | tf_op jit(solution)/shard_map/push/pallas_call | solution.py:514
  (137 shorter events, 51.7 us)
Async XLA Ops:
  6.1 4.4 %collective-permute-start.6 = (f32[2,16,8,128]{3,2,1,0:T(8,128)S(1)}, f32[2,16,8,128]{3,2,1,0:T(8,128)S(1)}, u32[]{:S(2)}, u32[]{:S(2)}) collective-permute-start(f32[2,16,8,128]{3,2,1,0:T(8,128)S(1)} %get-tuple-element.32), channel_id=1, source_target_pairs={{0,4},{8,12},{16,20},{24,28},{4,0},{12,8},{20,16},{28,24},{1,5},{9... | collective-permute-start | bytes 393224 | tf_op jit(solution)/shard_map/ppermute | solution.py:80
  7.4 6.6 %collective-permute-start.5 = (f32[2,16,8,128]{3,2,1,0:T(8,128)S(1)}, f32[2,16,8,128]{3,2,1,0:T(8,128)S(1)}, u32[]{:S(2)}, u32[]{:S(2)}) collective-permute-start(f32[2,16,8,128]{3,2,1,0:T(8,128)S(1)} %get-tuple-element.33), channel_id=1, source_target_pairs={{4,8},{12,16},{20,24},{8,4},{16,12},{24,20},{5,9},{13,17},{21,25},... | collective-permute-start | bytes 393224 | tf_op jit(solution)/shard_map/ppermute | solution.py:80
  14.1 17.2 %collective-permute-start.8 = (f32[12,2,8,128]{3,2,1,0:T(8,128)S(1)}, f32[12,2,8,128]{3,2,1,0:T(8,128)S(1)}, u32[]{:S(2)}, u32[]{:S(2)}) collective-permute-start(f32[12,2,8,128]{3,2,1,0:T(8,128)S(1)} %get-tuple-element.38), channel_id=1, source_target_pairs={{0,1},{2,3},{1,0},{3,2},{4,5},{6,7},{5,4},{7,6},{8,9},{10,11},{9,8... | collective-permute-start | bytes 294920 | tf_op jit(solution)/shard_map/ppermute | solution.py:80
  16.2 15.0 %collective-permute-start.7 = (f32[12,2,8,128]{3,2,1,0:T(8,128)S(1)}, f32[12,2,8,128]{3,2,1,0:T(8,128)S(1)}, u32[]{:S(2)}, u32[]{:S(2)}) collective-permute-start(f32[12,2,8,128]{3,2,1,0:T(8,128)S(1)} %get-tuple-element.39), channel_id=1, source_target_pairs={{1,2},{2,1},{5,6},{6,5},{9,10},{10,9},{13,14},{14,13},{17,18},{18,... | collective-permute-start | bytes 294920 | tf_op jit(solution)/shard_map/ppermute | solution.py:80
  20.5 2.5 collective-permute-start.1
  23.0 2.5 collective-permute-start.2
  25.5 2.5 collective-permute-start.3
  27.9 3.4 %collective-permute-start.4 = (f32[8,128]{1,0:T(8,128)S(1)}, f32[8,128]{1,0:T(8,128)S(1)}, u32[]{:S(2)}, u32[]{:S(2)}) collective-permute-start(f32[8,128]{1,0:T(8,128)S(1)} %max.18), channel_id=1, source_target_pairs={{0,16},{4,20},{8,24},{12,28},{16,0},{20,4},{24,8},{28,12},{1,17},{... | collective-permute-start | bytes 12296 | tf_op jit(solution)/shard_map/ppermute | solution.py:145
  68.4 3.3 %collective-permute-start.10 = (f32[16,128]{1,0:T(8,128)S(1)}, f32[16,128]{1,0:T(8,128)S(1)}, u32[]{:S(2)}, u32[]{:S(2)}) collective-permute-start(f32[16,128]{1,0:T(8,128)S(1)} %get-tuple-element.74), channel_id=1, source_target_pairs={{0,4},{8,12},{16,20},{24,28},{4,0},{12,8},{20,16},{28,24},{1,5},{9... | collective-permute-start | bytes 24584 | tf_op jit(solution)/shard_map/ppermute | solution.py:80
  68.6 5.3 %collective-permute-start.9 = (f32[16,128]{1,0:T(8,128)S(1)}, f32[16,128]{1,0:T(8,128)S(1)}, u32[]{:S(2)}, u32[]{:S(2)}) collective-permute-start(f32[16,128]{1,0:T(8,128)S(1)} %get-tuple-element.75), channel_id=1, source_target_pairs={{4,8},{12,16},{20,24},{8,4},{16,12},{24,20},{5,9},{13,17},{21,25},... | collective-permute-start | bytes 24584 | tf_op jit(solution)/shard_map/ppermute | solution.py:80
  74.0 78.9 %collective-permute-start.12 = (f32[10,128]{1,0:T(8,128)S(1)}, f32[10,128]{1,0:T(8,128)S(1)}, u32[]{:S(2)}, u32[]{:S(2)}) collective-permute-start(f32[10,128]{1,0:T(8,128)S(1)} %get-tuple-element.96), channel_id=1, source_target_pairs={{0,1},{2,3},{1,0},{3,2},{4,5},{6,7},{5,4},{7,6},{8,9},{10,11},{9,8... | collective-permute-start | bytes 15368 | tf_op jit(solution)/shard_map/ppermute | solution.py:80
  80.3 72.6 %collective-permute-start.11 = (f32[10,128]{1,0:T(8,128)S(1)}, f32[10,128]{1,0:T(8,128)S(1)}, u32[]{:S(2)}, u32[]{:S(2)}) collective-permute-start(f32[10,128]{1,0:T(8,128)S(1)} %get-tuple-element.97), channel_id=1, source_target_pairs={{1,2},{2,1},{5,6},{6,5},{9,10},{10,9},{13,14},{14,13},{17,18},{18,... | collective-permute-start | bytes 15368 | tf_op jit(solution)/shard_map/ppermute | solution.py:80
  155.5 3.3 %collective-permute-start.14 = (f32[16,128]{1,0:T(8,128)S(1)}, f32[16,128]{1,0:T(8,128)S(1)}, u32[]{:S(2)}, u32[]{:S(2)}) collective-permute-start(f32[16,128]{1,0:T(8,128)S(1)} %get-tuple-element.66), channel_id=1, source_target_pairs={{0,4},{8,12},{16,20},{24,28},{4,0},{12,8},{20,16},{28,24},{1,5},{9... | collective-permute-start | bytes 24584 | tf_op jit(solution)/shard_map/ppermute | solution.py:80
  156.8 5.3 %collective-permute-start.13 = (f32[16,128]{1,0:T(8,128)S(1)}, f32[16,128]{1,0:T(8,128)S(1)}, u32[]{:S(2)}, u32[]{:S(2)}) collective-permute-start(f32[16,128]{1,0:T(8,128)S(1)} %get-tuple-element.67), channel_id=1, source_target_pairs={{4,8},{12,16},{20,24},{8,4},{16,12},{24,20},{5,9},{13,17},{21,25},... | collective-permute-start | bytes 24584 | tf_op jit(solution)/shard_map/ppermute | solution.py:80
  162.2 16.9 %collective-permute-start.16 = (f32[10,128]{1,0:T(8,128)S(1)}, f32[10,128]{1,0:T(8,128)S(1)}, u32[]{:S(2)}, u32[]{:S(2)}) collective-permute-start(f32[10,128]{1,0:T(8,128)S(1)} %get-tuple-element.90), channel_id=1, source_target_pairs={{0,1},{2,3},{1,0},{3,2},{4,5},{6,7},{5,4},{7,6},{8,9},{10,11},{9,8... | collective-permute-start | bytes 15368 | tf_op jit(solution)/shard_map/ppermute | solution.py:80
  162.3 16.8 %collective-permute-start.15 = (f32[10,128]{1,0:T(8,128)S(1)}, f32[10,128]{1,0:T(8,128)S(1)}, u32[]{:S(2)}, u32[]{:S(2)}) collective-permute-start(f32[10,128]{1,0:T(8,128)S(1)} %get-tuple-element.91), channel_id=1, source_target_pairs={{1,2},{2,1},{5,6},{6,5},{9,10},{10,9},{13,14},{14,13},{17,18},{18,... | collective-permute-start | bytes 15368 | tf_op jit(solution)/shard_map/ppermute | solution.py:80
  186.6 3.3 %collective-permute-start.18 = (f32[16,128]{1,0:T(8,128)S(1)}, f32[16,128]{1,0:T(8,128)S(1)}, u32[]{:S(2)}, u32[]{:S(2)}) collective-permute-start(f32[16,128]{1,0:T(8,128)S(1)} %get-tuple-element.58), channel_id=1, source_target_pairs={{0,4},{8,12},{16,20},{24,28},{4,0},{12,8},{20,16},{28,24},{1,5},{9... | collective-permute-start | bytes 24584 | tf_op jit(solution)/shard_map/ppermute | solution.py:80
  187.0 5.3 %collective-permute-start.17 = (f32[16,128]{1,0:T(8,128)S(1)}, f32[16,128]{1,0:T(8,128)S(1)}, u32[]{:S(2)}, u32[]{:S(2)}) collective-permute-start(f32[16,128]{1,0:T(8,128)S(1)} %get-tuple-element.59), channel_id=1, source_target_pairs={{4,8},{12,16},{20,24},{8,4},{16,12},{24,20},{5,9},{13,17},{21,25},... | collective-permute-start | bytes 24584 | tf_op jit(solution)/shard_map/ppermute | solution.py:80
  192.4 15.8 %collective-permute-start.20 = (f32[10,128]{1,0:T(8,128)S(1)}, f32[10,128]{1,0:T(8,128)S(1)}, u32[]{:S(2)}, u32[]{:S(2)}) collective-permute-start(f32[10,128]{1,0:T(8,128)S(1)} %get-tuple-element.84), channel_id=1, source_target_pairs={{0,1},{2,3},{1,0},{3,2},{4,5},{6,7},{5,4},{7,6},{8,9},{10,11},{9,8... | collective-permute-start | bytes 15368 | tf_op jit(solution)/shard_map/ppermute | solution.py:80
  192.4 15.7 %collective-permute-start.19 = (f32[10,128]{1,0:T(8,128)S(1)}, f32[10,128]{1,0:T(8,128)S(1)}, u32[]{:S(2)}, u32[]{:S(2)}) collective-permute-start(f32[10,128]{1,0:T(8,128)S(1)} %get-tuple-element.85), channel_id=1, source_target_pairs={{1,2},{2,1},{5,6},{6,5},{9,10},{10,9},{13,14},{14,13},{17,18},{18,... | collective-permute-start | bytes 15368 | tf_op jit(solution)/shard_map/ppermute | solution.py:80
  211.7 3.3 %collective-permute-start.22 = (f32[16,128]{1,0:T(8,128)S(1)}, f32[16,128]{1,0:T(8,128)S(1)}, u32[]{:S(2)}, u32[]{:S(2)}) collective-permute-start(f32[16,128]{1,0:T(8,128)S(1)} %get-tuple-element.50), channel_id=1, source_target_pairs={{0,4},{8,12},{16,20},{24,28},{4,0},{12,8},{20,16},{28,24},{1,5},{9... | collective-permute-start | bytes 24584 | tf_op jit(solution)/shard_map/ppermute | solution.py:80
  213.0 5.3 %collective-permute-start.21 = (f32[16,128]{1,0:T(8,128)S(1)}, f32[16,128]{1,0:T(8,128)S(1)}, u32[]{:S(2)}, u32[]{:S(2)}) collective-permute-start(f32[16,128]{1,0:T(8,128)S(1)} %get-tuple-element.51), channel_id=1, source_target_pairs={{4,8},{12,16},{20,24},{8,4},{16,12},{24,20},{5,9},{13,17},{21,25},... | collective-permute-start | bytes 24584 | tf_op jit(solution)/shard_map/ppermute | solution.py:80
  218.4 32.7 %collective-permute-start.24 = (f32[10,128]{1,0:T(8,128)S(1)}, f32[10,128]{1,0:T(8,128)S(1)}, u32[]{:S(2)}, u32[]{:S(2)}) collective-permute-start(f32[10,128]{1,0:T(8,128)S(1)} %get-tuple-element.78), channel_id=1, source_target_pairs={{0,1},{2,3},{1,0},{3,2},{4,5},{6,7},{5,4},{7,6},{8,9},{10,11},{9,8... | collective-permute-start | bytes 15368 | tf_op jit(solution)/shard_map/ppermute | solution.py:80
  218.5 32.6 %collective-permute-start.23 = (f32[10,128]{1,0:T(8,128)S(1)}, f32[10,128]{1,0:T(8,128)S(1)}, u32[]{:S(2)}, u32[]{:S(2)}) collective-permute-start(f32[10,128]{1,0:T(8,128)S(1)} %get-tuple-element.79), channel_id=1, source_target_pairs={{1,2},{2,1},{5,6},{6,5},{9,10},{10,9},{13,14},{14,13},{17,18},{18,... | collective-permute-start | bytes 15368 | tf_op jit(solution)/shard_map/ppermute | solution.py:80
  (22 other events, 288.9 us)

commit v8 on v7

--- a/solution.py
+++ b/solution.py
@@ -11,8 +11,8 @@
 CFL = 0.25
 SPEED_EPS = 1e-06
 SOFT = 0.01
-CHUNK = 64
-VMEM_LIMIT = 20 * 1024 * 1024
+CHUNK = 128
+VMEM_LIMIT = 16 * 1024 * 1024
 
 X, Y, U, V, VOL, PRES, CODE = range(7)
 
@@ -21,6 +21,14 @@
     return pl.pallas_call(
         kernel, compiler_params=pltpu.CompilerParams(vmem_limit_bytes=VMEM_LIMIT), **kwargs
     )
+
+
+def in_hbm(array):
+    return pltpu.with_memory_space_constraint(array, pltpu.HBM)
+
+
+def once(array):
+    return pl.BlockSpec(array.shape, lambda group: (0,) * array.ndim)
 
 
 def row_index(width):
@@ -71,9 +79,8 @@
     )(position, velocity, volume, pressure, fill[:, :, None], code[:, :, None])
 
 
-def neighbours(axis, low, high):
+def neighbours(axis, even, low, high):
     devices = lax.axis_size(axis)
-    even = lax.axis_index(axis) % 2 == 0
 
     def swap(value, first):
         pairs = [(i, i + 1) for i in range(first, devices - 1, 2)]
@@ -84,25 +91,27 @@
     return jnp.where(even, two, one), jnp.where(even, one, two)
 
 
-def exchange_old(shard, depth):
-    above, below = neighbours("gx", shard[:depth], shard[-depth:])
+def exchange_old(even, shard, depth):
+    above, below = neighbours("gx", even[0], shard[:depth], shard[-depth:])
     low = jnp.concatenate([above[:, :depth], shard[:, :depth], below[:, :depth]], axis=0)
     high = jnp.concatenate([above[:, -depth:], shard[:, -depth:], below[:, -depth:]], axis=0)
-    left, right = neighbours("gy", low, high)
+    left, right = neighbours("gy", even[1], low, high)
     return above, below, left, right
 
 
-def exchange_edges(edge, rows):
-    above, below = neighbours("gx", edge[0], edge[1])
-    half = edge.shape[1] // 2
-    low = jnp.concatenate([above[:1], edge[0, :1], edge[2, : rows - 2], edge[1, :1], below[:1]], axis=0)
-    high = jnp.concatenate([above[-1:], edge[0, -1:], edge[2, half : half + rows - 2], edge[1, -1:], below[-1:]], axis=0)
-    left, right = neighbours("gy", low, high)
-    return above, below, left, right
+def exchange_edges(even, edge, left, right):
+    above, below = neighbours("gx", even[0], edge[0][None], edge[1][None])
+    low = jnp.concatenate([above[:, :1], left, below[:, :1]], axis=0)
+    high = jnp.concatenate([above[:, -1:], right, below[:, -1:]], axis=0)
+    return above, below, *neighbours("gy", even[1], low, high)
 
 
 def groups_of(edge, rows, cols):
     return (3, cols) if edge else (rows - 2, cols - 2)
+
+
+def first_of(edge, rows, cols):
+    return 0 if edge else 3 * cols
 
 
 def place_of(edge, group, index, rows, cols):
@@ -126,12 +135,21 @@
         out[at + row, at + 1 : at + cols - 1] = inner[row - 1]
 
 
+def write_sides(left, right, edge):
+    rows, half = left.shape[0], edge.shape[1] // 2
+    for out, corner, first in ((left, 0, 0), (right, 2 * half - 1, half)):
+        out[0] = edge[0, corner : corner + 1]
+        out[rows - 1] = edge[1, corner : corner + 1]
+        for row in range(1, rows - 1):
+            out[row] = edge[2, first + row - 1 : first + row]
+
+
 def frame(out, above, below, left, right, rows, cols):
-    out[0, 1 : cols + 1] = above[...]
-    out[rows + 1, 1 : cols + 1] = below[...]
+    out[0, 1 : cols + 1] = above[0]
+    out[rows + 1, 1 : cols + 1] = below[0]
     for row in range(rows + 2):
-        out[row, 0:1] = left[row : row + 1]
-        out[row, cols + 1 : cols + 2] = right[row : row + 1]
+        out[row, 0:1] = left[row]
+        out[row, cols + 1 : cols + 2] = right[row]
 
 
 def largest(value):
@@ -155,7 +173,7 @@
     out[:, depth + cols :] = right[...]
 
 
-def drift_kernel(top, center, above, below, left, right, fresh, old):
+def drift_kernel(top, center, above, below, left, right, out, fresh, old):
     rows, cols, _, width = fresh.shape
     assemble(old, center, above, below, left, right, 2)
     step = CFL / (jnp.max(top[...]) + SPEED_EPS)
@@ -175,14 +193,16 @@
         return carry
 
     lax.fori_loop(0, rows, one_row, 0)
+    pltpu.sync_copy(fresh, out)
 
 
 def drift(top, center, above, below, left, right):
     rows, cols, _, width = center.shape
     return call(
         drift_kernel,
-        out_shape=pltpu.VMEM((rows + 2, cols + 2, 8, width), jnp.float32),
-        scratch_shapes=[pltpu.VMEM((rows + 4, cols + 4, 8, width), jnp.float32)],
+        out_specs=pl.BlockSpec(memory_space=pltpu.HBM),
+        out_shape=pltpu.HBM((rows + 2, cols + 2, 8, width), jnp.float32),
+        scratch_shapes=[pltpu.VMEM((rows + 2, cols + 2, 8, width), jnp.float32), pltpu.VMEM((rows + 4, cols + 4, 8, width), jnp.float32)],
         name="drift",
     )(top, center, above, below, left, right)
 
@@ -191,9 +211,16 @@
     return lax.dot_general(left, right, (((1,), (1,)), ((), ())), preferred_element_type=jnp.float32)
 
 
-def setup_kernel(edge, fresh, coef, weight, xcol, ycol, out_a, out_b, sem):
-    groups, size, width, _ = coef.shape
+def setup_kernel(source, coef, edge_weight, inner_weight, fresh, xcol, ycol, out_a, out_b, sem):
+    pltpu.sync_copy(source, fresh)
+    for edge, weight in ((True, edge_weight), (False, inner_weight)):
+        setup_list(edge, fresh, coef, weight, xcol, ycol, out_a, out_b, sem)
+
+
+def setup_list(edge, fresh, coef, weight, xcol, ycol, out_a, out_b, sem):
+    groups, size, width, _ = weight.shape
     rows, cols = fresh.shape[0] - 2, fresh.shape[1] - 2
+    base = first_of(edge, rows, cols)
 
     def place(bin_id):
         return place_of(edge, bin_id // size, lax.rem(bin_id, size), rows, cols)
@@ -206,7 +233,7 @@
 
     def blocks(bin_id, slot, out):
         row, col = place(bin_id)
-        values = coef.at[bin_id // size, lax.rem(bin_id, size)]
+        values = coef.at[base + bin_id]
         around = [fresh[row + k // 3, col + k % 3] for k in range(9)]
         xj = [jnp.broadcast_to(around[k][X : X + 1] + (k // 3 - 1.0), (8, width)) for k in range(9)]
         yj = [jnp.broadcast_to(around[k][Y : Y + 1] + (k % 3 - 1.0), (8, width)) for k in range(9)]
@@ -264,19 +291,21 @@
     copy_out(count - 1, out_b, 1).wait()
 
 
-def setup(edge, fresh):
+def setup(fresh):
     rows, cols, _, width = fresh.shape
-    groups, size = groups_of(edge, rows - 2, cols - 2)
-    vmem = pl.BlockSpec(memory_space=pltpu.VMEM)
+    edge, inner = (groups_of(kind, rows - 2, cols - 2) for kind in (True, False))
+    vmem, hbm = pl.BlockSpec(memory_space=pltpu.VMEM), pl.BlockSpec(memory_space=pltpu.HBM)
     return call(
-        functools.partial(setup_kernel, edge),
-        in_specs=[vmem],
-        out_specs=(vmem, pl.BlockSpec(memory_space=pltpu.HBM)),
+        setup_kernel,
+        in_specs=[hbm],
+        out_specs=(vmem, hbm, hbm),
         out_shape=(
-            pltpu.VMEM((groups, size, width, 9 * width), jnp.bfloat16),
-            jax.ShapeDtypeStruct((groups, size, width, 9 * width), jnp.bfloat16),
+            pltpu.VMEM((edge[0] * edge[1] + inner[0] * inner[1], width, 9 * width), jnp.bfloat16),
+            pltpu.HBM((*edge, width, 9 * width), jnp.bfloat16),
+            pltpu.HBM((*inner, width, 9 * width), jnp.bfloat16),
         ),
         scratch_shapes=[
+            pltpu.VMEM(fresh.shape, jnp.float32),
             pltpu.VMEM((2, width, width), jnp.float32),
             pltpu.VMEM((2, width, width), jnp.float32),
             pltpu.VMEM((width, 9 * width), jnp.bfloat16),
@@ -284,10 +313,11 @@
             pltpu.SemaphoreType.DMA((2,)),
         ],
         name="setup",
-    )(fresh)
-
-
-def first_kernel(kappa, edge, fresh, coef, weight, sums, pv, feat):
+    )(in_hbm(fresh))
+
+
+def first_kernel(kappa, edge, fresh, coef, weight, sums, pv, *rest):
+    feat = rest[-1]
     group = pl.program_id(0)
     size, width, _ = weight.shape
 
@@ -312,6 +342,7 @@
 
         lax.fori_loop(0, fresh.shape[0], one_row, 0)
 
+    base = first_of(edge, fresh.shape[0] - 2, fresh.shape[1] - 2)
     outs = ([], [], [], [])
     for index in range(size):
         row, col = place_of(edge, group, index, fresh.shape[0] - 2, fresh.shape[1] - 2)
@@ -326,7 +357,7 @@
             around.append(split(features))
         around = jnp.concatenate(around, axis=1)
         total_w = dot_nt(weight[index], around)
-        total_c = dot_nt(coef[group, index], around)
+        total_c = dot_nt(coef[base + group * size + index], around)
         total_w = (total_w[:, :8] + total_w[:, 8:]).T
         total_c = (total_c[:, :8] + total_c[:, 8:]).T
         tile = fresh[row + 1, col + 1]
@@ -342,6 +373,11 @@
     for place in range(3):
         sums[place, group] = jnp.concatenate(outs[place], axis=0)
     pv[group] = jnp.concatenate(outs[3], axis=0)
+    if edge:
+
+        @pl.when(group == 2)
+        def _():
+            write_sides(*rest[:2], pv)
 
 
 def first_sweep(kappa, edge, fresh, coef, weight):
@@ -351,23 +387,26 @@
     return call(
         functools.partial(first_kernel, kappa, edge),
         grid=(groups,),
-        in_specs=[vmem, vmem, pl.BlockSpec((None, size, width, deep), lambda group: (group, 0, 0, 0))],
-        out_specs=(vmem, vmem),
-        out_shape=(
+        in_specs=[once(fresh), vmem, pl.BlockSpec((None, size, width, deep), lambda group: (group, 0, 0, 0))],
+        out_specs=[vmem] * (4 if edge else 2),
+        out_shape=[
             pltpu.VMEM((3, groups, size, width), jnp.float32),
             pltpu.VMEM((groups, size, width), jnp.float32),
-        ),
+        ]
+        + [pltpu.VMEM((rows - 2, 1, width), jnp.float32)] * (2 if edge else 0),
         scratch_shapes=[pltpu.VMEM((rows, cols, 3, 8, width), jnp.float32)],
         name="first_sweep",
-    )(fresh, pltpu.with_memory_space_constraint(coef, pltpu.VMEM), weight)
+    )(in_hbm(fresh), pltpu.with_memory_space_constraint(coef, pltpu.VMEM), in_hbm(weight))
 
 
 def sweep_kernel(kappa, last, edge, rows, cols, count, *refs):
     before_edge, before_inner, *halo = refs[: count - 2]
     coef, sums = refs[count - 2 : count]
-    pv, *pressure = refs[count:-2]
+    pv, *rest = refs[count:-2]
+    pressure = rest[-1] if last else None
     ext, tiles = refs[-2:]
-    groups, size, width, _ = coef.shape
+    groups, size, width = pv.shape
+    base = first_of(edge, rows, cols)
     join(ext, 1, before_edge, before_inner, rows, cols)
     if edge:
         frame(ext, *halo, rows, cols)
@@ -392,7 +431,7 @@
             for part in range(width // 16):
                 total = None
                 for k in range(9):
-                    term = coef[group, index, pl.ds(part * 16, 16), pl.ds(k * width, width)] * around[k]
+                    term = coef[base + group * size + index, pl.ds(part * 16, 16), pl.ds(k * width, width)] * around[k]
                     total = term if total is None else total + term
                 parts.append(total)
             totals.append(dot_nt(ones, jnp.concatenate(parts, axis=0))[0:1])
@@ -401,24 +440,27 @@
         vol = sums[2, group]
         pv[group] = value * vol
         if last:
-            pressure[0][group] = jnp.where(vol > 0.0, value, 0.0)
+            pressure[group] = jnp.where(vol > 0.0, value, 0.0)
         return carry
 
     lax.fori_loop(0, groups, one_group, 0)
+    if edge:
+        write_sides(*rest[:2], pv)
 
 
 def sweep(kappa, last, edge, shape, pv, halo, coef, sums):
     rows, cols, width = shape
-    groups, size = coef.shape[:2]
+    groups, size = groups_of(edge, rows, cols)
     vmem = pl.BlockSpec(memory_space=pltpu.VMEM)
     out = pltpu.VMEM((groups, size, width), jnp.float32)
-    outs = 2 if last else 1
+    side = pltpu.VMEM((rows, 1, width), jnp.float32)
+    outs = [out] + [side] * (2 if edge else 0) + [out] * (1 if last else 0)
     args = (*pv, *(halo if edge else ()), pltpu.with_memory_space_constraint(coef, pltpu.VMEM), sums)
     return call(
         functools.partial(sweep_kernel, kappa, last, edge, rows, cols, len(args)),
         in_specs=[vmem] * len(args),
-        out_specs=[vmem] * outs,
-        out_shape=[out] * outs,
+        out_specs=[vmem] * len(outs),
+        out_shape=outs,
         scratch_shapes=[
             pltpu.VMEM((rows + 2, cols + 2, width), jnp.float32),
             pltpu.VMEM((rows + 2, cols + 2, 16, width), jnp.bfloat16),
@@ -499,8 +541,10 @@
     groups, size, width, deep = weight.shape
     rows, cols = fresh.shape[:2]
     vmem = pl.BlockSpec(memory_space=pltpu.VMEM)
-    args = (*pv, *(halo if edge else ()), fresh, weight, pressure, *(inner if edge else ()))
+    weight = in_hbm(weight)
+    args = (*pv, *(halo if edge else ()), in_hbm(fresh), weight, pressure, *(inner if edge else ()))
     specs = [vmem] * len(args)
+    specs[len(pv) + (len(halo) if edge else 0)] = once(fresh)
     specs[len(pv) + (len(halo) if edge else 0) + 1] = pl.BlockSpec(
         (None, size, width, deep), lambda group: (group, 0, 0, 0)
     )
@@ -529,21 +573,23 @@
 def local(position, velocity, volume, pressure_prev, fill, drift_from):
     shape = volume.shape
     kappa = 1.0 / shape[2]
+    even = [lax.axis_index(axis) % 2 == 0 for axis in ("gx", "gy")]
+    position, even = lax.optimization_barrier((position, even))
     old, top = prepare(position, velocity, volume, pressure_prev, fill, drift_from)
     top = largest(top)
-    fresh = drift(top, old, *exchange_old(old, 2))
-    edge_coef, edge_weight = setup(True, fresh)
-    edge_sums, edge_pv = first_sweep(kappa, True, fresh, edge_coef, edge_weight)
-    inner_coef, inner_weight = setup(False, fresh)
-    inner_sums, inner_pv = first_sweep(kappa, False, fresh, inner_coef, inner_weight)
+    fresh = drift(top, old, *exchange_old(even, old, 2))
+    coef, edge_weight, inner_weight = setup(fresh)
+    edge_sums, edge_pv, *sides = first_sweep(kappa, True, fresh, coef, edge_weight)
+    inner_sums, inner_pv = first_sweep(kappa, False, fresh, coef, inner_weight)
     for step in range(1, SWEEPS):
         last = step == SWEEPS - 1
         before = (edge_pv, inner_pv)
-        halo = exchange_edges(edge_pv, shape[0])
-        inner_pv, *inner_pressure = sweep(kappa, last, False, shape, before, halo, inner_coef, inner_sums)
-        edge_pv, *edge_pressure = sweep(kappa, last, True, shape, before, halo, edge_coef, edge_sums)
+        halo = exchange_edges(even, edge_pv, *sides)
+        inner_pv, *inner_pressure = sweep(kappa, last, False, shape, before, halo, coef, inner_sums)
+        edge_pv, *rest = sweep(kappa, last, True, shape, before, halo, coef, edge_sums)
+        sides, edge_pressure = rest[:2], rest[2:]
     pv = (edge_pv, inner_pv)
-    halo = exchange_edges(edge_pv, shape[0])
+    halo = exchange_edges(even, edge_pv, *sides)
     (inner_new,) = push(kappa, False, pv, halo, fresh, inner_weight, inner_pressure[0], ())
     inner = (inner_pressure[0], inner_new)
     pressure, velocity_new = push(kappa, True, pv, halo, fresh, edge_weight, edge_pressure[0], inner)

time: 258 us -> 225 us (0.87)
  local copies, waits for them, and re-layouts: 48.6 us -> 5.15 us
  Pallas kernels: 137 us -> 148 us
    unnamed x42 -> x8, local copies, waits for them, and re-layouts: 46.6 us -> 3.49 us
    pallas_call x2, Pallas kernels: 14.5 us -> 22.2 us  [push(): call(functools.partial(push_kernel, kappa, edge, len(args)), grid=(groups...]
    pallas_call x3 -> x2, Pallas kernels: 68.6 us -> 76 us  [the longest x1 73.4 us: setup(): call(setup_kernel, in_specs=[hbm], out_specs=(vmem, hbm, hbm), out_shape=...]
    pallas_call x2, Pallas kernels: 33.7 us -> 29.8 us  [first_sweep(): call(functools.partial(first_kernel, kappa, edge), grid=(groups,), in_spe...]
  transfers between devices with their start and end apart: 25 -> 25, of which waited for: 11 -> 11; matrix products, arithmetic and copies ran while one was open for 0% -> 0% of each run, Pallas kernels for 35% -> 19%
where the time goes in v8:
time: 225 us
  Pallas kernels  148 us (66%)
  starting transfers between devices  44.4 us (20%)
  waiting for transfers between devices  25.5 us (11%)
  local copies, waits for them, and re-layouts  5.15 us (2%)
    pallas_call x1, Pallas kernels, setup(): call(setup_kernel, in_specs=[hbm], out_specs=(vmem, hbm, hbm), out_shape=...  73.4 us
    ppermute x20, starting transfers between devices, swap(): return lax.ppermute(value, axis, pairs + [(j, i) for i, j in pairs])  42.4 us
    pallas_call x2, Pallas kernels, first_sweep(): call(functools.partial(first_kernel, kappa, edge), grid=(groups,), in_spe...  29.8 us
    pallas_call x2, Pallas kernels, push(): call(functools.partial(push_kernel, kappa, edge, len(args)), grid=(groups...  22.2 us
    pallas_call x6, Pallas kernels, sweep(): call(functools.partial(sweep_kernel, kappa, last, edge, rows, cols, len(a...  19.9 us
    ppermute x20, waiting for transfers between devices, swap(): return lax.ppermute(value, axis, pairs + [(j, i) for i, j in pairs])  15.6 us
    ppermute x5, waiting for transfers between devices, largest(): value = jnp.maximum(value, lax.ppermute(value, axis, pairs))  9.96 us
  transfers between devices with their start and end apart: 25, of which 11 were waited for; matrix products, arithmetic and copies ran while one was open for 0% of the time, Pallas kernels for 19%

profile of v8, /device:TPU:17, one launch (start us, length us, event | category | flops | bytes accessed | tf_op | source)
XLA Modules:
  0.0 224.6 jit_solution(17325351474502644022)
XLA Ops:
  10.6 3.4 %collective-permute-done.5 = f32[2,16,8,128]{3,2,1,0:T(8,128)S(1)} collective-permute-done((f32[2,16,8,128]{3,2,1,0:T(8,128)S(1)}, f32[2,16,8,128]{3,2,1,0:T(8,128)S(1)}, u32[]{:S(2)}, u32[]{:S(2)}) %collective-permute-start.5) | collective-permute-done | bytes 131104 | tf_op jit(solution)/shard_map/ppermute | solution.py:87
  16.2 3.0 %collective-permute-start.7 = (f32[12,2,8,128]{3,2,1,0:T(8,128)S(1)}, f32[12,2,8,128]{3,2,1,0:T(8,128)S(1)}, u32[]{:S(2)}, u32[]{:S(2)}) collective-permute-start(f32[12,2,8,128]{3,2,1,0:T(8,128)S(1)} %get-tuple-element.63), channel_id=1, source_target_pairs={{1,2},{2,1},{5,6},{6,5},{9,10},{10,9},{13,14},{14,13},{17,18},{18,... | collective-permute-start | bytes 294920 | tf_op jit(solution)/shard_map/ppermute | solution.py:87
  27.9 3.4 %collective-permute-done.4 = f32[8,128]{1,0:T(8,128)S(1)} collective-permute-done((f32[8,128]{1,0:T(8,128)S(1)}, f32[8,128]{1,0:T(8,128)S(1)}, u32[]{:S(2)}, u32[]{:S(2)}) %collective-permute-start.4) | collective-permute-done | bytes 4128 | tf_op jit(solution)/shard_map/ppermute | solution.py:163
  31.3 2.6 %drift.1.source.fresh.refs_2_.refs_6_ = f32[10,18,8,128]{3,2,1,0:T(8,128)} custom-call(f32[8,128]{1,0:T(8,128)S(1)} %max.19.top, f32[8,16,8,128]{3,2,1,0:T(8,128)S(1)} %get-tuple-element.30.center, f32[2,16,8,128]{3,2,1,0:T(8,128)S(1)} %get-tuple-element.59.above, f32[2,16,8,128]{3,2,1,0:T(8,128)S(1)} %get-tuple-element.58.below, ...), custom_call_target="tpu_custom_call" | custom-call | tf_op jit(solution)/shard_map/drift/pallas_call | solution.py:201
  33.9 73.4 %setup.1 = (bf16[132,128,1152]{2,1,0:T(8,128)(2,1)S(1)}, bf16[3,16,128,1152]{3,2,1,0:T(8,128)(2,1)}, bf16[6,14,128,1152]{3,2,1,0:T(8,128)(2,1)}) custom-call(f32[10,18,8,128]{3,2,1,0:T(8,128)} %drift.1.source.fresh.refs_2_.refs_6_), custom_call_target="tpu_custom_call" | custom-call | tf_op jit(solution)/shard_map/setup/pallas_call | solution.py:298
  107.3 11.8 %first_sweep.2 = (f32[3,3,16,128]{3,2,1,0:T(8,128)S(1)}, f32[3,16,128]{2,1,0:T(8,128)S(1)}, f32[8,1,128]{2,1,0:T(1,128)S(1)}, f32[8,1,128]{2,1,0:T(1,128)S(1)}) custom-call(f32[10,18,8,128]{3,2,1,0:T(8,128)} %drift.1.source.fresh.refs_2_.refs_6_, bf16[132,128,1152]{2,1,0:T(8,128)(2,1)S(1)} %get-tuple-element.33.coef.refs_6_.refs_2_, ...), custom_call_target="tpu_custom_call" | custom-call | tf_op jit(solution)/shard_map/first_sweep/pallas_call | solution.py:387
  119.5 3.0 %collective-permute-start.9 = (f32[1,16,128]{2,1,0:T(8,128)S(1)}, f32[1,16,128]{2,1,0:T(8,128)S(1)}, u32[]{:S(2)}, u32[]{:S(2)}) collective-permute-start(f32[1,16,128]{2,1,0:T(8,128)S(1)} %get-tuple-element.75), channel_id=1, source_target_pairs={{4,8},{12,16},{20,24},{8,4},{16,12},{24,20},{5,9},{13,17},{21,25},... | collective-permute-start | bytes 24584 | tf_op jit(solution)/shard_map/ppermute | solution.py:87
  124.8 6.3 %collective-permute-start.12 = (f32[10,1,128]{2,1,0:T(1,128)S(1)}, f32[10,1,128]{2,1,0:T(1,128)S(1)}, u32[]{:S(2)}, u32[]{:S(2)}) collective-permute-start(f32[10,1,128]{2,1,0:T(1,128)S(1)} %get-tuple-element.98), channel_id=1, source_target_pairs={{0,1},{2,3},{1,0},{3,2},{4,5},{6,7},{5,4},{7,6},{8,9},{10,11},{9,8... | collective-permute-start | bytes 15368 | tf_op jit(solution)/shard_map/ppermute | solution.py:87
  131.1 2.3 %collective-permute-start.11 = (f32[10,1,128]{2,1,0:T(1,128)S(1)}, f32[10,1,128]{2,1,0:T(1,128)S(1)}, u32[]{:S(2)}, u32[]{:S(2)}) collective-permute-start(f32[10,1,128]{2,1,0:T(1,128)S(1)} %get-tuple-element.99), channel_id=1, source_target_pairs={{1,2},{2,1},{5,6},{6,5},{9,10},{10,9},{13,14},{14,13},{17,18},{18,... | collective-permute-start | bytes 15368 | tf_op jit(solution)/shard_map/ppermute | solution.py:87
  133.4 18.0 %first_sweep.3 = (f32[3,6,14,128]{3,2,1,0:T(8,128)S(1)}, f32[6,14,128]{2,1,0:T(8,128)S(1)}) custom-call(f32[10,18,8,128]{3,2,1,0:T(8,128)} %drift.1.source.fresh.refs_2_.refs_6_, bf16[132,128,1152]{2,1,0:T(8,128)(2,1)S(1)} %get-tuple-element.33.coef.refs_6_.refs_2_, bf16[6,14,128,1152]{3,2,1,0:T(8,128)(2,1)} %get-tuple-element.36.weight.refs_3_), custom_call_target="tpu_custom_call" | custom-call | tf_op jit(solution)/shard_map/first_sweep/pallas_call | solution.py:387
  151.4 2.5 %sweep.6 = (f32[3,16,128]{2,1,0:T(8,128)S(1)}, f32[8,1,128]{2,1,0:T(1,128)S(1)}, f32[8,1,128]{2,1,0:T(1,128)S(1)}) custom-call(f32[3,16,128]{2,1,0:T(8,128)S(1)} %get-tuple-element.35.refs_0_, f32[6,14,128]{2,1,0:T(8,128)S(1)} %get-tuple-element.37.refs_1_, f32[1,16,128]{2,1,0:T(8,128)S(1)} %get-tuple-element.83.refs_2_, ...), custom_call_target="tpu_custom_call" | custom-call | tf_op jit(solution)/shard_map/sweep/pallas_call | solution.py:459
  157.3 3.2 %collective-permute-done.13 = f32[1,16,128]{2,1,0:T(8,128)S(1)} collective-permute-done((f32[1,16,128]{2,1,0:T(8,128)S(1)}, f32[1,16,128]{2,1,0:T(8,128)S(1)}, u32[]{:S(2)}, u32[]{:S(2)}) %collective-permute-start.13) | collective-permute-done | bytes 8224 | tf_op jit(solution)/shard_map/ppermute | solution.py:87
  160.6 4.6 %collective-permute-start.15 = (f32[10,1,128]{2,1,0:T(1,128)S(1)}, f32[10,1,128]{2,1,0:T(1,128)S(1)}, u32[]{:S(2)}, u32[]{:S(2)}) collective-permute-start(f32[10,1,128]{2,1,0:T(1,128)S(1)} %get-tuple-element.95), channel_id=1, source_target_pairs={{1,2},{2,1},{5,6},{6,5},{9,10},{10,9},{13,14},{14,13},{17,18},{18,... | collective-permute-start | bytes 15368 | tf_op jit(solution)/shard_map/ppermute | solution.py:87
  165.3 4.1 %sweep.7.refs_1_ = f32[6,14,128]{2,1,0:T(8,128)S(1)} custom-call(f32[3,16,128]{2,1,0:T(8,128)S(1)} %get-tuple-element.35.refs_0_, f32[6,14,128]{2,1,0:T(8,128)S(1)} %get-tuple-element.37.refs_1_, bf16[132,128,1152]{2,1,0:T(8,128)(2,1)S(1)} %get-tuple-element.33.coef.refs_6_.refs_2_, f32[3,6,14,128]{3,2,1,0:T(8,128)S(1)} %get-tuple-element.42.refs_3_), custom_call_target="tpu_custom_call" | custom-call | tf_op jit(solution)/shard_map/sweep/pallas_call | solution.py:459
  169.4 2.5 %sweep.8 = (f32[3,16,128]{2,1,0:T(8,128)S(1)}, f32[8,1,128]{2,1,0:T(1,128)S(1)}, f32[8,1,128]{2,1,0:T(1,128)S(1)}) custom-call(f32[3,16,128]{2,1,0:T(8,128)S(1)} %get-tuple-element.41.refs_0_, f32[6,14,128]{2,1,0:T(8,128)S(1)} %sweep.7.refs_1_, f32[1,16,128]{2,1,0:T(8,128)S(1)} %get-tuple-element.81.refs_2_, f32[1,16,128]{2,1,0:T(8,128)S(1)} %get-tuple-element.80.refs_3_, ...), custom_call_target="tpu_custom_call" | custom-call | tf_op jit(solution)/shard_map/sweep/pallas_call | solution.py:459
  172.3 3.0 %collective-permute-start.17 = (f32[1,16,128]{2,1,0:T(8,128)S(1)}, f32[1,16,128]{2,1,0:T(8,128)S(1)}, u32[]{:S(2)}, u32[]{:S(2)}) collective-permute-start(f32[1,16,128]{2,1,0:T(8,128)S(1)} %get-tuple-element.71), channel_id=1, source_target_pairs={{4,8},{12,16},{20,24},{8,4},{16,12},{24,20},{5,9},{13,17},{21,25},... | collective-permute-start | bytes 24584 | tf_op jit(solution)/shard_map/ppermute | solution.py:87
  177.7 3.5 %collective-permute-start.19 = (f32[10,1,128]{2,1,0:T(1,128)S(1)}, f32[10,1,128]{2,1,0:T(1,128)S(1)}, u32[]{:S(2)}, u32[]{:S(2)}) collective-permute-start(f32[10,1,128]{2,1,0:T(1,128)S(1)} %get-tuple-element.91), channel_id=1, source_target_pairs={{1,2},{2,1},{5,6},{6,5},{9,10},{10,9},{13,14},{14,13},{17,18},{18,... | collective-permute-start | bytes 15368 | tf_op jit(solution)/shard_map/ppermute | solution.py:87
  181.2 4.1 %sweep.9.refs_1_ = f32[6,14,128]{2,1,0:T(8,128)S(1)} custom-call(f32[3,16,128]{2,1,0:T(8,128)S(1)} %get-tuple-element.41.refs_0_, f32[6,14,128]{2,1,0:T(8,128)S(1)} %sweep.7.refs_1_, bf16[132,128,1152]{2,1,0:T(8,128)(2,1)S(1)} %get-tuple-element.33.coef.refs_6_.refs_2_, f32[3,6,14,128]{3,2,1,0:T(8,128)S(1)} %get-tuple-element.42.refs_3_), custom_call_target="tpu_custom_call" | custom-call | tf_op jit(solution)/shard_map/sweep/pallas_call | solution.py:459
  185.4 2.5 %sweep.10 = (f32[3,16,128]{2,1,0:T(8,128)S(1)}, f32[8,1,128]{2,1,0:T(1,128)S(1)}, f32[8,1,128]{2,1,0:T(1,128)S(1)}, f32[3,16,128]{2,1,0:T(8,128)S(1)}) custom-call(f32[3,16,128]{2,1,0:T(8,128)S(1)} %get-tuple-element.45.refs_0_, f32[6,14,128]{2,1,0:T(8,128)S(1)} %sweep.9.refs_1_, f32[1,16,128]{2,1,0:T(8,128)S(1)} %get-tuple-element.79.refs_2_, ...), custom_call_target="tpu_custom_call" | custom-call | tf_op jit(solution)/shard_map/sweep/pallas_call | solution.py:459
  191.2 3.2 %collective-permute-done.21 = f32[1,16,128]{2,1,0:T(8,128)S(1)} collective-permute-done((f32[1,16,128]{2,1,0:T(8,128)S(1)}, f32[1,16,128]{2,1,0:T(8,128)S(1)}, u32[]{:S(2)}, u32[]{:S(2)}) %collective-permute-start.21) | collective-permute-done | bytes 8224 | tf_op jit(solution)/shard_map/ppermute | solution.py:87
  194.6 3.6 %collective-permute-start.23 = (f32[10,1,128]{2,1,0:T(1,128)S(1)}, f32[10,1,128]{2,1,0:T(1,128)S(1)}, u32[]{:S(2)}, u32[]{:S(2)}) collective-permute-start(f32[10,1,128]{2,1,0:T(1,128)S(1)} %get-tuple-element.87), channel_id=1, source_target_pairs={{1,2},{2,1},{5,6},{6,5},{9,10},{10,9},{13,14},{14,13},{17,18},{18,... | collective-permute-start | bytes 15368 | tf_op jit(solution)/shard_map/ppermute | solution.py:87
  198.2 4.1 %sweep.11 = (f32[6,14,128]{2,1,0:T(8,128)S(1)}, f32[6,14,128]{2,1,0:T(8,128)S(1)}) custom-call(f32[3,16,128]{2,1,0:T(8,128)S(1)} %get-tuple-element.45.refs_0_, f32[6,14,128]{2,1,0:T(8,128)S(1)} %sweep.9.refs_1_, bf16[132,128,1152]{2,1,0:T(8,128)(2,1)S(1)} %get-tuple-element.33.coef.refs_6_.refs_2_, f32[3,6,14,128]{3,2,1,0:T(8,128)S(1)} %get-tuple-element.42.refs_3_), custom_call_target="tpu_custom_call" | custom-call | tf_op jit(solution)/shard_map/sweep/pallas_call | solution.py:459
  202.3 13.0 %push.2.refs_10_ = f32[2,6,14,128]{3,2,1,0:T(8,128)S(1)} custom-call(f32[3,16,128]{2,1,0:T(8,128)S(1)} %get-tuple-element.48.refs_0_, f32[6,14,128]{2,1,0:T(8,128)S(1)} %get-tuple-element.49.refs_1_, f32[10,18,8,128]{3,2,1,0:T(8,128)} %drift.1.source.fresh.refs_2_.refs_6_, bf16[6,14,128,1152]{3,2,1,0:T(8,128)(2,1)} %get-tuple-element.36.weight.refs_3_, ...), custom_call_target="tpu_custom_call" | custom-call | tf_op jit(solution)/shard_map/push/pallas_call | solution.py:558
  215.4 9.1 %push.3 = (f32[8,16,128]{2,1,0:T(8,128)}, f32[2,8,16,128]{3,2,1,0:T(8,128)}) custom-call(f32[3,16,128]{2,1,0:T(8,128)S(1)} %get-tuple-element.48.refs_0_, f32[6,14,128]{2,1,0:T(8,128)S(1)} %get-tuple-element.49.refs_1_, f32[1,16,128]{2,1,0:T(8,128)S(1)} %get-tuple-element.77.refs_2_, f32[1,16,128]{2,1,0:T(8,128)S(1)} %get-tuple-element.76.refs_3_, ...), custom_call_target="tpu_custom_call" | custom-call | tf_op jit(solution)/shard_map/push/pallas_call | solution.py:558
  (84 shorter events, 33.0 us)
Async XLA Ops:
  6.1 4.4 %collective-permute-start.6 = (f32[2,16,8,128]{3,2,1,0:T(8,128)S(1)}, f32[2,16,8,128]{3,2,1,0:T(8,128)S(1)}, u32[]{:S(2)}, u32[]{:S(2)}) collective-permute-start(f32[2,16,8,128]{3,2,1,0:T(8,128)S(1)} %get-tuple-element.56), channel_id=1, source_target_pairs={{0,4},{8,12},{16,20},{24,28},{4,0},{12,8},{20,16},{28,24},{1,5},{9... | collective-permute-start | bytes 393224 | tf_op jit(solution)/shard_map/ppermute | solution.py:87
  7.4 6.6 %collective-permute-start.5 = (f32[2,16,8,128]{3,2,1,0:T(8,128)S(1)}, f32[2,16,8,128]{3,2,1,0:T(8,128)S(1)}, u32[]{:S(2)}, u32[]{:S(2)}) collective-permute-start(f32[2,16,8,128]{3,2,1,0:T(8,128)S(1)} %get-tuple-element.57), channel_id=1, source_target_pairs={{4,8},{12,16},{20,24},{8,4},{16,12},{24,20},{5,9},{13,17},{21,25},... | collective-permute-start | bytes 393224 | tf_op jit(solution)/shard_map/ppermute | solution.py:87
  14.1 17.2 %collective-permute-start.8 = (f32[12,2,8,128]{3,2,1,0:T(8,128)S(1)}, f32[12,2,8,128]{3,2,1,0:T(8,128)S(1)}, u32[]{:S(2)}, u32[]{:S(2)}) collective-permute-start(f32[12,2,8,128]{3,2,1,0:T(8,128)S(1)} %get-tuple-element.62), channel_id=1, source_target_pairs={{0,1},{2,3},{1,0},{3,2},{4,5},{6,7},{5,4},{7,6},{8,9},{10,11},{9,8... | collective-permute-start | bytes 294920 | tf_op jit(solution)/shard_map/ppermute | solution.py:87
  16.2 15.0 %collective-permute-start.7 = (f32[12,2,8,128]{3,2,1,0:T(8,128)S(1)}, f32[12,2,8,128]{3,2,1,0:T(8,128)S(1)}, u32[]{:S(2)}, u32[]{:S(2)}) collective-permute-start(f32[12,2,8,128]{3,2,1,0:T(8,128)S(1)} %get-tuple-element.63), channel_id=1, source_target_pairs={{1,2},{2,1},{5,6},{6,5},{9,10},{10,9},{13,14},{14,13},{17,18},{18,... | collective-permute-start | bytes 294920 | tf_op jit(solution)/shard_map/ppermute | solution.py:87
  20.5 2.5 %collective-permute-start.1 = (f32[8,128]{1,0:T(8,128)S(1)}, f32[8,128]{1,0:T(8,128)S(1)}, u32[]{:S(2)}, u32[]{:S(2)}) collective-permute-start(f32[8,128]{1,0:T(8,128)S(1)} %max.15), channel_id=1, source_target_pairs={{0,2},{1,3},{2,0},{3,1},{4,6},{5,7},{6,4},{7,5},{8,10},{9,11},{10,... | collective-permute-start | bytes 12296 | tf_op jit(solution)/shard_map/ppermute | solution.py:163
  23.0 2.5 %collective-permute-start.2 = (f32[8,128]{1,0:T(8,128)S(1)}, f32[8,128]{1,0:T(8,128)S(1)}, u32[]{:S(2)}, u32[]{:S(2)}) collective-permute-start(f32[8,128]{1,0:T(8,128)S(1)} %max.16), channel_id=1, source_target_pairs={{0,4},{4,0},{8,12},{12,8},{16,20},{20,16},{24,28},{28,24},{1,5},{5... | collective-permute-start | bytes 12296 | tf_op jit(solution)/shard_map/ppermute | solution.py:163
  25.5 2.5 %collective-permute-start.3 = (f32[8,128]{1,0:T(8,128)S(1)}, f32[8,128]{1,0:T(8,128)S(1)}, u32[]{:S(2)}, u32[]{:S(2)}) collective-permute-start(f32[8,128]{1,0:T(8,128)S(1)} %max.17), channel_id=1, source_target_pairs={{0,8},{4,12},{8,0},{12,4},{16,24},{20,28},{24,16},{28,20},{1,9},{5... | collective-permute-start | bytes 12296 | tf_op jit(solution)/shard_map/ppermute | solution.py:163
  27.9 3.4 %collective-permute-start.4 = (f32[8,128]{1,0:T(8,128)S(1)}, f32[8,128]{1,0:T(8,128)S(1)}, u32[]{:S(2)}, u32[]{:S(2)}) collective-permute-start(f32[8,128]{1,0:T(8,128)S(1)} %max.18), channel_id=1, source_target_pairs={{0,16},{4,20},{8,24},{12,28},{16,0},{20,4},{24,8},{28,12},{1,17},{... | collective-permute-start | bytes 12296 | tf_op jit(solution)/shard_map/ppermute | solution.py:163
  119.1 3.3 %collective-permute-start.10 = (f32[1,16,128]{2,1,0:T(8,128)S(1)}, f32[1,16,128]{2,1,0:T(8,128)S(1)}, u32[]{:S(2)}, u32[]{:S(2)}) collective-permute-start(f32[1,16,128]{2,1,0:T(8,128)S(1)} %get-tuple-element.74), channel_id=1, source_target_pairs={{0,4},{8,12},{16,20},{24,28},{4,0},{12,8},{20,16},{28,24},{1,5},{9... | collective-permute-start | bytes 24584 | tf_op jit(solution)/shard_map/ppermute | solution.py:87
  119.5 5.3 %collective-permute-start.9 = (f32[1,16,128]{2,1,0:T(8,128)S(1)}, f32[1,16,128]{2,1,0:T(8,128)S(1)}, u32[]{:S(2)}, u32[]{:S(2)}) collective-permute-start(f32[1,16,128]{2,1,0:T(8,128)S(1)} %get-tuple-element.75), channel_id=1, source_target_pairs={{4,8},{12,16},{20,24},{8,4},{16,12},{24,20},{5,9},{13,17},{21,25},... | collective-permute-start | bytes 24584 | tf_op jit(solution)/shard_map/ppermute | solution.py:87
  124.8 26.6 %collective-permute-start.12 = (f32[10,1,128]{2,1,0:T(1,128)S(1)}, f32[10,1,128]{2,1,0:T(1,128)S(1)}, u32[]{:S(2)}, u32[]{:S(2)}) collective-permute-start(f32[10,1,128]{2,1,0:T(1,128)S(1)} %get-tuple-element.98), channel_id=1, source_target_pairs={{0,1},{2,3},{1,0},{3,2},{4,5},{6,7},{5,4},{7,6},{8,9},{10,11},{9,8... | collective-permute-start | bytes 15368 | tf_op jit(solution)/shard_map/ppermute | solution.py:87
  131.1 20.3 %collective-permute-start.11 = (f32[10,1,128]{2,1,0:T(1,128)S(1)}, f32[10,1,128]{2,1,0:T(1,128)S(1)}, u32[]{:S(2)}, u32[]{:S(2)}) collective-permute-start(f32[10,1,128]{2,1,0:T(1,128)S(1)} %get-tuple-element.99), channel_id=1, source_target_pairs={{1,2},{2,1},{5,6},{6,5},{9,10},{10,9},{13,14},{14,13},{17,18},{18,... | collective-permute-start | bytes 15368 | tf_op jit(solution)/shard_map/ppermute | solution.py:87
  154.0 3.3 %collective-permute-start.14 = (f32[1,16,128]{2,1,0:T(8,128)S(1)}, f32[1,16,128]{2,1,0:T(8,128)S(1)}, u32[]{:S(2)}, u32[]{:S(2)}) collective-permute-start(f32[1,16,128]{2,1,0:T(8,128)S(1)} %get-tuple-element.72), channel_id=1, source_target_pairs={{0,4},{8,12},{16,20},{24,28},{4,0},{12,8},{20,16},{28,24},{1,5},{9... | collective-permute-start | bytes 24584 | tf_op jit(solution)/shard_map/ppermute | solution.py:87
  155.2 5.3 %collective-permute-start.13 = (f32[1,16,128]{2,1,0:T(8,128)S(1)}, f32[1,16,128]{2,1,0:T(8,128)S(1)}, u32[]{:S(2)}, u32[]{:S(2)}) collective-permute-start(f32[1,16,128]{2,1,0:T(8,128)S(1)} %get-tuple-element.73), channel_id=1, source_target_pairs={{4,8},{12,16},{20,24},{8,4},{16,12},{24,20},{5,9},{13,17},{21,25},... | collective-permute-start | bytes 24584 | tf_op jit(solution)/shard_map/ppermute | solution.py:87
  160.6 8.8 %collective-permute-start.16 = (f32[10,1,128]{2,1,0:T(1,128)S(1)}, f32[10,1,128]{2,1,0:T(1,128)S(1)}, u32[]{:S(2)}, u32[]{:S(2)}) collective-permute-start(f32[10,1,128]{2,1,0:T(1,128)S(1)} %get-tuple-element.94), channel_id=1, source_target_pairs={{0,1},{2,3},{1,0},{3,2},{4,5},{6,7},{5,4},{7,6},{8,9},{10,11},{9,8... | collective-permute-start | bytes 15368 | tf_op jit(solution)/shard_map/ppermute | solution.py:87
  160.6 8.8 %collective-permute-start.15 = (f32[10,1,128]{2,1,0:T(1,128)S(1)}, f32[10,1,128]{2,1,0:T(1,128)S(1)}, u32[]{:S(2)}, u32[]{:S(2)}) collective-permute-start(f32[10,1,128]{2,1,0:T(1,128)S(1)} %get-tuple-element.95), channel_id=1, source_target_pairs={{1,2},{2,1},{5,6},{6,5},{9,10},{10,9},{13,14},{14,13},{17,18},{18,... | collective-permute-start | bytes 15368 | tf_op jit(solution)/shard_map/ppermute | solution.py:87
  172.0 3.3 %collective-permute-start.18 = (f32[1,16,128]{2,1,0:T(8,128)S(1)}, f32[1,16,128]{2,1,0:T(8,128)S(1)}, u32[]{:S(2)}, u32[]{:S(2)}) collective-permute-start(f32[1,16,128]{2,1,0:T(8,128)S(1)} %get-tuple-element.70), channel_id=1, source_target_pairs={{0,4},{8,12},{16,20},{24,28},{4,0},{12,8},{20,16},{28,24},{1,5},{9... | collective-permute-start | bytes 24584 | tf_op jit(solution)/shard_map/ppermute | solution.py:87
  172.3 5.3 %collective-permute-start.17 = (f32[1,16,128]{2,1,0:T(8,128)S(1)}, f32[1,16,128]{2,1,0:T(8,128)S(1)}, u32[]{:S(2)}, u32[]{:S(2)}) collective-permute-start(f32[1,16,128]{2,1,0:T(8,128)S(1)} %get-tuple-element.71), channel_id=1, source_target_pairs={{4,8},{12,16},{20,24},{8,4},{16,12},{24,20},{5,9},{13,17},{21,25},... | collective-permute-start | bytes 24584 | tf_op jit(solution)/shard_map/ppermute | solution.py:87
  177.6 7.7 %collective-permute-start.20 = (f32[10,1,128]{2,1,0:T(1,128)S(1)}, f32[10,1,128]{2,1,0:T(1,128)S(1)}, u32[]{:S(2)}, u32[]{:S(2)}) collective-permute-start(f32[10,1,128]{2,1,0:T(1,128)S(1)} %get-tuple-element.90), channel_id=1, source_target_pairs={{0,1},{2,3},{1,0},{3,2},{4,5},{6,7},{5,4},{7,6},{8,9},{10,11},{9,8... | collective-permute-start | bytes 15368 | tf_op jit(solution)/shard_map/ppermute | solution.py:87
  177.7 7.7 %collective-permute-start.19 = (f32[10,1,128]{2,1,0:T(1,128)S(1)}, f32[10,1,128]{2,1,0:T(1,128)S(1)}, u32[]{:S(2)}, u32[]{:S(2)}) collective-permute-start(f32[10,1,128]{2,1,0:T(1,128)S(1)} %get-tuple-element.91), channel_id=1, source_target_pairs={{1,2},{2,1},{5,6},{6,5},{9,10},{10,9},{13,14},{14,13},{17,18},{18,... | collective-permute-start | bytes 15368 | tf_op jit(solution)/shard_map/ppermute | solution.py:87
  187.9 3.3 %collective-permute-start.22 = (f32[1,16,128]{2,1,0:T(8,128)S(1)}, f32[1,16,128]{2,1,0:T(8,128)S(1)}, u32[]{:S(2)}, u32[]{:S(2)}) collective-permute-start(f32[1,16,128]{2,1,0:T(8,128)S(1)} %get-tuple-element.68), channel_id=1, source_target_pairs={{0,4},{8,12},{16,20},{24,28},{4,0},{12,8},{20,16},{28,24},{1,5},{9... | collective-permute-start | bytes 24584 | tf_op jit(solution)/shard_map/ppermute | solution.py:87
  189.2 5.3 %collective-permute-start.21 = (f32[1,16,128]{2,1,0:T(8,128)S(1)}, f32[1,16,128]{2,1,0:T(8,128)S(1)}, u32[]{:S(2)}, u32[]{:S(2)}) collective-permute-start(f32[1,16,128]{2,1,0:T(8,128)S(1)} %get-tuple-element.69), channel_id=1, source_target_pairs={{4,8},{12,16},{20,24},{8,4},{16,12},{24,20},{5,9},{13,17},{21,25},... | collective-permute-start | bytes 24584 | tf_op jit(solution)/shard_map/ppermute | solution.py:87
  194.5 20.9 %collective-permute-start.24 = (f32[10,1,128]{2,1,0:T(1,128)S(1)}, f32[10,1,128]{2,1,0:T(1,128)S(1)}, u32[]{:S(2)}, u32[]{:S(2)}) collective-permute-start(f32[10,1,128]{2,1,0:T(1,128)S(1)} %get-tuple-element.86), channel_id=1, source_target_pairs={{0,1},{2,3},{1,0},{3,2},{4,5},{6,7},{5,4},{7,6},{8,9},{10,11},{9,8... | collective-permute-start | bytes 15368 | tf_op jit(solution)/shard_map/ppermute | solution.py:87
  194.6 20.8 %collective-permute-start.23 = (f32[10,1,128]{2,1,0:T(1,128)S(1)}, f32[10,1,128]{2,1,0:T(1,128)S(1)}, u32[]{:S(2)}, u32[]{:S(2)}) collective-permute-start(f32[10,1,128]{2,1,0:T(1,128)S(1)} %get-tuple-element.87), channel_id=1, source_target_pairs={{1,2},{2,1},{5,6},{6,5},{9,10},{10,9},{13,14},{14,13},{17,18},{18,... | collective-permute-start | bytes 15368 | tf_op jit(solution)/shard_map/ppermute | solution.py:87
  (5 other events, 4.7 us)

commit v9 on v8

--- a/solution.py
+++ b/solution.py
@@ -11,7 +11,7 @@
 CFL = 0.25
 SPEED_EPS = 1e-06
 SOFT = 0.01
-CHUNK = 128
+CHUNK = 64
 VMEM_LIMIT = 16 * 1024 * 1024
 
 X, Y, U, V, VOL, PRES, CODE = range(7)
@@ -211,13 +211,13 @@
     return lax.dot_general(left, right, (((1,), (1,)), ((), ())), preferred_element_type=jnp.float32)
 
 
-def setup_kernel(source, coef, edge_weight, inner_weight, fresh, xcol, ycol, out_a, out_b, sem):
+def setup_kernel(source, coef, edge_weight, inner_weight, fresh, out_a, out_b, sem):
     pltpu.sync_copy(source, fresh)
     for edge, weight in ((True, edge_weight), (False, inner_weight)):
-        setup_list(edge, fresh, coef, weight, xcol, ycol, out_a, out_b, sem)
-
-
-def setup_list(edge, fresh, coef, weight, xcol, ycol, out_a, out_b, sem):
+        setup_list(edge, fresh, coef, weight, out_a, out_b, sem)
+
+
+def setup_list(edge, fresh, coef, weight, out_a, out_b, sem):
     groups, size, width, _ = weight.shape
     rows, cols = fresh.shape[0] - 2, fresh.shape[1] - 2
     base = first_of(edge, rows, cols)
@@ -225,46 +225,57 @@
     def place(bin_id):
         return place_of(edge, bin_id // size, lax.rem(bin_id, size), rows, cols)
 
-    def columns(bin_id, slot):
-        row, col = place(bin_id)
-        tile = fresh[row + 1, col + 1]
-        xcol[slot] = jnp.broadcast_to(tile[X : X + 1], (width, width)).T
-        ycol[slot] = jnp.broadcast_to(tile[Y : Y + 1], (width, width)).T
-
-    def blocks(bin_id, slot, out):
+    index = row_index(width)
+
+    def three_parts(tile):
+        high = tile.astype(jnp.bfloat16).astype(jnp.float32)
+        rest = tile - high
+        middle = rest.astype(jnp.bfloat16).astype(jnp.float32)
+        return high, middle, rest - middle
+
+    def with_square(tile, off_x, off_y):
+        if off_x or off_y:
+            tile = tile + jnp.where(index == X, off_x, jnp.where(index == Y, off_y, 0.0))
+        square = tile * tile
+        square = pltpu.roll(square, 2, 0) + pltpu.roll(square, 1, 0)
+        return jnp.where(index < 2, tile, jnp.where(index == 2, square, jnp.where(index == 3, 1.0, 0.0)))
+
+    def blocks(bin_id, out):
         row, col = place(bin_id)
         values = coef.at[base + bin_id]
-        around = [fresh[row + k // 3, col + k % 3] for k in range(9)]
-        xj = [jnp.broadcast_to(around[k][X : X + 1] + (k // 3 - 1.0), (8, width)) for k in range(9)]
-        yj = [jnp.broadcast_to(around[k][Y : Y + 1] + (k % 3 - 1.0), (8, width)) for k in range(9)]
-        for part in range(width // CHUNK):
-            span = pl.ds(part * CHUNK, CHUNK)
-            spans = [pl.ds(part * CHUNK + 8 * i, 8) for i in range(CHUNK // 8)]
-            xi = [xcol[slot, piece] for piece in spans]
-            yi = [ycol[slot, piece] for piece in spans]
-            for k in range(9):
+        own = with_square(fresh[row + 1, col + 1], 0.0, 0.0)
+        swapped = jnp.where(index == 2, pltpu.roll(own, 7, 0), pltpu.roll(own, 1, 0))
+        own = jnp.where(index < 2, -2.0 * own, jnp.where(index < 4, swapped, 0.0))
+        high, middle, low = three_parts(own)
+        own = jnp.concatenate([high, high, middle, high, low, middle], axis=0).T.astype(jnp.bfloat16)
+        for first in range(0, 9, 2):
+            codes = range(first, min(first + 2, 9))
+            around = []
+            for k in codes:
+                high, middle, low = three_parts(
+                    with_square(fresh[row + k // 3, col + k % 3], k // 3 - 1.0, k % 3 - 1.0)
+                )
+                around.append(jnp.concatenate([high, middle, high, low, high, middle], axis=0))
+            distance = dot(own, jnp.concatenate(around, axis=1).astype(jnp.bfloat16))
+            for k in codes:
                 lanes = pl.ds(k * width, width)
-                squares, weights = [], []
-                for x, y in zip(xi, yi):
-                    dx = x - xj[k]
-                    dy = y - yj[k]
-                    square = jnp.maximum(dx * dx + dy * dy, 1e-14)
+                for part in range(width // CHUNK):
+                    span = pl.ds(part * CHUNK, CHUNK)
+                    at = (k - first) * width
+                    square = distance[part * CHUNK : (part + 1) * CHUNK, at : at + width]
+                    square = jnp.maximum(square, 1e-14)
                     remain = jnp.maximum(1.0 - square * lax.rsqrt(square), 0.0)
-                    squares.append(square)
-                    weights.append(remain * remain * remain)
-                squares = jnp.concatenate(squares, axis=0).astype(jnp.bfloat16)
-                weights = jnp.concatenate(weights, axis=0).astype(jnp.bfloat16)
-                ratio = squares * pltpu.reciprocal(squares + jnp.bfloat16(SOFT), approx=True)
-                out[span, lanes] = weights
-                values[span, lanes] = weights * ratio
+                    weights = (remain * remain * remain).astype(jnp.bfloat16)
+                    square = square.astype(jnp.bfloat16)
+                    ratio = square * pltpu.reciprocal(square + jnp.bfloat16(SOFT), approx=True)
+                    out[span, lanes] = weights
+                    values[span, lanes] = weights * ratio
 
     def copy_out(bin_id, out, slot):
         target = weight.at[bin_id // size, lax.rem(bin_id, size)]
         return pltpu.make_async_copy(out, target, sem.at[slot])
 
     count = groups * size
-    columns(0, 0)
-    columns(1, 1)
 
     def two_bins(step, carry):
         even = 2 * step
@@ -273,16 +284,14 @@
         def _():
             copy_out(even - 2, out_a, 0).wait()
 
-        blocks(even, 0, out_a)
-        columns(jnp.minimum(even + 2, count - 1), 0)
+        blocks(even, out_a)
         copy_out(even, out_a, 0).start()
 
         @pl.when(step > 0)
         def _():
             copy_out(even - 1, out_b, 1).wait()
 
-        blocks(even + 1, 1, out_b)
-        columns(jnp.minimum(even + 3, count - 1), 1)
+        blocks(even + 1, out_b)
         copy_out(even + 1, out_b, 1).start()
         return carry
 
@@ -306,8 +315,6 @@
         ),
         scratch_shapes=[
             pltpu.VMEM(fresh.shape, jnp.float32),
-            pltpu.VMEM((2, width, width), jnp.float32),
-            pltpu.VMEM((2, width, width), jnp.float32),
             pltpu.VMEM((width, 9 * width), jnp.bfloat16),
             pltpu.VMEM((width, 9 * width), jnp.bfloat16),
             pltpu.SemaphoreType.DMA((2,)),

time: 225 us -> 232 us (1.031)
  Pallas kernels: 148 us -> 155 us
    pallas_call x1, Pallas kernels: 73.4 us -> 80.4 us  [setup(): call(setup_kernel, in_specs=[hbm], out_specs=(vmem, hbm, hbm), out_shape=...]
where the time goes in v9:
time: 232 us
  Pallas kernels  155 us (67%)
  starting transfers between devices  44.4 us (19%)
  waiting for transfers between devices  25.5 us (11%)
  local copies, waits for them, and re-layouts  5.15 us (2%)
    pallas_call x1, Pallas kernels, setup(): call(setup_kernel, in_specs=[hbm], out_specs=(vmem, hbm, hbm), out_shape=...  80.4 us
    ppermute x20, starting transfers between devices, swap(): return lax.ppermute(value, axis, pairs + [(j, i) for i, j in pairs])  42.4 us
    pallas_call x2, Pallas kernels, first_sweep(): call(functools.partial(first_kernel, kappa, edge), grid=(groups,), in_spe...  29.8 us
    pallas_call x2, Pallas kernels, push(): call(functools.partial(push_kernel, kappa, edge, len(args)), grid=(groups...  22.2 us
    pallas_call x6, Pallas kernels, sweep(): call(functools.partial(sweep_kernel, kappa, last, edge, rows, cols, len(a...  19.9 us
    ppermute x20, waiting for transfers between devices, swap(): return lax.ppermute(value, axis, pairs + [(j, i) for i, j in pairs])  15.6 us
    ppermute x5, waiting for transfers between devices, largest(): value = jnp.maximum(value, lax.ppermute(value, axis, pairs))  9.96 us
  transfers between devices with their start and end apart: 25, of which 11 were waited for; matrix products, arithmetic and copies ran while one was open for 0% of the time, Pallas kernels for 19%

profile of v9, /device:TPU:17, one launch (start us, length us, event | category | flops | bytes accessed | tf_op | source)
XLA Modules:
  0.0 231.6 jit_solution(7977586587607089034)
XLA Ops:
  10.6 3.4 %collective-permute-done.5 = f32[2,16,8,128]{3,2,1,0:T(8,128)S(1)} collective-permute-done((f32[2,16,8,128]{3,2,1,0:T(8,128)S(1)}, f32[2,16,8,128]{3,2,1,0:T(8,128)S(1)}, u32[]{:S(2)}, u32[]{:S(2)}) %collective-permute-start.5) | collective-permute-done | bytes 131104 | tf_op jit(solution)/shard_map/ppermute | solution.py:87
  16.2 3.0 %collective-permute-start.7 = (f32[12,2,8,128]{3,2,1,0:T(8,128)S(1)}, f32[12,2,8,128]{3,2,1,0:T(8,128)S(1)}, u32[]{:S(2)}, u32[]{:S(2)}) collective-permute-start(f32[12,2,8,128]{3,2,1,0:T(8,128)S(1)} %get-tuple-element.63), channel_id=1, source_target_pairs={{1,2},{2,1},{5,6},{6,5},{9,10},{10,9},{13,14},{14,13},{17,18},{18,... | collective-permute-start | bytes 294920 | tf_op jit(solution)/shard_map/ppermute | solution.py:87
  27.9 3.4 %collective-permute-done.4 = f32[8,128]{1,0:T(8,128)S(1)} collective-permute-done((f32[8,128]{1,0:T(8,128)S(1)}, f32[8,128]{1,0:T(8,128)S(1)}, u32[]{:S(2)}, u32[]{:S(2)}) %collective-permute-start.4) | collective-permute-done | bytes 4128 | tf_op jit(solution)/shard_map/ppermute | solution.py:163
  31.3 2.6 %drift.1.source.fresh.refs_2_.refs_6_ = f32[10,18,8,128]{3,2,1,0:T(8,128)} custom-call(f32[8,128]{1,0:T(8,128)S(1)} %max.19.top, f32[8,16,8,128]{3,2,1,0:T(8,128)S(1)} %get-tuple-element.30.center, f32[2,16,8,128]{3,2,1,0:T(8,128)S(1)} %get-tuple-element.59.above, f32[2,16,8,128]{3,2,1,0:T(8,128)S(1)} %get-tuple-element.58.below, ...), custom_call_target="tpu_custom_call" | custom-call | tf_op jit(solution)/shard_map/drift/pallas_call | solution.py:201
  33.9 80.4 %setup.1 = (bf16[132,128,1152]{2,1,0:T(8,128)(2,1)S(1)}, bf16[3,16,128,1152]{3,2,1,0:T(8,128)(2,1)}, bf16[6,14,128,1152]{3,2,1,0:T(8,128)(2,1)}) custom-call(f32[10,18,8,128]{3,2,1,0:T(8,128)} %drift.1.source.fresh.refs_2_.refs_6_), custom_call_target="tpu_custom_call" | custom-call | tf_op jit(solution)/shard_map/setup/pallas_call | solution.py:307
  114.3 11.8 %first_sweep.2 = (f32[3,3,16,128]{3,2,1,0:T(8,128)S(1)}, f32[3,16,128]{2,1,0:T(8,128)S(1)}, f32[8,1,128]{2,1,0:T(1,128)S(1)}, f32[8,1,128]{2,1,0:T(1,128)S(1)}) custom-call(f32[10,18,8,128]{3,2,1,0:T(8,128)} %drift.1.source.fresh.refs_2_.refs_6_, bf16[132,128,1152]{2,1,0:T(8,128)(2,1)S(1)} %get-tuple-element.33.coef.refs_6_.refs_2_, ...), custom_call_target="tpu_custom_call" | custom-call | tf_op jit(solution)/shard_map/first_sweep/pallas_call | solution.py:394
  126.5 3.0 %collective-permute-start.9 = (f32[1,16,128]{2,1,0:T(8,128)S(1)}, f32[1,16,128]{2,1,0:T(8,128)S(1)}, u32[]{:S(2)}, u32[]{:S(2)}) collective-permute-start(f32[1,16,128]{2,1,0:T(8,128)S(1)} %get-tuple-element.75), channel_id=1, source_target_pairs={{4,8},{12,16},{20,24},{8,4},{16,12},{24,20},{5,9},{13,17},{21,25},... | collective-permute-start | bytes 24584 | tf_op jit(solution)/shard_map/ppermute | solution.py:87
  131.8 6.3 %collective-permute-start.12 = (f32[10,1,128]{2,1,0:T(1,128)S(1)}, f32[10,1,128]{2,1,0:T(1,128)S(1)}, u32[]{:S(2)}, u32[]{:S(2)}) collective-permute-start(f32[10,1,128]{2,1,0:T(1,128)S(1)} %get-tuple-element.98), channel_id=1, source_target_pairs={{0,1},{2,3},{1,0},{3,2},{4,5},{6,7},{5,4},{7,6},{8,9},{10,11},{9,8... | collective-permute-start | bytes 15368 | tf_op jit(solution)/shard_map/ppermute | solution.py:87
  138.1 2.3 %collective-permute-start.11 = (f32[10,1,128]{2,1,0:T(1,128)S(1)}, f32[10,1,128]{2,1,0:T(1,128)S(1)}, u32[]{:S(2)}, u32[]{:S(2)}) collective-permute-start(f32[10,1,128]{2,1,0:T(1,128)S(1)} %get-tuple-element.99), channel_id=1, source_target_pairs={{1,2},{2,1},{5,6},{6,5},{9,10},{10,9},{13,14},{14,13},{17,18},{18,... | collective-permute-start | bytes 15368 | tf_op jit(solution)/shard_map/ppermute | solution.py:87
  140.4 18.0 %first_sweep.3 = (f32[3,6,14,128]{3,2,1,0:T(8,128)S(1)}, f32[6,14,128]{2,1,0:T(8,128)S(1)}) custom-call(f32[10,18,8,128]{3,2,1,0:T(8,128)} %drift.1.source.fresh.refs_2_.refs_6_, bf16[132,128,1152]{2,1,0:T(8,128)(2,1)S(1)} %get-tuple-element.33.coef.refs_6_.refs_2_, bf16[6,14,128,1152]{3,2,1,0:T(8,128)(2,1)} %get-tuple-element.36.weight.refs_3_), custom_call_target="tpu_custom_call" | custom-call | tf_op jit(solution)/shard_map/first_sweep/pallas_call | solution.py:394
  158.4 2.5 %sweep.6 = (f32[3,16,128]{2,1,0:T(8,128)S(1)}, f32[8,1,128]{2,1,0:T(1,128)S(1)}, f32[8,1,128]{2,1,0:T(1,128)S(1)}) custom-call(f32[3,16,128]{2,1,0:T(8,128)S(1)} %get-tuple-element.35.refs_0_, f32[6,14,128]{2,1,0:T(8,128)S(1)} %get-tuple-element.37.refs_1_, f32[1,16,128]{2,1,0:T(8,128)S(1)} %get-tuple-element.83.refs_2_, ...), custom_call_target="tpu_custom_call" | custom-call | tf_op jit(solution)/shard_map/sweep/pallas_call | solution.py:466
  164.3 3.2 %collective-permute-done.13 = f32[1,16,128]{2,1,0:T(8,128)S(1)} collective-permute-done((f32[1,16,128]{2,1,0:T(8,128)S(1)}, f32[1,16,128]{2,1,0:T(8,128)S(1)}, u32[]{:S(2)}, u32[]{:S(2)}) %collective-permute-start.13) | collective-permute-done | bytes 8224 | tf_op jit(solution)/shard_map/ppermute | solution.py:87
  167.7 4.6 %collective-permute-start.15 = (f32[10,1,128]{2,1,0:T(1,128)S(1)}, f32[10,1,128]{2,1,0:T(1,128)S(1)}, u32[]{:S(2)}, u32[]{:S(2)}) collective-permute-start(f32[10,1,128]{2,1,0:T(1,128)S(1)} %get-tuple-element.95), channel_id=1, source_target_pairs={{1,2},{2,1},{5,6},{6,5},{9,10},{10,9},{13,14},{14,13},{17,18},{18,... | collective-permute-start | bytes 15368 | tf_op jit(solution)/shard_map/ppermute | solution.py:87
  172.3 4.1 %sweep.7.refs_1_ = f32[6,14,128]{2,1,0:T(8,128)S(1)} custom-call(f32[3,16,128]{2,1,0:T(8,128)S(1)} %get-tuple-element.35.refs_0_, f32[6,14,128]{2,1,0:T(8,128)S(1)} %get-tuple-element.37.refs_1_, bf16[132,128,1152]{2,1,0:T(8,128)(2,1)S(1)} %get-tuple-element.33.coef.refs_6_.refs_2_, f32[3,6,14,128]{3,2,1,0:T(8,128)S(1)} %get-tuple-element.42.refs_3_), custom_call_target="tpu_custom_call" | custom-call | tf_op jit(solution)/shard_map/sweep/pallas_call | solution.py:466
  176.4 2.5 %sweep.8 = (f32[3,16,128]{2,1,0:T(8,128)S(1)}, f32[8,1,128]{2,1,0:T(1,128)S(1)}, f32[8,1,128]{2,1,0:T(1,128)S(1)}) custom-call(f32[3,16,128]{2,1,0:T(8,128)S(1)} %get-tuple-element.41.refs_0_, f32[6,14,128]{2,1,0:T(8,128)S(1)} %sweep.7.refs_1_, f32[1,16,128]{2,1,0:T(8,128)S(1)} %get-tuple-element.81.refs_2_, f32[1,16,128]{2,1,0:T(8,128)S(1)} %get-tuple-element.80.refs_3_, ...), custom_call_target="tpu_custom_call" | custom-call | tf_op jit(solution)/shard_map/sweep/pallas_call | solution.py:466
  179.3 3.0 %collective-permute-start.17 = (f32[1,16,128]{2,1,0:T(8,128)S(1)}, f32[1,16,128]{2,1,0:T(8,128)S(1)}, u32[]{:S(2)}, u32[]{:S(2)}) collective-permute-start(f32[1,16,128]{2,1,0:T(8,128)S(1)} %get-tuple-element.71), channel_id=1, source_target_pairs={{4,8},{12,16},{20,24},{8,4},{16,12},{24,20},{5,9},{13,17},{21,25},... | collective-permute-start | bytes 24584 | tf_op jit(solution)/shard_map/ppermute | solution.py:87
  184.7 3.5 %collective-permute-start.19 = (f32[10,1,128]{2,1,0:T(1,128)S(1)}, f32[10,1,128]{2,1,0:T(1,128)S(1)}, u32[]{:S(2)}, u32[]{:S(2)}) collective-permute-start(f32[10,1,128]{2,1,0:T(1,128)S(1)} %get-tuple-element.91), channel_id=1, source_target_pairs={{1,2},{2,1},{5,6},{6,5},{9,10},{10,9},{13,14},{14,13},{17,18},{18,... | collective-permute-start | bytes 15368 | tf_op jit(solution)/shard_map/ppermute | solution.py:87
  188.2 4.1 %sweep.9.refs_1_ = f32[6,14,128]{2,1,0:T(8,128)S(1)} custom-call(f32[3,16,128]{2,1,0:T(8,128)S(1)} %get-tuple-element.41.refs_0_, f32[6,14,128]{2,1,0:T(8,128)S(1)} %sweep.7.refs_1_, bf16[132,128,1152]{2,1,0:T(8,128)(2,1)S(1)} %get-tuple-element.33.coef.refs_6_.refs_2_, f32[3,6,14,128]{3,2,1,0:T(8,128)S(1)} %get-tuple-element.42.refs_3_), custom_call_target="tpu_custom_call" | custom-call | tf_op jit(solution)/shard_map/sweep/pallas_call | solution.py:466
  192.4 2.5 %sweep.10 = (f32[3,16,128]{2,1,0:T(8,128)S(1)}, f32[8,1,128]{2,1,0:T(1,128)S(1)}, f32[8,1,128]{2,1,0:T(1,128)S(1)}, f32[3,16,128]{2,1,0:T(8,128)S(1)}) custom-call(f32[3,16,128]{2,1,0:T(8,128)S(1)} %get-tuple-element.45.refs_0_, f32[6,14,128]{2,1,0:T(8,128)S(1)} %sweep.9.refs_1_, f32[1,16,128]{2,1,0:T(8,128)S(1)} %get-tuple-element.79.refs_2_, ...), custom_call_target="tpu_custom_call" | custom-call | tf_op jit(solution)/shard_map/sweep/pallas_call | solution.py:466
  198.2 3.2 %collective-permute-done.21 = f32[1,16,128]{2,1,0:T(8,128)S(1)} collective-permute-done((f32[1,16,128]{2,1,0:T(8,128)S(1)}, f32[1,16,128]{2,1,0:T(8,128)S(1)}, u32[]{:S(2)}, u32[]{:S(2)}) %collective-permute-start.21) | collective-permute-done | bytes 8224 | tf_op jit(solution)/shard_map/ppermute | solution.py:87
  201.6 3.6 %collective-permute-start.23 = (f32[10,1,128]{2,1,0:T(1,128)S(1)}, f32[10,1,128]{2,1,0:T(1,128)S(1)}, u32[]{:S(2)}, u32[]{:S(2)}) collective-permute-start(f32[10,1,128]{2,1,0:T(1,128)S(1)} %get-tuple-element.87), channel_id=1, source_target_pairs={{1,2},{2,1},{5,6},{6,5},{9,10},{10,9},{13,14},{14,13},{17,18},{18,... | collective-permute-start | bytes 15368 | tf_op jit(solution)/shard_map/ppermute | solution.py:87
  205.2 4.1 %sweep.11 = (f32[6,14,128]{2,1,0:T(8,128)S(1)}, f32[6,14,128]{2,1,0:T(8,128)S(1)}) custom-call(f32[3,16,128]{2,1,0:T(8,128)S(1)} %get-tuple-element.45.refs_0_, f32[6,14,128]{2,1,0:T(8,128)S(1)} %sweep.9.refs_1_, bf16[132,128,1152]{2,1,0:T(8,128)(2,1)S(1)} %get-tuple-element.33.coef.refs_6_.refs_2_, f32[3,6,14,128]{3,2,1,0:T(8,128)S(1)} %get-tuple-element.42.refs_3_), custom_call_target="tpu_custom_call" | custom-call | tf_op jit(solution)/shard_map/sweep/pallas_call | solution.py:466
  209.4 13.0 %push.2.refs_10_ = f32[2,6,14,128]{3,2,1,0:T(8,128)S(1)} custom-call(f32[3,16,128]{2,1,0:T(8,128)S(1)} %get-tuple-element.48.refs_0_, f32[6,14,128]{2,1,0:T(8,128)S(1)} %get-tuple-element.49.refs_1_, f32[10,18,8,128]{3,2,1,0:T(8,128)} %drift.1.source.fresh.refs_2_.refs_6_, bf16[6,14,128,1152]{3,2,1,0:T(8,128)(2,1)} %get-tuple-element.36.weight.refs_3_, ...), custom_call_target="tpu_custom_call" | custom-call | tf_op jit(solution)/shard_map/push/pallas_call | solution.py:565
  222.4 9.1 %push.3 = (f32[8,16,128]{2,1,0:T(8,128)}, f32[2,8,16,128]{3,2,1,0:T(8,128)}) custom-call(f32[3,16,128]{2,1,0:T(8,128)S(1)} %get-tuple-element.48.refs_0_, f32[6,14,128]{2,1,0:T(8,128)S(1)} %get-tuple-element.49.refs_1_, f32[1,16,128]{2,1,0:T(8,128)S(1)} %get-tuple-element.77.refs_2_, f32[1,16,128]{2,1,0:T(8,128)S(1)} %get-tuple-element.76.refs_3_, ...), custom_call_target="tpu_custom_call" | custom-call | tf_op jit(solution)/shard_map/push/pallas_call | solution.py:565
  (84 shorter events, 33.0 us)
Async XLA Ops:
  6.1 4.4 %collective-permute-start.6 = (f32[2,16,8,128]{3,2,1,0:T(8,128)S(1)}, f32[2,16,8,128]{3,2,1,0:T(8,128)S(1)}, u32[]{:S(2)}, u32[]{:S(2)}) collective-permute-start(f32[2,16,8,128]{3,2,1,0:T(8,128)S(1)} %get-tuple-element.56), channel_id=1, source_target_pairs={{0,4},{8,12},{16,20},{24,28},{4,0},{12,8},{20,16},{28,24},{1,5},{9... | collective-permute-start | bytes 393224 | tf_op jit(solution)/shard_map/ppermute | solution.py:87
  7.4 6.6 %collective-permute-start.5 = (f32[2,16,8,128]{3,2,1,0:T(8,128)S(1)}, f32[2,16,8,128]{3,2,1,0:T(8,128)S(1)}, u32[]{:S(2)}, u32[]{:S(2)}) collective-permute-start(f32[2,16,8,128]{3,2,1,0:T(8,128)S(1)} %get-tuple-element.57), channel_id=1, source_target_pairs={{4,8},{12,16},{20,24},{8,4},{16,12},{24,20},{5,9},{13,17},{21,25},... | collective-permute-start | bytes 393224 | tf_op jit(solution)/shard_map/ppermute | solution.py:87
  14.1 17.2 %collective-permute-start.8 = (f32[12,2,8,128]{3,2,1,0:T(8,128)S(1)}, f32[12,2,8,128]{3,2,1,0:T(8,128)S(1)}, u32[]{:S(2)}, u32[]{:S(2)}) collective-permute-start(f32[12,2,8,128]{3,2,1,0:T(8,128)S(1)} %get-tuple-element.62), channel_id=1, source_target_pairs={{0,1},{2,3},{1,0},{3,2},{4,5},{6,7},{5,4},{7,6},{8,9},{10,11},{9,8... | collective-permute-start | bytes 294920 | tf_op jit(solution)/shard_map/ppermute | solution.py:87
  16.2 15.0 %collective-permute-start.7 = (f32[12,2,8,128]{3,2,1,0:T(8,128)S(1)}, f32[12,2,8,128]{3,2,1,0:T(8,128)S(1)}, u32[]{:S(2)}, u32[]{:S(2)}) collective-permute-start(f32[12,2,8,128]{3,2,1,0:T(8,128)S(1)} %get-tuple-element.63), channel_id=1, source_target_pairs={{1,2},{2,1},{5,6},{6,5},{9,10},{10,9},{13,14},{14,13},{17,18},{18,... | collective-permute-start | bytes 294920 | tf_op jit(solution)/shard_map/ppermute | solution.py:87
  20.5 2.5 %collective-permute-start.1 = (f32[8,128]{1,0:T(8,128)S(1)}, f32[8,128]{1,0:T(8,128)S(1)}, u32[]{:S(2)}, u32[]{:S(2)}) collective-permute-start(f32[8,128]{1,0:T(8,128)S(1)} %max.15), channel_id=1, source_target_pairs={{0,2},{1,3},{2,0},{3,1},{4,6},{5,7},{6,4},{7,5},{8,10},{9,11},{10,... | collective-permute-start | bytes 12296 | tf_op jit(solution)/shard_map/ppermute | solution.py:163
  23.0 2.5 %collective-permute-start.2 = (f32[8,128]{1,0:T(8,128)S(1)}, f32[8,128]{1,0:T(8,128)S(1)}, u32[]{:S(2)}, u32[]{:S(2)}) collective-permute-start(f32[8,128]{1,0:T(8,128)S(1)} %max.16), channel_id=1, source_target_pairs={{0,4},{4,0},{8,12},{12,8},{16,20},{20,16},{24,28},{28,24},{1,5},{5... | collective-permute-start | bytes 12296 | tf_op jit(solution)/shard_map/ppermute | solution.py:163
  25.5 2.5 %collective-permute-start.3 = (f32[8,128]{1,0:T(8,128)S(1)}, f32[8,128]{1,0:T(8,128)S(1)}, u32[]{:S(2)}, u32[]{:S(2)}) collective-permute-start(f32[8,128]{1,0:T(8,128)S(1)} %max.17), channel_id=1, source_target_pairs={{0,8},{4,12},{8,0},{12,4},{16,24},{20,28},{24,16},{28,20},{1,9},{5... | collective-permute-start | bytes 12296 | tf_op jit(solution)/shard_map/ppermute | solution.py:163
  27.9 3.4 %collective-permute-start.4 = (f32[8,128]{1,0:T(8,128)S(1)}, f32[8,128]{1,0:T(8,128)S(1)}, u32[]{:S(2)}, u32[]{:S(2)}) collective-permute-start(f32[8,128]{1,0:T(8,128)S(1)} %max.18), channel_id=1, source_target_pairs={{0,16},{4,20},{8,24},{12,28},{16,0},{20,4},{24,8},{28,12},{1,17},{... | collective-permute-start | bytes 12296 | tf_op jit(solution)/shard_map/ppermute | solution.py:163
  126.2 3.3 %collective-permute-start.10 = (f32[1,16,128]{2,1,0:T(8,128)S(1)}, f32[1,16,128]{2,1,0:T(8,128)S(1)}, u32[]{:S(2)}, u32[]{:S(2)}) collective-permute-start(f32[1,16,128]{2,1,0:T(8,128)S(1)} %get-tuple-element.74), channel_id=1, source_target_pairs={{0,4},{8,12},{16,20},{24,28},{4,0},{12,8},{20,16},{28,24},{1,5},{9... | collective-permute-start | bytes 24584 | tf_op jit(solution)/shard_map/ppermute | solution.py:87
  126.5 5.3 %collective-permute-start.9 = (f32[1,16,128]{2,1,0:T(8,128)S(1)}, f32[1,16,128]{2,1,0:T(8,128)S(1)}, u32[]{:S(2)}, u32[]{:S(2)}) collective-permute-start(f32[1,16,128]{2,1,0:T(8,128)S(1)} %get-tuple-element.75), channel_id=1, source_target_pairs={{4,8},{12,16},{20,24},{8,4},{16,12},{24,20},{5,9},{13,17},{21,25},... | collective-permute-start | bytes 24584 | tf_op jit(solution)/shard_map/ppermute | solution.py:87
  131.8 26.6 %collective-permute-start.12 = (f32[10,1,128]{2,1,0:T(1,128)S(1)}, f32[10,1,128]{2,1,0:T(1,128)S(1)}, u32[]{:S(2)}, u32[]{:S(2)}) collective-permute-start(f32[10,1,128]{2,1,0:T(1,128)S(1)} %get-tuple-element.98), channel_id=1, source_target_pairs={{0,1},{2,3},{1,0},{3,2},{4,5},{6,7},{5,4},{7,6},{8,9},{10,11},{9,8... | collective-permute-start | bytes 15368 | tf_op jit(solution)/shard_map/ppermute | solution.py:87
  138.1 20.3 %collective-permute-start.11 = (f32[10,1,128]{2,1,0:T(1,128)S(1)}, f32[10,1,128]{2,1,0:T(1,128)S(1)}, u32[]{:S(2)}, u32[]{:S(2)}) collective-permute-start(f32[10,1,128]{2,1,0:T(1,128)S(1)} %get-tuple-element.99), channel_id=1, source_target_pairs={{1,2},{2,1},{5,6},{6,5},{9,10},{10,9},{13,14},{14,13},{17,18},{18,... | collective-permute-start | bytes 15368 | tf_op jit(solution)/shard_map/ppermute | solution.py:87
  161.0 3.3 %collective-permute-start.14 = (f32[1,16,128]{2,1,0:T(8,128)S(1)}, f32[1,16,128]{2,1,0:T(8,128)S(1)}, u32[]{:S(2)}, u32[]{:S(2)}) collective-permute-start(f32[1,16,128]{2,1,0:T(8,128)S(1)} %get-tuple-element.72), channel_id=1, source_target_pairs={{0,4},{8,12},{16,20},{24,28},{4,0},{12,8},{20,16},{28,24},{1,5},{9... | collective-permute-start | bytes 24584 | tf_op jit(solution)/shard_map/ppermute | solution.py:87
  162.2 5.3 %collective-permute-start.13 = (f32[1,16,128]{2,1,0:T(8,128)S(1)}, f32[1,16,128]{2,1,0:T(8,128)S(1)}, u32[]{:S(2)}, u32[]{:S(2)}) collective-permute-start(f32[1,16,128]{2,1,0:T(8,128)S(1)} %get-tuple-element.73), channel_id=1, source_target_pairs={{4,8},{12,16},{20,24},{8,4},{16,12},{24,20},{5,9},{13,17},{21,25},... | collective-permute-start | bytes 24584 | tf_op jit(solution)/shard_map/ppermute | solution.py:87
  167.6 8.8 %collective-permute-start.16 = (f32[10,1,128]{2,1,0:T(1,128)S(1)}, f32[10,1,128]{2,1,0:T(1,128)S(1)}, u32[]{:S(2)}, u32[]{:S(2)}) collective-permute-start(f32[10,1,128]{2,1,0:T(1,128)S(1)} %get-tuple-element.94), channel_id=1, source_target_pairs={{0,1},{2,3},{1,0},{3,2},{4,5},{6,7},{5,4},{7,6},{8,9},{10,11},{9,8... | collective-permute-start | bytes 15368 | tf_op jit(solution)/shard_map/ppermute | solution.py:87
  167.7 8.8 %collective-permute-start.15 = (f32[10,1,128]{2,1,0:T(1,128)S(1)}, f32[10,1,128]{2,1,0:T(1,128)S(1)}, u32[]{:S(2)}, u32[]{:S(2)}) collective-permute-start(f32[10,1,128]{2,1,0:T(1,128)S(1)} %get-tuple-element.95), channel_id=1, source_target_pairs={{1,2},{2,1},{5,6},{6,5},{9,10},{10,9},{13,14},{14,13},{17,18},{18,... | collective-permute-start | bytes 15368 | tf_op jit(solution)/shard_map/ppermute | solution.py:87
  179.0 3.3 %collective-permute-start.18 = (f32[1,16,128]{2,1,0:T(8,128)S(1)}, f32[1,16,128]{2,1,0:T(8,128)S(1)}, u32[]{:S(2)}, u32[]{:S(2)}) collective-permute-start(f32[1,16,128]{2,1,0:T(8,128)S(1)} %get-tuple-element.70), channel_id=1, source_target_pairs={{0,4},{8,12},{16,20},{24,28},{4,0},{12,8},{20,16},{28,24},{1,5},{9... | collective-permute-start | bytes 24584 | tf_op jit(solution)/shard_map/ppermute | solution.py:87
  179.3 5.3 %collective-permute-start.17 = (f32[1,16,128]{2,1,0:T(8,128)S(1)}, f32[1,16,128]{2,1,0:T(8,128)S(1)}, u32[]{:S(2)}, u32[]{:S(2)}) collective-permute-start(f32[1,16,128]{2,1,0:T(8,128)S(1)} %get-tuple-element.71), channel_id=1, source_target_pairs={{4,8},{12,16},{20,24},{8,4},{16,12},{24,20},{5,9},{13,17},{21,25},... | collective-permute-start | bytes 24584 | tf_op jit(solution)/shard_map/ppermute | solution.py:87
  184.6 7.7 %collective-permute-start.20 = (f32[10,1,128]{2,1,0:T(1,128)S(1)}, f32[10,1,128]{2,1,0:T(1,128)S(1)}, u32[]{:S(2)}, u32[]{:S(2)}) collective-permute-start(f32[10,1,128]{2,1,0:T(1,128)S(1)} %get-tuple-element.90), channel_id=1, source_target_pairs={{0,1},{2,3},{1,0},{3,2},{4,5},{6,7},{5,4},{7,6},{8,9},{10,11},{9,8... | collective-permute-start | bytes 15368 | tf_op jit(solution)/shard_map/ppermute | solution.py:87
  184.7 7.7 %collective-permute-start.19 = (f32[10,1,128]{2,1,0:T(1,128)S(1)}, f32[10,1,128]{2,1,0:T(1,128)S(1)}, u32[]{:S(2)}, u32[]{:S(2)}) collective-permute-start(f32[10,1,128]{2,1,0:T(1,128)S(1)} %get-tuple-element.91), channel_id=1, source_target_pairs={{1,2},{2,1},{5,6},{6,5},{9,10},{10,9},{13,14},{14,13},{17,18},{18,... | collective-permute-start | bytes 15368 | tf_op jit(solution)/shard_map/ppermute | solution.py:87
  194.9 3.3 %collective-permute-start.22 = (f32[1,16,128]{2,1,0:T(8,128)S(1)}, f32[1,16,128]{2,1,0:T(8,128)S(1)}, u32[]{:S(2)}, u32[]{:S(2)}) collective-permute-start(f32[1,16,128]{2,1,0:T(8,128)S(1)} %get-tuple-element.68), channel_id=1, source_target_pairs={{0,4},{8,12},{16,20},{24,28},{4,0},{12,8},{20,16},{28,24},{1,5},{9... | collective-permute-start | bytes 24584 | tf_op jit(solution)/shard_map/ppermute | solution.py:87
  196.2 5.3 %collective-permute-start.21 = (f32[1,16,128]{2,1,0:T(8,128)S(1)}, f32[1,16,128]{2,1,0:T(8,128)S(1)}, u32[]{:S(2)}, u32[]{:S(2)}) collective-permute-start(f32[1,16,128]{2,1,0:T(8,128)S(1)} %get-tuple-element.69), channel_id=1, source_target_pairs={{4,8},{12,16},{20,24},{8,4},{16,12},{24,20},{5,9},{13,17},{21,25},... | collective-permute-start | bytes 24584 | tf_op jit(solution)/shard_map/ppermute | solution.py:87
  201.5 20.9 %collective-permute-start.24 = (f32[10,1,128]{2,1,0:T(1,128)S(1)}, f32[10,1,128]{2,1,0:T(1,128)S(1)}, u32[]{:S(2)}, u32[]{:S(2)}) collective-permute-start(f32[10,1,128]{2,1,0:T(1,128)S(1)} %get-tuple-element.86), channel_id=1, source_target_pairs={{0,1},{2,3},{1,0},{3,2},{4,5},{6,7},{5,4},{7,6},{8,9},{10,11},{9,8... | collective-permute-start | bytes 15368 | tf_op jit(solution)/shard_map/ppermute | solution.py:87
  201.6 20.8 %collective-permute-start.23 = (f32[10,1,128]{2,1,0:T(1,128)S(1)}, f32[10,1,128]{2,1,0:T(1,128)S(1)}, u32[]{:S(2)}, u32[]{:S(2)}) collective-permute-start(f32[10,1,128]{2,1,0:T(1,128)S(1)} %get-tuple-element.87), channel_id=1, source_target_pairs={{1,2},{2,1},{5,6},{6,5},{9,10},{10,9},{13,14},{14,13},{17,18},{18,... | collective-permute-start | bytes 15368 | tf_op jit(solution)/shard_map/ppermute | solution.py:87
  (5 other events, 4.7 us)

commit v10 on v8

--- a/solution.py
+++ b/solution.py
@@ -11,7 +11,7 @@
 CFL = 0.25
 SPEED_EPS = 1e-06
 SOFT = 0.01
-CHUNK = 128
+CHUNK = 64
 VMEM_LIMIT = 16 * 1024 * 1024
 
 X, Y, U, V, VOL, PRES, CODE = range(7)
@@ -29,6 +29,10 @@
 
 def once(array):
     return pl.BlockSpec(array.shape, lambda group: (0,) * array.ndim)
+
+
+def side_by_side(blocks):
+    return jnp.concatenate([blocks[k] for k in range(9)], axis=1)
 
 
 def row_index(width):
@@ -218,7 +222,7 @@
 
 
 def setup_list(edge, fresh, coef, weight, xcol, ycol, out_a, out_b, sem):
-    groups, size, width, _ = weight.shape
+    groups, size, _, width, _ = weight.shape
     rows, cols = fresh.shape[0] - 2, fresh.shape[1] - 2
     base = first_of(edge, rows, cols)
 
@@ -243,7 +247,6 @@
             xi = [xcol[slot, piece] for piece in spans]
             yi = [ycol[slot, piece] for piece in spans]
             for k in range(9):
-                lanes = pl.ds(k * width, width)
                 squares, weights = [], []
                 for x, y in zip(xi, yi):
                     dx = x - xj[k]
@@ -255,8 +258,8 @@
                 squares = jnp.concatenate(squares, axis=0).astype(jnp.bfloat16)
                 weights = jnp.concatenate(weights, axis=0).astype(jnp.bfloat16)
                 ratio = squares * pltpu.reciprocal(squares + jnp.bfloat16(SOFT), approx=True)
-                out[span, lanes] = weights
-                values[span, lanes] = weights * ratio
+                out[k, span] = weights
+                values[k, span] = weights * ratio
 
     def copy_out(bin_id, out, slot):
         target = weight.at[bin_id // size, lax.rem(bin_id, size)]
@@ -300,16 +303,16 @@
         in_specs=[hbm],
         out_specs=(vmem, hbm, hbm),
         out_shape=(
-            pltpu.VMEM((edge[0] * edge[1] + inner[0] * inner[1], width, 9 * width), jnp.bfloat16),
-            pltpu.HBM((*edge, width, 9 * width), jnp.bfloat16),
-            pltpu.HBM((*inner, width, 9 * width), jnp.bfloat16),
+            pltpu.VMEM((edge[0] * edge[1] + inner[0] * inner[1], 9, width, width), jnp.bfloat16),
+            pltpu.HBM((*edge, 9, width, width), jnp.bfloat16),
+            pltpu.HBM((*inner, 9, width, width), jnp.bfloat16),
         ),
         scratch_shapes=[
             pltpu.VMEM(fresh.shape, jnp.float32),
             pltpu.VMEM((2, width, width), jnp.float32),
             pltpu.VMEM((2, width, width), jnp.float32),
-            pltpu.VMEM((width, 9 * width), jnp.bfloat16),
-            pltpu.VMEM((width, 9 * width), jnp.bfloat16),
+            pltpu.VMEM((9, width, width), jnp.bfloat16),
+            pltpu.VMEM((9, width, width), jnp.bfloat16),
             pltpu.SemaphoreType.DMA((2,)),
         ],
         name="setup",
@@ -319,7 +322,7 @@
 def first_kernel(kappa, edge, fresh, coef, weight, sums, pv, *rest):
     feat = rest[-1]
     group = pl.program_id(0)
-    size, width, _ = weight.shape
+    size, _, width, _ = weight.shape
 
     @pl.when(group == 0)
     def _():
@@ -356,8 +359,8 @@
                 features = features + float(off_y) * feat[row + k // 3, col + k % 3, 2]
             around.append(split(features))
         around = jnp.concatenate(around, axis=1)
-        total_w = dot_nt(weight[index], around)
-        total_c = dot_nt(coef[base + group * size + index], around)
+        total_w = dot_nt(side_by_side(weight.at[index]), around)
+        total_c = dot_nt(side_by_side(coef.at[base + group * size + index]), around)
         total_w = (total_w[:, :8] + total_w[:, 8:]).T
         total_c = (total_c[:, :8] + total_c[:, 8:]).T
         tile = fresh[row + 1, col + 1]
@@ -381,13 +384,13 @@
 
 
 def first_sweep(kappa, edge, fresh, coef, weight):
-    groups, size, width, deep = weight.shape
+    groups, size, _, width, _ = weight.shape
     rows, cols = fresh.shape[:2]
     vmem = pl.BlockSpec(memory_space=pltpu.VMEM)
     return call(
         functools.partial(first_kernel, kappa, edge),
         grid=(groups,),
-        in_specs=[once(fresh), vmem, pl.BlockSpec((None, size, width, deep), lambda group: (group, 0, 0, 0))],
+        in_specs=[once(fresh), vmem, pl.BlockSpec((None, size, 9, width, width), lambda group: (group, 0, 0, 0, 0))],
         out_specs=[vmem] * (4 if edge else 2),
         out_shape=[
             pltpu.VMEM((3, groups, size, width), jnp.float32),
@@ -431,7 +434,7 @@
             for part in range(width // 16):
                 total = None
                 for k in range(9):
-                    term = coef[base + group * size + index, pl.ds(part * 16, 16), pl.ds(k * width, width)] * around[k]
+                    term = coef[base + group * size + index, k, pl.ds(part * 16, 16)] * around[k]
                     total = term if total is None else total + term
                 parts.append(total)
             totals.append(dot_nt(ones, jnp.concatenate(parts, axis=0))[0:1])
@@ -474,7 +477,7 @@
     fresh, weight, pressure = refs[count - (5 if edge else 3) : count][:3]
     ext, feat = refs[-2:]
     group = pl.program_id(0)
-    size, width, _ = weight.shape
+    size, _, width, _ = weight.shape
     rows, cols = fresh.shape[0] - 2, fresh.shape[1] - 2
 
     @pl.when(group == 0)
@@ -511,7 +514,7 @@
             if off_y:
                 tile = tile + jnp.where(feature == 2, off_y * pv, jnp.where(feature == 6, off_y * vol, 0.0))
             around.append(split(tile))
-        total = dot_nt(weight[index], jnp.concatenate(around, axis=1))
+        total = dot_nt(side_by_side(weight.at[index]), jnp.concatenate(around, axis=1))
         total = (total[:, :8] + total[:, 8:]).T
         tile = fresh[row + 1, col + 1]
         own = pressure[group, index : index + 1, :]
@@ -538,7 +541,7 @@
 
 
 def push(kappa, edge, pv, halo, fresh, weight, pressure, inner):
-    groups, size, width, deep = weight.shape
+    groups, size, _, width, _ = weight.shape
     rows, cols = fresh.shape[:2]
     vmem = pl.BlockSpec(memory_space=pltpu.VMEM)
     weight = in_hbm(weight)
@@ -546,7 +549,7 @@
     specs = [vmem] * len(args)
     specs[len(pv) + (len(halo) if edge else 0)] = once(fresh)
     specs[len(pv) + (len(halo) if edge else 0) + 1] = pl.BlockSpec(
-        (None, size, width, deep), lambda group: (group, 0, 0, 0)
+        (None, size, 9, width, width), lambda group: (group, 0, 0, 0, 0)
     )
     if edge:
         outs = [

time: 225 us -> 224 us (level)
  no operation moved by 1% of the time
where the time goes in v10:
time: 224 us
  Pallas kernels  147 us (66%)
  starting transfers between devices  44.4 us (20%)
  waiting for transfers between devices  25.5 us (11%)
  local copies, waits for them, and re-layouts  5.15 us (2%)
    pallas_call x1, Pallas kernels, setup(): call(setup_kernel, in_specs=[hbm], out_specs=(vmem, hbm, hbm), out_shape=...  72.1 us
    ppermute x20, starting transfers between devices, swap(): return lax.ppermute(value, axis, pairs + [(j, i) for i, j in pairs])  42.4 us
    pallas_call x2, Pallas kernels, first_sweep(): call(functools.partial(first_kernel, kappa, edge), grid=(groups,), in_spe...  29.8 us
    pallas_call x2, Pallas kernels, push(): call(functools.partial(push_kernel, kappa, edge, len(args)), grid=(groups...  22.2 us
    pallas_call x6, Pallas kernels, sweep(): call(functools.partial(sweep_kernel, kappa, last, edge, rows, cols, len(a...  20.2 us
    ppermute x20, waiting for transfers between devices, swap(): return lax.ppermute(value, axis, pairs + [(j, i) for i, j in pairs])  15.6 us
    ppermute x5, waiting for transfers between devices, largest(): value = jnp.maximum(value, lax.ppermute(value, axis, pairs))  9.96 us
  transfers between devices with their start and end apart: 25, of which 11 were waited for; matrix products, arithmetic and copies ran while one was open for 0% of the time, Pallas kernels for 19%

profile of v10, /device:TPU:17, one launch (start us, length us, event | category | flops | bytes accessed | tf_op | source)
XLA Modules:
  0.0 223.5 jit_solution(13569696304641091162)
XLA Ops:
  10.6 3.4 %collective-permute-done.5 = f32[2,16,8,128]{3,2,1,0:T(8,128)S(1)} collective-permute-done((f32[2,16,8,128]{3,2,1,0:T(8,128)S(1)}, f32[2,16,8,128]{3,2,1,0:T(8,128)S(1)}, u32[]{:S(2)}, u32[]{:S(2)}) %collective-permute-start.5) | collective-permute-done | bytes 131104 | tf_op jit(solution)/shard_map/ppermute | solution.py:91
  16.2 3.0 %collective-permute-start.7 = (f32[12,2,8,128]{3,2,1,0:T(8,128)S(1)}, f32[12,2,8,128]{3,2,1,0:T(8,128)S(1)}, u32[]{:S(2)}, u32[]{:S(2)}) collective-permute-start(f32[12,2,8,128]{3,2,1,0:T(8,128)S(1)} %get-tuple-element.63), channel_id=1, source_target_pairs={{1,2},{2,1},{5,6},{6,5},{9,10},{10,9},{13,14},{14,13},{17,18},{18,... | collective-permute-start | bytes 294920 | tf_op jit(solution)/shard_map/ppermute | solution.py:91
  27.9 3.4 %collective-permute-done.4 = f32[8,128]{1,0:T(8,128)S(1)} collective-permute-done((f32[8,128]{1,0:T(8,128)S(1)}, f32[8,128]{1,0:T(8,128)S(1)}, u32[]{:S(2)}, u32[]{:S(2)}) %collective-permute-start.4) | collective-permute-done | bytes 4128 | tf_op jit(solution)/shard_map/ppermute | solution.py:167
  31.3 2.6 %drift.1.source.fresh.refs_2_.refs_6_ = f32[10,18,8,128]{3,2,1,0:T(8,128)} custom-call(f32[8,128]{1,0:T(8,128)S(1)} %max.19.top, f32[8,16,8,128]{3,2,1,0:T(8,128)S(1)} %get-tuple-element.30.center, f32[2,16,8,128]{3,2,1,0:T(8,128)S(1)} %get-tuple-element.59.above, f32[2,16,8,128]{3,2,1,0:T(8,128)S(1)} %get-tuple-element.58.below, ...), custom_call_target="tpu_custom_call" | custom-call | tf_op jit(solution)/shard_map/drift/pallas_call | solution.py:205
  33.9 72.1 %setup.1 = (bf16[132,9,128,128]{3,2,1,0:T(8,128)(2,1)S(1)}, bf16[3,16,9,128,128]{4,3,2,1,0:T(8,128)(2,1)}, bf16[6,14,9,128,128]{4,3,2,1,0:T(8,128)(2,1)}) custom-call(f32[10,18,8,128]{3,2,1,0:T(8,128)} %drift.1.source.fresh.refs_2_.refs_6_), custom_call_target="tpu_custom_call" | custom-call | tf_op jit(solution)/shard_map/setup/pallas_call | solution.py:301
  106.0 11.8 %first_sweep.2 = (f32[3,3,16,128]{3,2,1,0:T(8,128)S(1)}, f32[3,16,128]{2,1,0:T(8,128)S(1)}, f32[8,1,128]{2,1,0:T(1,128)S(1)}, f32[8,1,128]{2,1,0:T(1,128)S(1)}) custom-call(f32[10,18,8,128]{3,2,1,0:T(8,128)} %drift.1.source.fresh.refs_2_.refs_6_, bf16[132,9,128,128]{3,2,1,0:T(8,128)(2,1)S(1)} %get-tuple-element.33.coef.refs_6_.refs_2_, ...), custom_call_target="tpu_custom_call" | custom-call | tf_op jit(solution)/shard_map/first_sweep/pallas_call | solution.py:390
  118.1 3.0 %collective-permute-start.9 = (f32[1,16,128]{2,1,0:T(8,128)S(1)}, f32[1,16,128]{2,1,0:T(8,128)S(1)}, u32[]{:S(2)}, u32[]{:S(2)}) collective-permute-start(f32[1,16,128]{2,1,0:T(8,128)S(1)} %get-tuple-element.75), channel_id=1, source_target_pairs={{4,8},{12,16},{20,24},{8,4},{16,12},{24,20},{5,9},{13,17},{21,25},... | collective-permute-start | bytes 24584 | tf_op jit(solution)/shard_map/ppermute | solution.py:91
  123.4 6.3 %collective-permute-start.12 = (f32[10,1,128]{2,1,0:T(1,128)S(1)}, f32[10,1,128]{2,1,0:T(1,128)S(1)}, u32[]{:S(2)}, u32[]{:S(2)}) collective-permute-start(f32[10,1,128]{2,1,0:T(1,128)S(1)} %get-tuple-element.98), channel_id=1, source_target_pairs={{0,1},{2,3},{1,0},{3,2},{4,5},{6,7},{5,4},{7,6},{8,9},{10,11},{9,8... | collective-permute-start | bytes 15368 | tf_op jit(solution)/shard_map/ppermute | solution.py:91
  129.7 2.3 %collective-permute-start.11 = (f32[10,1,128]{2,1,0:T(1,128)S(1)}, f32[10,1,128]{2,1,0:T(1,128)S(1)}, u32[]{:S(2)}, u32[]{:S(2)}) collective-permute-start(f32[10,1,128]{2,1,0:T(1,128)S(1)} %get-tuple-element.99), channel_id=1, source_target_pairs={{1,2},{2,1},{5,6},{6,5},{9,10},{10,9},{13,14},{14,13},{17,18},{18,... | collective-permute-start | bytes 15368 | tf_op jit(solution)/shard_map/ppermute | solution.py:91
  132.0 18.0 %first_sweep.3 = (f32[3,6,14,128]{3,2,1,0:T(8,128)S(1)}, f32[6,14,128]{2,1,0:T(8,128)S(1)}) custom-call(f32[10,18,8,128]{3,2,1,0:T(8,128)} %drift.1.source.fresh.refs_2_.refs_6_, bf16[132,9,128,128]{3,2,1,0:T(8,128)(2,1)S(1)} %get-tuple-element.33.coef.refs_6_.refs_2_, bf16[6,14,9,128,128]{4,3,2,1,0:T(8,128)(2,1)} %get-tuple-element.36.weight.refs_3_), custom_call_target="tpu_custom_call" | custom-call | tf_op jit(solution)/shard_map/first_sweep/pallas_call | solution.py:390
  150.1 2.6 %sweep.6 = (f32[3,16,128]{2,1,0:T(8,128)S(1)}, f32[8,1,128]{2,1,0:T(1,128)S(1)}, f32[8,1,128]{2,1,0:T(1,128)S(1)}) custom-call(f32[3,16,128]{2,1,0:T(8,128)S(1)} %get-tuple-element.35.refs_0_, f32[6,14,128]{2,1,0:T(8,128)S(1)} %get-tuple-element.37.refs_1_, f32[1,16,128]{2,1,0:T(8,128)S(1)} %get-tuple-element.83.refs_2_, ...), custom_call_target="tpu_custom_call" | custom-call | tf_op jit(solution)/shard_map/sweep/pallas_call | solution.py:462
  156.1 3.2 %collective-permute-done.13 = f32[1,16,128]{2,1,0:T(8,128)S(1)} collective-permute-done((f32[1,16,128]{2,1,0:T(8,128)S(1)}, f32[1,16,128]{2,1,0:T(8,128)S(1)}, u32[]{:S(2)}, u32[]{:S(2)}) %collective-permute-start.13) | collective-permute-done | bytes 8224 | tf_op jit(solution)/shard_map/ppermute | solution.py:91
  159.4 4.6 %collective-permute-start.15 = (f32[10,1,128]{2,1,0:T(1,128)S(1)}, f32[10,1,128]{2,1,0:T(1,128)S(1)}, u32[]{:S(2)}, u32[]{:S(2)}) collective-permute-start(f32[10,1,128]{2,1,0:T(1,128)S(1)} %get-tuple-element.95), channel_id=1, source_target_pairs={{1,2},{2,1},{5,6},{6,5},{9,10},{10,9},{13,14},{14,13},{17,18},{18,... | collective-permute-start | bytes 15368 | tf_op jit(solution)/shard_map/ppermute | solution.py:91
  164.0 4.1 %sweep.7.refs_1_ = f32[6,14,128]{2,1,0:T(8,128)S(1)} custom-call(f32[3,16,128]{2,1,0:T(8,128)S(1)} %get-tuple-element.35.refs_0_, f32[6,14,128]{2,1,0:T(8,128)S(1)} %get-tuple-element.37.refs_1_, bf16[132,9,128,128]{3,2,1,0:T(8,128)(2,1)S(1)} %get-tuple-element.33.coef.refs_6_.refs_2_, f32[3,6,14,128]{3,2,1,0:T(8,128)S(1)} %get-tuple-element.42.refs_3_), custom_call_target="tpu_custom_call" | custom-call | tf_op jit(solution)/shard_map/sweep/pallas_call | solution.py:462
  168.2 2.6 %sweep.8 = (f32[3,16,128]{2,1,0:T(8,128)S(1)}, f32[8,1,128]{2,1,0:T(1,128)S(1)}, f32[8,1,128]{2,1,0:T(1,128)S(1)}) custom-call(f32[3,16,128]{2,1,0:T(8,128)S(1)} %get-tuple-element.41.refs_0_, f32[6,14,128]{2,1,0:T(8,128)S(1)} %sweep.7.refs_1_, f32[1,16,128]{2,1,0:T(8,128)S(1)} %get-tuple-element.81.refs_2_, f32[1,16,128]{2,1,0:T(8,128)S(1)} %get-tuple-element.80.refs_3_, ...), custom_call_target="tpu_custom_call" | custom-call | tf_op jit(solution)/shard_map/sweep/pallas_call | solution.py:462
  171.2 3.0 %collective-permute-start.17 = (f32[1,16,128]{2,1,0:T(8,128)S(1)}, f32[1,16,128]{2,1,0:T(8,128)S(1)}, u32[]{:S(2)}, u32[]{:S(2)}) collective-permute-start(f32[1,16,128]{2,1,0:T(8,128)S(1)} %get-tuple-element.71), channel_id=1, source_target_pairs={{4,8},{12,16},{20,24},{8,4},{16,12},{24,20},{5,9},{13,17},{21,25},... | collective-permute-start | bytes 24584 | tf_op jit(solution)/shard_map/ppermute | solution.py:91
  176.6 3.5 %collective-permute-start.19 = (f32[10,1,128]{2,1,0:T(1,128)S(1)}, f32[10,1,128]{2,1,0:T(1,128)S(1)}, u32[]{:S(2)}, u32[]{:S(2)}) collective-permute-start(f32[10,1,128]{2,1,0:T(1,128)S(1)} %get-tuple-element.91), channel_id=1, source_target_pairs={{1,2},{2,1},{5,6},{6,5},{9,10},{10,9},{13,14},{14,13},{17,18},{18,... | collective-permute-start | bytes 15368 | tf_op jit(solution)/shard_map/ppermute | solution.py:91
  180.1 4.1 %sweep.9.refs_1_ = f32[6,14,128]{2,1,0:T(8,128)S(1)} custom-call(f32[3,16,128]{2,1,0:T(8,128)S(1)} %get-tuple-element.41.refs_0_, f32[6,14,128]{2,1,0:T(8,128)S(1)} %sweep.7.refs_1_, bf16[132,9,128,128]{3,2,1,0:T(8,128)(2,1)S(1)} %get-tuple-element.33.coef.refs_6_.refs_2_, f32[3,6,14,128]{3,2,1,0:T(8,128)S(1)} %get-tuple-element.42.refs_3_), custom_call_target="tpu_custom_call" | custom-call | tf_op jit(solution)/shard_map/sweep/pallas_call | solution.py:462
  184.2 2.6 %sweep.10 = (f32[3,16,128]{2,1,0:T(8,128)S(1)}, f32[8,1,128]{2,1,0:T(1,128)S(1)}, f32[8,1,128]{2,1,0:T(1,128)S(1)}, f32[3,16,128]{2,1,0:T(8,128)S(1)}) custom-call(f32[3,16,128]{2,1,0:T(8,128)S(1)} %get-tuple-element.45.refs_0_, f32[6,14,128]{2,1,0:T(8,128)S(1)} %sweep.9.refs_1_, f32[1,16,128]{2,1,0:T(8,128)S(1)} %get-tuple-element.79.refs_2_, ...), custom_call_target="tpu_custom_call" | custom-call | tf_op jit(solution)/shard_map/sweep/pallas_call | solution.py:462
  190.2 3.2 %collective-permute-done.21 = f32[1,16,128]{2,1,0:T(8,128)S(1)} collective-permute-done((f32[1,16,128]{2,1,0:T(8,128)S(1)}, f32[1,16,128]{2,1,0:T(8,128)S(1)}, u32[]{:S(2)}, u32[]{:S(2)}) %collective-permute-start.21) | collective-permute-done | bytes 8224 | tf_op jit(solution)/shard_map/ppermute | solution.py:91
  193.6 3.6 %collective-permute-start.23 = (f32[10,1,128]{2,1,0:T(1,128)S(1)}, f32[10,1,128]{2,1,0:T(1,128)S(1)}, u32[]{:S(2)}, u32[]{:S(2)}) collective-permute-start(f32[10,1,128]{2,1,0:T(1,128)S(1)} %get-tuple-element.87), channel_id=1, source_target_pairs={{1,2},{2,1},{5,6},{6,5},{9,10},{10,9},{13,14},{14,13},{17,18},{18,... | collective-permute-start | bytes 15368 | tf_op jit(solution)/shard_map/ppermute | solution.py:91
  197.2 4.1 %sweep.11 = (f32[6,14,128]{2,1,0:T(8,128)S(1)}, f32[6,14,128]{2,1,0:T(8,128)S(1)}) custom-call(f32[3,16,128]{2,1,0:T(8,128)S(1)} %get-tuple-element.45.refs_0_, f32[6,14,128]{2,1,0:T(8,128)S(1)} %sweep.9.refs_1_, bf16[132,9,128,128]{3,2,1,0:T(8,128)(2,1)S(1)} %get-tuple-element.33.coef.refs_6_.refs_2_, f32[3,6,14,128]{3,2,1,0:T(8,128)S(1)} %get-tuple-element.42.refs_3_), custom_call_target="tpu_custom_call" | custom-call | tf_op jit(solution)/shard_map/sweep/pallas_call | solution.py:462
  201.3 13.0 %push.2.refs_10_ = f32[2,6,14,128]{3,2,1,0:T(8,128)S(1)} custom-call(f32[3,16,128]{2,1,0:T(8,128)S(1)} %get-tuple-element.48.refs_0_, f32[6,14,128]{2,1,0:T(8,128)S(1)} %get-tuple-element.49.refs_1_, f32[10,18,8,128]{3,2,1,0:T(8,128)} %drift.1.source.fresh.refs_2_.refs_6_, bf16[6,14,9,128,128]{4,3,2,1,0:T(8,128)(2,1)} %get-tuple-element.36.weight.refs_3_, ...), custom_call_target="tpu_custom_call" | custom-call | tf_op jit(solution)/shard_map/push/pallas_call | solution.py:561
  214.4 9.1 %push.3 = (f32[8,16,128]{2,1,0:T(8,128)}, f32[2,8,16,128]{3,2,1,0:T(8,128)}) custom-call(f32[3,16,128]{2,1,0:T(8,128)S(1)} %get-tuple-element.48.refs_0_, f32[6,14,128]{2,1,0:T(8,128)S(1)} %get-tuple-element.49.refs_1_, f32[1,16,128]{2,1,0:T(8,128)S(1)} %get-tuple-element.77.refs_2_, f32[1,16,128]{2,1,0:T(8,128)S(1)} %get-tuple-element.76.refs_3_, ...), custom_call_target="tpu_custom_call" | custom-call | tf_op jit(solution)/shard_map/push/pallas_call | solution.py:561
  (84 shorter events, 33.0 us)
Async XLA Ops:
  6.1 4.4 %collective-permute-start.6 = (f32[2,16,8,128]{3,2,1,0:T(8,128)S(1)}, f32[2,16,8,128]{3,2,1,0:T(8,128)S(1)}, u32[]{:S(2)}, u32[]{:S(2)}) collective-permute-start(f32[2,16,8,128]{3,2,1,0:T(8,128)S(1)} %get-tuple-element.56), channel_id=1, source_target_pairs={{0,4},{8,12},{16,20},{24,28},{4,0},{12,8},{20,16},{28,24},{1,5},{9... | collective-permute-start | bytes 393224 | tf_op jit(solution)/shard_map/ppermute | solution.py:91
  7.4 6.6 %collective-permute-start.5 = (f32[2,16,8,128]{3,2,1,0:T(8,128)S(1)}, f32[2,16,8,128]{3,2,1,0:T(8,128)S(1)}, u32[]{:S(2)}, u32[]{:S(2)}) collective-permute-start(f32[2,16,8,128]{3,2,1,0:T(8,128)S(1)} %get-tuple-element.57), channel_id=1, source_target_pairs={{4,8},{12,16},{20,24},{8,4},{16,12},{24,20},{5,9},{13,17},{21,25},... | collective-permute-start | bytes 393224 | tf_op jit(solution)/shard_map/ppermute | solution.py:91
  14.1 17.2 %collective-permute-start.8 = (f32[12,2,8,128]{3,2,1,0:T(8,128)S(1)}, f32[12,2,8,128]{3,2,1,0:T(8,128)S(1)}, u32[]{:S(2)}, u32[]{:S(2)}) collective-permute-start(f32[12,2,8,128]{3,2,1,0:T(8,128)S(1)} %get-tuple-element.62), channel_id=1, source_target_pairs={{0,1},{2,3},{1,0},{3,2},{4,5},{6,7},{5,4},{7,6},{8,9},{10,11},{9,8... | collective-permute-start | bytes 294920 | tf_op jit(solution)/shard_map/ppermute | solution.py:91
  16.2 15.0 %collective-permute-start.7 = (f32[12,2,8,128]{3,2,1,0:T(8,128)S(1)}, f32[12,2,8,128]{3,2,1,0:T(8,128)S(1)}, u32[]{:S(2)}, u32[]{:S(2)}) collective-permute-start(f32[12,2,8,128]{3,2,1,0:T(8,128)S(1)} %get-tuple-element.63), channel_id=1, source_target_pairs={{1,2},{2,1},{5,6},{6,5},{9,10},{10,9},{13,14},{14,13},{17,18},{18,... | collective-permute-start | bytes 294920 | tf_op jit(solution)/shard_map/ppermute | solution.py:91
  20.5 2.5 %collective-permute-start.1 = (f32[8,128]{1,0:T(8,128)S(1)}, f32[8,128]{1,0:T(8,128)S(1)}, u32[]{:S(2)}, u32[]{:S(2)}) collective-permute-start(f32[8,128]{1,0:T(8,128)S(1)} %max.15), channel_id=1, source_target_pairs={{0,2},{1,3},{2,0},{3,1},{4,6},{5,7},{6,4},{7,5},{8,10},{9,11},{10,... | collective-permute-start | bytes 12296 | tf_op jit(solution)/shard_map/ppermute | solution.py:167
  23.0 2.5 %collective-permute-start.2 = (f32[8,128]{1,0:T(8,128)S(1)}, f32[8,128]{1,0:T(8,128)S(1)}, u32[]{:S(2)}, u32[]{:S(2)}) collective-permute-start(f32[8,128]{1,0:T(8,128)S(1)} %max.16), channel_id=1, source_target_pairs={{0,4},{4,0},{8,12},{12,8},{16,20},{20,16},{24,28},{28,24},{1,5},{5... | collective-permute-start | bytes 12296 | tf_op jit(solution)/shard_map/ppermute | solution.py:167
  25.5 2.5 %collective-permute-start.3 = (f32[8,128]{1,0:T(8,128)S(1)}, f32[8,128]{1,0:T(8,128)S(1)}, u32[]{:S(2)}, u32[]{:S(2)}) collective-permute-start(f32[8,128]{1,0:T(8,128)S(1)} %max.17), channel_id=1, source_target_pairs={{0,8},{4,12},{8,0},{12,4},{16,24},{20,28},{24,16},{28,20},{1,9},{5... | collective-permute-start | bytes 12296 | tf_op jit(solution)/shard_map/ppermute | solution.py:167
  27.9 3.4 %collective-permute-start.4 = (f32[8,128]{1,0:T(8,128)S(1)}, f32[8,128]{1,0:T(8,128)S(1)}, u32[]{:S(2)}, u32[]{:S(2)}) collective-permute-start(f32[8,128]{1,0:T(8,128)S(1)} %max.18), channel_id=1, source_target_pairs={{0,16},{4,20},{8,24},{12,28},{16,0},{20,4},{24,8},{28,12},{1,17},{... | collective-permute-start | bytes 12296 | tf_op jit(solution)/shard_map/ppermute | solution.py:167
  117.8 3.3 %collective-permute-start.10 = (f32[1,16,128]{2,1,0:T(8,128)S(1)}, f32[1,16,128]{2,1,0:T(8,128)S(1)}, u32[]{:S(2)}, u32[]{:S(2)}) collective-permute-start(f32[1,16,128]{2,1,0:T(8,128)S(1)} %get-tuple-element.74), channel_id=1, source_target_pairs={{0,4},{8,12},{16,20},{24,28},{4,0},{12,8},{20,16},{28,24},{1,5},{9... | collective-permute-start | bytes 24584 | tf_op jit(solution)/shard_map/ppermute | solution.py:91
  118.1 5.3 %collective-permute-start.9 = (f32[1,16,128]{2,1,0:T(8,128)S(1)}, f32[1,16,128]{2,1,0:T(8,128)S(1)}, u32[]{:S(2)}, u32[]{:S(2)}) collective-permute-start(f32[1,16,128]{2,1,0:T(8,128)S(1)} %get-tuple-element.75), channel_id=1, source_target_pairs={{4,8},{12,16},{20,24},{8,4},{16,12},{24,20},{5,9},{13,17},{21,25},... | collective-permute-start | bytes 24584 | tf_op jit(solution)/shard_map/ppermute | solution.py:91
  123.4 26.6 %collective-permute-start.12 = (f32[10,1,128]{2,1,0:T(1,128)S(1)}, f32[10,1,128]{2,1,0:T(1,128)S(1)}, u32[]{:S(2)}, u32[]{:S(2)}) collective-permute-start(f32[10,1,128]{2,1,0:T(1,128)S(1)} %get-tuple-element.98), channel_id=1, source_target_pairs={{0,1},{2,3},{1,0},{3,2},{4,5},{6,7},{5,4},{7,6},{8,9},{10,11},{9,8... | collective-permute-start | bytes 15368 | tf_op jit(solution)/shard_map/ppermute | solution.py:91
  129.7 20.3 %collective-permute-start.11 = (f32[10,1,128]{2,1,0:T(1,128)S(1)}, f32[10,1,128]{2,1,0:T(1,128)S(1)}, u32[]{:S(2)}, u32[]{:S(2)}) collective-permute-start(f32[10,1,128]{2,1,0:T(1,128)S(1)} %get-tuple-element.99), channel_id=1, source_target_pairs={{1,2},{2,1},{5,6},{6,5},{9,10},{10,9},{13,14},{14,13},{17,18},{18,... | collective-permute-start | bytes 15368 | tf_op jit(solution)/shard_map/ppermute | solution.py:91
  152.7 3.3 %collective-permute-start.14 = (f32[1,16,128]{2,1,0:T(8,128)S(1)}, f32[1,16,128]{2,1,0:T(8,128)S(1)}, u32[]{:S(2)}, u32[]{:S(2)}) collective-permute-start(f32[1,16,128]{2,1,0:T(8,128)S(1)} %get-tuple-element.72), channel_id=1, source_target_pairs={{0,4},{8,12},{16,20},{24,28},{4,0},{12,8},{20,16},{28,24},{1,5},{9... | collective-permute-start | bytes 24584 | tf_op jit(solution)/shard_map/ppermute | solution.py:91
  154.0 5.3 %collective-permute-start.13 = (f32[1,16,128]{2,1,0:T(8,128)S(1)}, f32[1,16,128]{2,1,0:T(8,128)S(1)}, u32[]{:S(2)}, u32[]{:S(2)}) collective-permute-start(f32[1,16,128]{2,1,0:T(8,128)S(1)} %get-tuple-element.73), channel_id=1, source_target_pairs={{4,8},{12,16},{20,24},{8,4},{16,12},{24,20},{5,9},{13,17},{21,25},... | collective-permute-start | bytes 24584 | tf_op jit(solution)/shard_map/ppermute | solution.py:91
  159.3 8.8 %collective-permute-start.16 = (f32[10,1,128]{2,1,0:T(1,128)S(1)}, f32[10,1,128]{2,1,0:T(1,128)S(1)}, u32[]{:S(2)}, u32[]{:S(2)}) collective-permute-start(f32[10,1,128]{2,1,0:T(1,128)S(1)} %get-tuple-element.94), channel_id=1, source_target_pairs={{0,1},{2,3},{1,0},{3,2},{4,5},{6,7},{5,4},{7,6},{8,9},{10,11},{9,8... | collective-permute-start | bytes 15368 | tf_op jit(solution)/shard_map/ppermute | solution.py:91
  159.4 8.7 %collective-permute-start.15 = (f32[10,1,128]{2,1,0:T(1,128)S(1)}, f32[10,1,128]{2,1,0:T(1,128)S(1)}, u32[]{:S(2)}, u32[]{:S(2)}) collective-permute-start(f32[10,1,128]{2,1,0:T(1,128)S(1)} %get-tuple-element.95), channel_id=1, source_target_pairs={{1,2},{2,1},{5,6},{6,5},{9,10},{10,9},{13,14},{14,13},{17,18},{18,... | collective-permute-start | bytes 15368 | tf_op jit(solution)/shard_map/ppermute | solution.py:91
  170.8 3.3 %collective-permute-start.18 = (f32[1,16,128]{2,1,0:T(8,128)S(1)}, f32[1,16,128]{2,1,0:T(8,128)S(1)}, u32[]{:S(2)}, u32[]{:S(2)}) collective-permute-start(f32[1,16,128]{2,1,0:T(8,128)S(1)} %get-tuple-element.70), channel_id=1, source_target_pairs={{0,4},{8,12},{16,20},{24,28},{4,0},{12,8},{20,16},{28,24},{1,5},{9... | collective-permute-start | bytes 24584 | tf_op jit(solution)/shard_map/ppermute | solution.py:91
  171.2 5.3 %collective-permute-start.17 = (f32[1,16,128]{2,1,0:T(8,128)S(1)}, f32[1,16,128]{2,1,0:T(8,128)S(1)}, u32[]{:S(2)}, u32[]{:S(2)}) collective-permute-start(f32[1,16,128]{2,1,0:T(8,128)S(1)} %get-tuple-element.71), channel_id=1, source_target_pairs={{4,8},{12,16},{20,24},{8,4},{16,12},{24,20},{5,9},{13,17},{21,25},... | collective-permute-start | bytes 24584 | tf_op jit(solution)/shard_map/ppermute | solution.py:91
  176.5 7.7 %collective-permute-start.20 = (f32[10,1,128]{2,1,0:T(1,128)S(1)}, f32[10,1,128]{2,1,0:T(1,128)S(1)}, u32[]{:S(2)}, u32[]{:S(2)}) collective-permute-start(f32[10,1,128]{2,1,0:T(1,128)S(1)} %get-tuple-element.90), channel_id=1, source_target_pairs={{0,1},{2,3},{1,0},{3,2},{4,5},{6,7},{5,4},{7,6},{8,9},{10,11},{9,8... | collective-permute-start | bytes 15368 | tf_op jit(solution)/shard_map/ppermute | solution.py:91
  176.6 7.6 %collective-permute-start.19 = (f32[10,1,128]{2,1,0:T(1,128)S(1)}, f32[10,1,128]{2,1,0:T(1,128)S(1)}, u32[]{:S(2)}, u32[]{:S(2)}) collective-permute-start(f32[10,1,128]{2,1,0:T(1,128)S(1)} %get-tuple-element.91), channel_id=1, source_target_pairs={{1,2},{2,1},{5,6},{6,5},{9,10},{10,9},{13,14},{14,13},{17,18},{18,... | collective-permute-start | bytes 15368 | tf_op jit(solution)/shard_map/ppermute | solution.py:91
  186.9 3.3 %collective-permute-start.22 = (f32[1,16,128]{2,1,0:T(8,128)S(1)}, f32[1,16,128]{2,1,0:T(8,128)S(1)}, u32[]{:S(2)}, u32[]{:S(2)}) collective-permute-start(f32[1,16,128]{2,1,0:T(8,128)S(1)} %get-tuple-element.68), channel_id=1, source_target_pairs={{0,4},{8,12},{16,20},{24,28},{4,0},{12,8},{20,16},{28,24},{1,5},{9... | collective-permute-start | bytes 24584 | tf_op jit(solution)/shard_map/ppermute | solution.py:91
  188.2 5.3 %collective-permute-start.21 = (f32[1,16,128]{2,1,0:T(8,128)S(1)}, f32[1,16,128]{2,1,0:T(8,128)S(1)}, u32[]{:S(2)}, u32[]{:S(2)}) collective-permute-start(f32[1,16,128]{2,1,0:T(8,128)S(1)} %get-tuple-element.69), channel_id=1, source_target_pairs={{4,8},{12,16},{20,24},{8,4},{16,12},{24,20},{5,9},{13,17},{21,25},... | collective-permute-start | bytes 24584 | tf_op jit(solution)/shard_map/ppermute | solution.py:91
  193.5 20.9 %collective-permute-start.24 = (f32[10,1,128]{2,1,0:T(1,128)S(1)}, f32[10,1,128]{2,1,0:T(1,128)S(1)}, u32[]{:S(2)}, u32[]{:S(2)}) collective-permute-start(f32[10,1,128]{2,1,0:T(1,128)S(1)} %get-tuple-element.86), channel_id=1, source_target_pairs={{0,1},{2,3},{1,0},{3,2},{4,5},{6,7},{5,4},{7,6},{8,9},{10,11},{9,8... | collective-permute-start | bytes 15368 | tf_op jit(solution)/shard_map/ppermute | solution.py:91
  193.6 20.8 %collective-permute-start.23 = (f32[10,1,128]{2,1,0:T(1,128)S(1)}, f32[10,1,128]{2,1,0:T(1,128)S(1)}, u32[]{:S(2)}, u32[]{:S(2)}) collective-permute-start(f32[10,1,128]{2,1,0:T(1,128)S(1)} %get-tuple-element.87), channel_id=1, source_target_pairs={{1,2},{2,1},{5,6},{6,5},{9,10},{10,9},{13,14},{14,13},{17,18},{18,... | collective-permute-start | bytes 15368 | tf_op jit(solution)/shard_map/ppermute | solution.py:91
  (5 other events, 4.7 us)

commit v11 on v10

--- a/solution.py
+++ b/solution.py
@@ -12,6 +12,7 @@
 SPEED_EPS = 1e-06
 SOFT = 0.01
 CHUNK = 64
+BUFFERS = 4
 VMEM_LIMIT = 16 * 1024 * 1024
 
 X, Y, U, V, VOL, PRES, CODE = range(7)
@@ -31,8 +32,12 @@
     return pl.BlockSpec(array.shape, lambda group: (0,) * array.ndim)
 
 
-def side_by_side(blocks):
-    return jnp.concatenate([blocks[k] for k in range(9)], axis=1)
+def side_by_side(*blocks):
+    return jnp.concatenate([part[k] for part in blocks for k in range(part.shape[0])], axis=1)
+
+
+def thirds(size, width):
+    return [pl.BlockSpec((None, size, 3, width, width), lambda group, i=i: (group, 0, i, 0, 0)) for i in range(3)]
 
 
 def row_index(width):
@@ -215,13 +220,13 @@
     return lax.dot_general(left, right, (((1,), (1,)), ((), ())), preferred_element_type=jnp.float32)
 
 
-def setup_kernel(source, coef, edge_weight, inner_weight, fresh, xcol, ycol, out_a, out_b, sem):
+def setup_kernel(source, coef, edge_weight, inner_weight, fresh, xcol, ycol, sem, *outs):
     pltpu.sync_copy(source, fresh)
     for edge, weight in ((True, edge_weight), (False, inner_weight)):
-        setup_list(edge, fresh, coef, weight, xcol, ycol, out_a, out_b, sem)
-
-
-def setup_list(edge, fresh, coef, weight, xcol, ycol, out_a, out_b, sem):
+        setup_list(edge, fresh, coef, weight, xcol, ycol, sem, outs)
+
+
+def setup_list(edge, fresh, coef, weight, xcol, ycol, sem, outs):
     groups, size, _, width, _ = weight.shape
     rows, cols = fresh.shape[0] - 2, fresh.shape[1] - 2
     base = first_of(edge, rows, cols)
@@ -261,37 +266,34 @@
                 out[k, span] = weights
                 values[k, span] = weights * ratio
 
-    def copy_out(bin_id, out, slot):
+    def copies(bin_id, slot):
         target = weight.at[bin_id // size, lax.rem(bin_id, size)]
-        return pltpu.make_async_copy(out, target, sem.at[slot])
+        third = [pl.ds(3 * i, 3) for i in range(3)]
+        return [pltpu.make_async_copy(outs[slot].at[at], target.at[at], sem.at[slot, i]) for i, at in enumerate(third)]
 
     count = groups * size
     columns(0, 0)
     columns(1, 1)
 
-    def two_bins(step, carry):
-        even = 2 * step
-
-        @pl.when(step > 0)
-        def _():
-            copy_out(even - 2, out_a, 0).wait()
-
-        blocks(even, 0, out_a)
-        columns(jnp.minimum(even + 2, count - 1), 0)
-        copy_out(even, out_a, 0).start()
-
-        @pl.when(step > 0)
-        def _():
-            copy_out(even - 1, out_b, 1).wait()
-
-        blocks(even + 1, 1, out_b)
-        columns(jnp.minimum(even + 3, count - 1), 1)
-        copy_out(even + 1, out_b, 1).start()
+    def some_bins(step, carry):
+        for slot in range(BUFFERS):
+            bin_id = BUFFERS * step + slot
+
+            @pl.when(step > 0)
+            def _():
+                for copy in copies(bin_id - BUFFERS, slot):
+                    copy.wait()
+
+            blocks(bin_id, slot % 2, outs[slot])
+            columns(jnp.minimum(bin_id + 2, count - 1), slot % 2)
+            for copy in copies(bin_id, slot):
+                copy.start()
         return carry
 
-    lax.fori_loop(0, count // 2, two_bins, 0)
-    copy_out(count - 2, out_a, 0).wait()
-    copy_out(count - 1, out_b, 1).wait()
+    lax.fori_loop(0, count // BUFFERS, some_bins, 0)
+    for slot in range(BUFFERS):
+        for copy in copies(count - BUFFERS + slot, slot):
+            copy.wait()
 
 
 def setup(fresh):
@@ -311,15 +313,14 @@
             pltpu.VMEM(fresh.shape, jnp.float32),
             pltpu.VMEM((2, width, width), jnp.float32),
             pltpu.VMEM((2, width, width), jnp.float32),
-            pltpu.VMEM((9, width, width), jnp.bfloat16),
-            pltpu.VMEM((9, width, width), jnp.bfloat16),
-            pltpu.SemaphoreType.DMA((2,)),
-        ],
+            pltpu.SemaphoreType.DMA((BUFFERS, 3)),
+        ]
+        + [pltpu.VMEM((9, width, width), jnp.bfloat16)] * BUFFERS,
         name="setup",
     )(in_hbm(fresh))
 
 
-def first_kernel(kappa, edge, fresh, coef, weight, sums, pv, *rest):
+def first_kernel(kappa, edge, fresh, coef, weight, second, third, sums, pv, *rest):
     feat = rest[-1]
     group = pl.program_id(0)
     size, _, width, _ = weight.shape
@@ -359,7 +360,7 @@
                 features = features + float(off_y) * feat[row + k // 3, col + k % 3, 2]
             around.append(split(features))
         around = jnp.concatenate(around, axis=1)
-        total_w = dot_nt(side_by_side(weight.at[index]), around)
+        total_w = dot_nt(side_by_side(*(part.at[index] for part in (weight, second, third))), around)
         total_c = dot_nt(side_by_side(coef.at[base + group * size + index]), around)
         total_w = (total_w[:, :8] + total_w[:, 8:]).T
         total_c = (total_c[:, :8] + total_c[:, 8:]).T
@@ -390,7 +391,7 @@
     return call(
         functools.partial(first_kernel, kappa, edge),
         grid=(groups,),
-        in_specs=[once(fresh), vmem, pl.BlockSpec((None, size, 9, width, width), lambda group: (group, 0, 0, 0, 0))],
+        in_specs=[once(fresh), vmem, *thirds(size, width)],
         out_specs=[vmem] * (4 if edge else 2),
         out_shape=[
             pltpu.VMEM((3, groups, size, width), jnp.float32),
@@ -399,7 +400,7 @@
         + [pltpu.VMEM((rows - 2, 1, width), jnp.float32)] * (2 if edge else 0),
         scratch_shapes=[pltpu.VMEM((rows, cols, 3, 8, width), jnp.float32)],
         name="first_sweep",
-    )(in_hbm(fresh), pltpu.with_memory_space_constraint(coef, pltpu.VMEM), in_hbm(weight))
+    )(in_hbm(fresh), pltpu.with_memory_space_constraint(coef, pltpu.VMEM), *[in_hbm(weight)] * 3)
 
 
 def sweep_kernel(kappa, last, edge, rows, cols, count, *refs):
@@ -473,8 +474,8 @@
 
 
 def push_kernel(kappa, edge, count, *refs):
-    before_edge, before_inner, *halo = refs[: count - (5 if edge else 3)]
-    fresh, weight, pressure = refs[count - (5 if edge else 3) : count][:3]
+    before_edge, before_inner, *halo = refs[: count - (7 if edge else 5)]
+    fresh, weight, second, third, pressure = refs[count - (7 if edge else 5) : count][:5]
     ext, feat = refs[-2:]
     group = pl.program_id(0)
     size, _, width, _ = weight.shape
@@ -514,7 +515,7 @@
             if off_y:
                 tile = tile + jnp.where(feature == 2, off_y * pv, jnp.where(feature == 6, off_y * vol, 0.0))
             around.append(split(tile))
-        total = dot_nt(side_by_side(weight.at[index]), jnp.concatenate(around, axis=1))
+        total = dot_nt(side_by_side(*(part.at[index] for part in (weight, second, third))), jnp.concatenate(around, axis=1))
         total = (total[:, :8] + total[:, 8:]).T
         tile = fresh[row + 1, col + 1]
         own = pressure[group, index : index + 1, :]
@@ -545,12 +546,10 @@
     rows, cols = fresh.shape[:2]
     vmem = pl.BlockSpec(memory_space=pltpu.VMEM)
     weight = in_hbm(weight)
-    args = (*pv, *(halo if edge else ()), in_hbm(fresh), weight, pressure, *(inner if edge else ()))
+    args = (*pv, *(halo if edge else ()), in_hbm(fresh), *[weight] * 3, pressure, *(inner if edge else ()))
     specs = [vmem] * len(args)
-    specs[len(pv) + (len(halo) if edge else 0)] = once(fresh)
-    specs[len(pv) + (len(halo) if edge else 0) + 1] = pl.BlockSpec(
-        (None, size, 9, width, width), lambda group: (group, 0, 0, 0, 0)
-    )
+    first = len(pv) + (len(halo) if edge else 0)
+    specs[first : first + 4] = [once(fresh), *thirds(size, width)]
     if edge:
         outs = [
             jax.ShapeDtypeStruct((rows - 2, cols - 2, width), jnp.float32),

time: 224 us -> 202 us (0.902)
  Pallas kernels: 147 us -> 125 us
    pallas_call x1, Pallas kernels: 72.1 us -> 49.9 us  [setup(): call(setup_kernel, in_specs=[hbm], out_specs=(vmem, hbm, hbm), out_shape=...]
  transfers between devices with their start and end apart: 25 -> 25, of which waited for: 11 -> 11; matrix products, arithmetic and copies ran while one was open for 0% -> 0% of each run, Pallas kernels for 19% -> 22%
where the time goes in v11:
time: 202 us
  Pallas kernels  125 us (62%)
  starting transfers between devices  44.4 us (22%)
  waiting for transfers between devices  25.5 us (13%)
  local copies, waits for them, and re-layouts  5.15 us (3%)
    pallas_call x1, Pallas kernels, setup(): call(setup_kernel, in_specs=[hbm], out_specs=(vmem, hbm, hbm), out_shape=...  49.9 us
    ppermute x20, starting transfers between devices, swap(): return lax.ppermute(value, axis, pairs + [(j, i) for i, j in pairs])  42.4 us
    pallas_call x2, Pallas kernels, first_sweep(): call(functools.partial(first_kernel, kappa, edge), grid=(groups,), in_spe...  29.8 us
    pallas_call x2, Pallas kernels, push(): call(functools.partial(push_kernel, kappa, edge, len(args)), grid=(groups...  22.2 us
    pallas_call x6, Pallas kernels, sweep(): call(functools.partial(sweep_kernel, kappa, last, edge, rows, cols, len(a...  20.2 us
    ppermute x20, waiting for transfers between devices, swap(): return lax.ppermute(value, axis, pairs + [(j, i) for i, j in pairs])  15.6 us
    ppermute x5, waiting for transfers between devices, largest(): value = jnp.maximum(value, lax.ppermute(value, axis, pairs))  9.96 us
  transfers between devices with their start and end apart: 25, of which 11 were waited for; matrix products, arithmetic and copies ran while one was open for 0% of the time, Pallas kernels for 22%

profile of v11, /device:TPU:17, one launch (start us, length us, event | category | flops | bytes accessed | tf_op | source)
XLA Modules:
  0.0 201.5 jit_solution(17517217467415690427)
XLA Ops:
  10.6 3.4 %collective-permute-done.5 = f32[2,16,8,128]{3,2,1,0:T(8,128)S(1)} collective-permute-done((f32[2,16,8,128]{3,2,1,0:T(8,128)S(1)}, f32[2,16,8,128]{3,2,1,0:T(8,128)S(1)}, u32[]{:S(2)}, u32[]{:S(2)}) %collective-permute-start.5) | collective-permute-done | bytes 131104 | tf_op jit(solution)/shard_map/ppermute | solution.py:96
  16.2 3.0 %collective-permute-start.7 = (f32[12,2,8,128]{3,2,1,0:T(8,128)S(1)}, f32[12,2,8,128]{3,2,1,0:T(8,128)S(1)}, u32[]{:S(2)}, u32[]{:S(2)}) collective-permute-start(f32[12,2,8,128]{3,2,1,0:T(8,128)S(1)} %get-tuple-element.63), channel_id=1, source_target_pairs={{1,2},{2,1},{5,6},{6,5},{9,10},{10,9},{13,14},{14,13},{17,18},{18,... | collective-permute-start | bytes 294920 | tf_op jit(solution)/shard_map/ppermute | solution.py:96
  27.9 3.4 %collective-permute-done.4 = f32[8,128]{1,0:T(8,128)S(1)} collective-permute-done((f32[8,128]{1,0:T(8,128)S(1)}, f32[8,128]{1,0:T(8,128)S(1)}, u32[]{:S(2)}, u32[]{:S(2)}) %collective-permute-start.4) | collective-permute-done | bytes 4128 | tf_op jit(solution)/shard_map/ppermute | solution.py:172
  31.3 2.6 %drift.1.source.fresh.refs_2_.refs_6_ = f32[10,18,8,128]{3,2,1,0:T(8,128)} custom-call(f32[8,128]{1,0:T(8,128)S(1)} %max.19.top, f32[8,16,8,128]{3,2,1,0:T(8,128)S(1)} %get-tuple-element.30.center, f32[2,16,8,128]{3,2,1,0:T(8,128)S(1)} %get-tuple-element.59.above, f32[2,16,8,128]{3,2,1,0:T(8,128)S(1)} %get-tuple-element.58.below, ...), custom_call_target="tpu_custom_call" | custom-call | tf_op jit(solution)/shard_map/drift/pallas_call | solution.py:210
  33.9 49.9 %setup.1 = (bf16[132,9,128,128]{3,2,1,0:T(8,128)(2,1)S(1)}, bf16[3,16,9,128,128]{4,3,2,1,0:T(8,128)(2,1)}, bf16[6,14,9,128,128]{4,3,2,1,0:T(8,128)(2,1)}) custom-call(f32[10,18,8,128]{3,2,1,0:T(8,128)} %drift.1.source.fresh.refs_2_.refs_6_), custom_call_target="tpu_custom_call" | custom-call | tf_op jit(solution)/shard_map/setup/pallas_call | solution.py:303
  83.8 11.8 %first_sweep.2 = (f32[3,3,16,128]{3,2,1,0:T(8,128)S(1)}, f32[3,16,128]{2,1,0:T(8,128)S(1)}, f32[8,1,128]{2,1,0:T(1,128)S(1)}, f32[8,1,128]{2,1,0:T(1,128)S(1)}) custom-call(f32[10,18,8,128]{3,2,1,0:T(8,128)} %drift.1.source.fresh.refs_2_.refs_6_, bf16[132,9,128,128]{3,2,1,0:T(8,128)(2,1)S(1)} %get-tuple-element.33.coef.refs_6_.refs_2_, ...), custom_call_target="tpu_custom_call" | custom-call | tf_op jit(solution)/shard_map/first_sweep/pallas_call | solution.py:391
  96.0 3.0 %collective-permute-start.9 = (f32[1,16,128]{2,1,0:T(8,128)S(1)}, f32[1,16,128]{2,1,0:T(8,128)S(1)}, u32[]{:S(2)}, u32[]{:S(2)}) collective-permute-start(f32[1,16,128]{2,1,0:T(8,128)S(1)} %get-tuple-element.75), channel_id=1, source_target_pairs={{4,8},{12,16},{20,24},{8,4},{16,12},{24,20},{5,9},{13,17},{21,25},... | collective-permute-start | bytes 24584 | tf_op jit(solution)/shard_map/ppermute | solution.py:96
  101.3 6.3 %collective-permute-start.12 = (f32[10,1,128]{2,1,0:T(1,128)S(1)}, f32[10,1,128]{2,1,0:T(1,128)S(1)}, u32[]{:S(2)}, u32[]{:S(2)}) collective-permute-start(f32[10,1,128]{2,1,0:T(1,128)S(1)} %get-tuple-element.98), channel_id=1, source_target_pairs={{0,1},{2,3},{1,0},{3,2},{4,5},{6,7},{5,4},{7,6},{8,9},{10,11},{9,8... | collective-permute-start | bytes 15368 | tf_op jit(solution)/shard_map/ppermute | solution.py:96
  107.6 2.4 %collective-permute-start.11 = (f32[10,1,128]{2,1,0:T(1,128)S(1)}, f32[10,1,128]{2,1,0:T(1,128)S(1)}, u32[]{:S(2)}, u32[]{:S(2)}) collective-permute-start(f32[10,1,128]{2,1,0:T(1,128)S(1)} %get-tuple-element.99), channel_id=1, source_target_pairs={{1,2},{2,1},{5,6},{6,5},{9,10},{10,9},{13,14},{14,13},{17,18},{18,... | collective-permute-start | bytes 15368 | tf_op jit(solution)/shard_map/ppermute | solution.py:96
  109.9 18.0 %first_sweep.3 = (f32[3,6,14,128]{3,2,1,0:T(8,128)S(1)}, f32[6,14,128]{2,1,0:T(8,128)S(1)}) custom-call(f32[10,18,8,128]{3,2,1,0:T(8,128)} %drift.1.source.fresh.refs_2_.refs_6_, bf16[132,9,128,128]{3,2,1,0:T(8,128)(2,1)S(1)} %get-tuple-element.33.coef.refs_6_.refs_2_, ...), custom_call_target="tpu_custom_call" | custom-call | tf_op jit(solution)/shard_map/first_sweep/pallas_call | solution.py:391
  128.0 2.6 %sweep.6 = (f32[3,16,128]{2,1,0:T(8,128)S(1)}, f32[8,1,128]{2,1,0:T(1,128)S(1)}, f32[8,1,128]{2,1,0:T(1,128)S(1)}) custom-call(f32[3,16,128]{2,1,0:T(8,128)S(1)} %get-tuple-element.35.refs_0_, f32[6,14,128]{2,1,0:T(8,128)S(1)} %get-tuple-element.37.refs_1_, f32[1,16,128]{2,1,0:T(8,128)S(1)} %get-tuple-element.83.refs_2_, ...), custom_call_target="tpu_custom_call" | custom-call | tf_op jit(solution)/shard_map/sweep/pallas_call | solution.py:463
  134.0 3.2 %collective-permute-done.13 = f32[1,16,128]{2,1,0:T(8,128)S(1)} collective-permute-done((f32[1,16,128]{2,1,0:T(8,128)S(1)}, f32[1,16,128]{2,1,0:T(8,128)S(1)}, u32[]{:S(2)}, u32[]{:S(2)}) %collective-permute-start.13) | collective-permute-done | bytes 8224 | tf_op jit(solution)/shard_map/ppermute | solution.py:96
  137.3 4.8 %collective-permute-start.15 = (f32[10,1,128]{2,1,0:T(1,128)S(1)}, f32[10,1,128]{2,1,0:T(1,128)S(1)}, u32[]{:S(2)}, u32[]{:S(2)}) collective-permute-start(f32[10,1,128]{2,1,0:T(1,128)S(1)} %get-tuple-element.95), channel_id=1, source_target_pairs={{1,2},{2,1},{5,6},{6,5},{9,10},{10,9},{13,14},{14,13},{17,18},{18,... | collective-permute-start | bytes 15368 | tf_op jit(solution)/shard_map/ppermute | solution.py:96
  142.1 4.1 %sweep.7.refs_1_ = f32[6,14,128]{2,1,0:T(8,128)S(1)} custom-call(f32[3,16,128]{2,1,0:T(8,128)S(1)} %get-tuple-element.35.refs_0_, f32[6,14,128]{2,1,0:T(8,128)S(1)} %get-tuple-element.37.refs_1_, bf16[132,9,128,128]{3,2,1,0:T(8,128)(2,1)S(1)} %get-tuple-element.33.coef.refs_6_.refs_2_, f32[3,6,14,128]{3,2,1,0:T(8,128)S(1)} %get-tuple-element.42.refs_3_), custom_call_target="tpu_custom_call" | custom-call | tf_op jit(solution)/shard_map/sweep/pallas_call | solution.py:463
  146.3 2.6 %sweep.8 = (f32[3,16,128]{2,1,0:T(8,128)S(1)}, f32[8,1,128]{2,1,0:T(1,128)S(1)}, f32[8,1,128]{2,1,0:T(1,128)S(1)}) custom-call(f32[3,16,128]{2,1,0:T(8,128)S(1)} %get-tuple-element.41.refs_0_, f32[6,14,128]{2,1,0:T(8,128)S(1)} %sweep.7.refs_1_, f32[1,16,128]{2,1,0:T(8,128)S(1)} %get-tuple-element.81.refs_2_, f32[1,16,128]{2,1,0:T(8,128)S(1)} %get-tuple-element.80.refs_3_, ...), custom_call_target="tpu_custom_call" | custom-call | tf_op jit(solution)/shard_map/sweep/pallas_call | solution.py:463
  149.3 3.0 %collective-permute-start.17 = (f32[1,16,128]{2,1,0:T(8,128)S(1)}, f32[1,16,128]{2,1,0:T(8,128)S(1)}, u32[]{:S(2)}, u32[]{:S(2)}) collective-permute-start(f32[1,16,128]{2,1,0:T(8,128)S(1)} %get-tuple-element.71), channel_id=1, source_target_pairs={{4,8},{12,16},{20,24},{8,4},{16,12},{24,20},{5,9},{13,17},{21,25},... | collective-permute-start | bytes 24584 | tf_op jit(solution)/shard_map/ppermute | solution.py:96
  154.7 3.4 %collective-permute-start.19 = (f32[10,1,128]{2,1,0:T(1,128)S(1)}, f32[10,1,128]{2,1,0:T(1,128)S(1)}, u32[]{:S(2)}, u32[]{:S(2)}) collective-permute-start(f32[10,1,128]{2,1,0:T(1,128)S(1)} %get-tuple-element.91), channel_id=1, source_target_pairs={{1,2},{2,1},{5,6},{6,5},{9,10},{10,9},{13,14},{14,13},{17,18},{18,... | collective-permute-start | bytes 15368 | tf_op jit(solution)/shard_map/ppermute | solution.py:96
  158.0 4.1 %sweep.9.refs_1_ = f32[6,14,128]{2,1,0:T(8,128)S(1)} custom-call(f32[3,16,128]{2,1,0:T(8,128)S(1)} %get-tuple-element.41.refs_0_, f32[6,14,128]{2,1,0:T(8,128)S(1)} %sweep.7.refs_1_, bf16[132,9,128,128]{3,2,1,0:T(8,128)(2,1)S(1)} %get-tuple-element.33.coef.refs_6_.refs_2_, f32[3,6,14,128]{3,2,1,0:T(8,128)S(1)} %get-tuple-element.42.refs_3_), custom_call_target="tpu_custom_call" | custom-call | tf_op jit(solution)/shard_map/sweep/pallas_call | solution.py:463
  162.2 2.6 %sweep.10 = (f32[3,16,128]{2,1,0:T(8,128)S(1)}, f32[8,1,128]{2,1,0:T(1,128)S(1)}, f32[8,1,128]{2,1,0:T(1,128)S(1)}, f32[3,16,128]{2,1,0:T(8,128)S(1)}) custom-call(f32[3,16,128]{2,1,0:T(8,128)S(1)} %get-tuple-element.45.refs_0_, f32[6,14,128]{2,1,0:T(8,128)S(1)} %sweep.9.refs_1_, f32[1,16,128]{2,1,0:T(8,128)S(1)} %get-tuple-element.79.refs_2_, ...), custom_call_target="tpu_custom_call" | custom-call | tf_op jit(solution)/shard_map/sweep/pallas_call | solution.py:463
  168.1 3.2 %collective-permute-done.21 = f32[1,16,128]{2,1,0:T(8,128)S(1)} collective-permute-done((f32[1,16,128]{2,1,0:T(8,128)S(1)}, f32[1,16,128]{2,1,0:T(8,128)S(1)}, u32[]{:S(2)}, u32[]{:S(2)}) %collective-permute-start.21) | collective-permute-done | bytes 8224 | tf_op jit(solution)/shard_map/ppermute | solution.py:96
  171.5 3.6 %collective-permute-start.23 = (f32[10,1,128]{2,1,0:T(1,128)S(1)}, f32[10,1,128]{2,1,0:T(1,128)S(1)}, u32[]{:S(2)}, u32[]{:S(2)}) collective-permute-start(f32[10,1,128]{2,1,0:T(1,128)S(1)} %get-tuple-element.87), channel_id=1, source_target_pairs={{1,2},{2,1},{5,6},{6,5},{9,10},{10,9},{13,14},{14,13},{17,18},{18,... | collective-permute-start | bytes 15368 | tf_op jit(solution)/shard_map/ppermute | solution.py:96
  175.1 4.1 %sweep.11 = (f32[6,14,128]{2,1,0:T(8,128)S(1)}, f32[6,14,128]{2,1,0:T(8,128)S(1)}) custom-call(f32[3,16,128]{2,1,0:T(8,128)S(1)} %get-tuple-element.45.refs_0_, f32[6,14,128]{2,1,0:T(8,128)S(1)} %sweep.9.refs_1_, bf16[132,9,128,128]{3,2,1,0:T(8,128)(2,1)S(1)} %get-tuple-element.33.coef.refs_6_.refs_2_, f32[3,6,14,128]{3,2,1,0:T(8,128)S(1)} %get-tuple-element.42.refs_3_), custom_call_target="tpu_custom_call" | custom-call | tf_op jit(solution)/shard_map/sweep/pallas_call | solution.py:463
  179.2 13.1 %push.2.refs_12_ = f32[2,6,14,128]{3,2,1,0:T(8,128)S(1)} custom-call(f32[3,16,128]{2,1,0:T(8,128)S(1)} %get-tuple-element.48.refs_0_, f32[6,14,128]{2,1,0:T(8,128)S(1)} %get-tuple-element.49.refs_1_, f32[10,18,8,128]{3,2,1,0:T(8,128)} %drift.1.source.fresh.refs_2_.refs_6_, ...), custom_call_target="tpu_custom_call" | custom-call | tf_op jit(solution)/shard_map/push/pallas_call | solution.py:560
  192.3 9.2 %push.3 = (f32[8,16,128]{2,1,0:T(8,128)}, f32[2,8,16,128]{3,2,1,0:T(8,128)}) custom-call(f32[3,16,128]{2,1,0:T(8,128)S(1)} %get-tuple-element.48.refs_0_, f32[6,14,128]{2,1,0:T(8,128)S(1)} %get-tuple-element.49.refs_1_, f32[1,16,128]{2,1,0:T(8,128)S(1)} %get-tuple-element.77.refs_2_, f32[1,16,128]{2,1,0:T(8,128)S(1)} %get-tuple-element.76.refs_3_, ...), custom_call_target="tpu_custom_call" | custom-call | tf_op jit(solution)/shard_map/push/pallas_call | solution.py:560
  (84 shorter events, 32.9 us)
Async XLA Ops:
  6.1 4.4 %collective-permute-start.6 = (f32[2,16,8,128]{3,2,1,0:T(8,128)S(1)}, f32[2,16,8,128]{3,2,1,0:T(8,128)S(1)}, u32[]{:S(2)}, u32[]{:S(2)}) collective-permute-start(f32[2,16,8,128]{3,2,1,0:T(8,128)S(1)} %get-tuple-element.56), channel_id=1, source_target_pairs={{0,4},{8,12},{16,20},{24,28},{4,0},{12,8},{20,16},{28,24},{1,5},{9... | collective-permute-start | bytes 393224 | tf_op jit(solution)/shard_map/ppermute | solution.py:96
  7.4 6.6 %collective-permute-start.5 = (f32[2,16,8,128]{3,2,1,0:T(8,128)S(1)}, f32[2,16,8,128]{3,2,1,0:T(8,128)S(1)}, u32[]{:S(2)}, u32[]{:S(2)}) collective-permute-start(f32[2,16,8,128]{3,2,1,0:T(8,128)S(1)} %get-tuple-element.57), channel_id=1, source_target_pairs={{4,8},{12,16},{20,24},{8,4},{16,12},{24,20},{5,9},{13,17},{21,25},... | collective-permute-start | bytes 393224 | tf_op jit(solution)/shard_map/ppermute | solution.py:96
  14.1 17.2 %collective-permute-start.8 = (f32[12,2,8,128]{3,2,1,0:T(8,128)S(1)}, f32[12,2,8,128]{3,2,1,0:T(8,128)S(1)}, u32[]{:S(2)}, u32[]{:S(2)}) collective-permute-start(f32[12,2,8,128]{3,2,1,0:T(8,128)S(1)} %get-tuple-element.62), channel_id=1, source_target_pairs={{0,1},{2,3},{1,0},{3,2},{4,5},{6,7},{5,4},{7,6},{8,9},{10,11},{9,8... | collective-permute-start | bytes 294920 | tf_op jit(solution)/shard_map/ppermute | solution.py:96
  16.2 15.0 %collective-permute-start.7 = (f32[12,2,8,128]{3,2,1,0:T(8,128)S(1)}, f32[12,2,8,128]{3,2,1,0:T(8,128)S(1)}, u32[]{:S(2)}, u32[]{:S(2)}) collective-permute-start(f32[12,2,8,128]{3,2,1,0:T(8,128)S(1)} %get-tuple-element.63), channel_id=1, source_target_pairs={{1,2},{2,1},{5,6},{6,5},{9,10},{10,9},{13,14},{14,13},{17,18},{18,... | collective-permute-start | bytes 294920 | tf_op jit(solution)/shard_map/ppermute | solution.py:96
  20.5 2.5 %collective-permute-start.1 = (f32[8,128]{1,0:T(8,128)S(1)}, f32[8,128]{1,0:T(8,128)S(1)}, u32[]{:S(2)}, u32[]{:S(2)}) collective-permute-start(f32[8,128]{1,0:T(8,128)S(1)} %max.15), channel_id=1, source_target_pairs={{0,2},{1,3},{2,0},{3,1},{4,6},{5,7},{6,4},{7,5},{8,10},{9,11},{10,... | collective-permute-start | bytes 12296 | tf_op jit(solution)/shard_map/ppermute | solution.py:172
  23.0 2.5 %collective-permute-start.2 = (f32[8,128]{1,0:T(8,128)S(1)}, f32[8,128]{1,0:T(8,128)S(1)}, u32[]{:S(2)}, u32[]{:S(2)}) collective-permute-start(f32[8,128]{1,0:T(8,128)S(1)} %max.16), channel_id=1, source_target_pairs={{0,4},{4,0},{8,12},{12,8},{16,20},{20,16},{24,28},{28,24},{1,5},{5... | collective-permute-start | bytes 12296 | tf_op jit(solution)/shard_map/ppermute | solution.py:172
  25.5 2.5 %collective-permute-start.3 = (f32[8,128]{1,0:T(8,128)S(1)}, f32[8,128]{1,0:T(8,128)S(1)}, u32[]{:S(2)}, u32[]{:S(2)}) collective-permute-start(f32[8,128]{1,0:T(8,128)S(1)} %max.17), channel_id=1, source_target_pairs={{0,8},{4,12},{8,0},{12,4},{16,24},{20,28},{24,16},{28,20},{1,9},{5... | collective-permute-start | bytes 12296 | tf_op jit(solution)/shard_map/ppermute | solution.py:172
  27.9 3.4 %collective-permute-start.4 = (f32[8,128]{1,0:T(8,128)S(1)}, f32[8,128]{1,0:T(8,128)S(1)}, u32[]{:S(2)}, u32[]{:S(2)}) collective-permute-start(f32[8,128]{1,0:T(8,128)S(1)} %max.18), channel_id=1, source_target_pairs={{0,16},{4,20},{8,24},{12,28},{16,0},{20,4},{24,8},{28,12},{1,17},{... | collective-permute-start | bytes 12296 | tf_op jit(solution)/shard_map/ppermute | solution.py:172
  95.7 3.3 %collective-permute-start.10 = (f32[1,16,128]{2,1,0:T(8,128)S(1)}, f32[1,16,128]{2,1,0:T(8,128)S(1)}, u32[]{:S(2)}, u32[]{:S(2)}) collective-permute-start(f32[1,16,128]{2,1,0:T(8,128)S(1)} %get-tuple-element.74), channel_id=1, source_target_pairs={{0,4},{8,12},{16,20},{24,28},{4,0},{12,8},{20,16},{28,24},{1,5},{9... | collective-permute-start | bytes 24584 | tf_op jit(solution)/shard_map/ppermute | solution.py:96
  96.0 5.3 %collective-permute-start.9 = (f32[1,16,128]{2,1,0:T(8,128)S(1)}, f32[1,16,128]{2,1,0:T(8,128)S(1)}, u32[]{:S(2)}, u32[]{:S(2)}) collective-permute-start(f32[1,16,128]{2,1,0:T(8,128)S(1)} %get-tuple-element.75), channel_id=1, source_target_pairs={{4,8},{12,16},{20,24},{8,4},{16,12},{24,20},{5,9},{13,17},{21,25},... | collective-permute-start | bytes 24584 | tf_op jit(solution)/shard_map/ppermute | solution.py:96
  101.3 26.6 %collective-permute-start.12 = (f32[10,1,128]{2,1,0:T(1,128)S(1)}, f32[10,1,128]{2,1,0:T(1,128)S(1)}, u32[]{:S(2)}, u32[]{:S(2)}) collective-permute-start(f32[10,1,128]{2,1,0:T(1,128)S(1)} %get-tuple-element.98), channel_id=1, source_target_pairs={{0,1},{2,3},{1,0},{3,2},{4,5},{6,7},{5,4},{7,6},{8,9},{10,11},{9,8... | collective-permute-start | bytes 15368 | tf_op jit(solution)/shard_map/ppermute | solution.py:96
  107.6 20.4 %collective-permute-start.11 = (f32[10,1,128]{2,1,0:T(1,128)S(1)}, f32[10,1,128]{2,1,0:T(1,128)S(1)}, u32[]{:S(2)}, u32[]{:S(2)}) collective-permute-start(f32[10,1,128]{2,1,0:T(1,128)S(1)} %get-tuple-element.99), channel_id=1, source_target_pairs={{1,2},{2,1},{5,6},{6,5},{9,10},{10,9},{13,14},{14,13},{17,18},{18,... | collective-permute-start | bytes 15368 | tf_op jit(solution)/shard_map/ppermute | solution.py:96
  130.6 3.3 %collective-permute-start.14 = (f32[1,16,128]{2,1,0:T(8,128)S(1)}, f32[1,16,128]{2,1,0:T(8,128)S(1)}, u32[]{:S(2)}, u32[]{:S(2)}) collective-permute-start(f32[1,16,128]{2,1,0:T(8,128)S(1)} %get-tuple-element.72), channel_id=1, source_target_pairs={{0,4},{8,12},{16,20},{24,28},{4,0},{12,8},{20,16},{28,24},{1,5},{9... | collective-permute-start | bytes 24584 | tf_op jit(solution)/shard_map/ppermute | solution.py:96
  131.9 5.3 %collective-permute-start.13 = (f32[1,16,128]{2,1,0:T(8,128)S(1)}, f32[1,16,128]{2,1,0:T(8,128)S(1)}, u32[]{:S(2)}, u32[]{:S(2)}) collective-permute-start(f32[1,16,128]{2,1,0:T(8,128)S(1)} %get-tuple-element.73), channel_id=1, source_target_pairs={{4,8},{12,16},{20,24},{8,4},{16,12},{24,20},{5,9},{13,17},{21,25},... | collective-permute-start | bytes 24584 | tf_op jit(solution)/shard_map/ppermute | solution.py:96
  137.2 9.0 %collective-permute-start.16 = (f32[10,1,128]{2,1,0:T(1,128)S(1)}, f32[10,1,128]{2,1,0:T(1,128)S(1)}, u32[]{:S(2)}, u32[]{:S(2)}) collective-permute-start(f32[10,1,128]{2,1,0:T(1,128)S(1)} %get-tuple-element.94), channel_id=1, source_target_pairs={{0,1},{2,3},{1,0},{3,2},{4,5},{6,7},{5,4},{7,6},{8,9},{10,11},{9,8... | collective-permute-start | bytes 15368 | tf_op jit(solution)/shard_map/ppermute | solution.py:96
  137.3 8.9 %collective-permute-start.15 = (f32[10,1,128]{2,1,0:T(1,128)S(1)}, f32[10,1,128]{2,1,0:T(1,128)S(1)}, u32[]{:S(2)}, u32[]{:S(2)}) collective-permute-start(f32[10,1,128]{2,1,0:T(1,128)S(1)} %get-tuple-element.95), channel_id=1, source_target_pairs={{1,2},{2,1},{5,6},{6,5},{9,10},{10,9},{13,14},{14,13},{17,18},{18,... | collective-permute-start | bytes 15368 | tf_op jit(solution)/shard_map/ppermute | solution.py:96
  148.9 3.3 %collective-permute-start.18 = (f32[1,16,128]{2,1,0:T(8,128)S(1)}, f32[1,16,128]{2,1,0:T(8,128)S(1)}, u32[]{:S(2)}, u32[]{:S(2)}) collective-permute-start(f32[1,16,128]{2,1,0:T(8,128)S(1)} %get-tuple-element.70), channel_id=1, source_target_pairs={{0,4},{8,12},{16,20},{24,28},{4,0},{12,8},{20,16},{28,24},{1,5},{9... | collective-permute-start | bytes 24584 | tf_op jit(solution)/shard_map/ppermute | solution.py:96
  149.3 5.3 %collective-permute-start.17 = (f32[1,16,128]{2,1,0:T(8,128)S(1)}, f32[1,16,128]{2,1,0:T(8,128)S(1)}, u32[]{:S(2)}, u32[]{:S(2)}) collective-permute-start(f32[1,16,128]{2,1,0:T(8,128)S(1)} %get-tuple-element.71), channel_id=1, source_target_pairs={{4,8},{12,16},{20,24},{8,4},{16,12},{24,20},{5,9},{13,17},{21,25},... | collective-permute-start | bytes 24584 | tf_op jit(solution)/shard_map/ppermute | solution.py:96
  154.6 7.5 %collective-permute-start.20 = (f32[10,1,128]{2,1,0:T(1,128)S(1)}, f32[10,1,128]{2,1,0:T(1,128)S(1)}, u32[]{:S(2)}, u32[]{:S(2)}) collective-permute-start(f32[10,1,128]{2,1,0:T(1,128)S(1)} %get-tuple-element.90), channel_id=1, source_target_pairs={{0,1},{2,3},{1,0},{3,2},{4,5},{6,7},{5,4},{7,6},{8,9},{10,11},{9,8... | collective-permute-start | bytes 15368 | tf_op jit(solution)/shard_map/ppermute | solution.py:96
  154.7 7.5 %collective-permute-start.19 = (f32[10,1,128]{2,1,0:T(1,128)S(1)}, f32[10,1,128]{2,1,0:T(1,128)S(1)}, u32[]{:S(2)}, u32[]{:S(2)}) collective-permute-start(f32[10,1,128]{2,1,0:T(1,128)S(1)} %get-tuple-element.91), channel_id=1, source_target_pairs={{1,2},{2,1},{5,6},{6,5},{9,10},{10,9},{13,14},{14,13},{17,18},{18,... | collective-permute-start | bytes 15368 | tf_op jit(solution)/shard_map/ppermute | solution.py:96
  164.8 3.3 %collective-permute-start.22 = (f32[1,16,128]{2,1,0:T(8,128)S(1)}, f32[1,16,128]{2,1,0:T(8,128)S(1)}, u32[]{:S(2)}, u32[]{:S(2)}) collective-permute-start(f32[1,16,128]{2,1,0:T(8,128)S(1)} %get-tuple-element.68), channel_id=1, source_target_pairs={{0,4},{8,12},{16,20},{24,28},{4,0},{12,8},{20,16},{28,24},{1,5},{9... | collective-permute-start | bytes 24584 | tf_op jit(solution)/shard_map/ppermute | solution.py:96
  166.1 5.3 %collective-permute-start.21 = (f32[1,16,128]{2,1,0:T(8,128)S(1)}, f32[1,16,128]{2,1,0:T(8,128)S(1)}, u32[]{:S(2)}, u32[]{:S(2)}) collective-permute-start(f32[1,16,128]{2,1,0:T(8,128)S(1)} %get-tuple-element.69), channel_id=1, source_target_pairs={{4,8},{12,16},{20,24},{8,4},{16,12},{24,20},{5,9},{13,17},{21,25},... | collective-permute-start | bytes 24584 | tf_op jit(solution)/shard_map/ppermute | solution.py:96
  171.4 20.9 %collective-permute-start.24 = (f32[10,1,128]{2,1,0:T(1,128)S(1)}, f32[10,1,128]{2,1,0:T(1,128)S(1)}, u32[]{:S(2)}, u32[]{:S(2)}) collective-permute-start(f32[10,1,128]{2,1,0:T(1,128)S(1)} %get-tuple-element.86), channel_id=1, source_target_pairs={{0,1},{2,3},{1,0},{3,2},{4,5},{6,7},{5,4},{7,6},{8,9},{10,11},{9,8... | collective-permute-start | bytes 15368 | tf_op jit(solution)/shard_map/ppermute | solution.py:96
  171.5 20.8 %collective-permute-start.23 = (f32[10,1,128]{2,1,0:T(1,128)S(1)}, f32[10,1,128]{2,1,0:T(1,128)S(1)}, u32[]{:S(2)}, u32[]{:S(2)}) collective-permute-start(f32[10,1,128]{2,1,0:T(1,128)S(1)} %get-tuple-element.87), channel_id=1, source_target_pairs={{1,2},{2,1},{5,6},{6,5},{9,10},{10,9},{13,14},{14,13},{17,18},{18,... | collective-permute-start | bytes 15368 | tf_op jit(solution)/shard_map/ppermute | solution.py:96
  (5 other events, 4.7 us)

commit v12 on v11

--- a/solution.py
+++ b/solution.py
@@ -53,12 +53,24 @@
     return jnp.dot(left, right, preferred_element_type=jnp.float32)
 
 
-def prepare_kernel(position, velocity, volume, pressure, fill, code, old, top):
+def prepare_kernel(*refs):
+    sources, (fill, code, old, top) = refs[:4], refs[4:8]
+    arrays, sem = refs[8:12], refs[12]
+    copies = [pltpu.make_async_copy(source, array, sem.at[i]) for i, (source, array) in enumerate(zip(sources, arrays))]
+    for copy in copies:
+        copy.start()
+    for copy in copies:
+        copy.wait()
+    position, velocity, volume, pressure = arrays
     rows, cols, width = volume.shape
-    slots = lax.broadcasted_iota(jnp.int32, (cols, width), 1)
+    slots = lax.broadcasted_iota(jnp.int32, (cols, width), 1).astype(jnp.float32)
     most = jnp.zeros((cols, width), jnp.float32)
+
+    def along_lanes(values):
+        return jnp.broadcast_to(values.astype(jnp.float32), (width, cols)).T
+
     for row in range(rows):
-        live = (slots < fill[row]).astype(jnp.float32)
+        live = (slots < along_lanes(fill[row : row + 1])).astype(jnp.float32)
         most = jnp.maximum(most, jnp.abs(velocity[0, row]) * live)
         most = jnp.maximum(most, jnp.abs(velocity[1, row]) * live)
         channels = [
@@ -68,7 +80,7 @@
             velocity[1, row],
             volume[row] * live,
             pressure[row],
-            jnp.broadcast_to((code[row] + 1).astype(jnp.float32), (cols, width)),
+            along_lanes(code[row : row + 1] + 1),
             jnp.zeros((cols, width), jnp.float32),
         ]
         for channel, value in enumerate(channels):
@@ -78,14 +90,19 @@
 
 def prepare(position, velocity, volume, pressure, fill, code):
     rows, cols, width = volume.shape
+    arrays = (position, velocity, volume, pressure)
+    vmem, hbm = pl.BlockSpec(memory_space=pltpu.VMEM), pl.BlockSpec(memory_space=pltpu.HBM)
     return call(
         prepare_kernel,
+        in_specs=[hbm] * 4 + [vmem] * 2,
+        out_specs=[vmem] * 2,
         out_shape=(
             pltpu.VMEM((rows, cols, 8, width), jnp.float32),
             pltpu.VMEM((8, width), jnp.float32),
         ),
+        scratch_shapes=[pltpu.VMEM(array.shape, jnp.float32) for array in arrays] + [pltpu.SemaphoreType.DMA((4,))],
         name="prepare",
-    )(position, velocity, volume, pressure, fill[:, :, None], code[:, :, None])
+    )(*(in_hbm(array) for array in arrays), fill, code)
 
 
 def neighbours(axis, even, low, high):
@@ -100,19 +117,24 @@
     return jnp.where(even, two, one), jnp.where(even, one, two)
 
 
-def exchange_old(even, shard, depth):
+def exchange_old(even, shard, top, depth):
     above, below = neighbours("gx", even[0], shard[:depth], shard[-depth:])
+    top = largest(top, "gy")
+    above, below, top = lax.optimization_barrier((above, below, top))
     low = jnp.concatenate([above[:, :depth], shard[:, :depth], below[:, :depth]], axis=0)
     high = jnp.concatenate([above[:, -depth:], shard[:, -depth:], below[:, -depth:]], axis=0)
     left, right = neighbours("gy", even[1], low, high)
-    return above, below, left, right
-
-
-def exchange_edges(even, edge, left, right):
-    above, below = neighbours("gx", even[0], edge[0][None], edge[1][None])
+    return (above, below, left, right), largest(top, "gx")
+
+
+def exchange_rows(even, edge):
+    return neighbours("gx", even[0], edge[0][None], edge[1][None])
+
+
+def exchange_sides(even, above, below, left, right):
     low = jnp.concatenate([above[:, :1], left, below[:, :1]], axis=0)
     high = jnp.concatenate([above[:, -1:], right, below[:, -1:]], axis=0)
-    return above, below, *neighbours("gy", even[1], low, high)
+    return neighbours("gy", even[1], low, high)
 
 
 def groups_of(edge, rows, cols):
@@ -161,15 +183,13 @@
         out[row, cols + 1 : cols + 2] = right[row]
 
 
-def largest(value):
-    for axis in ("gy", "gx"):
-        devices = lax.axis_size(axis)
-        if devices & (devices - 1):
-            value = lax.pmax(value, axis)
-            continue
-        for bit in range(devices.bit_length() - 1):
-            pairs = [(i, i ^ (1 << bit)) for i in range(devices)]
-            value = jnp.maximum(value, lax.ppermute(value, axis, pairs))
+def largest(value, axis):
+    devices = lax.axis_size(axis)
+    if devices & (devices - 1):
+        return lax.pmax(value, axis)
+    for bit in range(devices.bit_length() - 1):
+        pairs = [(i, i ^ (1 << bit)) for i in range(devices)]
+        value = jnp.maximum(value, lax.ppermute(value, axis, pairs))
     return value
 
 
@@ -360,10 +380,13 @@
                 features = features + float(off_y) * feat[row + k // 3, col + k % 3, 2]
             around.append(split(features))
         around = jnp.concatenate(around, axis=1)
-        total_w = dot_nt(side_by_side(*(part.at[index] for part in (weight, second, third))), around)
-        total_c = dot_nt(side_by_side(coef.at[base + group * size + index]), around)
-        total_w = (total_w[:, :8] + total_w[:, 8:]).T
-        total_c = (total_c[:, :8] + total_c[:, 8:]).T
+        both = [
+            side_by_side(*(part.at[index] for part in (weight, second, third))),
+            side_by_side(coef.at[base + group * size + index]),
+        ]
+        total = dot_nt(jnp.concatenate(both, axis=0), around)
+        total = (total[:, :8] + total[:, 8:]).T
+        total_w, total_c = total[:, :width], total[:, width:]
         tile = fresh[row + 1, col + 1]
         x, y, u, v = (tile[i : i + 1] for i in range(4))
         vol = tile[VOL : VOL + 1]
@@ -578,20 +601,25 @@
     even = [lax.axis_index(axis) % 2 == 0 for axis in ("gx", "gy")]
     position, even = lax.optimization_barrier((position, even))
     old, top = prepare(position, velocity, volume, pressure_prev, fill, drift_from)
-    top = largest(top)
-    fresh = drift(top, old, *exchange_old(even, old, 2))
+    around, top = exchange_old(even, old, top, 2)
+    fresh = drift(top, old, *around)
     coef, edge_weight, inner_weight = setup(fresh)
     edge_sums, edge_pv, *sides = first_sweep(kappa, True, fresh, coef, edge_weight)
+    above, below = exchange_rows(even, edge_pv)
     inner_sums, inner_pv = first_sweep(kappa, False, fresh, coef, inner_weight)
+    above, below, inner_pv = lax.optimization_barrier((above, below, inner_pv))
     for step in range(1, SWEEPS):
         last = step == SWEEPS - 1
         before = (edge_pv, inner_pv)
-        halo = exchange_edges(even, edge_pv, *sides)
-        inner_pv, *inner_pressure = sweep(kappa, last, False, shape, before, halo, coef, inner_sums)
+        left, right = exchange_sides(even, above, below, *sides)
+        inner_pv, *inner_pressure = sweep(kappa, last, False, shape, before, (), coef, inner_sums)
+        left, right, inner_pv = lax.optimization_barrier((left, right, inner_pv))
+        halo = (above, below, left, right)
         edge_pv, *rest = sweep(kappa, last, True, shape, before, halo, coef, edge_sums)
         sides, edge_pressure = rest[:2], rest[2:]
+        above, below = exchange_rows(even, edge_pv)
     pv = (edge_pv, inner_pv)
-    halo = exchange_edges(even, edge_pv, *sides)
+    halo = (above, below, *exchange_sides(even, above, below, *sides))
     (inner_new,) = push(kappa, False, pv, halo, fresh, inner_weight, inner_pressure[0], ())
     inner = (inner_pressure[0], inner_new)
     pressure, velocity_new = push(kappa, True, pv, halo, fresh, edge_weight, edge_pressure[0], inner)

time: 202 us -> 191 us (0.946)
  waiting for transfers between devices: 25.5 us -> 18.9 us
  local copies, waits for them, and re-layouts: 5.15 us -> 1.42 us
  starting transfers between devices: 44.4 us -> 42.2 us
    ppermute x20, waiting for transfers between devices: 15.6 us -> 11 us  [swap(): return lax.ppermute(value, axis, pairs + [(j, i) for i, j in pairs])]
    ppermute x20, starting transfers between devices: 42.4 us -> 38.5 us  [swap(): return lax.ppermute(value, axis, pairs + [(j, i) for i, j in pairs])]
    unnamed x8 -> x4, local copies, waits for them, and re-layouts: 3.49 us -> 1.37 us
    ppermute x5, waiting for transfers between devices: 9.96 us -> 7.93 us  [largest(): value = jnp.maximum(value, lax.ppermute(value, axis, pairs))]
  transfers between devices with their start and end apart: 25 -> 25, of which waited for: 11 -> 8; matrix products, arithmetic and copies ran while one was open for 0% -> 0% of each run, Pallas kernels for 22% -> 23%
where the time goes in v12:
time: 191 us; the launch traced here: 190 us
  Pallas kernels  127 us (66%)
  starting transfers between devices  42.2 us (22%)
  waiting for transfers between devices  18.9 us (10%)
    pallas_call x1, Pallas kernels, setup(): call(setup_kernel, in_specs=[hbm], out_specs=(vmem, hbm, hbm), out_shape=...  49.9 us
    ppermute x20, starting transfers between devices, swap(): return lax.ppermute(value, axis, pairs + [(j, i) for i, j in pairs])  38.5 us
    pallas_call x2, Pallas kernels, first_sweep(): call(functools.partial(first_kernel, kappa, edge), grid=(groups,), in_spe...  30 us
    pallas_call x2, Pallas kernels, push(): call(functools.partial(push_kernel, kappa, edge, len(args)), grid=(groups...  22.2 us
    pallas_call x6, Pallas kernels, sweep(): call(functools.partial(sweep_kernel, kappa, last, edge, rows, cols, len(a...  20.2 us
    ppermute x20, waiting for transfers between devices, swap(): return lax.ppermute(value, axis, pairs + [(j, i) for i, j in pairs])  11 us
    ppermute x5, waiting for transfers between devices, largest(): value = jnp.maximum(value, lax.ppermute(value, axis, pairs))  7.93 us
  transfers between devices with their start and end apart: 25, of which 8 were waited for; matrix products, arithmetic and copies ran while one was open for 0% of the time, Pallas kernels for 23%

profile of v12, /device:TPU:17, one launch (start us, length us, event | category | flops | bytes accessed | tf_op | source)
XLA Modules:
  0.0 190.4 jit_solution(12303972268755678925)
XLA Ops:
  10.3 3.0 %collective-permute-done = f32[2,16,8,128]{3,2,1,0:T(8,128)S(1)} collective-permute-done((f32[2,16,8,128]{3,2,1,0:T(8,128)S(1)}, f32[2,16,8,128]{3,2,1,0:T(8,128)S(1)}, u32[]{:S(2)}, u32[]{:S(2)}) %collective-permute-start) | collective-permute-done | bytes 131104 | tf_op jit(solution)/shard_map/ppermute | solution.py:113
  14.5 3.0 %collective-permute-start.7 = (f32[12,2,8,128]{3,2,1,0:T(8,128)S(1)}, f32[12,2,8,128]{3,2,1,0:T(8,128)S(1)}, u32[]{:S(2)}, u32[]{:S(2)}) collective-permute-start(f32[12,2,8,128]{3,2,1,0:T(8,128)S(1)} %get-tuple-element.93), channel_id=1, source_target_pairs={{1,2},{2,1},{5,6},{6,5},{9,10},{10,9},{13,14},{14,13},{17,18},{18,... | collective-permute-start | bytes 294920 | tf_op jit(solution)/shard_map/ppermute | solution.py:113
  22.5 3.4 %collective-permute-done.6 = f32[8,128]{1,0:T(8,128)S(1)} collective-permute-done((f32[8,128]{1,0:T(8,128)S(1)}, f32[8,128]{1,0:T(8,128)S(1)}, u32[]{:S(2)}, u32[]{:S(2)}) %collective-permute-start.6) | collective-permute-done | bytes 4128 | tf_op jit(solution)/shard_map/ppermute | solution.py:192
  25.9 2.6 %drift.1.source.fresh.refs_2_.refs_6_ = f32[10,18,8,128]{3,2,1,0:T(8,128)} custom-call(f32[8,128]{1,0:T(8,128)S(1)} %max.19.top, f32[8,16,8,128]{3,2,1,0:T(8,128)S(1)} %get-tuple-element.45.center, f32[2,16,8,128]{3,2,1,0:T(8,128)S(1)} %get-tuple-element.48.above, f32[2,16,8,128]{3,2,1,0:T(8,128)S(1)} %get-tuple-element.49.below, ...), custom_call_target="tpu_custom_call" | custom-call | tf_op jit(solution)/shard_map/drift/pallas_call | solution.py:230
  28.5 49.9 %setup.1 = (bf16[132,9,128,128]{3,2,1,0:T(8,128)(2,1)S(1)}, bf16[3,16,9,128,128]{4,3,2,1,0:T(8,128)(2,1)}, bf16[6,14,9,128,128]{4,3,2,1,0:T(8,128)(2,1)}) custom-call(f32[10,18,8,128]{3,2,1,0:T(8,128)} %drift.1.source.fresh.refs_2_.refs_6_), custom_call_target="tpu_custom_call" | custom-call | tf_op jit(solution)/shard_map/setup/pallas_call | solution.py:323
  78.4 11.9 %first_sweep.2 = (f32[3,3,16,128]{3,2,1,0:T(8,128)S(1)}, f32[3,16,128]{2,1,0:T(8,128)S(1)}, f32[8,1,128]{2,1,0:T(1,128)S(1)}, f32[8,1,128]{2,1,0:T(1,128)S(1)}) custom-call(f32[10,18,8,128]{3,2,1,0:T(8,128)} %drift.1.source.fresh.refs_2_.refs_6_, bf16[132,9,128,128]{3,2,1,0:T(8,128)(2,1)S(1)} %get-tuple-element.51.coef.refs_2_.refs_6_, ...), custom_call_target="tpu_custom_call" | custom-call | tf_op jit(solution)/shard_map/first_sweep/pallas_call | solution.py:414
  90.7 3.0 %collective-permute-start.9 = (f32[1,16,128]{2,1,0:T(8,128)S(1)}, f32[1,16,128]{2,1,0:T(8,128)S(1)}, u32[]{:S(2)}, u32[]{:S(2)}) collective-permute-start(f32[1,16,128]{2,1,0:T(8,128)S(1)} %get-tuple-element.105), channel_id=1, source_target_pairs={{4,8},{12,16},{20,24},{8,4},{16,12},{24,20},{5,9},{13,17},{21,25},... | collective-permute-start | bytes 24584 | tf_op jit(solution)/shard_map/ppermute | solution.py:113
  93.6 18.1 %first_sweep.3 = (f32[3,6,14,128]{3,2,1,0:T(8,128)S(1)}, f32[6,14,128]{2,1,0:T(8,128)S(1)}) custom-call(f32[10,18,8,128]{3,2,1,0:T(8,128)} %drift.1.source.fresh.refs_2_.refs_6_, bf16[132,9,128,128]{3,2,1,0:T(8,128)(2,1)S(1)} %get-tuple-element.51.coef.refs_2_.refs_6_, ...), custom_call_target="tpu_custom_call" | custom-call | tf_op jit(solution)/shard_map/first_sweep/pallas_call | solution.py:414
  113.6 4.9 %collective-permute-start.11 = (f32[10,1,128]{2,1,0:T(1,128)S(1)}, f32[10,1,128]{2,1,0:T(1,128)S(1)}, u32[]{:S(2)}, u32[]{:S(2)}) collective-permute-start(f32[10,1,128]{2,1,0:T(1,128)S(1)} %get-tuple-element.129), channel_id=1, source_target_pairs={{1,2},{2,1},{5,6},{6,5},{9,10},{10,9},{13,14},{14,13},{17,18},{18,... | collective-permute-start | bytes 15368 | tf_op jit(solution)/shard_map/ppermute | solution.py:113
  118.5 4.1 %sweep.6.refs_1_ = f32[6,14,128]{2,1,0:T(8,128)S(1)} custom-call(f32[3,16,128]{2,1,0:T(8,128)S(1)} %get-tuple-element.53.refs_0_, f32[6,14,128]{2,1,0:T(8,128)S(1)} %get-tuple-element.56.refs_1_, bf16[132,9,128,128]{3,2,1,0:T(8,128)(2,1)S(1)} %get-tuple-element.51.coef.refs_2_.refs_6_, f32[3,6,14,128]{3,2,1,0:T(8,128)S(1)} %get-tuple-element.61.refs_3_), custom_call_target="tpu_custom_call" | custom-call | tf_op jit(solution)/shard_map/sweep/pallas_call | solution.py:486
  122.6 2.6 %sweep.7 = (f32[3,16,128]{2,1,0:T(8,128)S(1)}, f32[8,1,128]{2,1,0:T(1,128)S(1)}, f32[8,1,128]{2,1,0:T(1,128)S(1)}) custom-call(f32[3,16,128]{2,1,0:T(8,128)S(1)} %get-tuple-element.53.refs_0_, f32[6,14,128]{2,1,0:T(8,128)S(1)} %get-tuple-element.56.refs_1_, f32[1,16,128]{2,1,0:T(8,128)S(1)} %get-tuple-element.57.refs_2_, ...), custom_call_target="tpu_custom_call" | custom-call | tf_op jit(solution)/shard_map/sweep/pallas_call | solution.py:486
  126.2 2.3 %collective-permute-start.13 = (f32[1,16,128]{2,1,0:T(8,128)S(1)}, f32[1,16,128]{2,1,0:T(8,128)S(1)}, u32[]{:S(2)}, u32[]{:S(2)}) collective-permute-start(f32[1,16,128]{2,1,0:T(8,128)S(1)} %get-tuple-element.103), channel_id=1, source_target_pairs={{4,8},{12,16},{20,24},{8,4},{16,12},{24,20},{5,9},{13,17},{21,25},... | collective-permute-start | bytes 24584 | tf_op jit(solution)/shard_map/ppermute | solution.py:113
  128.5 2.9 %collective-permute-done.13 = f32[1,16,128]{2,1,0:T(8,128)S(1)} collective-permute-done((f32[1,16,128]{2,1,0:T(8,128)S(1)}, f32[1,16,128]{2,1,0:T(8,128)S(1)}, u32[]{:S(2)}, u32[]{:S(2)}) %collective-permute-start.13) | collective-permute-done | bytes 8224 | tf_op jit(solution)/shard_map/ppermute | solution.py:113
  131.6 3.5 %collective-permute-start.15 = (f32[10,1,128]{2,1,0:T(1,128)S(1)}, f32[10,1,128]{2,1,0:T(1,128)S(1)}, u32[]{:S(2)}, u32[]{:S(2)}) collective-permute-start(f32[10,1,128]{2,1,0:T(1,128)S(1)} %get-tuple-element.125), channel_id=1, source_target_pairs={{1,2},{2,1},{5,6},{6,5},{9,10},{10,9},{13,14},{14,13},{17,18},{18,... | collective-permute-start | bytes 15368 | tf_op jit(solution)/shard_map/ppermute | solution.py:113
  135.2 4.1 %sweep.8.refs_1_ = f32[6,14,128]{2,1,0:T(8,128)S(1)} custom-call(f32[3,16,128]{2,1,0:T(8,128)S(1)} %get-tuple-element.65.refs_0_, f32[6,14,128]{2,1,0:T(8,128)S(1)} %sweep.6.refs_1_, bf16[132,9,128,128]{3,2,1,0:T(8,128)(2,1)S(1)} %get-tuple-element.51.coef.refs_2_.refs_6_, f32[3,6,14,128]{3,2,1,0:T(8,128)S(1)} %get-tuple-element.61.refs_3_), custom_call_target="tpu_custom_call" | custom-call | tf_op jit(solution)/shard_map/sweep/pallas_call | solution.py:486
  139.3 2.6 %sweep.9 = (f32[3,16,128]{2,1,0:T(8,128)S(1)}, f32[8,1,128]{2,1,0:T(1,128)S(1)}, f32[8,1,128]{2,1,0:T(1,128)S(1)}) custom-call(f32[3,16,128]{2,1,0:T(8,128)S(1)} %get-tuple-element.65.refs_0_, f32[6,14,128]{2,1,0:T(8,128)S(1)} %sweep.6.refs_1_, f32[1,16,128]{2,1,0:T(8,128)S(1)} %get-tuple-element.111.refs_2_, f32[1,16,128]{2,1,0:T(8,128)S(1)} %get-tuple-element.110.refs_3_, ...), custom_call_target="tpu_custom_call" | custom-call | tf_op jit(solution)/shard_map/sweep/pallas_call | solution.py:486
  142.6 3.2 %collective-permute-start.17 = (f32[1,16,128]{2,1,0:T(8,128)S(1)}, f32[1,16,128]{2,1,0:T(8,128)S(1)}, u32[]{:S(2)}, u32[]{:S(2)}) collective-permute-start(f32[1,16,128]{2,1,0:T(8,128)S(1)} %get-tuple-element.101), channel_id=1, source_target_pairs={{4,8},{12,16},{20,24},{8,4},{16,12},{24,20},{5,9},{13,17},{21,25},... | collective-permute-start | bytes 24584 | tf_op jit(solution)/shard_map/ppermute | solution.py:113
  148.0 3.6 %collective-permute-start.19 = (f32[10,1,128]{2,1,0:T(1,128)S(1)}, f32[10,1,128]{2,1,0:T(1,128)S(1)}, u32[]{:S(2)}, u32[]{:S(2)}) collective-permute-start(f32[10,1,128]{2,1,0:T(1,128)S(1)} %get-tuple-element.121), channel_id=1, source_target_pairs={{1,2},{2,1},{5,6},{6,5},{9,10},{10,9},{13,14},{14,13},{17,18},{18,... | collective-permute-start | bytes 15368 | tf_op jit(solution)/shard_map/ppermute | solution.py:113
  151.7 4.1 %sweep.10 = (f32[6,14,128]{2,1,0:T(8,128)S(1)}, f32[6,14,128]{2,1,0:T(8,128)S(1)}) custom-call(f32[3,16,128]{2,1,0:T(8,128)S(1)} %get-tuple-element.71.refs_0_, f32[6,14,128]{2,1,0:T(8,128)S(1)} %sweep.8.refs_1_, bf16[132,9,128,128]{3,2,1,0:T(8,128)(2,1)S(1)} %get-tuple-element.51.coef.refs_2_.refs_6_, f32[3,6,14,128]{3,2,1,0:T(8,128)S(1)} %get-tuple-element.61.refs_3_), custom_call_target="tpu_custom_call" | custom-call | tf_op jit(solution)/shard_map/sweep/pallas_call | solution.py:486
  155.8 2.6 %sweep.11 = (f32[3,16,128]{2,1,0:T(8,128)S(1)}, f32[8,1,128]{2,1,0:T(1,128)S(1)}, f32[8,1,128]{2,1,0:T(1,128)S(1)}, f32[3,16,128]{2,1,0:T(8,128)S(1)}) custom-call(f32[3,16,128]{2,1,0:T(8,128)S(1)} %get-tuple-element.71.refs_0_, f32[6,14,128]{2,1,0:T(8,128)S(1)} %sweep.8.refs_1_, f32[1,16,128]{2,1,0:T(8,128)S(1)} %get-tuple-element.109.refs_2_, ...), custom_call_target="tpu_custom_call" | custom-call | tf_op jit(solution)/shard_map/sweep/pallas_call | solution.py:486
  161.7 2.9 %collective-permute-done.21 = f32[1,16,128]{2,1,0:T(8,128)S(1)} collective-permute-done((f32[1,16,128]{2,1,0:T(8,128)S(1)}, f32[1,16,128]{2,1,0:T(8,128)S(1)}, u32[]{:S(2)}, u32[]{:S(2)}) %collective-permute-start.21) | collective-permute-done | bytes 8224 | tf_op jit(solution)/shard_map/ppermute | solution.py:113
  164.8 3.4 %collective-permute-start.23 = (f32[10,1,128]{2,1,0:T(1,128)S(1)}, f32[10,1,128]{2,1,0:T(1,128)S(1)}, u32[]{:S(2)}, u32[]{:S(2)}) collective-permute-start(f32[10,1,128]{2,1,0:T(1,128)S(1)} %get-tuple-element.117), channel_id=1, source_target_pairs={{1,2},{2,1},{5,6},{6,5},{9,10},{10,9},{13,14},{14,13},{17,18},{18,... | collective-permute-start | bytes 15368 | tf_op jit(solution)/shard_map/ppermute | solution.py:113
  168.1 13.1 %push.2.refs_12_ = f32[2,6,14,128]{3,2,1,0:T(8,128)S(1)} custom-call(f32[3,16,128]{2,1,0:T(8,128)S(1)} %get-tuple-element.78.refs_0_, f32[6,14,128]{2,1,0:T(8,128)S(1)} %get-tuple-element.79.refs_1_, f32[10,18,8,128]{3,2,1,0:T(8,128)} %drift.1.source.fresh.refs_2_.refs_6_, ...), custom_call_target="tpu_custom_call" | custom-call | tf_op jit(solution)/shard_map/push/pallas_call | solution.py:583
  181.2 9.2 %push.3 = (f32[8,16,128]{2,1,0:T(8,128)}, f32[2,8,16,128]{3,2,1,0:T(8,128)}) custom-call(f32[3,16,128]{2,1,0:T(8,128)S(1)} %get-tuple-element.78.refs_0_, f32[6,14,128]{2,1,0:T(8,128)S(1)} %get-tuple-element.79.refs_1_, f32[1,16,128]{2,1,0:T(8,128)S(1)} %get-tuple-element.107.refs_2_, f32[1,16,128]{2,1,0:T(8,128)S(1)} %get-tuple-element.106.refs_3_, ...), custom_call_target="tpu_custom_call" | custom-call | tf_op jit(solution)/shard_map/push/pallas_call | solution.py:583
  (78 shorter events, 25.2 us)
Async XLA Ops:
  3.6 4.1 %collective-permute-start.2 = (f32[8,128]{1,0:T(8,128)S(1)}, f32[8,128]{1,0:T(8,128)S(1)}, u32[]{:S(2)}, u32[]{:S(2)}) collective-permute-start(f32[8,128]{1,0:T(8,128)S(1)} %get-tuple-element.46), channel_id=1, source_target_pairs={{0,1},{1,0},{2,3},{3,2},{4,5},{5,4},{6,7},{7,6},{8,9},{9,8},{10,11... | collective-permute-start | bytes 12296 | tf_op jit(solution)/shard_map/ppermute | solution.py:192
  4.4 5.9 %collective-permute-start.1 = (f32[2,16,8,128]{3,2,1,0:T(8,128)S(1)}, f32[2,16,8,128]{3,2,1,0:T(8,128)S(1)}, u32[]{:S(2)}, u32[]{:S(2)}) collective-permute-start(f32[2,16,8,128]{3,2,1,0:T(8,128)S(1)} %get-tuple-element.86), channel_id=1, source_target_pairs={{0,4},{8,12},{16,20},{24,28},{4,0},{12,8},{20,16},{28,24},{1,5},{9... | collective-permute-start | bytes 393224 | tf_op jit(solution)/shard_map/ppermute | solution.py:113
  5.7 7.6 %collective-permute-start = (f32[2,16,8,128]{3,2,1,0:T(8,128)S(1)}, f32[2,16,8,128]{3,2,1,0:T(8,128)S(1)}, u32[]{:S(2)}, u32[]{:S(2)}) collective-permute-start(f32[2,16,8,128]{3,2,1,0:T(8,128)S(1)} %get-tuple-element.87), channel_id=1, source_target_pairs={{4,8},{12,16},{20,24},{8,4},{16,12},{24,20},{5,9},{13,17},{21,25},... | collective-permute-start | bytes 393224 | tf_op jit(solution)/shard_map/ppermute | solution.py:113
  7.7 2.5 %collective-permute-start.3 = (f32[8,128]{1,0:T(8,128)S(1)}, f32[8,128]{1,0:T(8,128)S(1)}, u32[]{:S(2)}, u32[]{:S(2)}) collective-permute-start(f32[8,128]{1,0:T(8,128)S(1)} %max.15), channel_id=1, source_target_pairs={{0,2},{1,3},{2,0},{3,1},{4,6},{5,7},{6,4},{7,5},{8,10},{9,11},{10,... | collective-permute-start | bytes 12296 | tf_op jit(solution)/shard_map/ppermute | solution.py:192
  13.3 12.6 %collective-permute-start.8 = (f32[12,2,8,128]{3,2,1,0:T(8,128)S(1)}, f32[12,2,8,128]{3,2,1,0:T(8,128)S(1)}, u32[]{:S(2)}, u32[]{:S(2)}) collective-permute-start(f32[12,2,8,128]{3,2,1,0:T(8,128)S(1)} %get-tuple-element.92), channel_id=1, source_target_pairs={{0,1},{2,3},{1,0},{3,2},{4,5},{6,7},{5,4},{7,6},{8,9},{10,11},{9,8... | collective-permute-start | bytes 294920 | tf_op jit(solution)/shard_map/ppermute | solution.py:113
  14.5 11.4 %collective-permute-start.7 = (f32[12,2,8,128]{3,2,1,0:T(8,128)S(1)}, f32[12,2,8,128]{3,2,1,0:T(8,128)S(1)}, u32[]{:S(2)}, u32[]{:S(2)}) collective-permute-start(f32[12,2,8,128]{3,2,1,0:T(8,128)S(1)} %get-tuple-element.93), channel_id=1, source_target_pairs={{1,2},{2,1},{5,6},{6,5},{9,10},{10,9},{13,14},{14,13},{17,18},{18,... | collective-permute-start | bytes 294920 | tf_op jit(solution)/shard_map/ppermute | solution.py:113
  17.5 2.5 %collective-permute-start.4 = (f32[8,128]{1,0:T(8,128)S(1)}, f32[8,128]{1,0:T(8,128)S(1)}, u32[]{:S(2)}, u32[]{:S(2)}) collective-permute-start(f32[8,128]{1,0:T(8,128)S(1)} %max.16), channel_id=1, source_target_pairs={{0,4},{4,0},{8,12},{12,8},{16,20},{20,16},{24,28},{28,24},{1,5},{5... | collective-permute-start | bytes 12296 | tf_op jit(solution)/shard_map/ppermute | solution.py:192
  22.5 3.4 %collective-permute-start.6 = (f32[8,128]{1,0:T(8,128)S(1)}, f32[8,128]{1,0:T(8,128)S(1)}, u32[]{:S(2)}, u32[]{:S(2)}) collective-permute-start(f32[8,128]{1,0:T(8,128)S(1)} %max.18), channel_id=1, source_target_pairs={{0,16},{4,20},{8,24},{12,28},{16,0},{20,4},{24,8},{28,12},{1,17},{... | collective-permute-start | bytes 12296 | tf_op jit(solution)/shard_map/ppermute | solution.py:192
  90.3 21.5 %collective-permute-start.10 = (f32[1,16,128]{2,1,0:T(8,128)S(1)}, f32[1,16,128]{2,1,0:T(8,128)S(1)}, u32[]{:S(2)}, u32[]{:S(2)}) collective-permute-start(f32[1,16,128]{2,1,0:T(8,128)S(1)} %get-tuple-element.104), channel_id=1, source_target_pairs={{0,4},{8,12},{16,20},{24,28},{4,0},{12,8},{20,16},{28,24},{1,5},{9... | collective-permute-start | bytes 24584 | tf_op jit(solution)/shard_map/ppermute | solution.py:113
  90.7 21.1 %collective-permute-start.9 = (f32[1,16,128]{2,1,0:T(8,128)S(1)}, f32[1,16,128]{2,1,0:T(8,128)S(1)}, u32[]{:S(2)}, u32[]{:S(2)}) collective-permute-start(f32[1,16,128]{2,1,0:T(8,128)S(1)} %get-tuple-element.105), channel_id=1, source_target_pairs={{4,8},{12,16},{20,24},{8,4},{16,12},{24,20},{5,9},{13,17},{21,25},... | collective-permute-start | bytes 24584 | tf_op jit(solution)/shard_map/ppermute | solution.py:113
  111.9 10.7 %collective-permute-start.12 = (f32[10,1,128]{2,1,0:T(1,128)S(1)}, f32[10,1,128]{2,1,0:T(1,128)S(1)}, u32[]{:S(2)}, u32[]{:S(2)}) collective-permute-start(f32[10,1,128]{2,1,0:T(1,128)S(1)} %get-tuple-element.128), channel_id=1, source_target_pairs={{0,1},{2,3},{1,0},{3,2},{4,5},{6,7},{5,4},{7,6},{8,9},{10,11},{9,8... | collective-permute-start | bytes 15368 | tf_op jit(solution)/shard_map/ppermute | solution.py:113
  113.6 9.0 %collective-permute-start.11 = (f32[10,1,128]{2,1,0:T(1,128)S(1)}, f32[10,1,128]{2,1,0:T(1,128)S(1)}, u32[]{:S(2)}, u32[]{:S(2)}) collective-permute-start(f32[10,1,128]{2,1,0:T(1,128)S(1)} %get-tuple-element.129), channel_id=1, source_target_pairs={{1,2},{2,1},{5,6},{6,5},{9,10},{10,9},{13,14},{14,13},{17,18},{18,... | collective-permute-start | bytes 15368 | tf_op jit(solution)/shard_map/ppermute | solution.py:113
  125.3 3.3 %collective-permute-start.14 = (f32[1,16,128]{2,1,0:T(8,128)S(1)}, f32[1,16,128]{2,1,0:T(8,128)S(1)}, u32[]{:S(2)}, u32[]{:S(2)}) collective-permute-start(f32[1,16,128]{2,1,0:T(8,128)S(1)} %get-tuple-element.102), channel_id=1, source_target_pairs={{0,4},{8,12},{16,20},{24,28},{4,0},{12,8},{20,16},{28,24},{1,5},{9... | collective-permute-start | bytes 24584 | tf_op jit(solution)/shard_map/ppermute | solution.py:113
  126.2 5.3 %collective-permute-start.13 = (f32[1,16,128]{2,1,0:T(8,128)S(1)}, f32[1,16,128]{2,1,0:T(8,128)S(1)}, u32[]{:S(2)}, u32[]{:S(2)}) collective-permute-start(f32[1,16,128]{2,1,0:T(8,128)S(1)} %get-tuple-element.103), channel_id=1, source_target_pairs={{4,8},{12,16},{20,24},{8,4},{16,12},{24,20},{5,9},{13,17},{21,25},... | collective-permute-start | bytes 24584 | tf_op jit(solution)/shard_map/ppermute | solution.py:113
  131.5 7.7 %collective-permute-start.16 = (f32[10,1,128]{2,1,0:T(1,128)S(1)}, f32[10,1,128]{2,1,0:T(1,128)S(1)}, u32[]{:S(2)}, u32[]{:S(2)}) collective-permute-start(f32[10,1,128]{2,1,0:T(1,128)S(1)} %get-tuple-element.124), channel_id=1, source_target_pairs={{0,1},{2,3},{1,0},{3,2},{4,5},{6,7},{5,4},{7,6},{8,9},{10,11},{9,8... | collective-permute-start | bytes 15368 | tf_op jit(solution)/shard_map/ppermute | solution.py:113
  131.6 7.6 %collective-permute-start.15 = (f32[10,1,128]{2,1,0:T(1,128)S(1)}, f32[10,1,128]{2,1,0:T(1,128)S(1)}, u32[]{:S(2)}, u32[]{:S(2)}) collective-permute-start(f32[10,1,128]{2,1,0:T(1,128)S(1)} %get-tuple-element.125), channel_id=1, source_target_pairs={{1,2},{2,1},{5,6},{6,5},{9,10},{10,9},{13,14},{14,13},{17,18},{18,... | collective-permute-start | bytes 15368 | tf_op jit(solution)/shard_map/ppermute | solution.py:113
  142.0 3.8 %collective-permute-start.18 = (f32[1,16,128]{2,1,0:T(8,128)S(1)}, f32[1,16,128]{2,1,0:T(8,128)S(1)}, u32[]{:S(2)}, u32[]{:S(2)}) collective-permute-start(f32[1,16,128]{2,1,0:T(8,128)S(1)} %get-tuple-element.100), channel_id=1, source_target_pairs={{0,4},{8,12},{16,20},{24,28},{4,0},{12,8},{20,16},{28,24},{1,5},{9... | collective-permute-start | bytes 24584 | tf_op jit(solution)/shard_map/ppermute | solution.py:113
  142.6 5.3 %collective-permute-start.17 = (f32[1,16,128]{2,1,0:T(8,128)S(1)}, f32[1,16,128]{2,1,0:T(8,128)S(1)}, u32[]{:S(2)}, u32[]{:S(2)}) collective-permute-start(f32[1,16,128]{2,1,0:T(8,128)S(1)} %get-tuple-element.101), channel_id=1, source_target_pairs={{4,8},{12,16},{20,24},{8,4},{16,12},{24,20},{5,9},{13,17},{21,25},... | collective-permute-start | bytes 24584 | tf_op jit(solution)/shard_map/ppermute | solution.py:113
  147.9 7.8 %collective-permute-start.20 = (f32[10,1,128]{2,1,0:T(1,128)S(1)}, f32[10,1,128]{2,1,0:T(1,128)S(1)}, u32[]{:S(2)}, u32[]{:S(2)}) collective-permute-start(f32[10,1,128]{2,1,0:T(1,128)S(1)} %get-tuple-element.120), channel_id=1, source_target_pairs={{0,1},{2,3},{1,0},{3,2},{4,5},{6,7},{5,4},{7,6},{8,9},{10,11},{9,8... | collective-permute-start | bytes 15368 | tf_op jit(solution)/shard_map/ppermute | solution.py:113
  148.0 7.8 %collective-permute-start.19 = (f32[10,1,128]{2,1,0:T(1,128)S(1)}, f32[10,1,128]{2,1,0:T(1,128)S(1)}, u32[]{:S(2)}, u32[]{:S(2)}) collective-permute-start(f32[10,1,128]{2,1,0:T(1,128)S(1)} %get-tuple-element.121), channel_id=1, source_target_pairs={{1,2},{2,1},{5,6},{6,5},{9,10},{10,9},{13,14},{14,13},{17,18},{18,... | collective-permute-start | bytes 15368 | tf_op jit(solution)/shard_map/ppermute | solution.py:113
  158.4 3.3 %collective-permute-start.22 = (f32[1,16,128]{2,1,0:T(8,128)S(1)}, f32[1,16,128]{2,1,0:T(8,128)S(1)}, u32[]{:S(2)}, u32[]{:S(2)}) collective-permute-start(f32[1,16,128]{2,1,0:T(8,128)S(1)} %get-tuple-element.98), channel_id=1, source_target_pairs={{0,4},{8,12},{16,20},{24,28},{4,0},{12,8},{20,16},{28,24},{1,5},{9... | collective-permute-start | bytes 24584 | tf_op jit(solution)/shard_map/ppermute | solution.py:113
  159.4 5.3 %collective-permute-start.21 = (f32[1,16,128]{2,1,0:T(8,128)S(1)}, f32[1,16,128]{2,1,0:T(8,128)S(1)}, u32[]{:S(2)}, u32[]{:S(2)}) collective-permute-start(f32[1,16,128]{2,1,0:T(8,128)S(1)} %get-tuple-element.99), channel_id=1, source_target_pairs={{4,8},{12,16},{20,24},{8,4},{16,12},{24,20},{5,9},{13,17},{21,25},... | collective-permute-start | bytes 24584 | tf_op jit(solution)/shard_map/ppermute | solution.py:113
  164.7 16.5 %collective-permute-start.24 = (f32[10,1,128]{2,1,0:T(1,128)S(1)}, f32[10,1,128]{2,1,0:T(1,128)S(1)}, u32[]{:S(2)}, u32[]{:S(2)}) collective-permute-start(f32[10,1,128]{2,1,0:T(1,128)S(1)} %get-tuple-element.116), channel_id=1, source_target_pairs={{0,1},{2,3},{1,0},{3,2},{4,5},{6,7},{5,4},{7,6},{8,9},{10,11},{9,8... | collective-permute-start | bytes 15368 | tf_op jit(solution)/shard_map/ppermute | solution.py:113
  164.8 16.4 %collective-permute-start.23 = (f32[10,1,128]{2,1,0:T(1,128)S(1)}, f32[10,1,128]{2,1,0:T(1,128)S(1)}, u32[]{:S(2)}, u32[]{:S(2)}) collective-permute-start(f32[10,1,128]{2,1,0:T(1,128)S(1)} %get-tuple-element.117), channel_id=1, source_target_pairs={{1,2},{2,1},{5,6},{6,5},{9,10},{10,9},{13,14},{14,13},{17,18},{18,... | collective-permute-start | bytes 15368 | tf_op jit(solution)/shard_map/ppermute | solution.py:113
  (3 other events, 3.8 us)

commit v13 on v12

--- a/solution.py
+++ b/solution.py
@@ -11,8 +11,8 @@
 CFL = 0.25
 SPEED_EPS = 1e-06
 SOFT = 0.01
-CHUNK = 64
-BUFFERS = 4
+CHUNK = 32
+BUFFERS = 6
 VMEM_LIMIT = 16 * 1024 * 1024
 
 X, Y, U, V, VOL, PRES, CODE = range(7)

time: 191 us -> 191 us (level)
  no operation moved by 1% of the time
where the time goes in v13:
time: 191 us; the launch traced here: 190 us
  Pallas kernels  127 us (66%)
  starting transfers between devices  42.2 us (22%)
  waiting for transfers between devices  19 us (10%)
    pallas_call x1, Pallas kernels, setup(): call(setup_kernel, in_specs=[hbm], out_specs=(vmem, hbm, hbm), out_shape=...  50 us
    ppermute x20, starting transfers between devices, swap(): return lax.ppermute(value, axis, pairs + [(j, i) for i, j in pairs])  38.5 us
    pallas_call x2, Pallas kernels, first_sweep(): call(functools.partial(first_kernel, kappa, edge), grid=(groups,), in_spe...  30 us
    pallas_call x2, Pallas kernels, push(): call(functools.partial(push_kernel, kappa, edge, len(args)), grid=(groups...  22.2 us
    pallas_call x6, Pallas kernels, sweep(): call(functools.partial(sweep_kernel, kappa, last, edge, rows, cols, len(a...  20.2 us
    ppermute x20, waiting for transfers between devices, swap(): return lax.ppermute(value, axis, pairs + [(j, i) for i, j in pairs])  11 us
    ppermute x5, waiting for transfers between devices, largest(): value = jnp.maximum(value, lax.ppermute(value, axis, pairs))  7.93 us
  transfers between devices with their start and end apart: 25, of which 8 were waited for; matrix products, arithmetic and copies ran while one was open for 0% of the time, Pallas kernels for 23%

profile of v13, /device:TPU:17, one launch (start us, length us, event | category | flops | bytes accessed | tf_op | source)
XLA Modules:
  0.0 190.5 jit_solution(12609212353830129888)
XLA Ops:
  10.3 3.0 %collective-permute-done = f32[2,16,8,128]{3,2,1,0:T(8,128)S(1)} collective-permute-done((f32[2,16,8,128]{3,2,1,0:T(8,128)S(1)}, f32[2,16,8,128]{3,2,1,0:T(8,128)S(1)}, u32[]{:S(2)}, u32[]{:S(2)}) %collective-permute-start) | collective-permute-done | bytes 131104 | tf_op jit(solution)/shard_map/ppermute | solution.py:113
  14.5 3.0 %collective-permute-start.7 = (f32[12,2,8,128]{3,2,1,0:T(8,128)S(1)}, f32[12,2,8,128]{3,2,1,0:T(8,128)S(1)}, u32[]{:S(2)}, u32[]{:S(2)}) collective-permute-start(f32[12,2,8,128]{3,2,1,0:T(8,128)S(1)} %get-tuple-element.93), channel_id=1, source_target_pairs={{1,2},{2,1},{5,6},{6,5},{9,10},{10,9},{13,14},{14,13},{17,18},{18,... | collective-permute-start | bytes 294920 | tf_op jit(solution)/shard_map/ppermute | solution.py:113
  22.5 3.4 %collective-permute-done.6 = f32[8,128]{1,0:T(8,128)S(1)} collective-permute-done((f32[8,128]{1,0:T(8,128)S(1)}, f32[8,128]{1,0:T(8,128)S(1)}, u32[]{:S(2)}, u32[]{:S(2)}) %collective-permute-start.6) | collective-permute-done | bytes 4128 | tf_op jit(solution)/shard_map/ppermute | solution.py:192
  25.9 2.6 %drift.1.source.fresh.refs_2_.refs_6_ = f32[10,18,8,128]{3,2,1,0:T(8,128)} custom-call(f32[8,128]{1,0:T(8,128)S(1)} %max.19.top, f32[8,16,8,128]{3,2,1,0:T(8,128)S(1)} %get-tuple-element.45.center, f32[2,16,8,128]{3,2,1,0:T(8,128)S(1)} %get-tuple-element.48.above, f32[2,16,8,128]{3,2,1,0:T(8,128)S(1)} %get-tuple-element.49.below, ...), custom_call_target="tpu_custom_call" | custom-call | tf_op jit(solution)/shard_map/drift/pallas_call | solution.py:230
  28.5 50.0 %setup.1 = (bf16[132,9,128,128]{3,2,1,0:T(8,128)(2,1)S(1)}, bf16[3,16,9,128,128]{4,3,2,1,0:T(8,128)(2,1)}, bf16[6,14,9,128,128]{4,3,2,1,0:T(8,128)(2,1)}) custom-call(f32[10,18,8,128]{3,2,1,0:T(8,128)} %drift.1.source.fresh.refs_2_.refs_6_), custom_call_target="tpu_custom_call" | custom-call | tf_op jit(solution)/shard_map/setup/pallas_call | solution.py:323
  78.4 11.9 %first_sweep.2 = (f32[3,3,16,128]{3,2,1,0:T(8,128)S(1)}, f32[3,16,128]{2,1,0:T(8,128)S(1)}, f32[8,1,128]{2,1,0:T(1,128)S(1)}, f32[8,1,128]{2,1,0:T(1,128)S(1)}) custom-call(f32[10,18,8,128]{3,2,1,0:T(8,128)} %drift.1.source.fresh.refs_2_.refs_6_, bf16[132,9,128,128]{3,2,1,0:T(8,128)(2,1)S(1)} %get-tuple-element.51.coef.refs_2_.refs_6_, ...), custom_call_target="tpu_custom_call" | custom-call | tf_op jit(solution)/shard_map/first_sweep/pallas_call | solution.py:414
  90.7 3.0 %collective-permute-start.9 = (f32[1,16,128]{2,1,0:T(8,128)S(1)}, f32[1,16,128]{2,1,0:T(8,128)S(1)}, u32[]{:S(2)}, u32[]{:S(2)}) collective-permute-start(f32[1,16,128]{2,1,0:T(8,128)S(1)} %get-tuple-element.105), channel_id=1, source_target_pairs={{4,8},{12,16},{20,24},{8,4},{16,12},{24,20},{5,9},{13,17},{21,25},... | collective-permute-start | bytes 24584 | tf_op jit(solution)/shard_map/ppermute | solution.py:113
  93.7 18.1 %first_sweep.3 = (f32[3,6,14,128]{3,2,1,0:T(8,128)S(1)}, f32[6,14,128]{2,1,0:T(8,128)S(1)}) custom-call(f32[10,18,8,128]{3,2,1,0:T(8,128)} %drift.1.source.fresh.refs_2_.refs_6_, bf16[132,9,128,128]{3,2,1,0:T(8,128)(2,1)S(1)} %get-tuple-element.51.coef.refs_2_.refs_6_, ...), custom_call_target="tpu_custom_call" | custom-call | tf_op jit(solution)/shard_map/first_sweep/pallas_call | solution.py:414
  113.6 5.1 %collective-permute-start.11 = (f32[10,1,128]{2,1,0:T(1,128)S(1)}, f32[10,1,128]{2,1,0:T(1,128)S(1)}, u32[]{:S(2)}, u32[]{:S(2)}) collective-permute-start(f32[10,1,128]{2,1,0:T(1,128)S(1)} %get-tuple-element.129), channel_id=1, source_target_pairs={{1,2},{2,1},{5,6},{6,5},{9,10},{10,9},{13,14},{14,13},{17,18},{18,... | collective-permute-start | bytes 15368 | tf_op jit(solution)/shard_map/ppermute | solution.py:113
  118.7 4.1 %sweep.6.refs_1_ = f32[6,14,128]{2,1,0:T(8,128)S(1)} custom-call(f32[3,16,128]{2,1,0:T(8,128)S(1)} %get-tuple-element.53.refs_0_, f32[6,14,128]{2,1,0:T(8,128)S(1)} %get-tuple-element.56.refs_1_, bf16[132,9,128,128]{3,2,1,0:T(8,128)(2,1)S(1)} %get-tuple-element.51.coef.refs_2_.refs_6_, f32[3,6,14,128]{3,2,1,0:T(8,128)S(1)} %get-tuple-element.61.refs_3_), custom_call_target="tpu_custom_call" | custom-call | tf_op jit(solution)/shard_map/sweep/pallas_call | solution.py:486
  122.8 2.6 %sweep.7 = (f32[3,16,128]{2,1,0:T(8,128)S(1)}, f32[8,1,128]{2,1,0:T(1,128)S(1)}, f32[8,1,128]{2,1,0:T(1,128)S(1)}) custom-call(f32[3,16,128]{2,1,0:T(8,128)S(1)} %get-tuple-element.53.refs_0_, f32[6,14,128]{2,1,0:T(8,128)S(1)} %get-tuple-element.56.refs_1_, f32[1,16,128]{2,1,0:T(8,128)S(1)} %get-tuple-element.57.refs_2_, ...), custom_call_target="tpu_custom_call" | custom-call | tf_op jit(solution)/shard_map/sweep/pallas_call | solution.py:486
  126.5 2.3 %collective-permute-start.13 = (f32[1,16,128]{2,1,0:T(8,128)S(1)}, f32[1,16,128]{2,1,0:T(8,128)S(1)}, u32[]{:S(2)}, u32[]{:S(2)}) collective-permute-start(f32[1,16,128]{2,1,0:T(8,128)S(1)} %get-tuple-element.103), channel_id=1, source_target_pairs={{4,8},{12,16},{20,24},{8,4},{16,12},{24,20},{5,9},{13,17},{21,25},... | collective-permute-start | bytes 24584 | tf_op jit(solution)/shard_map/ppermute | solution.py:113
  128.8 3.0 %collective-permute-done.13 = f32[1,16,128]{2,1,0:T(8,128)S(1)} collective-permute-done((f32[1,16,128]{2,1,0:T(8,128)S(1)}, f32[1,16,128]{2,1,0:T(8,128)S(1)}, u32[]{:S(2)}, u32[]{:S(2)}) %collective-permute-start.13) | collective-permute-done | bytes 8224 | tf_op jit(solution)/shard_map/ppermute | solution.py:113
  131.9 3.4 %collective-permute-start.15 = (f32[10,1,128]{2,1,0:T(1,128)S(1)}, f32[10,1,128]{2,1,0:T(1,128)S(1)}, u32[]{:S(2)}, u32[]{:S(2)}) collective-permute-start(f32[10,1,128]{2,1,0:T(1,128)S(1)} %get-tuple-element.125), channel_id=1, source_target_pairs={{1,2},{2,1},{5,6},{6,5},{9,10},{10,9},{13,14},{14,13},{17,18},{18,... | collective-permute-start | bytes 15368 | tf_op jit(solution)/shard_map/ppermute | solution.py:113
  135.2 4.1 %sweep.8.refs_1_ = f32[6,14,128]{2,1,0:T(8,128)S(1)} custom-call(f32[3,16,128]{2,1,0:T(8,128)S(1)} %get-tuple-element.65.refs_0_, f32[6,14,128]{2,1,0:T(8,128)S(1)} %sweep.6.refs_1_, bf16[132,9,128,128]{3,2,1,0:T(8,128)(2,1)S(1)} %get-tuple-element.51.coef.refs_2_.refs_6_, f32[3,6,14,128]{3,2,1,0:T(8,128)S(1)} %get-tuple-element.61.refs_3_), custom_call_target="tpu_custom_call" | custom-call | tf_op jit(solution)/shard_map/sweep/pallas_call | solution.py:486
  139.4 2.6 %sweep.9 = (f32[3,16,128]{2,1,0:T(8,128)S(1)}, f32[8,1,128]{2,1,0:T(1,128)S(1)}, f32[8,1,128]{2,1,0:T(1,128)S(1)}) custom-call(f32[3,16,128]{2,1,0:T(8,128)S(1)} %get-tuple-element.65.refs_0_, f32[6,14,128]{2,1,0:T(8,128)S(1)} %sweep.6.refs_1_, f32[1,16,128]{2,1,0:T(8,128)S(1)} %get-tuple-element.111.refs_2_, f32[1,16,128]{2,1,0:T(8,128)S(1)} %get-tuple-element.110.refs_3_, ...), custom_call_target="tpu_custom_call" | custom-call | tf_op jit(solution)/shard_map/sweep/pallas_call | solution.py:486
  142.7 3.2 %collective-permute-start.17 = (f32[1,16,128]{2,1,0:T(8,128)S(1)}, f32[1,16,128]{2,1,0:T(8,128)S(1)}, u32[]{:S(2)}, u32[]{:S(2)}) collective-permute-start(f32[1,16,128]{2,1,0:T(8,128)S(1)} %get-tuple-element.101), channel_id=1, source_target_pairs={{4,8},{12,16},{20,24},{8,4},{16,12},{24,20},{5,9},{13,17},{21,25},... | collective-permute-start | bytes 24584 | tf_op jit(solution)/shard_map/ppermute | solution.py:113
  148.1 3.6 %collective-permute-start.19 = (f32[10,1,128]{2,1,0:T(1,128)S(1)}, f32[10,1,128]{2,1,0:T(1,128)S(1)}, u32[]{:S(2)}, u32[]{:S(2)}) collective-permute-start(f32[10,1,128]{2,1,0:T(1,128)S(1)} %get-tuple-element.121), channel_id=1, source_target_pairs={{1,2},{2,1},{5,6},{6,5},{9,10},{10,9},{13,14},{14,13},{17,18},{18,... | collective-permute-start | bytes 15368 | tf_op jit(solution)/shard_map/ppermute | solution.py:113
  151.7 4.1 %sweep.10 = (f32[6,14,128]{2,1,0:T(8,128)S(1)}, f32[6,14,128]{2,1,0:T(8,128)S(1)}) custom-call(f32[3,16,128]{2,1,0:T(8,128)S(1)} %get-tuple-element.71.refs_0_, f32[6,14,128]{2,1,0:T(8,128)S(1)} %sweep.8.refs_1_, bf16[132,9,128,128]{3,2,1,0:T(8,128)(2,1)S(1)} %get-tuple-element.51.coef.refs_2_.refs_6_, f32[3,6,14,128]{3,2,1,0:T(8,128)S(1)} %get-tuple-element.61.refs_3_), custom_call_target="tpu_custom_call" | custom-call | tf_op jit(solution)/shard_map/sweep/pallas_call | solution.py:486
  155.9 2.6 %sweep.11 = (f32[3,16,128]{2,1,0:T(8,128)S(1)}, f32[8,1,128]{2,1,0:T(1,128)S(1)}, f32[8,1,128]{2,1,0:T(1,128)S(1)}, f32[3,16,128]{2,1,0:T(8,128)S(1)}) custom-call(f32[3,16,128]{2,1,0:T(8,128)S(1)} %get-tuple-element.71.refs_0_, f32[6,14,128]{2,1,0:T(8,128)S(1)} %sweep.8.refs_1_, f32[1,16,128]{2,1,0:T(8,128)S(1)} %get-tuple-element.109.refs_2_, ...), custom_call_target="tpu_custom_call" | custom-call | tf_op jit(solution)/shard_map/sweep/pallas_call | solution.py:486
  161.8 3.0 %collective-permute-done.21 = f32[1,16,128]{2,1,0:T(8,128)S(1)} collective-permute-done((f32[1,16,128]{2,1,0:T(8,128)S(1)}, f32[1,16,128]{2,1,0:T(8,128)S(1)}, u32[]{:S(2)}, u32[]{:S(2)}) %collective-permute-start.21) | collective-permute-done | bytes 8224 | tf_op jit(solution)/shard_map/ppermute | solution.py:113
  164.8 3.4 %collective-permute-start.23 = (f32[10,1,128]{2,1,0:T(1,128)S(1)}, f32[10,1,128]{2,1,0:T(1,128)S(1)}, u32[]{:S(2)}, u32[]{:S(2)}) collective-permute-start(f32[10,1,128]{2,1,0:T(1,128)S(1)} %get-tuple-element.117), channel_id=1, source_target_pairs={{1,2},{2,1},{5,6},{6,5},{9,10},{10,9},{13,14},{14,13},{17,18},{18,... | collective-permute-start | bytes 15368 | tf_op jit(solution)/shard_map/ppermute | solution.py:113
  168.2 13.1 %push.2.refs_12_ = f32[2,6,14,128]{3,2,1,0:T(8,128)S(1)} custom-call(f32[3,16,128]{2,1,0:T(8,128)S(1)} %get-tuple-element.78.refs_0_, f32[6,14,128]{2,1,0:T(8,128)S(1)} %get-tuple-element.79.refs_1_, f32[10,18,8,128]{3,2,1,0:T(8,128)} %drift.1.source.fresh.refs_2_.refs_6_, ...), custom_call_target="tpu_custom_call" | custom-call | tf_op jit(solution)/shard_map/push/pallas_call | solution.py:583
  181.3 9.2 %push.3 = (f32[8,16,128]{2,1,0:T(8,128)}, f32[2,8,16,128]{3,2,1,0:T(8,128)}) custom-call(f32[3,16,128]{2,1,0:T(8,128)S(1)} %get-tuple-element.78.refs_0_, f32[6,14,128]{2,1,0:T(8,128)S(1)} %get-tuple-element.79.refs_1_, f32[1,16,128]{2,1,0:T(8,128)S(1)} %get-tuple-element.107.refs_2_, f32[1,16,128]{2,1,0:T(8,128)S(1)} %get-tuple-element.106.refs_3_, ...), custom_call_target="tpu_custom_call" | custom-call | tf_op jit(solution)/shard_map/push/pallas_call | solution.py:583
  (78 shorter events, 25.2 us)
Async XLA Ops:
  3.6 4.1 %collective-permute-start.2 = (f32[8,128]{1,0:T(8,128)S(1)}, f32[8,128]{1,0:T(8,128)S(1)}, u32[]{:S(2)}, u32[]{:S(2)}) collective-permute-start(f32[8,128]{1,0:T(8,128)S(1)} %get-tuple-element.46), channel_id=1, source_target_pairs={{0,1},{1,0},{2,3},{3,2},{4,5},{5,4},{6,7},{7,6},{8,9},{9,8},{10,11... | collective-permute-start | bytes 12296 | tf_op jit(solution)/shard_map/ppermute | solution.py:192
  4.4 5.9 %collective-permute-start.1 = (f32[2,16,8,128]{3,2,1,0:T(8,128)S(1)}, f32[2,16,8,128]{3,2,1,0:T(8,128)S(1)}, u32[]{:S(2)}, u32[]{:S(2)}) collective-permute-start(f32[2,16,8,128]{3,2,1,0:T(8,128)S(1)} %get-tuple-element.86), channel_id=1, source_target_pairs={{0,4},{8,12},{16,20},{24,28},{4,0},{12,8},{20,16},{28,24},{1,5},{9... | collective-permute-start | bytes 393224 | tf_op jit(solution)/shard_map/ppermute | solution.py:113
  5.7 7.6 %collective-permute-start = (f32[2,16,8,128]{3,2,1,0:T(8,128)S(1)}, f32[2,16,8,128]{3,2,1,0:T(8,128)S(1)}, u32[]{:S(2)}, u32[]{:S(2)}) collective-permute-start(f32[2,16,8,128]{3,2,1,0:T(8,128)S(1)} %get-tuple-element.87), channel_id=1, source_target_pairs={{4,8},{12,16},{20,24},{8,4},{16,12},{24,20},{5,9},{13,17},{21,25},... | collective-permute-start | bytes 393224 | tf_op jit(solution)/shard_map/ppermute | solution.py:113
  7.7 2.5 %collective-permute-start.3 = (f32[8,128]{1,0:T(8,128)S(1)}, f32[8,128]{1,0:T(8,128)S(1)}, u32[]{:S(2)}, u32[]{:S(2)}) collective-permute-start(f32[8,128]{1,0:T(8,128)S(1)} %max.15), channel_id=1, source_target_pairs={{0,2},{1,3},{2,0},{3,1},{4,6},{5,7},{6,4},{7,5},{8,10},{9,11},{10,... | collective-permute-start | bytes 12296 | tf_op jit(solution)/shard_map/ppermute | solution.py:192
  13.3 12.6 %collective-permute-start.8 = (f32[12,2,8,128]{3,2,1,0:T(8,128)S(1)}, f32[12,2,8,128]{3,2,1,0:T(8,128)S(1)}, u32[]{:S(2)}, u32[]{:S(2)}) collective-permute-start(f32[12,2,8,128]{3,2,1,0:T(8,128)S(1)} %get-tuple-element.92), channel_id=1, source_target_pairs={{0,1},{2,3},{1,0},{3,2},{4,5},{6,7},{5,4},{7,6},{8,9},{10,11},{9,8... | collective-permute-start | bytes 294920 | tf_op jit(solution)/shard_map/ppermute | solution.py:113
  14.5 11.4 %collective-permute-start.7 = (f32[12,2,8,128]{3,2,1,0:T(8,128)S(1)}, f32[12,2,8,128]{3,2,1,0:T(8,128)S(1)}, u32[]{:S(2)}, u32[]{:S(2)}) collective-permute-start(f32[12,2,8,128]{3,2,1,0:T(8,128)S(1)} %get-tuple-element.93), channel_id=1, source_target_pairs={{1,2},{2,1},{5,6},{6,5},{9,10},{10,9},{13,14},{14,13},{17,18},{18,... | collective-permute-start | bytes 294920 | tf_op jit(solution)/shard_map/ppermute | solution.py:113
  17.5 2.5 %collective-permute-start.4 = (f32[8,128]{1,0:T(8,128)S(1)}, f32[8,128]{1,0:T(8,128)S(1)}, u32[]{:S(2)}, u32[]{:S(2)}) collective-permute-start(f32[8,128]{1,0:T(8,128)S(1)} %max.16), channel_id=1, source_target_pairs={{0,4},{4,0},{8,12},{12,8},{16,20},{20,16},{24,28},{28,24},{1,5},{5... | collective-permute-start | bytes 12296 | tf_op jit(solution)/shard_map/ppermute | solution.py:192
  22.5 3.4 %collective-permute-start.6 = (f32[8,128]{1,0:T(8,128)S(1)}, f32[8,128]{1,0:T(8,128)S(1)}, u32[]{:S(2)}, u32[]{:S(2)}) collective-permute-start(f32[8,128]{1,0:T(8,128)S(1)} %max.18), channel_id=1, source_target_pairs={{0,16},{4,20},{8,24},{12,28},{16,0},{20,4},{24,8},{28,12},{1,17},{... | collective-permute-start | bytes 12296 | tf_op jit(solution)/shard_map/ppermute | solution.py:192
  90.4 21.5 %collective-permute-start.10 = (f32[1,16,128]{2,1,0:T(8,128)S(1)}, f32[1,16,128]{2,1,0:T(8,128)S(1)}, u32[]{:S(2)}, u32[]{:S(2)}) collective-permute-start(f32[1,16,128]{2,1,0:T(8,128)S(1)} %get-tuple-element.104), channel_id=1, source_target_pairs={{0,4},{8,12},{16,20},{24,28},{4,0},{12,8},{20,16},{28,24},{1,5},{9... | collective-permute-start | bytes 24584 | tf_op jit(solution)/shard_map/ppermute | solution.py:113
  90.7 21.1 %collective-permute-start.9 = (f32[1,16,128]{2,1,0:T(8,128)S(1)}, f32[1,16,128]{2,1,0:T(8,128)S(1)}, u32[]{:S(2)}, u32[]{:S(2)}) collective-permute-start(f32[1,16,128]{2,1,0:T(8,128)S(1)} %get-tuple-element.105), channel_id=1, source_target_pairs={{4,8},{12,16},{20,24},{8,4},{16,12},{24,20},{5,9},{13,17},{21,25},... | collective-permute-start | bytes 24584 | tf_op jit(solution)/shard_map/ppermute | solution.py:113
  111.9 10.9 %collective-permute-start.12 = (f32[10,1,128]{2,1,0:T(1,128)S(1)}, f32[10,1,128]{2,1,0:T(1,128)S(1)}, u32[]{:S(2)}, u32[]{:S(2)}) collective-permute-start(f32[10,1,128]{2,1,0:T(1,128)S(1)} %get-tuple-element.128), channel_id=1, source_target_pairs={{0,1},{2,3},{1,0},{3,2},{4,5},{6,7},{5,4},{7,6},{8,9},{10,11},{9,8... | collective-permute-start | bytes 15368 | tf_op jit(solution)/shard_map/ppermute | solution.py:113
  113.6 9.2 %collective-permute-start.11 = (f32[10,1,128]{2,1,0:T(1,128)S(1)}, f32[10,1,128]{2,1,0:T(1,128)S(1)}, u32[]{:S(2)}, u32[]{:S(2)}) collective-permute-start(f32[10,1,128]{2,1,0:T(1,128)S(1)} %get-tuple-element.129), channel_id=1, source_target_pairs={{1,2},{2,1},{5,6},{6,5},{9,10},{10,9},{13,14},{14,13},{17,18},{18,... | collective-permute-start | bytes 15368 | tf_op jit(solution)/shard_map/ppermute | solution.py:113
  125.5 3.3 %collective-permute-start.14 = (f32[1,16,128]{2,1,0:T(8,128)S(1)}, f32[1,16,128]{2,1,0:T(8,128)S(1)}, u32[]{:S(2)}, u32[]{:S(2)}) collective-permute-start(f32[1,16,128]{2,1,0:T(8,128)S(1)} %get-tuple-element.102), channel_id=1, source_target_pairs={{0,4},{8,12},{16,20},{24,28},{4,0},{12,8},{20,16},{28,24},{1,5},{9... | collective-permute-start | bytes 24584 | tf_op jit(solution)/shard_map/ppermute | solution.py:113
  126.5 5.3 %collective-permute-start.13 = (f32[1,16,128]{2,1,0:T(8,128)S(1)}, f32[1,16,128]{2,1,0:T(8,128)S(1)}, u32[]{:S(2)}, u32[]{:S(2)}) collective-permute-start(f32[1,16,128]{2,1,0:T(8,128)S(1)} %get-tuple-element.103), channel_id=1, source_target_pairs={{4,8},{12,16},{20,24},{8,4},{16,12},{24,20},{5,9},{13,17},{21,25},... | collective-permute-start | bytes 24584 | tf_op jit(solution)/shard_map/ppermute | solution.py:113
  131.8 7.5 %collective-permute-start.16 = (f32[10,1,128]{2,1,0:T(1,128)S(1)}, f32[10,1,128]{2,1,0:T(1,128)S(1)}, u32[]{:S(2)}, u32[]{:S(2)}) collective-permute-start(f32[10,1,128]{2,1,0:T(1,128)S(1)} %get-tuple-element.124), channel_id=1, source_target_pairs={{0,1},{2,3},{1,0},{3,2},{4,5},{6,7},{5,4},{7,6},{8,9},{10,11},{9,8... | collective-permute-start | bytes 15368 | tf_op jit(solution)/shard_map/ppermute | solution.py:113
  131.9 7.5 %collective-permute-start.15 = (f32[10,1,128]{2,1,0:T(1,128)S(1)}, f32[10,1,128]{2,1,0:T(1,128)S(1)}, u32[]{:S(2)}, u32[]{:S(2)}) collective-permute-start(f32[10,1,128]{2,1,0:T(1,128)S(1)} %get-tuple-element.125), channel_id=1, source_target_pairs={{1,2},{2,1},{5,6},{6,5},{9,10},{10,9},{13,14},{14,13},{17,18},{18,... | collective-permute-start | bytes 15368 | tf_op jit(solution)/shard_map/ppermute | solution.py:113
  142.0 3.8 %collective-permute-start.18 = (f32[1,16,128]{2,1,0:T(8,128)S(1)}, f32[1,16,128]{2,1,0:T(8,128)S(1)}, u32[]{:S(2)}, u32[]{:S(2)}) collective-permute-start(f32[1,16,128]{2,1,0:T(8,128)S(1)} %get-tuple-element.100), channel_id=1, source_target_pairs={{0,4},{8,12},{16,20},{24,28},{4,0},{12,8},{20,16},{28,24},{1,5},{9... | collective-permute-start | bytes 24584 | tf_op jit(solution)/shard_map/ppermute | solution.py:113
  142.7 5.3 %collective-permute-start.17 = (f32[1,16,128]{2,1,0:T(8,128)S(1)}, f32[1,16,128]{2,1,0:T(8,128)S(1)}, u32[]{:S(2)}, u32[]{:S(2)}) collective-permute-start(f32[1,16,128]{2,1,0:T(8,128)S(1)} %get-tuple-element.101), channel_id=1, source_target_pairs={{4,8},{12,16},{20,24},{8,4},{16,12},{24,20},{5,9},{13,17},{21,25},... | collective-permute-start | bytes 24584 | tf_op jit(solution)/shard_map/ppermute | solution.py:113
  148.0 7.8 %collective-permute-start.20 = (f32[10,1,128]{2,1,0:T(1,128)S(1)}, f32[10,1,128]{2,1,0:T(1,128)S(1)}, u32[]{:S(2)}, u32[]{:S(2)}) collective-permute-start(f32[10,1,128]{2,1,0:T(1,128)S(1)} %get-tuple-element.120), channel_id=1, source_target_pairs={{0,1},{2,3},{1,0},{3,2},{4,5},{6,7},{5,4},{7,6},{8,9},{10,11},{9,8... | collective-permute-start | bytes 15368 | tf_op jit(solution)/shard_map/ppermute | solution.py:113
  148.1 7.8 %collective-permute-start.19 = (f32[10,1,128]{2,1,0:T(1,128)S(1)}, f32[10,1,128]{2,1,0:T(1,128)S(1)}, u32[]{:S(2)}, u32[]{:S(2)}) collective-permute-start(f32[10,1,128]{2,1,0:T(1,128)S(1)} %get-tuple-element.121), channel_id=1, source_target_pairs={{1,2},{2,1},{5,6},{6,5},{9,10},{10,9},{13,14},{14,13},{17,18},{18,... | collective-permute-start | bytes 15368 | tf_op jit(solution)/shard_map/ppermute | solution.py:113
  158.5 3.3 %collective-permute-start.22 = (f32[1,16,128]{2,1,0:T(8,128)S(1)}, f32[1,16,128]{2,1,0:T(8,128)S(1)}, u32[]{:S(2)}, u32[]{:S(2)}) collective-permute-start(f32[1,16,128]{2,1,0:T(8,128)S(1)} %get-tuple-element.98), channel_id=1, source_target_pairs={{0,4},{8,12},{16,20},{24,28},{4,0},{12,8},{20,16},{28,24},{1,5},{9... | collective-permute-start | bytes 24584 | tf_op jit(solution)/shard_map/ppermute | solution.py:113
  159.4 5.3 %collective-permute-start.21 = (f32[1,16,128]{2,1,0:T(8,128)S(1)}, f32[1,16,128]{2,1,0:T(8,128)S(1)}, u32[]{:S(2)}, u32[]{:S(2)}) collective-permute-start(f32[1,16,128]{2,1,0:T(8,128)S(1)} %get-tuple-element.99), channel_id=1, source_target_pairs={{4,8},{12,16},{20,24},{8,4},{16,12},{24,20},{5,9},{13,17},{21,25},... | collective-permute-start | bytes 24584 | tf_op jit(solution)/shard_map/ppermute | solution.py:113
  164.8 16.5 %collective-permute-start.24 = (f32[10,1,128]{2,1,0:T(1,128)S(1)}, f32[10,1,128]{2,1,0:T(1,128)S(1)}, u32[]{:S(2)}, u32[]{:S(2)}) collective-permute-start(f32[10,1,128]{2,1,0:T(1,128)S(1)} %get-tuple-element.116), channel_id=1, source_target_pairs={{0,1},{2,3},{1,0},{3,2},{4,5},{6,7},{5,4},{7,6},{8,9},{10,11},{9,8... | collective-permute-start | bytes 15368 | tf_op jit(solution)/shard_map/ppermute | solution.py:113
  164.8 16.4 %collective-permute-start.23 = (f32[10,1,128]{2,1,0:T(1,128)S(1)}, f32[10,1,128]{2,1,0:T(1,128)S(1)}, u32[]{:S(2)}, u32[]{:S(2)}) collective-permute-start(f32[10,1,128]{2,1,0:T(1,128)S(1)} %get-tuple-element.117), channel_id=1, source_target_pairs={{1,2},{2,1},{5,6},{6,5},{9,10},{10,9},{13,14},{14,13},{17,18},{18,... | collective-permute-start | bytes 15368 | tf_op jit(solution)/shard_map/ppermute | solution.py:113
  (3 other events, 3.8 us)

commit v14 on v12

--- a/solution.py
+++ b/solution.py
@@ -611,8 +611,10 @@
     for step in range(1, SWEEPS):
         last = step == SWEEPS - 1
         before = (edge_pv, inner_pv)
+        inner_pv, *inner_pressure = sweep(kappa, last, False, shape, before, (), coef, inner_sums)
+        if step > 1:
+            above, below, inner_pv = lax.optimization_barrier((above, below, inner_pv))
         left, right = exchange_sides(even, above, below, *sides)
-        inner_pv, *inner_pressure = sweep(kappa, last, False, shape, before, (), coef, inner_sums)
         left, right, inner_pv = lax.optimization_barrier((left, right, inner_pv))
         halo = (above, below, left, right)
         edge_pv, *rest = sweep(kappa, last, True, shape, before, halo, coef, edge_sums)

time: 191 us -> 190 us (level)
  no operation moved by 1% of the time
where the time goes in v14:
time: 190 us; the launch traced here: 189 us
  Pallas kernels  127 us (67%)
  starting transfers between devices  41.7 us (22%)
  waiting for transfers between devices  17.7 us (9%)
    pallas_call x1, Pallas kernels, setup(): call(setup_kernel, in_specs=[hbm], out_specs=(vmem, hbm, hbm), out_shape=...  49.9 us
    ppermute x20, starting transfers between devices, swap(): return lax.ppermute(value, axis, pairs + [(j, i) for i, j in pairs])  38 us
    pallas_call x2, Pallas kernels, first_sweep(): call(functools.partial(first_kernel, kappa, edge), grid=(groups,), in_spe...  30 us
    pallas_call x2, Pallas kernels, push(): call(functools.partial(push_kernel, kappa, edge, len(args)), grid=(groups...  22.2 us
    pallas_call x6, Pallas kernels, sweep(): call(functools.partial(sweep_kernel, kappa, last, edge, rows, cols, len(a...  20.2 us
    ppermute x20, waiting for transfers between devices, swap(): return lax.ppermute(value, axis, pairs + [(j, i) for i, j in pairs])  9.81 us
    ppermute x5, waiting for transfers between devices, largest(): value = jnp.maximum(value, lax.ppermute(value, axis, pairs))  7.93 us
  transfers between devices with their start and end apart: 25, of which 8 were waited for; matrix products, arithmetic and copies ran while one was open for 0% of the time, Pallas kernels for 23%

profile of v14, /device:TPU:17, one launch (start us, length us, event | category | flops | bytes accessed | tf_op | source)
XLA Modules:
  0.0 188.7 jit_solution(5015873504203302453)
XLA Ops:
  10.3 3.0 %collective-permute-done = f32[2,16,8,128]{3,2,1,0:T(8,128)S(1)} collective-permute-done((f32[2,16,8,128]{3,2,1,0:T(8,128)S(1)}, f32[2,16,8,128]{3,2,1,0:T(8,128)S(1)}, u32[]{:S(2)}, u32[]{:S(2)}) %collective-permute-start) | collective-permute-done | bytes 131104 | tf_op jit(solution)/shard_map/ppermute | solution.py:113
  14.5 3.0 %collective-permute-start.7 = (f32[12,2,8,128]{3,2,1,0:T(8,128)S(1)}, f32[12,2,8,128]{3,2,1,0:T(8,128)S(1)}, u32[]{:S(2)}, u32[]{:S(2)}) collective-permute-start(f32[12,2,8,128]{3,2,1,0:T(8,128)S(1)} %get-tuple-element.105), channel_id=1, source_target_pairs={{1,2},{2,1},{5,6},{6,5},{9,10},{10,9},{13,14},{14,13},{17,18},{18,... | collective-permute-start | bytes 294920 | tf_op jit(solution)/shard_map/ppermute | solution.py:113
  22.5 3.4 %collective-permute-done.6 = f32[8,128]{1,0:T(8,128)S(1)} collective-permute-done((f32[8,128]{1,0:T(8,128)S(1)}, f32[8,128]{1,0:T(8,128)S(1)}, u32[]{:S(2)}, u32[]{:S(2)}) %collective-permute-start.6) | collective-permute-done | bytes 4128 | tf_op jit(solution)/shard_map/ppermute | solution.py:192
  25.9 2.6 %drift.1.source.fresh.refs_2_.refs_6_ = f32[10,18,8,128]{3,2,1,0:T(8,128)} custom-call(f32[8,128]{1,0:T(8,128)S(1)} %max.19.top, f32[8,16,8,128]{3,2,1,0:T(8,128)S(1)} %get-tuple-element.51.center, f32[2,16,8,128]{3,2,1,0:T(8,128)S(1)} %get-tuple-element.54.above, f32[2,16,8,128]{3,2,1,0:T(8,128)S(1)} %get-tuple-element.55.below, ...), custom_call_target="tpu_custom_call" | custom-call | tf_op jit(solution)/shard_map/drift/pallas_call | solution.py:230
  28.5 49.9 %setup.1 = (bf16[132,9,128,128]{3,2,1,0:T(8,128)(2,1)S(1)}, bf16[3,16,9,128,128]{4,3,2,1,0:T(8,128)(2,1)}, bf16[6,14,9,128,128]{4,3,2,1,0:T(8,128)(2,1)}) custom-call(f32[10,18,8,128]{3,2,1,0:T(8,128)} %drift.1.source.fresh.refs_2_.refs_6_), custom_call_target="tpu_custom_call" | custom-call | tf_op jit(solution)/shard_map/setup/pallas_call | solution.py:323
  78.4 11.9 %first_sweep.2 = (f32[3,3,16,128]{3,2,1,0:T(8,128)S(1)}, f32[3,16,128]{2,1,0:T(8,128)S(1)}, f32[8,1,128]{2,1,0:T(1,128)S(1)}, f32[8,1,128]{2,1,0:T(1,128)S(1)}) custom-call(f32[10,18,8,128]{3,2,1,0:T(8,128)} %drift.1.source.fresh.refs_2_.refs_6_, bf16[132,9,128,128]{3,2,1,0:T(8,128)(2,1)S(1)} %get-tuple-element.57.coef.refs_2_.refs_6_, ...), custom_call_target="tpu_custom_call" | custom-call | tf_op jit(solution)/shard_map/first_sweep/pallas_call | solution.py:414
  90.7 3.0 %collective-permute-start.9 = (f32[1,16,128]{2,1,0:T(8,128)S(1)}, f32[1,16,128]{2,1,0:T(8,128)S(1)}, u32[]{:S(2)}, u32[]{:S(2)}) collective-permute-start(f32[1,16,128]{2,1,0:T(8,128)S(1)} %get-tuple-element.117), channel_id=1, source_target_pairs={{4,8},{12,16},{20,24},{8,4},{16,12},{24,20},{5,9},{13,17},{21,25},... | collective-permute-start | bytes 24584 | tf_op jit(solution)/shard_map/ppermute | solution.py:113
  93.6 18.1 %first_sweep.3 = (f32[3,6,14,128]{3,2,1,0:T(8,128)S(1)}, f32[6,14,128]{2,1,0:T(8,128)S(1)}) custom-call(f32[10,18,8,128]{3,2,1,0:T(8,128)} %drift.1.source.fresh.refs_2_.refs_6_, bf16[132,9,128,128]{3,2,1,0:T(8,128)(2,1)S(1)} %get-tuple-element.57.coef.refs_2_.refs_6_, ...), custom_call_target="tpu_custom_call" | custom-call | tf_op jit(solution)/shard_map/first_sweep/pallas_call | solution.py:414
  113.6 4.9 %collective-permute-start.11 = (f32[10,1,128]{2,1,0:T(1,128)S(1)}, f32[10,1,128]{2,1,0:T(1,128)S(1)}, u32[]{:S(2)}, u32[]{:S(2)}) collective-permute-start(f32[10,1,128]{2,1,0:T(1,128)S(1)} %get-tuple-element.141), channel_id=1, source_target_pairs={{1,2},{2,1},{5,6},{6,5},{9,10},{10,9},{13,14},{14,13},{17,18},{18,... | collective-permute-start | bytes 15368 | tf_op jit(solution)/shard_map/ppermute | solution.py:113
  118.5 4.1 %sweep.6.refs_1_ = f32[6,14,128]{2,1,0:T(8,128)S(1)} custom-call(f32[3,16,128]{2,1,0:T(8,128)S(1)} %get-tuple-element.59.refs_0_, f32[6,14,128]{2,1,0:T(8,128)S(1)} %get-tuple-element.62.refs_1_, bf16[132,9,128,128]{3,2,1,0:T(8,128)(2,1)S(1)} %get-tuple-element.57.coef.refs_2_.refs_6_, f32[3,6,14,128]{3,2,1,0:T(8,128)S(1)} %get-tuple-element.67.refs_3_), custom_call_target="tpu_custom_call" | custom-call | tf_op jit(solution)/shard_map/sweep/pallas_call | solution.py:486
  122.6 2.6 %sweep.7 = (f32[3,16,128]{2,1,0:T(8,128)S(1)}, f32[8,1,128]{2,1,0:T(1,128)S(1)}, f32[8,1,128]{2,1,0:T(1,128)S(1)}) custom-call(f32[3,16,128]{2,1,0:T(8,128)S(1)} %get-tuple-element.59.refs_0_, f32[6,14,128]{2,1,0:T(8,128)S(1)} %get-tuple-element.62.refs_1_, f32[1,16,128]{2,1,0:T(8,128)S(1)} %get-tuple-element.63.refs_2_, ...), custom_call_target="tpu_custom_call" | custom-call | tf_op jit(solution)/shard_map/sweep/pallas_call | solution.py:486
  126.2 2.3 %collective-permute-start.13 = (f32[1,16,128]{2,1,0:T(8,128)S(1)}, f32[1,16,128]{2,1,0:T(8,128)S(1)}, u32[]{:S(2)}, u32[]{:S(2)}) collective-permute-start(f32[1,16,128]{2,1,0:T(8,128)S(1)} %get-tuple-element.115), channel_id=1, source_target_pairs={{4,8},{12,16},{20,24},{8,4},{16,12},{24,20},{5,9},{13,17},{21,25},... | collective-permute-start | bytes 24584 | tf_op jit(solution)/shard_map/ppermute | solution.py:113
  128.5 4.1 %sweep.8.refs_1_ = f32[6,14,128]{2,1,0:T(8,128)S(1)} custom-call(f32[3,16,128]{2,1,0:T(8,128)S(1)} %get-tuple-element.71.refs_0_, f32[6,14,128]{2,1,0:T(8,128)S(1)} %sweep.6.refs_1_, bf16[132,9,128,128]{3,2,1,0:T(8,128)(2,1)S(1)} %get-tuple-element.57.coef.refs_2_.refs_6_, f32[3,6,14,128]{3,2,1,0:T(8,128)S(1)} %get-tuple-element.67.refs_3_), custom_call_target="tpu_custom_call" | custom-call | tf_op jit(solution)/shard_map/sweep/pallas_call | solution.py:486
  132.8 2.4 %collective-permute-start.15 = (f32[10,1,128]{2,1,0:T(1,128)S(1)}, f32[10,1,128]{2,1,0:T(1,128)S(1)}, u32[]{:S(2)}, u32[]{:S(2)}) collective-permute-start(f32[10,1,128]{2,1,0:T(1,128)S(1)} %get-tuple-element.137), channel_id=1, source_target_pairs={{1,2},{2,1},{5,6},{6,5},{9,10},{10,9},{13,14},{14,13},{17,18},{18,... | collective-permute-start | bytes 15368 | tf_op jit(solution)/shard_map/ppermute | solution.py:113
  135.2 2.5 %collective-permute-done.15 = f32[10,1,128]{2,1,0:T(1,128)S(1)} collective-permute-done((f32[10,1,128]{2,1,0:T(1,128)S(1)}, f32[10,1,128]{2,1,0:T(1,128)S(1)}, u32[]{:S(2)}, u32[]{:S(2)}) %collective-permute-start.15) | collective-permute-done | bytes 5152 | tf_op jit(solution)/shard_map/ppermute | solution.py:113
  137.7 2.6 %sweep.9 = (f32[3,16,128]{2,1,0:T(8,128)S(1)}, f32[8,1,128]{2,1,0:T(1,128)S(1)}, f32[8,1,128]{2,1,0:T(1,128)S(1)}) custom-call(f32[3,16,128]{2,1,0:T(8,128)S(1)} %get-tuple-element.71.refs_0_, f32[6,14,128]{2,1,0:T(8,128)S(1)} %sweep.6.refs_1_, f32[1,16,128]{2,1,0:T(8,128)S(1)} %get-tuple-element.73.refs_2_, f32[1,16,128]{2,1,0:T(8,128)S(1)} %get-tuple-element.74.refs_3_, ...), custom_call_target="tpu_custom_call" | custom-call | tf_op jit(solution)/shard_map/sweep/pallas_call | solution.py:486
  141.7 2.7 %collective-permute-start.17 = (f32[1,16,128]{2,1,0:T(8,128)S(1)}, f32[1,16,128]{2,1,0:T(8,128)S(1)}, u32[]{:S(2)}, u32[]{:S(2)}) collective-permute-start(f32[1,16,128]{2,1,0:T(8,128)S(1)} %get-tuple-element.113), channel_id=1, source_target_pairs={{4,8},{12,16},{20,24},{8,4},{16,12},{24,20},{5,9},{13,17},{21,25},... | collective-permute-start | bytes 24584 | tf_op jit(solution)/shard_map/ppermute | solution.py:113
  144.3 4.1 %sweep.10 = (f32[6,14,128]{2,1,0:T(8,128)S(1)}, f32[6,14,128]{2,1,0:T(8,128)S(1)}) custom-call(f32[3,16,128]{2,1,0:T(8,128)S(1)} %get-tuple-element.80.refs_0_, f32[6,14,128]{2,1,0:T(8,128)S(1)} %sweep.8.refs_1_, bf16[132,9,128,128]{3,2,1,0:T(8,128)(2,1)S(1)} %get-tuple-element.57.coef.refs_2_.refs_6_, f32[3,6,14,128]{3,2,1,0:T(8,128)S(1)} %get-tuple-element.67.refs_3_), custom_call_target="tpu_custom_call" | custom-call | tf_op jit(solution)/shard_map/sweep/pallas_call | solution.py:486
  148.6 2.8 %collective-permute-start.19 = (f32[10,1,128]{2,1,0:T(1,128)S(1)}, f32[10,1,128]{2,1,0:T(1,128)S(1)}, u32[]{:S(2)}, u32[]{:S(2)}) collective-permute-start(f32[10,1,128]{2,1,0:T(1,128)S(1)} %get-tuple-element.133), channel_id=1, source_target_pairs={{1,2},{2,1},{5,6},{6,5},{9,10},{10,9},{13,14},{14,13},{17,18},{18,... | collective-permute-start | bytes 15368 | tf_op jit(solution)/shard_map/ppermute | solution.py:113
  153.5 2.6 %sweep.11 = (f32[3,16,128]{2,1,0:T(8,128)S(1)}, f32[8,1,128]{2,1,0:T(1,128)S(1)}, f32[8,1,128]{2,1,0:T(1,128)S(1)}, f32[3,16,128]{2,1,0:T(8,128)S(1)}) custom-call(f32[3,16,128]{2,1,0:T(8,128)S(1)} %get-tuple-element.80.refs_0_, f32[6,14,128]{2,1,0:T(8,128)S(1)} %sweep.8.refs_1_, f32[1,16,128]{2,1,0:T(8,128)S(1)} %get-tuple-element.83.refs_2_, ...), custom_call_target="tpu_custom_call" | custom-call | tf_op jit(solution)/shard_map/sweep/pallas_call | solution.py:486
  156.8 3.2 %collective-permute-start.21 = (f32[1,16,128]{2,1,0:T(8,128)S(1)}, f32[1,16,128]{2,1,0:T(8,128)S(1)}, u32[]{:S(2)}, u32[]{:S(2)}) collective-permute-start(f32[1,16,128]{2,1,0:T(8,128)S(1)} %get-tuple-element.111), channel_id=1, source_target_pairs={{4,8},{12,16},{20,24},{8,4},{16,12},{24,20},{5,9},{13,17},{21,25},... | collective-permute-start | bytes 24584 | tf_op jit(solution)/shard_map/ppermute | solution.py:113
  162.2 4.2 %collective-permute-start.23 = (f32[10,1,128]{2,1,0:T(1,128)S(1)}, f32[10,1,128]{2,1,0:T(1,128)S(1)}, u32[]{:S(2)}, u32[]{:S(2)}) collective-permute-start(f32[10,1,128]{2,1,0:T(1,128)S(1)} %get-tuple-element.129), channel_id=1, source_target_pairs={{1,2},{2,1},{5,6},{6,5},{9,10},{10,9},{13,14},{14,13},{17,18},{18,... | collective-permute-start | bytes 15368 | tf_op jit(solution)/shard_map/ppermute | solution.py:113
  166.4 13.1 %push.2.refs_12_ = f32[2,6,14,128]{3,2,1,0:T(8,128)S(1)} custom-call(f32[3,16,128]{2,1,0:T(8,128)S(1)} %get-tuple-element.90.refs_0_, f32[6,14,128]{2,1,0:T(8,128)S(1)} %get-tuple-element.91.refs_1_, f32[10,18,8,128]{3,2,1,0:T(8,128)} %drift.1.source.fresh.refs_2_.refs_6_, ...), custom_call_target="tpu_custom_call" | custom-call | tf_op jit(solution)/shard_map/push/pallas_call | solution.py:583
  179.5 9.2 %push.3 = (f32[8,16,128]{2,1,0:T(8,128)}, f32[2,8,16,128]{3,2,1,0:T(8,128)}) custom-call(f32[3,16,128]{2,1,0:T(8,128)S(1)} %get-tuple-element.90.refs_0_, f32[6,14,128]{2,1,0:T(8,128)S(1)} %get-tuple-element.91.refs_1_, f32[1,16,128]{2,1,0:T(8,128)S(1)} %get-tuple-element.119.refs_2_, f32[1,16,128]{2,1,0:T(8,128)S(1)} %get-tuple-element.118.refs_3_, ...), custom_call_target="tpu_custom_call" | custom-call | tf_op jit(solution)/shard_map/push/pallas_call | solution.py:583
  (78 shorter events, 25.4 us)
Async XLA Ops:
  3.6 4.1 %collective-permute-start.2 = (f32[8,128]{1,0:T(8,128)S(1)}, f32[8,128]{1,0:T(8,128)S(1)}, u32[]{:S(2)}, u32[]{:S(2)}) collective-permute-start(f32[8,128]{1,0:T(8,128)S(1)} %get-tuple-element.52), channel_id=1, source_target_pairs={{0,1},{1,0},{2,3},{3,2},{4,5},{5,4},{6,7},{7,6},{8,9},{9,8},{10,11... | collective-permute-start | bytes 12296 | tf_op jit(solution)/shard_map/ppermute | solution.py:192
  4.4 5.9 %collective-permute-start.1 = (f32[2,16,8,128]{3,2,1,0:T(8,128)S(1)}, f32[2,16,8,128]{3,2,1,0:T(8,128)S(1)}, u32[]{:S(2)}, u32[]{:S(2)}) collective-permute-start(f32[2,16,8,128]{3,2,1,0:T(8,128)S(1)} %get-tuple-element.98), channel_id=1, source_target_pairs={{0,4},{8,12},{16,20},{24,28},{4,0},{12,8},{20,16},{28,24},{1,5},{9... | collective-permute-start | bytes 393224 | tf_op jit(solution)/shard_map/ppermute | solution.py:113
  5.7 7.6 %collective-permute-start = (f32[2,16,8,128]{3,2,1,0:T(8,128)S(1)}, f32[2,16,8,128]{3,2,1,0:T(8,128)S(1)}, u32[]{:S(2)}, u32[]{:S(2)}) collective-permute-start(f32[2,16,8,128]{3,2,1,0:T(8,128)S(1)} %get-tuple-element.99), channel_id=1, source_target_pairs={{4,8},{12,16},{20,24},{8,4},{16,12},{24,20},{5,9},{13,17},{21,25},... | collective-permute-start | bytes 393224 | tf_op jit(solution)/shard_map/ppermute | solution.py:113
  7.7 2.5 %collective-permute-start.3 = (f32[8,128]{1,0:T(8,128)S(1)}, f32[8,128]{1,0:T(8,128)S(1)}, u32[]{:S(2)}, u32[]{:S(2)}) collective-permute-start(f32[8,128]{1,0:T(8,128)S(1)} %max.15), channel_id=1, source_target_pairs={{0,2},{1,3},{2,0},{3,1},{4,6},{5,7},{6,4},{7,5},{8,10},{9,11},{10,... | collective-permute-start | bytes 12296 | tf_op jit(solution)/shard_map/ppermute | solution.py:192
  13.3 12.6 %collective-permute-start.8 = (f32[12,2,8,128]{3,2,1,0:T(8,128)S(1)}, f32[12,2,8,128]{3,2,1,0:T(8,128)S(1)}, u32[]{:S(2)}, u32[]{:S(2)}) collective-permute-start(f32[12,2,8,128]{3,2,1,0:T(8,128)S(1)} %get-tuple-element.104), channel_id=1, source_target_pairs={{0,1},{2,3},{1,0},{3,2},{4,5},{6,7},{5,4},{7,6},{8,9},{10,11},{9,8... | collective-permute-start | bytes 294920 | tf_op jit(solution)/shard_map/ppermute | solution.py:113
  14.5 11.4 %collective-permute-start.7 = (f32[12,2,8,128]{3,2,1,0:T(8,128)S(1)}, f32[12,2,8,128]{3,2,1,0:T(8,128)S(1)}, u32[]{:S(2)}, u32[]{:S(2)}) collective-permute-start(f32[12,2,8,128]{3,2,1,0:T(8,128)S(1)} %get-tuple-element.105), channel_id=1, source_target_pairs={{1,2},{2,1},{5,6},{6,5},{9,10},{10,9},{13,14},{14,13},{17,18},{18,... | collective-permute-start | bytes 294920 | tf_op jit(solution)/shard_map/ppermute | solution.py:113
  17.5 2.5 %collective-permute-start.4 = (f32[8,128]{1,0:T(8,128)S(1)}, f32[8,128]{1,0:T(8,128)S(1)}, u32[]{:S(2)}, u32[]{:S(2)}) collective-permute-start(f32[8,128]{1,0:T(8,128)S(1)} %max.16), channel_id=1, source_target_pairs={{0,4},{4,0},{8,12},{12,8},{16,20},{20,16},{24,28},{28,24},{1,5},{5... | collective-permute-start | bytes 12296 | tf_op jit(solution)/shard_map/ppermute | solution.py:192
  22.5 3.4 %collective-permute-start.6 = (f32[8,128]{1,0:T(8,128)S(1)}, f32[8,128]{1,0:T(8,128)S(1)}, u32[]{:S(2)}, u32[]{:S(2)}) collective-permute-start(f32[8,128]{1,0:T(8,128)S(1)} %max.18), channel_id=1, source_target_pairs={{0,16},{4,20},{8,24},{12,28},{16,0},{20,4},{24,8},{28,12},{1,17},{... | collective-permute-start | bytes 12296 | tf_op jit(solution)/shard_map/ppermute | solution.py:192
  90.3 21.5 %collective-permute-start.10 = (f32[1,16,128]{2,1,0:T(8,128)S(1)}, f32[1,16,128]{2,1,0:T(8,128)S(1)}, u32[]{:S(2)}, u32[]{:S(2)}) collective-permute-start(f32[1,16,128]{2,1,0:T(8,128)S(1)} %get-tuple-element.116), channel_id=1, source_target_pairs={{0,4},{8,12},{16,20},{24,28},{4,0},{12,8},{20,16},{28,24},{1,5},{9... | collective-permute-start | bytes 24584 | tf_op jit(solution)/shard_map/ppermute | solution.py:113
  90.7 21.1 %collective-permute-start.9 = (f32[1,16,128]{2,1,0:T(8,128)S(1)}, f32[1,16,128]{2,1,0:T(8,128)S(1)}, u32[]{:S(2)}, u32[]{:S(2)}) collective-permute-start(f32[1,16,128]{2,1,0:T(8,128)S(1)} %get-tuple-element.117), channel_id=1, source_target_pairs={{4,8},{12,16},{20,24},{8,4},{16,12},{24,20},{5,9},{13,17},{21,25},... | collective-permute-start | bytes 24584 | tf_op jit(solution)/shard_map/ppermute | solution.py:113
  111.9 10.7 %collective-permute-start.12 = (f32[10,1,128]{2,1,0:T(1,128)S(1)}, f32[10,1,128]{2,1,0:T(1,128)S(1)}, u32[]{:S(2)}, u32[]{:S(2)}) collective-permute-start(f32[10,1,128]{2,1,0:T(1,128)S(1)} %get-tuple-element.140), channel_id=1, source_target_pairs={{0,1},{2,3},{1,0},{3,2},{4,5},{6,7},{5,4},{7,6},{8,9},{10,11},{9,8... | collective-permute-start | bytes 15368 | tf_op jit(solution)/shard_map/ppermute | solution.py:113
  113.6 9.0 %collective-permute-start.11 = (f32[10,1,128]{2,1,0:T(1,128)S(1)}, f32[10,1,128]{2,1,0:T(1,128)S(1)}, u32[]{:S(2)}, u32[]{:S(2)}) collective-permute-start(f32[10,1,128]{2,1,0:T(1,128)S(1)} %get-tuple-element.141), channel_id=1, source_target_pairs={{1,2},{2,1},{5,6},{6,5},{9,10},{10,9},{13,14},{14,13},{17,18},{18,... | collective-permute-start | bytes 15368 | tf_op jit(solution)/shard_map/ppermute | solution.py:113
  125.3 7.4 %collective-permute-start.14 = (f32[1,16,128]{2,1,0:T(8,128)S(1)}, f32[1,16,128]{2,1,0:T(8,128)S(1)}, u32[]{:S(2)}, u32[]{:S(2)}) collective-permute-start(f32[1,16,128]{2,1,0:T(8,128)S(1)} %get-tuple-element.114), channel_id=1, source_target_pairs={{0,4},{8,12},{16,20},{24,28},{4,0},{12,8},{20,16},{28,24},{1,5},{9... | collective-permute-start | bytes 24584 | tf_op jit(solution)/shard_map/ppermute | solution.py:113
  126.2 6.4 %collective-permute-start.13 = (f32[1,16,128]{2,1,0:T(8,128)S(1)}, f32[1,16,128]{2,1,0:T(8,128)S(1)}, u32[]{:S(2)}, u32[]{:S(2)}) collective-permute-start(f32[1,16,128]{2,1,0:T(8,128)S(1)} %get-tuple-element.115), channel_id=1, source_target_pairs={{4,8},{12,16},{20,24},{8,4},{16,12},{24,20},{5,9},{13,17},{21,25},... | collective-permute-start | bytes 24584 | tf_op jit(solution)/shard_map/ppermute | solution.py:113
  132.7 2.5 %collective-permute-start.16 = (f32[10,1,128]{2,1,0:T(1,128)S(1)}, f32[10,1,128]{2,1,0:T(1,128)S(1)}, u32[]{:S(2)}, u32[]{:S(2)}) collective-permute-start(f32[10,1,128]{2,1,0:T(1,128)S(1)} %get-tuple-element.136), channel_id=1, source_target_pairs={{0,1},{2,3},{1,0},{3,2},{4,5},{6,7},{5,4},{7,6},{8,9},{10,11},{9,8... | collective-permute-start | bytes 15368 | tf_op jit(solution)/shard_map/ppermute | solution.py:113
  132.8 4.9 %collective-permute-start.15 = (f32[10,1,128]{2,1,0:T(1,128)S(1)}, f32[10,1,128]{2,1,0:T(1,128)S(1)}, u32[]{:S(2)}, u32[]{:S(2)}) collective-permute-start(f32[10,1,128]{2,1,0:T(1,128)S(1)} %get-tuple-element.137), channel_id=1, source_target_pairs={{1,2},{2,1},{5,6},{6,5},{9,10},{10,9},{13,14},{14,13},{17,18},{18,... | collective-permute-start | bytes 15368 | tf_op jit(solution)/shard_map/ppermute | solution.py:113
  140.4 8.0 %collective-permute-start.18 = (f32[1,16,128]{2,1,0:T(8,128)S(1)}, f32[1,16,128]{2,1,0:T(8,128)S(1)}, u32[]{:S(2)}, u32[]{:S(2)}) collective-permute-start(f32[1,16,128]{2,1,0:T(8,128)S(1)} %get-tuple-element.112), channel_id=1, source_target_pairs={{0,4},{8,12},{16,20},{24,28},{4,0},{12,8},{20,16},{28,24},{1,5},{9... | collective-permute-start | bytes 24584 | tf_op jit(solution)/shard_map/ppermute | solution.py:113
  141.7 6.8 %collective-permute-start.17 = (f32[1,16,128]{2,1,0:T(8,128)S(1)}, f32[1,16,128]{2,1,0:T(8,128)S(1)}, u32[]{:S(2)}, u32[]{:S(2)}) collective-permute-start(f32[1,16,128]{2,1,0:T(8,128)S(1)} %get-tuple-element.113), channel_id=1, source_target_pairs={{4,8},{12,16},{20,24},{8,4},{16,12},{24,20},{5,9},{13,17},{21,25},... | collective-permute-start | bytes 24584 | tf_op jit(solution)/shard_map/ppermute | solution.py:113
  148.5 2.9 %collective-permute-start.20 = (f32[10,1,128]{2,1,0:T(1,128)S(1)}, f32[10,1,128]{2,1,0:T(1,128)S(1)}, u32[]{:S(2)}, u32[]{:S(2)}) collective-permute-start(f32[10,1,128]{2,1,0:T(1,128)S(1)} %get-tuple-element.132), channel_id=1, source_target_pairs={{0,1},{2,3},{1,0},{3,2},{4,5},{6,7},{5,4},{7,6},{8,9},{10,11},{9,8... | collective-permute-start | bytes 15368 | tf_op jit(solution)/shard_map/ppermute | solution.py:113
  148.6 4.9 %collective-permute-start.19 = (f32[10,1,128]{2,1,0:T(1,128)S(1)}, f32[10,1,128]{2,1,0:T(1,128)S(1)}, u32[]{:S(2)}, u32[]{:S(2)}) collective-permute-start(f32[10,1,128]{2,1,0:T(1,128)S(1)} %get-tuple-element.133), channel_id=1, source_target_pairs={{1,2},{2,1},{5,6},{6,5},{9,10},{10,9},{13,14},{14,13},{17,18},{18,... | collective-permute-start | bytes 15368 | tf_op jit(solution)/shard_map/ppermute | solution.py:113
  156.2 3.8 %collective-permute-start.22 = (f32[1,16,128]{2,1,0:T(8,128)S(1)}, f32[1,16,128]{2,1,0:T(8,128)S(1)}, u32[]{:S(2)}, u32[]{:S(2)}) collective-permute-start(f32[1,16,128]{2,1,0:T(8,128)S(1)} %get-tuple-element.110), channel_id=1, source_target_pairs={{0,4},{8,12},{16,20},{24,28},{4,0},{12,8},{20,16},{28,24},{1,5},{9... | collective-permute-start | bytes 24584 | tf_op jit(solution)/shard_map/ppermute | solution.py:113
  156.8 5.3 %collective-permute-start.21 = (f32[1,16,128]{2,1,0:T(8,128)S(1)}, f32[1,16,128]{2,1,0:T(8,128)S(1)}, u32[]{:S(2)}, u32[]{:S(2)}) collective-permute-start(f32[1,16,128]{2,1,0:T(8,128)S(1)} %get-tuple-element.111), channel_id=1, source_target_pairs={{4,8},{12,16},{20,24},{8,4},{16,12},{24,20},{5,9},{13,17},{21,25},... | collective-permute-start | bytes 24584 | tf_op jit(solution)/shard_map/ppermute | solution.py:113
  162.2 17.4 %collective-permute-start.24 = (f32[10,1,128]{2,1,0:T(1,128)S(1)}, f32[10,1,128]{2,1,0:T(1,128)S(1)}, u32[]{:S(2)}, u32[]{:S(2)}) collective-permute-start(f32[10,1,128]{2,1,0:T(1,128)S(1)} %get-tuple-element.128), channel_id=1, source_target_pairs={{0,1},{2,3},{1,0},{3,2},{4,5},{6,7},{5,4},{7,6},{8,9},{10,11},{9,8... | collective-permute-start | bytes 15368 | tf_op jit(solution)/shard_map/ppermute | solution.py:113
  162.2 17.3 %collective-permute-start.23 = (f32[10,1,128]{2,1,0:T(1,128)S(1)}, f32[10,1,128]{2,1,0:T(1,128)S(1)}, u32[]{:S(2)}, u32[]{:S(2)}) collective-permute-start(f32[10,1,128]{2,1,0:T(1,128)S(1)} %get-tuple-element.129), channel_id=1, source_target_pairs={{1,2},{2,1},{5,6},{6,5},{9,10},{10,9},{13,14},{14,13},{17,18},{18,... | collective-permute-start | bytes 15368 | tf_op jit(solution)/shard_map/ppermute | solution.py:113
  (3 other events, 3.8 us)
